TPU v7x, 32 devices: a whole 2x2x4 slice. The times are simulated.
32 devices in a mesh: grp: 4 (over x, core), mem: 8 (over z, y).
Axes of the slice: x: 2, y: 2, z: 4, core: 2. Of those that a mesh axis runs over, the one named last changes fastest.
Arguments:
- embeddings: bfloat16 [32768, 768], P(('grp', 'mem'))
- cluster: int32 [32768], P(('grp', 'mem')), may hold values from -1 to 7, as said below
- rank: int32 [32768], P(('grp', 'mem')), may hold values from -1 to 4095, as said below
Outputs:
- best_match: float32 [32768], P(('grp', 'mem'))
Inputs may be any that keep to these rules, and one draw needn't show every extreme that they name: cluster is -1 exactly where rank is -1. Ranks are distinct within a cluster; among the rows of one device, at most 16 have the same cluster // 2 and the same rank // 256, and every device reaches 16 for some such pair.
All inputs are finite; a program needn't handle non-finite values.
Results may differ from a plain program's by a relative error of at most 0.0004.
Values may be sent and summed in bfloat16 or wider, within the bound.
No kernel may reach another device: no remote copies, remote signals or barrier semaphores. Data moves between devices by JAX's collectives and lax.ppermute only.
A program may use at most 128 MiB of HBM per device.

v0:
```python
import jax
import jax.numpy as jnp
from jax import lax
from jax.sharding import PartitionSpec as P

CLUS_GRP = 2


def unit_rows(embeddings):
    wide = embeddings.astype(jnp.float32)
    total = jnp.sum(wide * wide, axis=1, keepdims=True)
    return (wide * lax.rsqrt(total + 1e-06)).astype(jnp.bfloat16)


def half_of(device, which):
    return 2 * device + which


def owner_of(half_id):
    return (half_id // 2, half_id % 2)


def on_device(embeddings, cluster, rank):
    rows_dev, width = embeddings.shape
    groups = lax.axis_size("grp")
    members = lax.axis_size("mem")
    devices = groups * members
    clus_grp = CLUS_GRP
    slot_dev = rows_dev // clus_grp
    half = slot_dev // 2
    quota = rows_dev // devices
    unit = unit_rows(embeddings)
    alive = cluster >= 0
    safe_cluster = jnp.maximum(cluster, 0)
    safe_rank = jnp.maximum(rank, 0)
    member_id, which_half = owner_of(safe_rank // half)
    target = safe_cluster // clus_grp * members + member_id
    slot = safe_cluster % clus_grp * slot_dev + which_half * half + safe_rank % half
    hits = (target[:, None] == jnp.arange(devices, dtype=jnp.int32)[None, :]) & alive[:, None]
    hit_count = hits.astype(jnp.int32)
    before = jnp.cumsum(hit_count, axis=0) - hit_count
    position = jnp.sum(jnp.where(hits, before, 0), axis=1)
    send_at = jnp.where(alive, target * quota + position, devices * quota)
    outgoing = jnp.zeros((devices * quota + 1, width), jnp.bfloat16).at[send_at].set(unit)[:-1]
    labels = (
        jnp.full((devices * quota + 1,), -1, jnp.int32)
        .at[send_at]
        .set(jnp.where(alive, slot, -1))[:-1]
    )
    arrived, arrived_slot = (
        lax.all_to_all(outgoing, ("grp", "mem"), split_axis=0, concat_axis=0, tiled=True),
        lax.all_to_all(labels, ("grp", "mem"), split_axis=0, concat_axis=0, tiled=True),
    )
    filled = arrived_slot >= 0
    place_at = jnp.where(filled, arrived_slot, clus_grp * slot_dev)
    grid = (
        jnp.zeros((clus_grp * slot_dev + 1, width), jnp.bfloat16)
        .at[place_at]
        .set(arrived)[:-1]
        .reshape(clus_grp, slot_dev, width)
    )
    present = (
        jnp.zeros((clus_grp * slot_dev + 1,), jnp.bfloat16)
        .at[place_at]
        .set(jnp.ones_like(arrived_slot, jnp.bfloat16))[:-1]
        .reshape(clus_grp, slot_dev)
    )
    me = lax.axis_index("mem")
    my_halves = (half_of(me, 0), half_of(me, 1))
    offsets = jnp.arange(half, dtype=jnp.int32)

    def column_ranks(spots):
        return half_of(spots // slot_dev, spots % slot_dev // half) * half + spots % half

    def compare(rows, row_half, cols, col_rank, col_live):
        sims = jnp.einsum("crd,cjd->crj", rows, cols, preferred_element_type=jnp.float32)
        row_rank = row_half * half + offsets
        keep = (col_rank[None, None, :] < row_rank[None, :, None]) & (col_live[:, None, :] > 0)
        return jnp.max(jnp.where(keep, sims, jnp.float32(-1.0)), axis=2)

    initial = jnp.full((clus_grp, slot_dev), -1.0, jnp.float32)
    cols_all = lax.all_gather(grid, "mem", axis=1, tiled=True)
    live_all = lax.all_gather(present, "mem", axis=1, tiled=True)
    span = cols_all.shape[1]

    def one_tile(step, acc):
        anchor = step * half
        cols = lax.dynamic_slice_in_dim(cols_all, step * half, half, 1)
        live = lax.dynamic_slice_in_dim(live_all, step * half, half, 1)
        col_rank = column_ranks(anchor + offsets)
        results = []
        for which in range(2):
            rows = grid[:, which * half : (which + 1) * half]
            row_half = my_halves[which]
            fresh = lax.cond(
                jnp.min(col_rank) < (row_half + 1) * half,
                lambda operands: compare(*operands),
                lambda operands: jnp.full((clus_grp, half), -1.0, jnp.float32),
                (rows, row_half, cols, col_rank, live),
            )
            results.append(fresh)
        return jnp.maximum(acc, jnp.concatenate(results, axis=1))

    best = lax.fori_loop(0, span // half, one_tile, initial)
    reply = jnp.where(
        filled, best.reshape(-1)[jnp.where(filled, arrived_slot, 0)], jnp.float32(-1.0)
    )
    back = lax.all_to_all(reply, ("grp", "mem"), split_axis=0, concat_axis=0, tiled=True)
    return jnp.where(alive, back[jnp.minimum(send_at, devices * quota - 1)], jnp.float32(-1.0))


def solution(mesh):
    in_specs = (P(("grp", "mem"), None), P(("grp", "mem")), P(("grp", "mem")))
    out_specs = P(("grp", "mem"))
    return jax.shard_map(
        on_device, mesh=mesh, in_specs=in_specs, out_specs=out_specs, check_vma=False
    )
```

profile of v0, /device:TPU:0, one launch (start us, length us, event | category | flops | bytes accessed | tf_op | source)
XLA Modules:
  0.0 360.9 jit_solution(12341732573781480606)
XLA Ops:
  7.4 9.0 %reduce-window.6 = s32[32,8,128]{2,1,0:T(8,128)S(1)} reduce-window(s32[32,8,128]{2,1,0:T(8,128)S(1)} %fusion.21, s32[]{:T(128)} %constant.263.clone.1), window={size=1x1x128 pad=0_0x0_0x127_0}, to_apply=%region_0.0 | reduce-window | flops 4161536 | bytes 262148 | tf_op jit(solution)/shard_map/reduce-window
  16.9 4.3 %scatter_custom_fusion = s32[1025]{0:T(1024)S(1)} fusion(s32[1024]{0:T(1024)S(1)} %get-tuple-element.412, s32[1024]{0:T(1024)S(1)} %get-tuple-element.407, s32[]{:T(128)} %constant.264.clone.1), kind=kCustom, calls=%fused_computation.83 | custom fusion | bytes 4104 | tf_op jit(solution)/shard_map/scatter | solution.py:48
  22.0 7.3 %all-to-all-start = ((s32[32,32,1]{1,2,0:T(1,128)}), s32[32,32,1]{1,2,0:T(1,128)S(1)}, u32[]{:S(2)}, u32[]{:S(2)}) async-start(s32[32,32,1]{1,2,0:T(1,128)} %bitcast.4), calls=%async_computation | async-start | bytes 32768 | tf_op jit(solution)/shard_map/all_to_all | solution.py:52
  29.3 1.8 fusion.8
  31.1 6.0 %scatter_custom_fusion.1 = bf16[1025,768]{1,0:T(8,128)(2,1)S(1)} fusion(s32[1024]{0:T(1024)S(1)} %get-tuple-element.412, bf16[1024,768]{1,0:T(8,128)(2,1)S(1)} %copy-done.1, f32[1024]{0:T(1024)S(1)} %add_rsqrt_fusion, bf16[]{:T(256)} %constant.275.clone.1), kind=kCustom, calls=%fused_computation.39 | custom fusion | flops 2359296 | bytes 3151362 | tf_op jit(solution)/shard_map/scatter | solution.py:44
  37.1 1.3 slice.49
  38.4 5.8 %all-to-all-start.1 = ((bf16[32,32,768]{2,1,0:T(8,128)(2,1)}), bf16[32,32,768]{2,1,0:T(8,128)(2,1)S(1)}, u32[]{:S(2)}, u32[]{:S(2)}) async-start(bf16[32,32,768]{2,1,0:T(8,128)(2,1)} %bitcast.7), calls=%async_computation.1 | async-start | bytes 3145728 | tf_op jit(solution)/shard_map/all_to_all | solution.py:51
  45.6 37.5 %all-to-all-done.1 = bf16[32,32,768]{2,1,0:T(8,128)(2,1)S(1)} async-done(((bf16[32,32,768]{2,1,0:T(8,128)(2,1)}), bf16[32,32,768]{2,1,0:T(8,128)(2,1)S(1)}, u32[]{:S(2)}, u32[]{:S(2)}) %all-to-all-start.1) | async-done | bytes 1572896 | tf_op jit(solution)/shard_map/all_to_all | solution.py:51
  83.0 5.8 %scatter_custom_fusion.2 = bf16[1025,768]{1,0:T(8,128)(2,1)S(1)} fusion(s32[1024]{0:T(1024)S(1)} %bitcast.46, bf16[1024,768]{1,0:T(8,128)(2,1)S(1)} %bitcast.37, bf16[]{:T(256)} %constant.275.clone.1), kind=kCustom, calls=%fused_computation.41 | custom fusion | bytes 1574402 | tf_op jit(solution)/shard_map/scatter | solution.py:59
  88.8 1.3 slice.50
  90.2 7.6 %scatter_custom_fusion.3 = bf16[1025]{0:T(1024)(128)(2,1)S(1)} fusion(s32[1024]{0:T(1024)S(1)} %bitcast.47, bf16[1024]{0:T(1024)(128)(2,1)S(1)} %broadcast.285, bf16[]{:T(256)} %constant.275.clone.1), kind=kCustom, calls=%fused_computation.93 | custom fusion | bytes 2052 | tf_op jit(solution)/shard_map/scatter | solution.py:65
  97.8 26.5 %all_gather.7 = bf16[2,4096]{1,0:T(2,128)(2,1)S(1)} all-gather(bf16[2,512]{1,0:T(2,128)(2,1)S(1)} %reshape.163), channel_id=1, replica_groups=mesh['grp'=4,'mem'=8] {'mem'}, dimensions={1}, use_global_device_ids=true | all-gather | bytes 18432 | tf_op jit(solution)/shard_map/all_gather | solution.py:83
  124.3 140.3 %all-gather.2.cloned.1.call-done = bf16[2,4096,768]{2,1,0:T(8,128)(2,1)} async-done(((bf16[2,512,768]{2,1,0:T(8,128)(2,1)}), bf16[2,4096,768]{2,1,0:T(8,128)(2,1)}) %all-gather.2.cloned.1.call-update) | async-done | bytes 12582928 | tf_op jit(solution)/shard_map/all_gather | solution.py:82
  264.7 53.1 %while.18 = (s32[]{:T(128)}, f32[2,512]{1,0:T(2,128)S(1)}, s32[]{:T(128)}, bf16[2,4096,768]{2,1,0:T(8,128)(2,1)}, bf16[2,4096]{1,0:T(2,128)(2,1)S(1)}, /*index=5...) while((s32[]{:T(128)}, f32[2,512]{1,0:T(2,128)S(1)}, ...), condition=%wide.region_16.17_spmd.clone.clone, body=%wide.region_8.16_spmd.clone.clone.sunk | while | flops 403586560 | bytes 5014897 | solution.py:104
  269.0 1.2 constant_dynamic-slice_fusion.5
  272.8 1.2 constant_dynamic-slice_fusion.5
  276.0 1.2 constant_dynamic-slice_fusion.5
  279.2 1.2 constant_dynamic-slice_fusion.5
  282.4 1.2 constant_dynamic-slice_fusion.5
  292.1 1.2 constant_dynamic-slice_fusion.5
  305.0 1.2 constant_dynamic-slice_fusion.5
  317.8 4.5 %gather_fusion = f32[1024]{0:T(1024)S(1)} fusion(f32[1024]{0:T(1024)S(1)} %bitcast.34, s32[1024]{0:T(1024)S(1)} %broadcast_clamp_fusion), kind=kCustom, calls=%fused_computation | custom fusion | bytes 12288 | tf_op jit(solution)/shard_map/gather | solution.py:106
  322.4 25.2 %all_to_all.33 = f32[32,32,1]{1,2,0:T(1,128)S(1)} all-to-all(f32[32,32,1]{1,2,0:T(1,128)S(1)} %bitcast.42), channel_id=1, replica_groups=mesh['grp'=4,'mem'=8] {'grp','mem'}, dimensions={0} | all-to-all | bytes 8192 | tf_op jit(solution)/shard_map/all_to_all | solution.py:108
  349.0 4.5 %gather_fusion.1 = f32[1024]{0:T(1024)S(1)} fusion(f32[1024]{0:T(1024)S(1)} %all_to_all.29, s32[1024]{0:T(1024)S(1)} %get-tuple-element.411), kind=kCustom, calls=%fused_computation.1 | custom fusion | bytes 12288 | tf_op jit(solution)/shard_map/gather | solution.py:109
  (182 shorter events, 31.5 us)
Async XLA Ops:
  6.5 24.5 %copy-start.1 = (bf16[1024,768]{1,0:T(8,128)(2,1)S(1)}, bf16[1024,768]{1,0:T(8,128)(2,1)}, u32[]{:S(2)}) copy-start(bf16[1024,768]{1,0:T(8,128)(2,1)} %param.9) | copy-start | bytes 4718596
  22.0 16.4 %all-to-all-start = ((s32[32,32,1]{1,2,0:T(1,128)}), s32[32,32,1]{1,2,0:T(1,128)S(1)}, u32[]{:S(2)}, u32[]{:S(2)}) async-start(s32[32,32,1]{1,2,0:T(1,128)} %bitcast.4), calls=%async_computation | async-start | bytes 32768 | tf_op jit(solution)/shard_map/all_to_all | solution.py:52
  38.4 44.7 %all-to-all-start.1 = ((bf16[32,32,768]{2,1,0:T(8,128)(2,1)}), bf16[32,32,768]{2,1,0:T(8,128)(2,1)S(1)}, u32[]{:S(2)}, u32[]{:S(2)}) async-start(bf16[32,32,768]{2,1,0:T(8,128)(2,1)} %bitcast.7), calls=%async_computation.1 | async-start | bytes 3145728 | tf_op jit(solution)/shard_map/all_to_all | solution.py:51
  44.2 220.5 %all-gather.2.cloned.1.call-start = ((), (), s32[]{:S(2)}) async-start(), calls=%async_computation.3 | async-start | bytes 14155776 | tf_op jit(solution)/shard_map/all_gather | solution.py:82
  90.1 174.5 %copy-start = (bf16[1024,768]{1,0:T(8,128)(2,1)S(1)}, bf16[1024,768]{1,0:T(8,128)(2,1)}, u32[]{:S(2)}) copy-start(bf16[1024,768]{1,0:T(8,128)(2,1)} %slice.50) | copy-start | bytes 4718596
Sparse Core Ops, SparseCore 0:
  90.3 174.3 all-gather.1
where the time goes:
time: 362 us; the launch traced here: 361 us
  waiting for transfers between devices  178 us (49%)
  blocking collectives  51.7 us (14%)
  local copies, waits for them, and re-layouts  50.9 us (14%)
  other arithmetic  31.3 us (9%)
  loops' own time  21 us (6%)
  between operations  13.6 us (4%)
  starting transfers between devices  13.2 us (4%)
    all_gather x1, waiting for transfers between devices, on_device(): cols_all = lax.all_gather(grid, 'mem', axis=1, tiled=True)  140 us
    all_to_all x1, waiting for transfers between devices, on_device(): lax.all_to_all(outgoing, ('grp', 'mem'), split_axis=0, concat_axis=0, til...  37.5 us
    all_gather x1, blocking collectives, on_device(): live_all = lax.all_gather(present, 'mem', axis=1, tiled=True)  26.5 us
    all_to_all x1, blocking collectives, on_device(): lax.all_to_all(reply, ('grp', 'mem'), split_axis=0, concat_axis=0, tiled=...  25.2 us
    another operation x1, loops' own time, on_device(): best = lax.fori_loop(0, span // half, one_tile, initial)  20.3 us
    dynamic_slice x16, local copies, waits for them, and re-layouts, one_tile(): cols = lax.dynamic_slice_in_dim(cols_all, step * half, half, 1)  19.1 us
    add x16, other arithmetic, column_ranks(): half_of(spots // slot_dev, spots % slot_dev // half) * half + spots % half  10.9 us
    another operation x3, other arithmetic  9.15 us
  transfers between devices with their start and end apart: 3, of which 2 were waited for; matrix products, arithmetic and copies ran while one was open for 5% of the time, Pallas kernels for 0%

commit v1 on v0

v1 whole, which is shorter than its diff:
```python
import functools

import jax
import jax.numpy as jnp
from jax import lax
from jax.experimental import pallas as pl
from jax.experimental.pallas import tpu as pltpu
from jax.sharding import PartitionSpec as P

CLUS_GRP = 2
TILES = 4
LABEL_ROWS = 16
FAR = 1.0e9
NT = (((1,), (1,)), ((), ()))


def cover(members):
    bits = [1 << i for i in range(members.bit_length() - 1)]
    offsets = [0] + bits

    def missing(held):
        return set(range(members)) - {a ^ b for a in held for b in held}

    while missing(offsets):
        offsets.append(
            min(
                (d for d in range(members) if d not in offsets),
                key=lambda d: (len(missing(offsets + [d])), bin(d).count("1"), -d),
            )
        )
    pairs = {}
    for delta in range(members):
        pairs[delta] = min(
            (a, a ^ delta) for a in offsets if a ^ delta in offsets
        )
    return offsets, pairs


def pack_kernel(sizes, block_ref, emb_ref, cluster_ref, rank_ref, *out_refs):
    groups, halves, half, cap, blk = sizes
    dest_ref, sends = out_refs[0], out_refs[1:]
    rows = emb_ref.shape[0]
    cluster = cluster_ref[...]
    rank = rank_ref[...]
    alive = cluster >= 0
    pair = lax.shift_right_logical(jnp.maximum(cluster, 0), 1)
    parity = jnp.maximum(cluster, 0) - 2 * pair
    safe_rank = jnp.maximum(rank, 0)
    which = safe_rank // half
    units = groups * halves
    unit_id = jnp.where(alive, (pair ^ block_ref[0]) * halves + which, -1)
    step = 256
    before_rows = lax.broadcasted_iota(jnp.int32, (step, step), 0)
    before_cols = lax.broadcasted_iota(jnp.int32, (step, step), 1)
    upper = (before_rows < before_cols).astype(jnp.float32).astype(jnp.bfloat16)
    unit_iota = lax.broadcasted_iota(jnp.int32, (units, step), 0)
    carry = jnp.zeros((units, 1), jnp.float32)
    places = []
    for j in range(rows // step):
        mine = unit_id[:, j * step : (j + 1) * step]
        hit = (unit_iota == mine).astype(jnp.float32)
        before = jnp.dot(hit.astype(jnp.bfloat16), upper, preferred_element_type=jnp.float32) + carry
        position = jnp.sum(hit * before, axis=0, keepdims=True)
        carry = carry + jnp.sum(hit, axis=1, keepdims=True)
        places.append(jnp.where(mine >= 0, mine * cap + position.astype(jnp.int32), -1))
    dest = jnp.concatenate(places, axis=1)
    dest_ref[...] = dest

    wide = emb_ref[...].astype(jnp.float32)
    total = jnp.sum(wide * wide, axis=1, keepdims=True)
    unit = (wide * lax.rsqrt(total + 1e-06)).astype(jnp.bfloat16)

    field = lax.broadcasted_iota(jnp.int32, (LABEL_ROWS, rows), 0)
    labels = jnp.where(
        field == 0, safe_rank - which * half, jnp.where(field == 1, parity + 1, 0)
    )
    labels = jnp.where(alive, labels, 0).astype(jnp.float32).astype(jnp.bfloat16)
    per_tile = blk // TILES
    wide_tile = groups * per_tile
    spread = (
        lax.broadcasted_iota(jnp.int32, (blk, wide_tile), 0) % per_tile
        == lax.broadcasted_iota(jnp.int32, (blk, wide_tile), 1) % per_tile
    )
    spread = spread.astype(jnp.float32).astype(jnp.bfloat16)
    own_tile = lax.broadcasted_iota(jnp.int32, (LABEL_ROWS, blk), 0) == lax.div(
        lax.broadcasted_iota(jnp.int32, (LABEL_ROWS, blk), 1), per_tile
    )
    slot = lax.broadcasted_iota(jnp.int32, (blk, rows), 0)
    for k in range(groups):
        pick = (slot + k * blk == dest).astype(jnp.float32).astype(jnp.bfloat16)
        sends[k][0:blk, :] = jnp.dot(pick, unit, preferred_element_type=jnp.float32).astype(
            jnp.bfloat16
        )
        mine = lax.dot_general(labels, pick, NT, preferred_element_type=jnp.float32)
        parts = []
        for f in range(2):
            line = jnp.where(own_tile, mine[f : f + 1, :], 0.0).astype(jnp.bfloat16)
            parts.append(jnp.dot(line, spread, preferred_element_type=jnp.float32))
        width = sends[k].shape[1]
        parts.append(jnp.zeros((LABEL_ROWS, width - 2 * wide_tile), jnp.float32))
        sends[k][blk : blk + LABEL_ROWS, :] = jnp.concatenate(parts, axis=1).astype(jnp.bfloat16)


def pack(block, embeddings, cluster, rank, sizes):
    groups, halves, half, cap, blk = sizes
    rows, width = embeddings.shape
    vmem = pl.BlockSpec(memory_space=pltpu.VMEM)
    out_shape = [jax.ShapeDtypeStruct((1, rows), jnp.int32)]
    out_shape += [jax.ShapeDtypeStruct((blk + LABEL_ROWS, width), jnp.bfloat16)] * groups
    return pl.pallas_call(
        functools.partial(pack_kernel, sizes),
        out_shape=out_shape,
        in_specs=[pl.BlockSpec(memory_space=pltpu.SMEM), vmem, vmem, vmem],
        out_specs=[vmem] * len(out_shape),
        compiler_params=pltpu.CompilerParams(vmem_limit_bytes=48 * 1024 * 1024),
    )(block, embeddings, cluster.reshape(1, rows), rank.reshape(1, rows))


def compare_kernel(sizes, plan, n_sets, *refs):
    groups, halves, half, cap, blk = sizes
    blocks = [refs[i * groups : (i + 1) * groups] for i in range(n_sets)]
    n_out = len(plan)
    outs = refs[n_sets * groups : n_sets * groups + n_out]
    table, key_col, key_row, low_row, best, sems = refs[n_sets * groups + n_out :]
    rows = groups * blk
    per_tile = blk // TILES
    tile = rows // TILES

    for i in range(n_sets):
        for t in range(TILES):
            for k in range(groups):
                pltpu.make_async_copy(
                    blocks[i][k].at[pl.ds(t * per_tile, per_tile)],
                    table.at[pl.ds(i * rows + t * tile + k * per_tile, per_tile)],
                    sems.at[i],
                ).start()

    lane = lax.broadcasted_iota(jnp.int32, (LABEL_ROWS, tile), 1)
    line = lax.broadcasted_iota(jnp.int32, (LABEL_ROWS, tile), 0)
    from_block = lax.div(lane, per_tile)
    which = line * (halves // TILES) + lax.div(lane - from_block * per_tile, cap)
    for i in range(n_sets):
        rest = jnp.zeros((LABEL_ROWS, tile), jnp.float32)
        code = jnp.zeros((LABEL_ROWS, tile), jnp.float32)
        for k in range(groups):
            label = blocks[i][k][blk : blk + LABEL_ROWS, 0 : 2 * tile].astype(jnp.float32)
            rest = jnp.where(from_block == k, label[:, :tile], rest)
            code = jnp.where(from_block == k, label[:, tile:], code)
        cap_all = float(halves * half)
        low = (code - 1.0) * cap_all
        key = low + (which * half).astype(jnp.float32) + rest
        live = code > 0.5
        key = jnp.where(live, key, FAR)
        key_row[i] = key[0:8]
        low_row[i] = low[0:8]
        for t in range(TILES):
            for part in range(tile // 128):
                square = jnp.broadcast_to(key[t : t + 1, part * 128 : (part + 1) * 128], (128, 128))
                key_col[pl.ds(i * rows + t * tile + part * 128, 128), :] = square.T

    for i in range(n_sets):
        here = table.at[pl.ds(i * rows, rows)]
        pltpu.make_async_copy(here, here, sems.at[i]).wait()

    for o, (a, cols) in enumerate(plan):

        def one_tile(t, _, a=a, cols=cols, o=o):
            queries = table[pl.ds(pl.multiple_of(a * rows + t * tile, tile), tile), :]
            mine = key_row[a, pl.ds(t, 1), :]
            floor = low_row[a, pl.ds(t, 1), :]

            def one_col(s, acc):
                for b in cols:
                    at = pl.multiple_of(b * rows + s * tile, tile)
                    sims = lax.dot_general(
                        table[pl.ds(at, tile), :], queries, NT, preferred_element_type=jnp.float32
                    )
                    theirs = key_col[pl.ds(at, tile), :]
                    theirs = jnp.concatenate([theirs] * (tile // 128), axis=1)
                    keep = (theirs >= floor) & (theirs < mine)
                    sims = jnp.where(keep, sims, -1.0)
                    acc = jnp.maximum(acc, jnp.max(sims.reshape(tile // 8, 8, tile), axis=0))
                return acc

            acc = lax.fori_loop(0, t + 1, one_col, jnp.full((8, tile), -1.0, jnp.float32))
            best[o, pl.ds(t, 1), :] = jnp.max(acc, axis=0, keepdims=True)
            return 0

        lax.fori_loop(0, TILES, one_tile, 0)

    lane = lax.broadcasted_iota(jnp.int32, (8, tile), 1)
    for o in range(n_out):
        found = best[o]
        for k in range(groups):
            total = jnp.full((1, tile), -1.0, jnp.float32)
            for t in range(TILES):
                turn = ((t - k) * per_tile) % tile
                moved = pltpu.roll(found, turn, 1) if turn else found
                total = jnp.where(lax.div(lane, per_tile)[0:1] == t, moved[t : t + 1], total)
            outs[o][k : k + 1, :] = total[:, :blk]


def compare(sets, plan, sizes):
    groups, halves, half, cap, blk = sizes
    n_sets = len(sets)
    flat = [piece for one in sets for piece in one]
    rows, width = groups * blk, flat[0].shape[1]
    tile = rows // TILES
    vmem = pl.BlockSpec(memory_space=pltpu.VMEM)
    combos = sum(len(cols) for _, cols in plan) * TILES * (TILES + 1) // 2
    return pl.pallas_call(
        functools.partial(compare_kernel, sizes, plan, n_sets),
        out_shape=[jax.ShapeDtypeStruct((groups, blk), jnp.float32)] * len(plan),
        in_specs=[vmem] * len(flat),
        out_specs=[vmem] * len(plan),
        scratch_shapes=[
            pltpu.VMEM((n_sets * rows, width), jnp.bfloat16),
            pltpu.VMEM((n_sets * rows, 128), jnp.float32),
            pltpu.VMEM((n_sets, 8, tile), jnp.float32),
            pltpu.VMEM((n_sets, 8, tile), jnp.float32),
            pltpu.VMEM((len(plan), 8, tile), jnp.float32),
            pltpu.SemaphoreType.DMA((n_sets,)),
        ],
        compiler_params=pltpu.CompilerParams(vmem_limit_bytes=48 * 1024 * 1024),
        cost_estimate=pl.CostEstimate(
            flops=2 * combos * tile * tile * width, bytes_accessed=2 * n_sets * rows * width, transcendentals=0
        ),
    )(*flat)


def unpack_kernel(sizes, dest_ref, *refs):
    groups, halves, half, cap, blk = sizes
    out_ref = refs[-1]
    pieces = refs[:-1]
    rows = dest_ref.shape[1]
    dest = dest_ref[...]
    slot = lax.broadcasted_iota(jnp.int32, (blk, rows), 0)
    field = lax.broadcasted_iota(jnp.int32, (LABEL_ROWS, blk), 0)
    total = jnp.zeros((LABEL_ROWS, rows), jnp.float32)
    for k in range(groups):
        value = pieces[k][...]
        for more in range(k + groups, len(pieces), groups):
            value = jnp.maximum(value, pieces[more][...])
        top = value.astype(jnp.bfloat16).astype(jnp.float32)
        rest = value - top
        mid = rest.astype(jnp.bfloat16).astype(jnp.float32)
        low = rest - mid
        stack = jnp.where(field == 0, top, jnp.where(field == 1, mid, jnp.where(field == 2, low, 0.0)))
        pick = (slot + k * blk == dest).astype(jnp.float32).astype(jnp.bfloat16)
        total = total + jnp.dot(stack.astype(jnp.bfloat16), pick, preferred_element_type=jnp.float32)
    value = (total[0:1] + total[1:2]) + total[2:3]
    out_ref[...] = jnp.where(dest >= 0, value, -1.0)


def unpack(dest, pieces, sizes):
    vmem = pl.BlockSpec(memory_space=pltpu.VMEM)
    return pl.pallas_call(
        functools.partial(unpack_kernel, sizes),
        out_shape=jax.ShapeDtypeStruct(dest.shape, jnp.float32),
        in_specs=[vmem] * (1 + len(pieces)),
        out_specs=vmem,
        compiler_params=pltpu.CompilerParams(vmem_limit_bytes=48 * 1024 * 1024),
    )(dest, *pieces)


def on_device(embeddings, cluster, rank):
    rows_dev, width = embeddings.shape
    groups = lax.axis_size("grp")
    members = lax.axis_size("mem")
    devices = groups * members
    halves = 2 * members
    half = rows_dev // CLUS_GRP // 2
    blk = rows_dev // groups
    cap = blk // halves
    sizes = (groups, halves, half, cap, blk)
    side = members // groups

    def swap(value, block_step, member_step):
        mask = member_step // side * members + block_step * side + member_step % side
        if mask == 0:
            return value
        return lax.ppermute(value, ("grp", "mem"), [(i, i ^ mask) for i in range(devices)])

    offsets, pairs = cover(members)
    block = (lax.axis_index("mem") // side).astype(jnp.int32).reshape(1)
    packed = pack(block, embeddings, cluster, rank, sizes)
    dest, sends = packed[0], packed[1:]

    held = {0: [swap(sends[k], k, 0) for k in range(groups)]}
    for d in offsets[1:]:
        via = next((e for e in held if bin(d ^ e).count("1") == 1 and (e == 0 or d ^ e > 1)), 0)
        held[d] = [swap(piece, 0, d ^ via) for piece in held[via]]

    index = {d: i for i, d in enumerate(offsets)}
    starts = sorted({a for a, _ in pairs.values()})
    plan = [(index[a], [index[b] for _, (e, b) in sorted(pairs.items()) if e == a]) for a in starts]
    found = compare([held[d] for d in offsets], plan, sizes)

    best = {}
    for a, value in zip(starts, found):
        near = a % side
        value = swap(value, 0, a - near)
        best[near] = jnp.maximum(best[near], value) if near in best else value

    pieces = []
    for near in sorted(best):
        for k in range(groups):
            pieces.append(swap(best[near][k : k + 1], k, near))
    return unpack(dest, pieces, sizes).reshape(rows_dev)


def solution(mesh):
    in_specs = (P(("grp", "mem"), None), P(("grp", "mem")), P(("grp", "mem")))
    out_specs = P(("grp", "mem"))
    return jax.shard_map(
        on_device, mesh=mesh, in_specs=in_specs, out_specs=out_specs, check_vma=False
    )
```

time: 362 us -> 146 us (0.40)
  waiting for transfers between devices: 178 us -> 72.8 us
  blocking collectives: 51.7 us -> 0 us
  local copies, waits for them, and re-layouts: 50.9 us -> 3.57 us
  other arithmetic: 31.3 us -> 0 us
  Pallas kernels: 0 us -> 30.2 us
  starting transfers between devices: 13.2 us -> 38.7 us
  loops' own time: 21 us -> 0 us
  between operations: 13.6 us -> 0.08 us
    all_gather x1 -> x0, waiting for transfers between devices: 140 us -> none  [on_device(): cols_all = lax.all_gather(grid, 'mem', axis=1, tiled=True)]
    ppermute x0 -> x26, waiting for transfers between devices: none -> 72.8 us  [swap(): lax.ppermute(value, ('grp', 'mem'), [(i, i ^ mask) for i in range(devices)])]
    ppermute x0 -> x26, starting transfers between devices: none -> 38.7 us  [swap(): lax.ppermute(value, ('grp', 'mem'), [(i, i ^ mask) for i in range(devices)])]
    all_to_all x2 -> x0, waiting for transfers between devices: 37.5 us -> none  [the longest x1 37.5 us: on_device(): lax.all_to_all(outgoing, ('grp', 'mem'), split_axis=0, concat_axis=0, til...]
    pallas_call x0 -> x3, Pallas kernels: none -> 30.2 us  [the longest x1 25.9 us: compare(): pl.pallas_call(functools.partial(compare_kernel, sizes, plan, n_sets), ou...]
    all_gather x1 -> x0, blocking collectives: 26.5 us -> none  [on_device(): live_all = lax.all_gather(present, 'mem', axis=1, tiled=True)]
    all_to_all x1 -> x0, blocking collectives: 25.2 us -> none  [on_device(): lax.all_to_all(reply, ('grp', 'mem'), split_axis=0, concat_axis=0, tiled=...]
    another operation x33 -> x0, loops' own time: 21 us -> none  [the longest x1 20.3 us: on_device(): best = lax.fori_loop(0, span // half, one_tile, initial)]
  transfers between devices with their start and end apart: 3 -> 26, of which waited for: 2 -> 13; matrix products, arithmetic and copies ran while one was open for 5% -> 0% of each run, Pallas kernels for 0% -> 0%
where the time goes in v1:
time: 146 us; the launch traced here: 145 us
  waiting for transfers between devices  72.8 us (50%)
  starting transfers between devices  38.7 us (27%)
  Pallas kernels  30.2 us (21%)
  local copies, waits for them, and re-layouts  3.57 us (2%)
    ppermute x26, waiting for transfers between devices, swap(): lax.ppermute(value, ('grp', 'mem'), [(i, i ^ mask) for i in range(devices)])  72.8 us
    ppermute x26, starting transfers between devices, swap(): lax.ppermute(value, ('grp', 'mem'), [(i, i ^ mask) for i in range(devices)])  38.7 us
    pallas_call x1, Pallas kernels, compare(): pl.pallas_call(functools.partial(compare_kernel, sizes, plan, n_sets), ou...  25.9 us
    unnamed x18, local copies, waits for them, and re-layouts  3.56 us
    pallas_call x1, Pallas kernels, pack(): pl.pallas_call(functools.partial(pack_kernel, sizes), out_shape=out_shape...  3.14 us
  transfers between devices with their start and end apart: 26, of which 13 were waited for; matrix products, arithmetic and copies ran while one was open for 0% of the time, Pallas kernels for 0%

profile of v1, /device:TPU:0, one launch (start us, length us, event | category | flops | bytes accessed | tf_op | source)
XLA Modules:
  0.0 145.3 jit_solution(15137884058224288007)
XLA Ops:
  2.8 3.1 %shard_map.37 = (s32[1,1024]{1,0:T(1,128)S(1)}, bf16[272,768]{1,0:T(8,128)(2,1)S(1)}, bf16[272,768]{1,0:T(8,128)(2,1)S(1)}, bf16[272,768]{1,0:T(8,128)(2,1)S(1)}, bf16[272,768]{1,0:T(8,128)(2,1)S(1)}) custom-call(s32[1]{0:T(128)} %bitcast.block_ref, bf16[1024,768]{1,0:T(8,128)(2,1)S(1)} %copy-done, s32[1,1024]{1,0:T(1,128)S(1)} %bitcast.4, s32[1,1024]{1,0:T(1,128)S(1)} %bitcast.5), custom_call_target="tpu_custom_call" | custom-call | tf_op jit(solution)/shard_map/pallas_call | solution.py:110
  5.9 3.1 %collective-permute-start = (bf16[272,768]{1,0:T(8,128)(2,1)S(1)}, bf16[272,768]{1,0:T(8,128)(2,1)S(1)}, u32[]{:S(2)}, u32[]{:S(2)}) collective-permute-start(bf16[272,768]{1,0:T(8,128)(2,1)S(1)} %get-tuple-element.14), channel_id=1, source_target_pairs={{0,2},{1,3},{2,0},{3,1},{4,6},{5,7},{6,4},{7,5},{8,10},{9,11},{10,... | collective-permute-start | bytes 1253384 | tf_op jit(solution)/shard_map/ppermute | solution.py:282
  9.0 2.6 %collective-permute-start.1 = (bf16[272,768]{1,0:T(8,128)(2,1)S(1)}, bf16[272,768]{1,0:T(8,128)(2,1)S(1)}, u32[]{:S(2)}, u32[]{:S(2)}) collective-permute-start(bf16[272,768]{1,0:T(8,128)(2,1)S(1)} %get-tuple-element.15), channel_id=1, source_target_pairs={{0,4},{1,5},{2,6},{3,7},{4,0},{5,1},{6,2},{7,3},{8,12},{9,13},{10,... | collective-permute-start | bytes 1253384 | tf_op jit(solution)/shard_map/ppermute | solution.py:282
  11.6 1.7 %collective-permute-start.11 = (bf16[272,768]{1,0:T(8,128)(2,1)S(1)}, bf16[272,768]{1,0:T(8,128)(2,1)S(1)}, u32[]{:S(2)}, u32[]{:S(2)}) collective-permute-start(bf16[272,768]{1,0:T(8,128)(2,1)S(1)} %get-tuple-element.13.refs_0_), channel_id=1, source_target_pairs={{0,16},{1,17},{2,18},{3,19},{4,20},{5,21},{6,22},{7,23},{8,24},{9,... | collective-permute-start | bytes 1253384 | tf_op jit(solution)/shard_map/ppermute | solution.py:282
  13.3 13.5 %collective-permute-done.refs_1_ = bf16[272,768]{1,0:T(8,128)(2,1)S(1)} collective-permute-done((bf16[272,768]{1,0:T(8,128)(2,1)S(1)}, bf16[272,768]{1,0:T(8,128)(2,1)S(1)}, u32[]{:S(2)}, u32[]{:S(2)}) %collective-permute-start) | collective-permute-done | bytes 417824 | tf_op jit(solution)/shard_map/ppermute | solution.py:282
  26.8 1.7 %collective-permute-start.3 = (bf16[272,768]{1,0:T(8,128)(2,1)S(1)}, bf16[272,768]{1,0:T(8,128)(2,1)S(1)}, u32[]{:S(2)}, u32[]{:S(2)}) collective-permute-start(bf16[272,768]{1,0:T(8,128)(2,1)S(1)} %get-tuple-element.13.refs_0_), channel_id=1, source_target_pairs={{0,1},{1,0},{2,3},{3,2},{4,5},{5,4},{6,7},{7,6},{8,9},{9,8},{10,11... | collective-permute-start | bytes 1253384 | tf_op jit(solution)/shard_map/ppermute | solution.py:282
  28.5 11.9 %collective-permute-done.1.refs_2_ = bf16[272,768]{1,0:T(8,128)(2,1)S(1)} collective-permute-done((bf16[272,768]{1,0:T(8,128)(2,1)S(1)}, bf16[272,768]{1,0:T(8,128)(2,1)S(1)}, u32[]{:S(2)}, u32[]{:S(2)}) %collective-permute-start.1) | collective-permute-done | bytes 417824 | tf_op jit(solution)/shard_map/ppermute | solution.py:282
  44.0 6.5 %collective-permute-done.12.refs_13_ = bf16[272,768]{1,0:T(8,128)(2,1)S(1)} collective-permute-done((bf16[272,768]{1,0:T(8,128)(2,1)S(1)}, bf16[272,768]{1,0:T(8,128)(2,1)S(1)}, u32[]{:S(2)}, u32[]{:S(2)}) %collective-permute-start.12) | collective-permute-done | bytes 417824 | tf_op jit(solution)/shard_map/ppermute | solution.py:282
  50.5 2.6 %collective-permute-start.5 = (bf16[272,768]{1,0:T(8,128)(2,1)S(1)}, bf16[272,768]{1,0:T(8,128)(2,1)S(1)}, u32[]{:S(2)}, u32[]{:S(2)}) collective-permute-start(bf16[272,768]{1,0:T(8,128)(2,1)S(1)} %collective-permute-done.1.refs_2_), channel_id=1, source_target_pairs={{0,1},{1,0},{2,3},{3,2},{4,5},{5,4},{6,7},{7,6},{8,9},{9,8},{10,11... | collective-permute-start | bytes 1253384 | tf_op jit(solution)/shard_map/ppermute | solution.py:282
  53.1 2.4 %collective-permute-start.14 = (bf16[272,768]{1,0:T(8,128)(2,1)S(1)}, bf16[272,768]{1,0:T(8,128)(2,1)S(1)}, u32[]{:S(2)}, u32[]{:S(2)}) collective-permute-start(bf16[272,768]{1,0:T(8,128)(2,1)S(1)} %collective-permute-done.2.refs_3_), channel_id=1, source_target_pairs={{0,16},{1,17},{2,18},{3,19},{4,20},{5,21},{6,22},{7,23},{8,24},{9,... | collective-permute-start | bytes 1253384 | tf_op jit(solution)/shard_map/ppermute | solution.py:282
  55.5 3.9 %collective-permute-done.13.refs_14_ = bf16[272,768]{1,0:T(8,128)(2,1)S(1)} collective-permute-done((bf16[272,768]{1,0:T(8,128)(2,1)S(1)}, bf16[272,768]{1,0:T(8,128)(2,1)S(1)}, u32[]{:S(2)}, u32[]{:S(2)}) %collective-permute-start.13) | collective-permute-done | bytes 417824 | tf_op jit(solution)/shard_map/ppermute | solution.py:282
  59.5 2.6 %collective-permute-start.6 = (bf16[272,768]{1,0:T(8,128)(2,1)S(1)}, bf16[272,768]{1,0:T(8,128)(2,1)S(1)}, u32[]{:S(2)}, u32[]{:S(2)}) collective-permute-start(bf16[272,768]{1,0:T(8,128)(2,1)S(1)} %collective-permute-done.2.refs_3_), channel_id=1, source_target_pairs={{0,1},{1,0},{2,3},{3,2},{4,5},{5,4},{6,7},{7,6},{8,9},{9,8},{10,11... | collective-permute-start | bytes 1253384 | tf_op jit(solution)/shard_map/ppermute | solution.py:282
  62.1 2.4 %collective-permute-start.15 = (bf16[272,768]{1,0:T(8,128)(2,1)S(1)}, bf16[272,768]{1,0:T(8,128)(2,1)S(1)}, u32[]{:S(2)}, u32[]{:S(2)}) collective-permute-start(bf16[272,768]{1,0:T(8,128)(2,1)S(1)} %collective-permute-done.7.refs_8_), channel_id=1, source_target_pairs={{0,16},{1,17},{2,18},{3,19},{4,20},{5,21},{6,22},{7,23},{8,24},{9,... | collective-permute-start | bytes 1253384 | tf_op jit(solution)/shard_map/ppermute | solution.py:282
  66.1 2.4 %collective-permute-done.14.refs_15_ = bf16[272,768]{1,0:T(8,128)(2,1)S(1)} collective-permute-done((bf16[272,768]{1,0:T(8,128)(2,1)S(1)}, bf16[272,768]{1,0:T(8,128)(2,1)S(1)}, u32[]{:S(2)}, u32[]{:S(2)}) %collective-permute-start.14) | collective-permute-done | bytes 417824 | tf_op jit(solution)/shard_map/ppermute | solution.py:282
  68.4 2.4 %collective-permute-start.17 = (bf16[272,768]{1,0:T(8,128)(2,1)S(1)}, bf16[272,768]{1,0:T(8,128)(2,1)S(1)}, u32[]{:S(2)}, u32[]{:S(2)}) collective-permute-start(bf16[272,768]{1,0:T(8,128)(2,1)S(1)} %collective-permute-done.9.refs_10_), channel_id=1, source_target_pairs={{0,16},{1,17},{2,18},{3,19},{4,20},{5,21},{6,22},{7,23},{8,24},{9,... | collective-permute-start | bytes 1253384 | tf_op jit(solution)/shard_map/ppermute | solution.py:282
  71.8 5.6 %collective-permute-done.15.refs_16_ = bf16[272,768]{1,0:T(8,128)(2,1)S(1)} collective-permute-done((bf16[272,768]{1,0:T(8,128)(2,1)S(1)}, bf16[272,768]{1,0:T(8,128)(2,1)S(1)}, u32[]{:S(2)}, u32[]{:S(2)}) %collective-permute-start.15) | collective-permute-done | bytes 417824 | tf_op jit(solution)/shard_map/ppermute | solution.py:282
  77.4 9.0 %collective-permute-done.16.refs_17_ = bf16[272,768]{1,0:T(8,128)(2,1)S(1)} collective-permute-done((bf16[272,768]{1,0:T(8,128)(2,1)S(1)}, bf16[272,768]{1,0:T(8,128)(2,1)S(1)}, u32[]{:S(2)}, u32[]{:S(2)}) %collective-permute-start.16) | collective-permute-done | bytes 417824 | tf_op jit(solution)/shard_map/ppermute | solution.py:282
  86.4 9.0 %collective-permute-done.17.refs_18_ = bf16[272,768]{1,0:T(8,128)(2,1)S(1)} collective-permute-done((bf16[272,768]{1,0:T(8,128)(2,1)S(1)}, bf16[272,768]{1,0:T(8,128)(2,1)S(1)}, u32[]{:S(2)}, u32[]{:S(2)}) %collective-permute-start.17) | collective-permute-done | bytes 417824 | tf_op jit(solution)/shard_map/ppermute | solution.py:282
  95.3 6.8 %collective-permute-done.18.refs_19_ = bf16[272,768]{1,0:T(8,128)(2,1)S(1)} collective-permute-done((bf16[272,768]{1,0:T(8,128)(2,1)S(1)}, bf16[272,768]{1,0:T(8,128)(2,1)S(1)}, u32[]{:S(2)}, u32[]{:S(2)}) %collective-permute-start.18) | collective-permute-done | bytes 417824 | tf_op jit(solution)/shard_map/ppermute | solution.py:282
  102.9 25.9 %shard_map.38 = (f32[4,256]{1,0:T(4,128)S(1)}, f32[4,256]{1,0:T(4,128)S(1)}) custom-call(bf16[272,768]{1,0:T(8,128)(2,1)S(1)} %get-tuple-element.13.refs_0_, bf16[272,768]{1,0:T(8,128)(2,1)S(1)} %collective-permute-done.refs_1_, bf16[272,768]{1,0:T(8,128)(2,1)S(1)} %collective-permute-done.1.refs_2_, bf16[272,768]{1,0:T(8,128)(2,1)S(1)} %collective-permute-done.2.refs_3_, ...), custom_call_target="tpu_custom_call" | custom-call | flops 8053063680 | bytes 7864320 | tf_op jit(solution)/shard_map/pallas_call | solution.py:211
  128.9 3.5 %collective-permute-start.25 = (f32[1,256]{1,0:T(1,128)S(1)}, f32[1,256]{1,0:T(1,128)S(1)}, u32[]{:S(2)}, u32[]{:S(2)}) collective-permute-start(f32[1,256]{1,0:T(1,128)S(1)} %get-tuple-element.19), channel_id=1, source_target_pairs={{0,7},{1,6},{2,5},{3,4},{4,3},{5,2},{6,1},{7,0},{8,15},{9,14},{10,... | collective-permute-start | bytes 3080 | tf_op jit(solution)/shard_map/ppermute | solution.py:282
  132.4 3.3 %collective-permute-start.24 = (f32[1,256]{1,0:T(1,128)S(1)}, f32[1,256]{1,0:T(1,128)S(1)}, u32[]{:S(2)}, u32[]{:S(2)}) collective-permute-start(f32[1,256]{1,0:T(1,128)S(1)} %get-tuple-element.20), channel_id=1, source_target_pairs={{0,5},{1,4},{2,7},{3,6},{4,1},{5,0},{6,3},{7,2},{8,13},{9,12},{10,... | collective-permute-start | bytes 3080 | tf_op jit(solution)/shard_map/ppermute | solution.py:282
  136.4 2.4 %collective-permute-start.21 = (f32[1,256]{1,0:T(1,128)S(1)}, f32[1,256]{1,0:T(1,128)S(1)}, u32[]{:S(2)}, u32[]{:S(2)}) collective-permute-start(f32[1,256]{1,0:T(1,128)S(1)} %get-tuple-element.23), channel_id=1, source_target_pairs={{0,6},{1,7},{2,4},{3,5},{4,2},{5,3},{6,0},{7,1},{8,14},{9,15},{10,... | collective-permute-start | bytes 3080 | tf_op jit(solution)/shard_map/ppermute | solution.py:282
  138.8 1.9 %collective-permute-start.20 = (f32[1,256]{1,0:T(1,128)S(1)}, f32[1,256]{1,0:T(1,128)S(1)}, u32[]{:S(2)}, u32[]{:S(2)}) collective-permute-start(f32[1,256]{1,0:T(1,128)S(1)} %get-tuple-element.24), channel_id=1, source_target_pairs={{0,4},{1,5},{2,6},{3,7},{4,0},{5,1},{6,2},{7,3},{8,12},{9,13},{10,... | collective-permute-start | bytes 3080 | tf_op jit(solution)/shard_map/ppermute | solution.py:282
  (51 shorter events, 15.1 us)
Async XLA Ops:
  5.9 20.9 %collective-permute-start = (bf16[272,768]{1,0:T(8,128)(2,1)S(1)}, bf16[272,768]{1,0:T(8,128)(2,1)S(1)}, u32[]{:S(2)}, u32[]{:S(2)}) collective-permute-start(bf16[272,768]{1,0:T(8,128)(2,1)S(1)} %get-tuple-element.14), channel_id=1, source_target_pairs={{0,2},{1,3},{2,0},{3,1},{4,6},{5,7},{6,4},{7,5},{8,10},{9,11},{10,... | collective-permute-start | bytes 1253384 | tf_op jit(solution)/shard_map/ppermute | solution.py:282
  9.0 31.4 %collective-permute-start.1 = (bf16[272,768]{1,0:T(8,128)(2,1)S(1)}, bf16[272,768]{1,0:T(8,128)(2,1)S(1)}, u32[]{:S(2)}, u32[]{:S(2)}) collective-permute-start(bf16[272,768]{1,0:T(8,128)(2,1)S(1)} %get-tuple-element.15), channel_id=1, source_target_pairs={{0,4},{1,5},{2,6},{3,7},{4,0},{5,1},{6,2},{7,3},{8,12},{9,13},{10,... | collective-permute-start | bytes 1253384 | tf_op jit(solution)/shard_map/ppermute | solution.py:282
  11.6 30.3 %collective-permute-start.2 = (bf16[272,768]{1,0:T(8,128)(2,1)S(1)}, bf16[272,768]{1,0:T(8,128)(2,1)S(1)}, u32[]{:S(2)}, u32[]{:S(2)}) collective-permute-start(bf16[272,768]{1,0:T(8,128)(2,1)S(1)} %get-tuple-element.16), channel_id=1, source_target_pairs={{0,6},{1,7},{2,4},{3,5},{4,2},{5,3},{6,0},{7,1},{8,14},{9,15},{10,... | collective-permute-start | bytes 1253384 | tf_op jit(solution)/shard_map/ppermute | solution.py:282
  11.6 30.3 %collective-permute-start.11 = (bf16[272,768]{1,0:T(8,128)(2,1)S(1)}, bf16[272,768]{1,0:T(8,128)(2,1)S(1)}, u32[]{:S(2)}, u32[]{:S(2)}) collective-permute-start(bf16[272,768]{1,0:T(8,128)(2,1)S(1)} %get-tuple-element.13.refs_0_), channel_id=1, source_target_pairs={{0,16},{1,17},{2,18},{3,19},{4,20},{5,21},{6,22},{7,23},{8,24},{9,... | collective-permute-start | bytes 1253384 | tf_op jit(solution)/shard_map/ppermute | solution.py:282
  13.3 30.2 %collective-permute-start.7 = (bf16[272,768]{1,0:T(8,128)(2,1)S(1)}, bf16[272,768]{1,0:T(8,128)(2,1)S(1)}, u32[]{:S(2)}, u32[]{:S(2)}) collective-permute-start(bf16[272,768]{1,0:T(8,128)(2,1)S(1)} %get-tuple-element.13.refs_0_), channel_id=1, source_target_pairs={{0,8},{1,9},{2,10},{3,11},{4,12},{5,13},{6,14},{7,15},{8,0},{9,1},... | collective-permute-start | bytes 1253384 | tf_op jit(solution)/shard_map/ppermute | solution.py:282
  26.8 17.2 %collective-permute-start.3 = (bf16[272,768]{1,0:T(8,128)(2,1)S(1)}, bf16[272,768]{1,0:T(8,128)(2,1)S(1)}, u32[]{:S(2)}, u32[]{:S(2)}) collective-permute-start(bf16[272,768]{1,0:T(8,128)(2,1)S(1)} %get-tuple-element.13.refs_0_), channel_id=1, source_target_pairs={{0,1},{1,0},{2,3},{3,2},{4,5},{5,4},{6,7},{7,6},{8,9},{9,8},{10,11... | collective-permute-start | bytes 1253384 | tf_op jit(solution)/shard_map/ppermute | solution.py:282
  40.4 10.2 %collective-permute-start.12 = (bf16[272,768]{1,0:T(8,128)(2,1)S(1)}, bf16[272,768]{1,0:T(8,128)(2,1)S(1)}, u32[]{:S(2)}, u32[]{:S(2)}) collective-permute-start(bf16[272,768]{1,0:T(8,128)(2,1)S(1)} %collective-permute-done.refs_1_), channel_id=1, source_target_pairs={{0,16},{1,17},{2,18},{3,19},{4,20},{5,21},{6,22},{7,23},{8,24},{9,... | collective-permute-start | bytes 1253384 | tf_op jit(solution)/shard_map/ppermute | solution.py:282
  41.8 11.3 %collective-permute-start.8 = (bf16[272,768]{1,0:T(8,128)(2,1)S(1)}, bf16[272,768]{1,0:T(8,128)(2,1)S(1)}, u32[]{:S(2)}, u32[]{:S(2)}) collective-permute-start(bf16[272,768]{1,0:T(8,128)(2,1)S(1)} %collective-permute-done.refs_1_), channel_id=1, source_target_pairs={{0,8},{1,9},{2,10},{3,11},{4,12},{5,13},{6,14},{7,15},{8,0},{9,1},... | collective-permute-start | bytes 1253384 | tf_op jit(solution)/shard_map/ppermute | solution.py:282
  41.9 13.7 %collective-permute-start.4 = (bf16[272,768]{1,0:T(8,128)(2,1)S(1)}, bf16[272,768]{1,0:T(8,128)(2,1)S(1)}, u32[]{:S(2)}, u32[]{:S(2)}) collective-permute-start(bf16[272,768]{1,0:T(8,128)(2,1)S(1)} %collective-permute-done.refs_1_), channel_id=1, source_target_pairs={{0,1},{1,0},{2,3},{3,2},{4,5},{5,4},{6,7},{7,6},{8,9},{9,8},{10,11... | collective-permute-start | bytes 1253384 | tf_op jit(solution)/shard_map/ppermute | solution.py:282
  43.4 16.1 %collective-permute-start.13 = (bf16[272,768]{1,0:T(8,128)(2,1)S(1)}, bf16[272,768]{1,0:T(8,128)(2,1)S(1)}, u32[]{:S(2)}, u32[]{:S(2)}) collective-permute-start(bf16[272,768]{1,0:T(8,128)(2,1)S(1)} %collective-permute-done.1.refs_2_), channel_id=1, source_target_pairs={{0,16},{1,17},{2,18},{3,19},{4,20},{5,21},{6,22},{7,23},{8,24},{9,... | collective-permute-start | bytes 1253384 | tf_op jit(solution)/shard_map/ppermute | solution.py:282
  44.0 18.1 %collective-permute-start.9 = (bf16[272,768]{1,0:T(8,128)(2,1)S(1)}, bf16[272,768]{1,0:T(8,128)(2,1)S(1)}, u32[]{:S(2)}, u32[]{:S(2)}) collective-permute-start(bf16[272,768]{1,0:T(8,128)(2,1)S(1)} %collective-permute-done.1.refs_2_), channel_id=1, source_target_pairs={{0,8},{1,9},{2,10},{3,11},{4,12},{5,13},{6,14},{7,15},{8,0},{9,1},... | collective-permute-start | bytes 1253384 | tf_op jit(solution)/shard_map/ppermute | solution.py:282
  50.5 14.0 %collective-permute-start.5 = (bf16[272,768]{1,0:T(8,128)(2,1)S(1)}, bf16[272,768]{1,0:T(8,128)(2,1)S(1)}, u32[]{:S(2)}, u32[]{:S(2)}) collective-permute-start(bf16[272,768]{1,0:T(8,128)(2,1)S(1)} %collective-permute-done.1.refs_2_), channel_id=1, source_target_pairs={{0,1},{1,0},{2,3},{3,2},{4,5},{5,4},{6,7},{7,6},{8,9},{9,8},{10,11... | collective-permute-start | bytes 1253384 | tf_op jit(solution)/shard_map/ppermute | solution.py:282
  53.1 15.3 %collective-permute-start.14 = (bf16[272,768]{1,0:T(8,128)(2,1)S(1)}, bf16[272,768]{1,0:T(8,128)(2,1)S(1)}, u32[]{:S(2)}, u32[]{:S(2)}) collective-permute-start(bf16[272,768]{1,0:T(8,128)(2,1)S(1)} %collective-permute-done.2.refs_3_), channel_id=1, source_target_pairs={{0,16},{1,17},{2,18},{3,19},{4,20},{5,21},{6,22},{7,23},{8,24},{9,... | collective-permute-start | bytes 1253384 | tf_op jit(solution)/shard_map/ppermute | solution.py:282
  55.5 15.3 %collective-permute-start.10 = (bf16[272,768]{1,0:T(8,128)(2,1)S(1)}, bf16[272,768]{1,0:T(8,128)(2,1)S(1)}, u32[]{:S(2)}, u32[]{:S(2)}) collective-permute-start(bf16[272,768]{1,0:T(8,128)(2,1)S(1)} %collective-permute-done.2.refs_3_), channel_id=1, source_target_pairs={{0,8},{1,9},{2,10},{3,11},{4,12},{5,13},{6,14},{7,15},{8,0},{9,1},... | collective-permute-start | bytes 1253384 | tf_op jit(solution)/shard_map/ppermute | solution.py:282
  59.5 12.3 %collective-permute-start.6 = (bf16[272,768]{1,0:T(8,128)(2,1)S(1)}, bf16[272,768]{1,0:T(8,128)(2,1)S(1)}, u32[]{:S(2)}, u32[]{:S(2)}) collective-permute-start(bf16[272,768]{1,0:T(8,128)(2,1)S(1)} %collective-permute-done.2.refs_3_), channel_id=1, source_target_pairs={{0,1},{1,0},{2,3},{3,2},{4,5},{5,4},{6,7},{7,6},{8,9},{9,8},{10,11... | collective-permute-start | bytes 1253384 | tf_op jit(solution)/shard_map/ppermute | solution.py:282
  62.1 15.3 %collective-permute-start.15 = (bf16[272,768]{1,0:T(8,128)(2,1)S(1)}, bf16[272,768]{1,0:T(8,128)(2,1)S(1)}, u32[]{:S(2)}, u32[]{:S(2)}) collective-permute-start(bf16[272,768]{1,0:T(8,128)(2,1)S(1)} %collective-permute-done.7.refs_8_), channel_id=1, source_target_pairs={{0,16},{1,17},{2,18},{3,19},{4,20},{5,21},{6,22},{7,23},{8,24},{9,... | collective-permute-start | bytes 1253384 | tf_op jit(solution)/shard_map/ppermute | solution.py:282
  64.5 21.9 %collective-permute-start.16 = (bf16[272,768]{1,0:T(8,128)(2,1)S(1)}, bf16[272,768]{1,0:T(8,128)(2,1)S(1)}, u32[]{:S(2)}, u32[]{:S(2)}) collective-permute-start(bf16[272,768]{1,0:T(8,128)(2,1)S(1)} %collective-permute-done.8.refs_9_), channel_id=1, source_target_pairs={{0,16},{1,17},{2,18},{3,19},{4,20},{5,21},{6,22},{7,23},{8,24},{9,... | collective-permute-start | bytes 1253384 | tf_op jit(solution)/shard_map/ppermute | solution.py:282
  68.4 26.9 %collective-permute-start.17 = (bf16[272,768]{1,0:T(8,128)(2,1)S(1)}, bf16[272,768]{1,0:T(8,128)(2,1)S(1)}, u32[]{:S(2)}, u32[]{:S(2)}) collective-permute-start(bf16[272,768]{1,0:T(8,128)(2,1)S(1)} %collective-permute-done.9.refs_10_), channel_id=1, source_target_pairs={{0,16},{1,17},{2,18},{3,19},{4,20},{5,21},{6,22},{7,23},{8,24},{9,... | collective-permute-start | bytes 1253384 | tf_op jit(solution)/shard_map/ppermute | solution.py:282
  70.9 31.2 %collective-permute-start.18 = (bf16[272,768]{1,0:T(8,128)(2,1)S(1)}, bf16[272,768]{1,0:T(8,128)(2,1)S(1)}, u32[]{:S(2)}, u32[]{:S(2)}) collective-permute-start(bf16[272,768]{1,0:T(8,128)(2,1)S(1)} %collective-permute-done.10.refs_11_), channel_id=1, source_target_pairs={{0,16},{1,17},{2,18},{3,19},{4,20},{5,21},{6,22},{7,23},{8,24},{9,... | collective-permute-start | bytes 1253384 | tf_op jit(solution)/shard_map/ppermute | solution.py:282
  128.9 9.9 %collective-permute-start.25 = (f32[1,256]{1,0:T(1,128)S(1)}, f32[1,256]{1,0:T(1,128)S(1)}, u32[]{:S(2)}, u32[]{:S(2)}) collective-permute-start(f32[1,256]{1,0:T(1,128)S(1)} %get-tuple-element.19), channel_id=1, source_target_pairs={{0,7},{1,6},{2,5},{3,4},{4,3},{5,2},{6,1},{7,0},{8,15},{9,14},{10,... | collective-permute-start | bytes 3080 | tf_op jit(solution)/shard_map/ppermute | solution.py:282
  132.4 8.3 %collective-permute-start.24 = (f32[1,256]{1,0:T(1,128)S(1)}, f32[1,256]{1,0:T(1,128)S(1)}, u32[]{:S(2)}, u32[]{:S(2)}) collective-permute-start(f32[1,256]{1,0:T(1,128)S(1)} %get-tuple-element.20), channel_id=1, source_target_pairs={{0,5},{1,4},{2,7},{3,6},{4,1},{5,0},{6,3},{7,2},{8,13},{9,12},{10,... | collective-permute-start | bytes 3080 | tf_op jit(solution)/shard_map/ppermute | solution.py:282
  135.7 5.2 %collective-permute-start.23 = (f32[1,256]{1,0:T(1,128)S(1)}, f32[1,256]{1,0:T(1,128)S(1)}, u32[]{:S(2)}, u32[]{:S(2)}) collective-permute-start(f32[1,256]{1,0:T(1,128)S(1)} %get-tuple-element.21), channel_id=1, source_target_pairs={{0,3},{1,2},{2,1},{3,0},{4,7},{5,6},{6,5},{7,4},{8,11},{9,10},{10,... | collective-permute-start | bytes 3080 | tf_op jit(solution)/shard_map/ppermute | solution.py:282
  135.9 5.0 %collective-permute-start.22 = (f32[1,256]{1,0:T(1,128)S(1)}, f32[1,256]{1,0:T(1,128)S(1)}, u32[]{:S(2)}, u32[]{:S(2)}) collective-permute-start(f32[1,256]{1,0:T(1,128)S(1)} %get-tuple-element.22), channel_id=1, source_target_pairs={{0,1},{1,0},{2,3},{3,2},{4,5},{5,4},{6,7},{7,6},{8,9},{9,8},{10,11... | collective-permute-start | bytes 3080 | tf_op jit(solution)/shard_map/ppermute | solution.py:282
  136.4 5.4 %collective-permute-start.21 = (f32[1,256]{1,0:T(1,128)S(1)}, f32[1,256]{1,0:T(1,128)S(1)}, u32[]{:S(2)}, u32[]{:S(2)}) collective-permute-start(f32[1,256]{1,0:T(1,128)S(1)} %get-tuple-element.23), channel_id=1, source_target_pairs={{0,6},{1,7},{2,4},{3,5},{4,2},{5,3},{6,0},{7,1},{8,14},{9,15},{10,... | collective-permute-start | bytes 3080 | tf_op jit(solution)/shard_map/ppermute | solution.py:282
  (11 other events, 135.2 us)

commit v2 on v1

v2 whole, which is shorter than its diff:
```python
import functools

import jax
import jax.numpy as jnp
from jax import lax
from jax.experimental import pallas as pl
from jax.experimental.pallas import tpu as pltpu
from jax.sharding import PartitionSpec as P

CLUS_GRP = 2
TILES = 4
LABEL_ROWS = 16
FAR = 1.0e9
NT = (((1,), (1,)), ((), ()))
TN = (((0,), (0,)), ((), ()))


def cover(members):
    bits = [1 << i for i in range(members.bit_length() - 1)]
    offsets = [0] + bits

    def missing(held):
        return set(range(members)) - {a ^ b for a in held for b in held}

    while missing(offsets):
        offsets.append(
            min(
                (d for d in range(members) if d not in offsets),
                key=lambda d: (len(missing(offsets + [d])), bin(d).count("1"), -d),
            )
        )
    pairs = {}
    for delta in range(members):
        pairs[delta] = min(
            (a, a ^ delta) for a in offsets if a ^ delta in offsets
        )
    return offsets, pairs


def pack_kernel(sizes, place_ref, emb_hbm, cluster_hbm, rank_hbm, *refs):
    groups, halves, half, cap, blk = sizes
    dest_ref, sends = refs[0], refs[1 : 1 + groups]
    emb_ref, cluster_ref, rank_ref, sems = refs[1 + groups :]
    rows = emb_ref.shape[0]
    step = 256
    loads = [
        pltpu.make_async_copy(cluster_hbm, cluster_ref, sems.at[0]),
        pltpu.make_async_copy(rank_hbm, rank_ref, sems.at[1]),
    ]
    for j in range(rows // step):
        at = pl.ds(j * step, step)
        loads.append(pltpu.make_async_copy(emb_hbm.at[at], emb_ref.at[at], sems.at[2 + j]))
    for load in loads:
        load.start()
    for load in loads[:2]:
        load.wait()
    cluster = cluster_ref[...]
    rank = rank_ref[...]
    alive = cluster >= 0
    pair = lax.shift_right_logical(jnp.maximum(cluster, 0), 1)
    parity = jnp.maximum(cluster, 0) - 2 * pair
    safe_rank = jnp.maximum(rank, 0)
    which = safe_rank // half
    units = groups * halves
    unit_id = jnp.where(alive, pair * halves + which, -1)
    before_rows = lax.broadcasted_iota(jnp.int32, (step, step), 0)
    before_cols = lax.broadcasted_iota(jnp.int32, (step, step), 1)
    upper = (before_rows < before_cols).astype(jnp.float32).astype(jnp.bfloat16)
    unit_iota = lax.broadcasted_iota(jnp.int32, (units, step), 0)
    carry = jnp.zeros((units, 1), jnp.float32)
    places = []
    for j in range(rows // step):
        mine = unit_id[:, j * step : (j + 1) * step]
        hit = (unit_iota == mine).astype(jnp.float32)
        before = jnp.dot(hit.astype(jnp.bfloat16), upper, preferred_element_type=jnp.float32) + carry
        position = jnp.sum(hit * before, axis=0, keepdims=True)
        carry = carry + jnp.sum(hit, axis=1, keepdims=True)
        places.append(jnp.where(mine >= 0, mine * cap + position.astype(jnp.int32), -1))
    dest = jnp.concatenate(places, axis=1)
    dest_ref[...] = dest
    dest = jnp.where(dest >= 0, dest ^ (place_ref[0] * blk), -1)

    units_of = []
    for j in range(rows // step):
        loads[2 + j].wait()
        wide = emb_ref[j * step : (j + 1) * step, :].astype(jnp.float32)
        total = jnp.sum(wide * wide, axis=1, keepdims=True)
        units_of.append((wide * lax.rsqrt(total + 1e-06)).astype(jnp.bfloat16))
    unit = jnp.concatenate(units_of, axis=0)

    field = lax.broadcasted_iota(jnp.int32, (LABEL_ROWS, rows), 0)
    labels = jnp.where(
        field == 0, safe_rank - which * half, jnp.where(field == 1, parity + 1, 0)
    )
    labels = jnp.where(alive, labels, 0).astype(jnp.float32).astype(jnp.bfloat16)
    per_tile = blk // TILES
    wide_tile = groups * per_tile
    spread = (
        lax.broadcasted_iota(jnp.int32, (blk, wide_tile), 0) % per_tile
        == lax.broadcasted_iota(jnp.int32, (blk, wide_tile), 1) % per_tile
    )
    spread = spread.astype(jnp.float32).astype(jnp.bfloat16)
    label_row = lax.broadcasted_iota(jnp.int32, (LABEL_ROWS, blk), 0)
    label_col = lax.broadcasted_iota(jnp.int32, (LABEL_ROWS, blk), 1)
    own_tile = label_row == lax.div(label_col, per_tile)
    unit_col = lax.div(label_col, cap).astype(jnp.float32)
    slot = lax.broadcasted_iota(jnp.int32, (blk, rows), 0)
    width = sends[0].shape[1]
    for k in range(groups):
        pick = (slot + k * blk == dest).astype(jnp.float32).astype(jnp.bfloat16)
        sends[k][0:blk, :] = jnp.dot(pick, unit, preferred_element_type=jnp.float32).astype(
            jnp.bfloat16
        )
        mine = lax.dot_general(labels, pick, NT, preferred_element_type=jnp.float32)
        plain = jnp.where(label_row == 2, unit_col, mine)
        parts = [plain] + [jnp.zeros_like(plain)] * ((wide_tile - blk) // blk)
        for f in range(2):
            line = jnp.where(own_tile, mine[f : f + 1, :], 0.0).astype(jnp.bfloat16)
            parts.append(jnp.dot(line, spread, preferred_element_type=jnp.float32))
        if width > 3 * wide_tile:
            parts.append(jnp.zeros((LABEL_ROWS, width - 3 * wide_tile), jnp.float32))
        sends[k][blk : blk + LABEL_ROWS, :] = jnp.concatenate(parts, axis=1).astype(jnp.bfloat16)


def pack(place, embeddings, cluster, rank, sizes):
    groups, halves, half, cap, blk = sizes
    rows, width = embeddings.shape
    vmem = pl.BlockSpec(memory_space=pltpu.VMEM)
    hbm = pl.BlockSpec(memory_space=pltpu.HBM)
    out_shape = [jax.ShapeDtypeStruct((1, rows), jnp.int32)]
    out_shape += [jax.ShapeDtypeStruct((blk + LABEL_ROWS, width), jnp.bfloat16)] * groups
    return pl.pallas_call(
        functools.partial(pack_kernel, sizes),
        out_shape=out_shape,
        in_specs=[pl.BlockSpec(memory_space=pltpu.SMEM), hbm, hbm, hbm],
        out_specs=[vmem] * len(out_shape),
        scratch_shapes=[
            pltpu.VMEM((rows, width), jnp.bfloat16),
            pltpu.VMEM((1, rows), jnp.int32),
            pltpu.VMEM((1, rows), jnp.int32),
            pltpu.SemaphoreType.DMA((2 + rows // 256,)),
        ],
        compiler_params=pltpu.CompilerParams(vmem_limit_bytes=48 * 1024 * 1024),
    )(place, embeddings, cluster.reshape(1, rows), rank.reshape(1, rows))


def compare_kernel(sizes, plan, n_sets, joined, place_ref, *refs):
    groups, halves, half, cap, blk = sizes
    blocks = [refs[i * groups : (i + 1) * groups] for i in range(n_sets)]
    n_out = 1 if joined else len(plan)
    outs = refs[n_sets * groups : n_sets * groups + n_out]
    key_col, key_row, low_row, turned, best = refs[n_sets * groups + n_out :]
    rows = groups * blk
    per_tile = blk // TILES
    tile = rows // TILES
    cap_all = float(halves * half)

    lane = lax.broadcasted_iota(jnp.int32, (LABEL_ROWS, tile), 1)
    line = lax.broadcasted_iota(jnp.int32, (LABEL_ROWS, tile), 0)
    from_block = lax.div(lane, per_tile)
    which = line * (halves // TILES) + lax.div(lane - from_block * per_tile, cap)
    weight_row = lax.broadcasted_iota(jnp.int32, (LABEL_ROWS, 128), 0)
    weights = jnp.where(
        weight_row == 0,
        1.0,
        jnp.where(weight_row == 1, cap_all, jnp.where(weight_row == 2, float(half), 0.0)),
    ).astype(jnp.bfloat16)
    for i in range(n_sets):
        for k in range(groups):
            key_col[pl.ds((i * groups + k) * blk, blk), :] = lax.dot_general(
                blocks[i][k][blk : blk + LABEL_ROWS, 0:blk], weights, TN, preferred_element_type=jnp.float32
            )
    for o, (a, _) in enumerate(plan):
        rest = jnp.zeros((LABEL_ROWS, tile), jnp.float32)
        code = jnp.zeros((LABEL_ROWS, tile), jnp.float32)
        for k in range(groups):
            label = blocks[a][k][blk : blk + LABEL_ROWS, tile : 3 * tile].astype(jnp.float32)
            rest = jnp.where(from_block == k, label[:, :tile], rest)
            code = jnp.where(from_block == k, label[:, tile:], code)
        low = code * cap_all
        key = low + (which * half).astype(jnp.float32) + rest
        low = jnp.where(code > 0.5, low, FAR)
        key_row[o] = key[0:8]
        low_row[o] = low[0:8]

    def tile_of(i, t):
        at = pl.ds(pl.multiple_of(t * per_tile, per_tile), per_tile)
        return [blocks[i][k][at, :] for k in range(groups)]

    for o, (a, cols) in enumerate(plan):

        def one_tile(t, _, a=a, cols=cols, o=o):
            turned[...] = jnp.concatenate(tile_of(a, t), axis=0).T
            mine = key_row[o, pl.ds(t, 1), :]
            floor = low_row[o, pl.ds(t, 1), :]

            def one_col(s, acc):
                theirs = []
                pieces = []
                for b in cols:
                    pieces += tile_of(b, s)
                    for k in range(groups):
                        at = pl.multiple_of((b * groups + k) * blk + s * per_tile, per_tile)
                        theirs.append(key_col[pl.ds(at, per_tile), :])
                theirs = jnp.concatenate(theirs, axis=0)
                theirs = jnp.concatenate([theirs] * (tile // 128), axis=1)
                sims = jnp.dot(
                    jnp.concatenate(pieces, axis=0), turned[...], preferred_element_type=jnp.float32
                )
                keep = (theirs >= floor) & (theirs < mine)
                sims = jnp.where(keep, sims, -1.0)
                top = jnp.max(sims.reshape(len(cols) * tile // 8, 8, tile), axis=0)
                return jnp.maximum(acc, top)

            acc = lax.fori_loop(0, t + 1, one_col, jnp.full((8, tile), -1.0, jnp.float32))
            best[o, pl.ds(t, 1), :] = jnp.max(acc, axis=0, keepdims=True)
            return 0

        lax.fori_loop(0, TILES, one_tile, 0)

    lane = lax.broadcasted_iota(jnp.int32, (1, tile), 1)
    for o, (a, _) in enumerate(plan):
        found = best[o]
        for k in range(groups):
            total = jnp.full((1, tile), -1.0, jnp.float32)
            for t in range(TILES):
                turn = ((t - k) * per_tile) % tile
                moved = pltpu.roll(found, turn, 1) if turn else found
                total = jnp.where(lax.div(lane, per_tile) == t, moved[t : t + 1], total)
            block = place_ref[0] ^ k
            if joined:
                side = joined
                outs[0][pl.ds(block * side + (place_ref[1] ^ a), 1), 0, :] = total[:, :blk]
            else:
                outs[o][pl.ds(block, 1), 0, :] = total[:, :blk]


def compare(place, sets, plan, joined, sizes):
    groups, halves, half, cap, blk = sizes
    n_sets = len(sets)
    flat = [piece for one in sets for piece in one]
    rows, width = groups * blk, flat[0].shape[1]
    tile = rows // TILES
    vmem = pl.BlockSpec(memory_space=pltpu.VMEM)
    combos = sum(len(cols) for _, cols in plan) * TILES * (TILES + 1) // 2
    if joined:
        out_shape = [jax.ShapeDtypeStruct((groups * joined, 1, blk), jnp.float32)]
    else:
        out_shape = [jax.ShapeDtypeStruct((groups, 1, blk), jnp.float32)] * len(plan)
    return pl.pallas_call(
        functools.partial(compare_kernel, sizes, plan, n_sets, joined),
        out_shape=out_shape,
        in_specs=[pl.BlockSpec(memory_space=pltpu.SMEM)] + [vmem] * len(flat),
        out_specs=[vmem] * len(out_shape),
        scratch_shapes=[
            pltpu.VMEM((n_sets * rows, 128), jnp.float32),
            pltpu.VMEM((len(plan), 8, tile), jnp.float32),
            pltpu.VMEM((len(plan), 8, tile), jnp.float32),
            pltpu.VMEM((width, tile), jnp.bfloat16),
            pltpu.VMEM((len(plan), 8, tile), jnp.float32),
        ],
        compiler_params=pltpu.CompilerParams(vmem_limit_bytes=48 * 1024 * 1024),
        cost_estimate=pl.CostEstimate(
            flops=2 * combos * tile * tile * width, bytes_accessed=2 * n_sets * rows * width, transcendentals=0
        ),
    )(place, *flat)


def unpack_kernel(sizes, dest_ref, back_ref, out_ref):
    groups, halves, half, cap, blk = sizes
    side = back_ref.shape[0] // groups
    rows = dest_ref.shape[1]
    dest = dest_ref[...]
    slot = lax.broadcasted_iota(jnp.int32, (blk, rows), 0)
    field = lax.broadcasted_iota(jnp.int32, (LABEL_ROWS, blk), 0)
    total = jnp.zeros((LABEL_ROWS, rows), jnp.float32)
    for k in range(groups):
        value = back_ref[k * side]
        for more in range(1, side):
            value = jnp.maximum(value, back_ref[k * side + more])
        top = value.astype(jnp.bfloat16).astype(jnp.float32)
        rest = value - top
        mid = rest.astype(jnp.bfloat16).astype(jnp.float32)
        low = rest - mid
        stack = jnp.where(field == 0, top, jnp.where(field == 1, mid, jnp.where(field == 2, low, 0.0)))
        pick = (slot + k * blk == dest).astype(jnp.float32).astype(jnp.bfloat16)
        total = total + jnp.dot(stack.astype(jnp.bfloat16), pick, preferred_element_type=jnp.float32)
    value = (total[0:1] + total[1:2]) + total[2:3]
    out_ref[...] = jnp.where(dest >= 0, value, -1.0)


def unpack(dest, back, sizes):
    vmem = pl.BlockSpec(memory_space=pltpu.VMEM)
    return pl.pallas_call(
        functools.partial(unpack_kernel, sizes),
        out_shape=jax.ShapeDtypeStruct(dest.shape, jnp.float32),
        in_specs=[vmem] * 2,
        out_specs=vmem,
        compiler_params=pltpu.CompilerParams(vmem_limit_bytes=48 * 1024 * 1024),
    )(dest, back)


def on_device(embeddings, cluster, rank):
    rows_dev, width = embeddings.shape
    groups = lax.axis_size("grp")
    members = lax.axis_size("mem")
    devices = groups * members
    halves = 2 * members
    half = rows_dev // CLUS_GRP // 2
    blk = rows_dev // groups
    cap = blk // halves
    sizes = (groups, halves, half, cap, blk)
    side = members // groups

    def swap(value, block_step, member_step):
        mask = member_step // side * members + block_step * side + member_step % side
        if mask == 0:
            return value
        return lax.ppermute(value, ("grp", "mem"), [(i, i ^ mask) for i in range(devices)])

    offsets, pairs = cover(members)
    here = lax.axis_index("mem").astype(jnp.int32)
    place = jnp.stack([here // side, here % side])
    packed = pack(place, embeddings, cluster, rank, sizes)
    dest, sends = packed[0], packed[1:]

    own = [sends[0]]
    for k in range(1, groups):
        send = sends[k]
        if k > 2:
            send, own[k - 1] = lax.optimization_barrier((send, own[k - 1]))
        own.append(swap(send, k, 0))
    held = {0: own}
    for d in offsets[1:]:
        core_bit = d & ~side
        via = core_bit if d & side and core_bit in held else 0
        held[d] = [swap(piece, 0, d ^ via) for piece in held[via]]

    index = {d: i for i, d in enumerate(offsets)}
    starts = sorted({a for a, _ in pairs.values()})
    plan = [(index[a], [index[b] for _, (e, b) in sorted(pairs.items()) if e == a]) for a in starts]
    joined = side if all(a < side for a in starts) else 0
    found = compare(place, [held[d] for d in offsets], plan, joined, sizes)
    if joined:
        back = found[0]
    else:
        best = {}
        for a, value in zip(starts, found):
            near = a % side
            value = swap(value, 0, a - near)
            best[near] = jnp.maximum(best[near], value) if near in best else value
        none = jnp.full_like(found[0], -1.0)
        near_of = [best.get(near, none) for near in range(side)]
        rows_of = []
        for spot in range(side):
            value = near_of[spot]
            for mine in range(1, side):
                value = jnp.where(place[1] == mine, near_of[spot ^ mine], value)
            rows_of.append(value)
        back = jnp.stack(rows_of, axis=1).reshape(groups * side, 1, blk)
    back = lax.all_to_all(back, "mem", split_axis=0, concat_axis=0, tiled=True)
    return unpack(dest, back, sizes).reshape(rows_dev)


def solution(mesh):
    in_specs = (P(("grp", "mem"), None), P(("grp", "mem")), P(("grp", "mem")))
    out_specs = P(("grp", "mem"))
    return jax.shard_map(
        on_device, mesh=mesh, in_specs=in_specs, out_specs=out_specs, check_vma=False
    )
```

time: 146 us -> 94.5 us (0.65)
  waiting for transfers between devices: 72.8 us -> 35.6 us
  starting transfers between devices: 38.7 us -> 20.8 us
  blocking collectives: 0 us -> 12 us
  Pallas kernels: 30.2 us -> 21.4 us
    ppermute x26 -> x19, waiting for transfers between devices: 72.8 us -> 35.6 us  [swap(): lax.ppermute(value, ('grp', 'mem'), [(i, i ^ mask) for i in range(devices)])]
    ppermute x26 -> x19, starting transfers between devices: 38.7 us -> 20.8 us  [swap(): lax.ppermute(value, ('grp', 'mem'), [(i, i ^ mask) for i in range(devices)])]
    all_to_all x0 -> x1, blocking collectives: none -> 12 us  [on_device(): back = lax.all_to_all(back, 'mem', split_axis=0, concat_axis=0, tiled=True)]
    pallas_call x1, Pallas kernels: 25.9 us -> 15.5 us  [compare(): pl.pallas_call(functools.partial(compare_kernel, sizes, plan, n_sets, joi...]
    pallas_call x1, Pallas kernels: 3.14 us -> 4.82 us  [pack(): pl.pallas_call(functools.partial(pack_kernel, sizes), out_shape=out_shape...]
  transfers between devices with their start and end apart: 26 -> 19, of which waited for: 13 -> 8; matrix products, arithmetic and copies ran while one was open for 0% -> 0% of each run, Pallas kernels for 0% -> 0%
where the time goes in v2:
time: 94.5 us; the launch traced here: 94.2 us
  waiting for transfers between devices  35.6 us (38%)
  Pallas kernels  21.4 us (23%)
  starting transfers between devices  20.8 us (22%)
  blocking collectives  12 us (13%)
  local copies, waits for them, and re-layouts  4.27 us (5%)
    ppermute x19, waiting for transfers between devices, swap(): lax.ppermute(value, ('grp', 'mem'), [(i, i ^ mask) for i in range(devices)])  35.6 us
    ppermute x19, starting transfers between devices, swap(): lax.ppermute(value, ('grp', 'mem'), [(i, i ^ mask) for i in range(devices)])  20.8 us
    pallas_call x1, Pallas kernels, compare(): pl.pallas_call(functools.partial(compare_kernel, sizes, plan, n_sets, joi...  15.5 us
    all_to_all x1, blocking collectives, on_device(): back = lax.all_to_all(back, 'mem', split_axis=0, concat_axis=0, tiled=True)  12 us
    pallas_call x1, Pallas kernels, pack(): pl.pallas_call(functools.partial(pack_kernel, sizes), out_shape=out_shape...  4.82 us
    unnamed x18, local copies, waits for them, and re-layouts  4.27 us
  transfers between devices with their start and end apart: 19, of which 8 were waited for; matrix products, arithmetic and copies ran while one was open for 0% of the time, Pallas kernels for 0%

profile of v2, /device:TPU:0, one launch (start us, length us, event | category | flops | bytes accessed | tf_op | source)
XLA Modules:
  0.0 94.2 jit_solution(11467830585632218679)
XLA Ops:
  0.1 1.4 %copy-done = bf16[1024,768]{1,0:T(8,128)(2,1)S(1)} copy-done((bf16[1024,768]{1,0:T(8,128)(2,1)S(1)}, bf16[1024,768]{1,0:T(8,128)(2,1)}, u32[]{:S(2)}) %copy-start) | copy-done | bytes 1572888
  2.2 0.7 copy-done.2
  2.9 4.8 %shard_map.37 = (s32[1,1024]{1,0:T(1,128)S(1)}, bf16[272,768]{1,0:T(8,128)(2,1)S(1)}, bf16[272,768]{1,0:T(8,128)(2,1)S(1)}, bf16[272,768]{1,0:T(8,128)(2,1)S(1)}, bf16[272,768]{1,0:T(8,128)(2,1)S(1)}) custom-call(s32[2]{0:T(128)S(1)} %pad_add_fusion.place_ref, bf16[1024,768]{1,0:T(8,128)(2,1)S(1)} %copy-done, s32[1,1024]{1,0:T(1,128)S(1)} %bitcast.5, ...), custom_call_target="tpu_custom_call" | custom-call | tf_op jit(solution)/shard_map/pallas_call | solution.py:132
  7.7 4.1 %collective-permute-start.1 = (bf16[272,768]{1,0:T(8,128)(2,1)S(1)}, bf16[272,768]{1,0:T(8,128)(2,1)S(1)}, u32[]{:S(2)}, u32[]{:S(2)}) collective-permute-start(bf16[272,768]{1,0:T(8,128)(2,1)S(1)} %get-tuple-element.16), channel_id=1, source_target_pairs={{0,4},{1,5},{2,6},{3,7},{4,0},{5,1},{6,2},{7,3},{8,12},{9,13},{10,... | collective-permute-start | bytes 1253384 | tf_op jit(solution)/shard_map/ppermute | solution.py:319
  11.8 1.6 %collective-permute-start = (bf16[272,768]{1,0:T(8,128)(2,1)S(1)}, bf16[272,768]{1,0:T(8,128)(2,1)S(1)}, u32[]{:S(2)}, u32[]{:S(2)}) collective-permute-start(bf16[272,768]{1,0:T(8,128)(2,1)S(1)} %get-tuple-element.14), channel_id=1, source_target_pairs={{0,2},{1,3},{2,0},{3,1},{4,6},{5,7},{6,4},{7,5},{8,10},{9,11},{10,... | collective-permute-start | bytes 1253384 | tf_op jit(solution)/shard_map/ppermute | solution.py:319
  13.4 1.5 %collective-permute-start.11 = (bf16[272,768]{1,0:T(8,128)(2,1)S(1)}, bf16[272,768]{1,0:T(8,128)(2,1)S(1)}, u32[]{:S(2)}, u32[]{:S(2)}) collective-permute-start(bf16[272,768]{1,0:T(8,128)(2,1)S(1)} %get-tuple-element.13.refs_0_), channel_id=1, source_target_pairs={{0,16},{1,17},{2,18},{3,19},{4,20},{5,21},{6,22},{7,23},{8,24},{9,... | collective-permute-start | bytes 1253384 | tf_op jit(solution)/shard_map/ppermute | solution.py:319
  14.9 1.5 %collective-permute-start.3 = (bf16[272,768]{1,0:T(8,128)(2,1)S(1)}, bf16[272,768]{1,0:T(8,128)(2,1)S(1)}, u32[]{:S(2)}, u32[]{:S(2)}) collective-permute-start(bf16[272,768]{1,0:T(8,128)(2,1)S(1)} %get-tuple-element.13.refs_0_), channel_id=1, source_target_pairs={{0,1},{1,0},{2,3},{3,2},{4,5},{5,4},{6,7},{7,6},{8,9},{9,8},{10,11... | collective-permute-start | bytes 1253384 | tf_op jit(solution)/shard_map/ppermute | solution.py:319
  16.4 14.1 %collective-permute-done.1.refs_2_ = bf16[272,768]{1,0:T(8,128)(2,1)S(1)} collective-permute-done((bf16[272,768]{1,0:T(8,128)(2,1)S(1)}, bf16[272,768]{1,0:T(8,128)(2,1)S(1)}, u32[]{:S(2)}, u32[]{:S(2)}) %collective-permute-start.1) | collective-permute-done | bytes 417824 | tf_op jit(solution)/shard_map/ppermute | solution.py:319
  30.7 1.6 %collective-permute-start.12 = (bf16[272,768]{1,0:T(8,128)(2,1)S(1)}, bf16[272,768]{1,0:T(8,128)(2,1)S(1)}, u32[]{:S(2)}, u32[]{:S(2)}) collective-permute-start(bf16[272,768]{1,0:T(8,128)(2,1)S(1)} %collective-permute-done.refs_1_), channel_id=1, source_target_pairs={{0,16},{1,17},{2,18},{3,19},{4,20},{5,21},{6,22},{7,23},{8,24},{9,... | collective-permute-start | bytes 1253384 | tf_op jit(solution)/shard_map/ppermute | solution.py:319
  32.2 1.5 %collective-permute-start.4 = (bf16[272,768]{1,0:T(8,128)(2,1)S(1)}, bf16[272,768]{1,0:T(8,128)(2,1)S(1)}, u32[]{:S(2)}, u32[]{:S(2)}) collective-permute-start(bf16[272,768]{1,0:T(8,128)(2,1)S(1)} %collective-permute-done.refs_1_), channel_id=1, source_target_pairs={{0,1},{1,0},{2,3},{3,2},{4,5},{5,4},{6,7},{7,6},{8,9},{9,8},{10,11... | collective-permute-start | bytes 1253384 | tf_op jit(solution)/shard_map/ppermute | solution.py:319
  33.8 3.2 %collective-permute-start.2 = (bf16[272,768]{1,0:T(8,128)(2,1)S(1)}, bf16[272,768]{1,0:T(8,128)(2,1)S(1)}, u32[]{:S(2)}, u32[]{:S(2)}) collective-permute-start(bf16[272,768]{1,0:T(8,128)(2,1)S(1)} %get-tuple-element.18), channel_id=1, source_target_pairs={{0,6},{1,7},{2,4},{3,5},{4,2},{5,3},{6,0},{7,1},{8,14},{9,15},{10,... | collective-permute-start | bytes 1253384 | tf_op jit(solution)/shard_map/ppermute | solution.py:319
  37.5 5.4 %collective-permute-done.12.refs_13_ = bf16[272,768]{1,0:T(8,128)(2,1)S(1)} collective-permute-done((bf16[272,768]{1,0:T(8,128)(2,1)S(1)}, bf16[272,768]{1,0:T(8,128)(2,1)S(1)}, u32[]{:S(2)}, u32[]{:S(2)}) %collective-permute-start.12) | collective-permute-done | bytes 417824 | tf_op jit(solution)/shard_map/ppermute | solution.py:319
  42.9 1.9 %collective-permute-start.5 = (bf16[272,768]{1,0:T(8,128)(2,1)S(1)}, bf16[272,768]{1,0:T(8,128)(2,1)S(1)}, u32[]{:S(2)}, u32[]{:S(2)}) collective-permute-start(bf16[272,768]{1,0:T(8,128)(2,1)S(1)} %collective-permute-done.1.refs_2_), channel_id=1, source_target_pairs={{0,1},{1,0},{2,3},{3,2},{4,5},{5,4},{6,7},{7,6},{8,9},{9,8},{10,11... | collective-permute-start | bytes 1253384 | tf_op jit(solution)/shard_map/ppermute | solution.py:319
  45.1 2.4 %collective-permute-done.2.refs_3_ = bf16[272,768]{1,0:T(8,128)(2,1)S(1)} collective-permute-done((bf16[272,768]{1,0:T(8,128)(2,1)S(1)}, bf16[272,768]{1,0:T(8,128)(2,1)S(1)}, u32[]{:S(2)}, u32[]{:S(2)}) %collective-permute-start.2) | collective-permute-done | bytes 417824 | tf_op jit(solution)/shard_map/ppermute | solution.py:319
  48.0 3.0 %collective-permute-done.13.refs_14_ = bf16[272,768]{1,0:T(8,128)(2,1)S(1)} collective-permute-done((bf16[272,768]{1,0:T(8,128)(2,1)S(1)}, bf16[272,768]{1,0:T(8,128)(2,1)S(1)}, u32[]{:S(2)}, u32[]{:S(2)}) %collective-permute-start.13) | collective-permute-done | bytes 417824 | tf_op jit(solution)/shard_map/ppermute | solution.py:319
  51.0 2.1 %collective-permute-start.6 = (bf16[272,768]{1,0:T(8,128)(2,1)S(1)}, bf16[272,768]{1,0:T(8,128)(2,1)S(1)}, u32[]{:S(2)}, u32[]{:S(2)}) collective-permute-start(bf16[272,768]{1,0:T(8,128)(2,1)S(1)} %collective-permute-done.2.refs_3_), channel_id=1, source_target_pairs={{0,1},{1,0},{2,3},{3,2},{4,5},{5,4},{6,7},{7,6},{8,9},{9,8},{10,11... | collective-permute-start | bytes 1253384 | tf_op jit(solution)/shard_map/ppermute | solution.py:319
  53.1 2.3 %collective-permute-done.5.refs_6_ = bf16[272,768]{1,0:T(8,128)(2,1)S(1)} collective-permute-done((bf16[272,768]{1,0:T(8,128)(2,1)S(1)}, bf16[272,768]{1,0:T(8,128)(2,1)S(1)}, u32[]{:S(2)}, u32[]{:S(2)}) %collective-permute-start.5) | collective-permute-done | bytes 417824 | tf_op jit(solution)/shard_map/ppermute | solution.py:319
  56.0 3.2 %collective-permute-done.14.refs_15_ = bf16[272,768]{1,0:T(8,128)(2,1)S(1)} collective-permute-done((bf16[272,768]{1,0:T(8,128)(2,1)S(1)}, bf16[272,768]{1,0:T(8,128)(2,1)S(1)}, u32[]{:S(2)}, u32[]{:S(2)}) %collective-permute-start.14) | collective-permute-done | bytes 417824 | tf_op jit(solution)/shard_map/ppermute | solution.py:319
  59.2 4.9 %collective-permute-done.6.refs_7_ = bf16[272,768]{1,0:T(8,128)(2,1)S(1)} collective-permute-done((bf16[272,768]{1,0:T(8,128)(2,1)S(1)}, bf16[272,768]{1,0:T(8,128)(2,1)S(1)}, u32[]{:S(2)}, u32[]{:S(2)}) %collective-permute-start.6) | collective-permute-done | bytes 417824 | tf_op jit(solution)/shard_map/ppermute | solution.py:319
  64.1 0.7 copy-done.7
  64.9 0.8 copy-done.8
  65.6 15.5 %shard_map.38 = f32[8,1,256]{2,1,0:T(1,128)S(1)} custom-call(s32[2]{0:T(128)S(1)} %pad_add_fusion.place_ref, bf16[272,768]{1,0:T(8,128)(2,1)S(1)} %get-tuple-element.13.refs_0_, bf16[272,768]{1,0:T(8,128)(2,1)S(1)} %collective-permute-done.refs_1_, bf16[272,768]{1,0:T(8,128)(2,1)S(1)} %collective-permute-done.1.refs_2_, ...), custom_call_target="tpu_custom_call" | custom-call | flops 8053063680 | bytes 7864320 | tf_op jit(solution)/shard_map/pallas_call | solution.py:250
  81.1 12.0 %all_to_all.5.back_ref = f32[8,1,256]{2,1,0:T(1,128)S(1)} all-to-all(f32[8,1,256]{2,1,0:T(1,128)S(1)} %shard_map.38), channel_id=1, replica_groups=mesh['grp'=4,'mem'=8] {'mem'}, dimensions={0} | all-to-all | bytes 16384 | tf_op jit(solution)/shard_map/all_to_all | solution.py:361
  93.1 1.1 %shard_map.39 = f32[1,1024]{1,0:T(1,128)} custom-call(s32[1,1024]{1,0:T(1,128)S(1)} %get-tuple-element.12.dest_ref, f32[8,1,256]{2,1,0:T(1,128)S(1)} %all_to_all.5.back_ref), custom_call_target="tpu_custom_call" | custom-call | tf_op jit(solution)/shard_map/pallas_call | solution.py:294
  (37 shorter events, 2.8 us)
Async XLA Ops:
  0.1 1.4 %copy-start = (bf16[1024,768]{1,0:T(8,128)(2,1)S(1)}, bf16[1024,768]{1,0:T(8,128)(2,1)}, u32[]{:S(2)}) copy-start(bf16[1024,768]{1,0:T(8,128)(2,1)} %emb_hbm.1) | copy-start | bytes 4718596
  7.7 22.8 %collective-permute-start.1 = (bf16[272,768]{1,0:T(8,128)(2,1)S(1)}, bf16[272,768]{1,0:T(8,128)(2,1)S(1)}, u32[]{:S(2)}, u32[]{:S(2)}) collective-permute-start(bf16[272,768]{1,0:T(8,128)(2,1)S(1)} %get-tuple-element.16), channel_id=1, source_target_pairs={{0,4},{1,5},{2,6},{3,7},{4,0},{5,1},{6,2},{7,3},{8,12},{9,13},{10,... | collective-permute-start | bytes 1253384 | tf_op jit(solution)/shard_map/ppermute | solution.py:319
  11.8 18.9 %collective-permute-start = (bf16[272,768]{1,0:T(8,128)(2,1)S(1)}, bf16[272,768]{1,0:T(8,128)(2,1)S(1)}, u32[]{:S(2)}, u32[]{:S(2)}) collective-permute-start(bf16[272,768]{1,0:T(8,128)(2,1)S(1)} %get-tuple-element.14), channel_id=1, source_target_pairs={{0,2},{1,3},{2,0},{3,1},{4,6},{5,7},{6,4},{7,5},{8,10},{9,11},{10,... | collective-permute-start | bytes 1253384 | tf_op jit(solution)/shard_map/ppermute | solution.py:319
  13.4 18.9 %collective-permute-start.11 = (bf16[272,768]{1,0:T(8,128)(2,1)S(1)}, bf16[272,768]{1,0:T(8,128)(2,1)S(1)}, u32[]{:S(2)}, u32[]{:S(2)}) collective-permute-start(bf16[272,768]{1,0:T(8,128)(2,1)S(1)} %get-tuple-element.13.refs_0_), channel_id=1, source_target_pairs={{0,16},{1,17},{2,18},{3,19},{4,20},{5,21},{6,22},{7,23},{8,24},{9,... | collective-permute-start | bytes 1253384 | tf_op jit(solution)/shard_map/ppermute | solution.py:319
  14.9 18.9 %collective-permute-start.7 = (bf16[272,768]{1,0:T(8,128)(2,1)S(1)}, bf16[272,768]{1,0:T(8,128)(2,1)S(1)}, u32[]{:S(2)}, u32[]{:S(2)}) collective-permute-start(bf16[272,768]{1,0:T(8,128)(2,1)S(1)} %get-tuple-element.13.refs_0_), channel_id=1, source_target_pairs={{0,8},{1,9},{2,10},{3,11},{4,12},{5,13},{6,14},{7,15},{8,0},{9,1},... | collective-permute-start | bytes 1253384 | tf_op jit(solution)/shard_map/ppermute | solution.py:319
  14.9 22.1 %collective-permute-start.3 = (bf16[272,768]{1,0:T(8,128)(2,1)S(1)}, bf16[272,768]{1,0:T(8,128)(2,1)S(1)}, u32[]{:S(2)}, u32[]{:S(2)}) collective-permute-start(bf16[272,768]{1,0:T(8,128)(2,1)S(1)} %get-tuple-element.13.refs_0_), channel_id=1, source_target_pairs={{0,1},{1,0},{2,3},{3,2},{4,5},{5,4},{6,7},{7,6},{8,9},{9,8},{10,11... | collective-permute-start | bytes 1253384 | tf_op jit(solution)/shard_map/ppermute | solution.py:319
  30.7 12.2 %collective-permute-start.12 = (bf16[272,768]{1,0:T(8,128)(2,1)S(1)}, bf16[272,768]{1,0:T(8,128)(2,1)S(1)}, u32[]{:S(2)}, u32[]{:S(2)}) collective-permute-start(bf16[272,768]{1,0:T(8,128)(2,1)S(1)} %collective-permute-done.refs_1_), channel_id=1, source_target_pairs={{0,16},{1,17},{2,18},{3,19},{4,20},{5,21},{6,22},{7,23},{8,24},{9,... | collective-permute-start | bytes 1253384 | tf_op jit(solution)/shard_map/ppermute | solution.py:319
  32.2 10.7 %collective-permute-start.8 = (bf16[272,768]{1,0:T(8,128)(2,1)S(1)}, bf16[272,768]{1,0:T(8,128)(2,1)S(1)}, u32[]{:S(2)}, u32[]{:S(2)}) collective-permute-start(bf16[272,768]{1,0:T(8,128)(2,1)S(1)} %collective-permute-done.refs_1_), channel_id=1, source_target_pairs={{0,8},{1,9},{2,10},{3,11},{4,12},{5,13},{6,14},{7,15},{8,0},{9,1},... | collective-permute-start | bytes 1253384 | tf_op jit(solution)/shard_map/ppermute | solution.py:319
  32.2 12.6 %collective-permute-start.4 = (bf16[272,768]{1,0:T(8,128)(2,1)S(1)}, bf16[272,768]{1,0:T(8,128)(2,1)S(1)}, u32[]{:S(2)}, u32[]{:S(2)}) collective-permute-start(bf16[272,768]{1,0:T(8,128)(2,1)S(1)} %collective-permute-done.refs_1_), channel_id=1, source_target_pairs={{0,1},{1,0},{2,3},{3,2},{4,5},{5,4},{6,7},{7,6},{8,9},{9,8},{10,11... | collective-permute-start | bytes 1253384 | tf_op jit(solution)/shard_map/ppermute | solution.py:319
  33.8 13.7 %collective-permute-start.2 = (bf16[272,768]{1,0:T(8,128)(2,1)S(1)}, bf16[272,768]{1,0:T(8,128)(2,1)S(1)}, u32[]{:S(2)}, u32[]{:S(2)}) collective-permute-start(bf16[272,768]{1,0:T(8,128)(2,1)S(1)} %get-tuple-element.18), channel_id=1, source_target_pairs={{0,6},{1,7},{2,4},{3,5},{4,2},{5,3},{6,0},{7,1},{8,14},{9,15},{10,... | collective-permute-start | bytes 1253384 | tf_op jit(solution)/shard_map/ppermute | solution.py:319
  37.0 14.0 %collective-permute-start.13 = (bf16[272,768]{1,0:T(8,128)(2,1)S(1)}, bf16[272,768]{1,0:T(8,128)(2,1)S(1)}, u32[]{:S(2)}, u32[]{:S(2)}) collective-permute-start(bf16[272,768]{1,0:T(8,128)(2,1)S(1)} %collective-permute-done.1.refs_2_), channel_id=1, source_target_pairs={{0,16},{1,17},{2,18},{3,19},{4,20},{5,21},{6,22},{7,23},{8,24},{9,... | collective-permute-start | bytes 1253384 | tf_op jit(solution)/shard_map/ppermute | solution.py:319
  42.9 8.0 %collective-permute-start.9 = (bf16[272,768]{1,0:T(8,128)(2,1)S(1)}, bf16[272,768]{1,0:T(8,128)(2,1)S(1)}, u32[]{:S(2)}, u32[]{:S(2)}) collective-permute-start(bf16[272,768]{1,0:T(8,128)(2,1)S(1)} %collective-permute-done.1.refs_2_), channel_id=1, source_target_pairs={{0,8},{1,9},{2,10},{3,11},{4,12},{5,13},{6,14},{7,15},{8,0},{9,1},... | collective-permute-start | bytes 1253384 | tf_op jit(solution)/shard_map/ppermute | solution.py:319
  42.9 12.5 %collective-permute-start.5 = (bf16[272,768]{1,0:T(8,128)(2,1)S(1)}, bf16[272,768]{1,0:T(8,128)(2,1)S(1)}, u32[]{:S(2)}, u32[]{:S(2)}) collective-permute-start(bf16[272,768]{1,0:T(8,128)(2,1)S(1)} %collective-permute-done.1.refs_2_), channel_id=1, source_target_pairs={{0,1},{1,0},{2,3},{3,2},{4,5},{5,4},{6,7},{7,6},{8,9},{9,8},{10,11... | collective-permute-start | bytes 1253384 | tf_op jit(solution)/shard_map/ppermute | solution.py:319
  44.8 10.6 %collective-permute-start.15 = (bf16[272,768]{1,0:T(8,128)(2,1)S(1)}, bf16[272,768]{1,0:T(8,128)(2,1)S(1)}, u32[]{:S(2)}, u32[]{:S(2)}) collective-permute-start(bf16[272,768]{1,0:T(8,128)(2,1)S(1)} %collective-permute-done.11.refs_12_), channel_id=1, source_target_pairs={{0,8},{1,9},{2,10},{3,11},{4,12},{5,13},{6,14},{7,15},{8,0},{9,1},... | collective-permute-start | bytes 1253384 | tf_op jit(solution)/shard_map/ppermute | solution.py:319
  47.4 11.7 %collective-permute-start.14 = (bf16[272,768]{1,0:T(8,128)(2,1)S(1)}, bf16[272,768]{1,0:T(8,128)(2,1)S(1)}, u32[]{:S(2)}, u32[]{:S(2)}) collective-permute-start(bf16[272,768]{1,0:T(8,128)(2,1)S(1)} %collective-permute-done.2.refs_3_), channel_id=1, source_target_pairs={{0,16},{1,17},{2,18},{3,19},{4,20},{5,21},{6,22},{7,23},{8,24},{9,... | collective-permute-start | bytes 1253384 | tf_op jit(solution)/shard_map/ppermute | solution.py:319
  51.0 13.1 %copy-start.3 = (bf16[272,768]{1,0:T(8,128)(2,1)}, bf16[272,768]{1,0:T(8,128)(2,1)S(1)}, u32[]{:S(2)}) copy-start(bf16[272,768]{1,0:T(8,128)(2,1)S(1)} %collective-permute-done.13.refs_14_) | copy-start | bytes 1253380
  51.0 8.2 %collective-permute-start.10 = (bf16[272,768]{1,0:T(8,128)(2,1)S(1)}, bf16[272,768]{1,0:T(8,128)(2,1)S(1)}, u32[]{:S(2)}, u32[]{:S(2)}) collective-permute-start(bf16[272,768]{1,0:T(8,128)(2,1)S(1)} %collective-permute-done.2.refs_3_), channel_id=1, source_target_pairs={{0,8},{1,9},{2,10},{3,11},{4,12},{5,13},{6,14},{7,15},{8,0},{9,1},... | collective-permute-start | bytes 1253384 | tf_op jit(solution)/shard_map/ppermute | solution.py:319
  51.0 13.1 %collective-permute-start.6 = (bf16[272,768]{1,0:T(8,128)(2,1)S(1)}, bf16[272,768]{1,0:T(8,128)(2,1)S(1)}, u32[]{:S(2)}, u32[]{:S(2)}) collective-permute-start(bf16[272,768]{1,0:T(8,128)(2,1)S(1)} %collective-permute-done.2.refs_3_), channel_id=1, source_target_pairs={{0,1},{1,0},{2,3},{3,2},{4,5},{5,4},{6,7},{7,6},{8,9},{9,8},{10,11... | collective-permute-start | bytes 1253384 | tf_op jit(solution)/shard_map/ppermute | solution.py:319
  55.4 3.7 %collective-permute-start.16 = (bf16[272,768]{1,0:T(8,128)(2,1)S(1)}, bf16[272,768]{1,0:T(8,128)(2,1)S(1)}, u32[]{:S(2)}, u32[]{:S(2)}) collective-permute-start(bf16[272,768]{1,0:T(8,128)(2,1)S(1)} %collective-permute-done.12.refs_13_), channel_id=1, source_target_pairs={{0,8},{1,9},{2,10},{3,11},{4,12},{5,13},{6,14},{7,15},{8,0},{9,1},... | collective-permute-start | bytes 1253384 | tf_op jit(solution)/shard_map/ppermute | solution.py:319
  55.5 8.7 %copy-start.4 = (bf16[272,768]{1,0:T(8,128)(2,1)}, bf16[272,768]{1,0:T(8,128)(2,1)S(1)}, u32[]{:S(2)}) copy-start(bf16[272,768]{1,0:T(8,128)(2,1)S(1)} %collective-permute-done.15.refs_16_) | copy-start | bytes 1253380
  55.5 8.6 %collective-permute-start.17 = (bf16[272,768]{1,0:T(8,128)(2,1)S(1)}, bf16[272,768]{1,0:T(8,128)(2,1)S(1)}, u32[]{:S(2)}, u32[]{:S(2)}) collective-permute-start(bf16[272,768]{1,0:T(8,128)(2,1)S(1)} %collective-permute-done.13.refs_14_), channel_id=1, source_target_pairs={{0,8},{1,9},{2,10},{3,11},{4,12},{5,13},{6,14},{7,15},{8,0},{9,1},... | collective-permute-start | bytes 1253384 | tf_op jit(solution)/shard_map/ppermute | solution.py:319
  59.2 5.0 %copy-start.5 = (bf16[272,768]{1,0:T(8,128)(2,1)}, bf16[272,768]{1,0:T(8,128)(2,1)S(1)}, u32[]{:S(2)}) copy-start(bf16[272,768]{1,0:T(8,128)(2,1)S(1)} %collective-permute-done.14.refs_15_) | copy-start | bytes 1253380
  59.2 4.9 %collective-permute-start.18 = (bf16[272,768]{1,0:T(8,128)(2,1)S(1)}, bf16[272,768]{1,0:T(8,128)(2,1)S(1)}, u32[]{:S(2)}, u32[]{:S(2)}) collective-permute-start(bf16[272,768]{1,0:T(8,128)(2,1)S(1)} %collective-permute-done.14.refs_15_), channel_id=1, source_target_pairs={{0,8},{1,9},{2,10},{3,11},{4,12},{5,13},{6,14},{7,15},{8,0},{9,1},... | collective-permute-start | bytes 1253384 | tf_op jit(solution)/shard_map/ppermute | solution.py:319
  59.2 5.0 %copy-start.6 = (bf16[272,768]{1,0:T(8,128)(2,1)}, bf16[272,768]{1,0:T(8,128)(2,1)S(1)}, u32[]{:S(2)}) copy-start(bf16[272,768]{1,0:T(8,128)(2,1)S(1)} %collective-permute-done.16.refs_17_) | copy-start | bytes 1253380
  (4 other events, 2.9 us)

commit v3 on v2

--- a/solution.py
+++ b/solution.py
@@ -11,6 +11,7 @@
 TILES = 4
 LABEL_ROWS = 16
 FAR = 1.0e9
+VMEM_LIMIT = 32 * 1024 * 1024
 NT = (((1,), (1,)), ((), ()))
 TN = (((0,), (0,)), ((), ()))
 
@@ -37,10 +38,10 @@
     return offsets, pairs
 
 
-def pack_kernel(sizes, place_ref, emb_hbm, cluster_hbm, rank_hbm, *refs):
-    groups, halves, half, cap, blk = sizes
-    dest_ref, sends = refs[0], refs[1 : 1 + groups]
-    emb_ref, cluster_ref, rank_ref, sems = refs[1 + groups :]
+def pack_kernel(sizes, emb_hbm, cluster_hbm, rank_hbm, *refs):
+    groups, halves, half, cap, blk = sizes
+    dest_ref, sends = refs[0], refs[1 : 1 + TILES]
+    emb_ref, cluster_ref, rank_ref, sems = refs[1 + TILES :]
     rows = emb_ref.shape[0]
     step = 256
     loads = [
@@ -78,7 +79,6 @@
         places.append(jnp.where(mine >= 0, mine * cap + position.astype(jnp.int32), -1))
     dest = jnp.concatenate(places, axis=1)
     dest_ref[...] = dest
-    dest = jnp.where(dest >= 0, dest ^ (place_ref[0] * blk), -1)
 
     units_of = []
     for j in range(rows // step):
@@ -104,14 +104,41 @@
     label_col = lax.broadcasted_iota(jnp.int32, (LABEL_ROWS, blk), 1)
     own_tile = label_row == lax.div(label_col, per_tile)
     unit_col = lax.div(label_col, cap).astype(jnp.float32)
-    slot = lax.broadcasted_iota(jnp.int32, (blk, rows), 0)
+    slot = lax.broadcasted_iota(jnp.int32, (wide_tile, rows), 0)
+    slot = lax.div(slot, per_tile) * blk + slot % per_tile
     width = sends[0].shape[1]
+    picks = []
+    for t in range(TILES):
+        pick = (slot + t * per_tile == dest).astype(jnp.float32).astype(jnp.bfloat16)
+        picks.append(pick)
+        packed = jnp.dot(pick, unit, preferred_element_type=jnp.float32).astype(jnp.bfloat16)
+        if t:
+            sends[t][...] = packed
+        else:
+            for k in range(groups):
+                at = k * (per_tile + LABEL_ROWS)
+                sends[0][at : at + per_tile, :] = packed[k * per_tile : (k + 1) * per_tile]
+    by_tile = [
+        lax.dot_general(labels, pick, NT, preferred_element_type=jnp.float32) for pick in picks
+    ]
+    fold = [
+        jnp.where(
+            lax.broadcasted_iota(jnp.int32, (wide_tile, blk), 0)
+            == lax.broadcasted_iota(jnp.int32, (wide_tile, blk), 1) % per_tile
+            + lax.div(lax.broadcasted_iota(jnp.int32, (wide_tile, blk), 1), per_tile) * 0
+            + k * per_tile,
+            1.0,
+            0.0,
+        ).astype(jnp.bfloat16)
+        for k in range(groups)
+    ]
     for k in range(groups):
-        pick = (slot + k * blk == dest).astype(jnp.float32).astype(jnp.bfloat16)
-        sends[k][0:blk, :] = jnp.dot(pick, unit, preferred_element_type=jnp.float32).astype(
-            jnp.bfloat16
-        )
-        mine = lax.dot_general(labels, pick, NT, preferred_element_type=jnp.float32)
+        mine = jnp.zeros((LABEL_ROWS, blk), jnp.float32)
+        for t in range(TILES):
+            spread_t = jnp.dot(
+                by_tile[t].astype(jnp.bfloat16), fold[k], preferred_element_type=jnp.float32
+            )
+            mine = jnp.where(lax.div(label_col, per_tile) == t, spread_t, mine)
         plain = jnp.where(label_row == 2, unit_col, mine)
         parts = [plain] + [jnp.zeros_like(plain)] * ((wide_tile - blk) // blk)
         for f in range(2):
@@ -119,20 +146,24 @@
             parts.append(jnp.dot(line, spread, preferred_element_type=jnp.float32))
         if width > 3 * wide_tile:
             parts.append(jnp.zeros((LABEL_ROWS, width - 3 * wide_tile), jnp.float32))
-        sends[k][blk : blk + LABEL_ROWS, :] = jnp.concatenate(parts, axis=1).astype(jnp.bfloat16)
-
-
-def pack(place, embeddings, cluster, rank, sizes):
+        at = k * (per_tile + LABEL_ROWS) + per_tile
+        sends[0][at : at + LABEL_ROWS, :] = jnp.concatenate(parts, axis=1).astype(jnp.bfloat16)
+
+
+def pack(embeddings, cluster, rank, sizes):
     groups, halves, half, cap, blk = sizes
     rows, width = embeddings.shape
     vmem = pl.BlockSpec(memory_space=pltpu.VMEM)
     hbm = pl.BlockSpec(memory_space=pltpu.HBM)
     out_shape = [jax.ShapeDtypeStruct((1, rows), jnp.int32)]
-    out_shape += [jax.ShapeDtypeStruct((blk + LABEL_ROWS, width), jnp.bfloat16)] * groups
+    tile = rows // TILES
+    for t in range(TILES):
+        extra = 0 if t else groups * LABEL_ROWS
+        out_shape.append(jax.ShapeDtypeStruct((tile + extra, width), jnp.bfloat16))
     return pl.pallas_call(
         functools.partial(pack_kernel, sizes),
         out_shape=out_shape,
-        in_specs=[pl.BlockSpec(memory_space=pltpu.SMEM), hbm, hbm, hbm],
+        in_specs=[hbm, hbm, hbm],
         out_specs=[vmem] * len(out_shape),
         scratch_shapes=[
             pltpu.VMEM((rows, width), jnp.bfloat16),
@@ -140,19 +171,18 @@
             pltpu.VMEM((1, rows), jnp.int32),
             pltpu.SemaphoreType.DMA((2 + rows // 256,)),
         ],
-        compiler_params=pltpu.CompilerParams(vmem_limit_bytes=48 * 1024 * 1024),
-    )(place, embeddings, cluster.reshape(1, rows), rank.reshape(1, rows))
-
-
-def compare_kernel(sizes, plan, n_sets, joined, place_ref, *refs):
-    groups, halves, half, cap, blk = sizes
-    blocks = [refs[i * groups : (i + 1) * groups] for i in range(n_sets)]
-    n_out = 1 if joined else len(plan)
-    outs = refs[n_sets * groups : n_sets * groups + n_out]
-    key_col, key_row, low_row, turned, best = refs[n_sets * groups + n_out :]
-    rows = groups * blk
+        compiler_params=pltpu.CompilerParams(vmem_limit_bytes=VMEM_LIMIT),
+    )(embeddings, cluster.reshape(1, rows), rank.reshape(1, rows))
+
+
+def compare_kernel(sizes, plan, n_sets, t, *refs):
+    groups, halves, half, cap, blk = sizes
+    blocks = [refs[i * (t + 1) : (i + 1) * (t + 1)] for i in range(n_sets)]
+    best_ref = refs[n_sets * (t + 1)]
+    key_col, turned = refs[n_sets * (t + 1) + 1 :]
     per_tile = blk // TILES
-    tile = rows // TILES
+    tile = groups * per_tile
+    pitch = per_tile + LABEL_ROWS
     cap_all = float(halves * half)
 
     lane = lax.broadcasted_iota(jnp.int32, (LABEL_ROWS, tile), 1)
@@ -165,105 +195,109 @@
         1.0,
         jnp.where(weight_row == 1, cap_all, jnp.where(weight_row == 2, float(half), 0.0)),
     ).astype(jnp.bfloat16)
+
+    def label(i, k):
+        return blocks[i][0][k * pitch + per_tile : (k + 1) * pitch, :]
+
     for i in range(n_sets):
         for k in range(groups):
-            key_col[pl.ds((i * groups + k) * blk, blk), :] = lax.dot_general(
-                blocks[i][k][blk : blk + LABEL_ROWS, 0:blk], weights, TN, preferred_element_type=jnp.float32
+            keys = lax.dot_general(
+                label(i, k)[:, 0:blk], weights, TN, preferred_element_type=jnp.float32
             )
-    for o, (a, _) in enumerate(plan):
+            for s in range(t + 1):
+                at = (i * (t + 1) + s) * tile + k * per_tile
+                key_col[at : at + per_tile, :] = keys[s * per_tile : (s + 1) * per_tile]
+
+    def tile_of(i, s):
+        if s:
+            return [blocks[i][s][...]]
+        return [blocks[i][0][k * pitch : k * pitch + per_tile, :] for k in range(groups)]
+
+    for o, (a, cols) in enumerate(plan):
         rest = jnp.zeros((LABEL_ROWS, tile), jnp.float32)
         code = jnp.zeros((LABEL_ROWS, tile), jnp.float32)
         for k in range(groups):
-            label = blocks[a][k][blk : blk + LABEL_ROWS, tile : 3 * tile].astype(jnp.float32)
-            rest = jnp.where(from_block == k, label[:, :tile], rest)
-            code = jnp.where(from_block == k, label[:, tile:], code)
+            spread = label(a, k)[:, tile : 3 * tile].astype(jnp.float32)
+            rest = jnp.where(from_block == k, spread[:, :tile], rest)
+            code = jnp.where(from_block == k, spread[:, tile:], code)
         low = code * cap_all
-        key = low + (which * half).astype(jnp.float32) + rest
-        low = jnp.where(code > 0.5, low, FAR)
-        key_row[o] = key[0:8]
-        low_row[o] = low[0:8]
-
-    def tile_of(i, t):
-        at = pl.ds(pl.multiple_of(t * per_tile, per_tile), per_tile)
-        return [blocks[i][k][at, :] for k in range(groups)]
-
-    for o, (a, cols) in enumerate(plan):
-
-        def one_tile(t, _, a=a, cols=cols, o=o):
-            turned[...] = jnp.concatenate(tile_of(a, t), axis=0).T
-            mine = key_row[o, pl.ds(t, 1), :]
-            floor = low_row[o, pl.ds(t, 1), :]
-
-            def one_col(s, acc):
-                theirs = []
-                pieces = []
-                for b in cols:
-                    pieces += tile_of(b, s)
-                    for k in range(groups):
-                        at = pl.multiple_of((b * groups + k) * blk + s * per_tile, per_tile)
-                        theirs.append(key_col[pl.ds(at, per_tile), :])
-                theirs = jnp.concatenate(theirs, axis=0)
+        mine = (low + (which * half).astype(jnp.float32) + rest)[t : t + 1]
+        floor = jnp.where(code > 0.5, low, FAR)[t : t + 1]
+        turned[o] = jnp.concatenate(tile_of(a, t), axis=0).T
+        acc = jnp.full((8, tile), -1.0, jnp.float32)
+        for s in range(t + 1):
+            for b in cols:
+                at = (b * (t + 1) + s) * tile
+                theirs = key_col[at : at + tile, :]
                 theirs = jnp.concatenate([theirs] * (tile // 128), axis=1)
                 sims = jnp.dot(
-                    jnp.concatenate(pieces, axis=0), turned[...], preferred_element_type=jnp.float32
+                    jnp.concatenate(tile_of(b, s), axis=0), turned[o], preferred_element_type=jnp.float32
                 )
                 keep = (theirs >= floor) & (theirs < mine)
                 sims = jnp.where(keep, sims, -1.0)
-                top = jnp.max(sims.reshape(len(cols) * tile // 8, 8, tile), axis=0)
-                return jnp.maximum(acc, top)
-
-            acc = lax.fori_loop(0, t + 1, one_col, jnp.full((8, tile), -1.0, jnp.float32))
-            best[o, pl.ds(t, 1), :] = jnp.max(acc, axis=0, keepdims=True)
-            return 0
-
-        lax.fori_loop(0, TILES, one_tile, 0)
-
+                acc = jnp.maximum(acc, jnp.max(sims.reshape(tile // 8, 8, tile), axis=0))
+        best_ref[o] = jnp.broadcast_to(jnp.max(acc, axis=0, keepdims=True), (8, tile))
+
+
+def compare(sets, plan, t, sizes):
+    groups, halves, half, cap, blk = sizes
+    n_sets = len(sets)
+    flat = [piece for one in sets for piece in one[: t + 1]]
+    rows, width = groups * blk, flat[0].shape[1]
+    tile = rows // TILES
+    vmem = pl.BlockSpec(memory_space=pltpu.VMEM)
+    combos = sum(len(cols) for _, cols in plan) * (t + 1)
+    return pl.pallas_call(
+        functools.partial(compare_kernel, sizes, plan, n_sets, t),
+        out_shape=jax.ShapeDtypeStruct((len(plan), 8, tile), jnp.float32),
+        in_specs=[vmem] * len(flat),
+        out_specs=vmem,
+        scratch_shapes=[
+            pltpu.VMEM((n_sets * (t + 1) * tile, 128), jnp.float32),
+            pltpu.VMEM((len(plan), width, tile), jnp.bfloat16),
+        ],
+        compiler_params=pltpu.CompilerParams(vmem_limit_bytes=VMEM_LIMIT),
+        cost_estimate=pl.CostEstimate(
+            flops=2 * combos * tile * tile * width,
+            bytes_accessed=2 * n_sets * (t + 1) * tile * width,
+            transcendentals=0,
+        ),
+    )(*flat)
+
+
+def order_kernel(sizes, starts, joined, place_ref, *refs):
+    groups, halves, half, cap, blk = sizes
+    found, outs = refs[:TILES], refs[TILES:]
+    per_tile = blk // TILES
+    tile = groups * per_tile
     lane = lax.broadcasted_iota(jnp.int32, (1, tile), 1)
-    for o, (a, _) in enumerate(plan):
-        found = best[o]
+    for o, a in enumerate(starts):
         for k in range(groups):
             total = jnp.full((1, tile), -1.0, jnp.float32)
             for t in range(TILES):
                 turn = ((t - k) * per_tile) % tile
-                moved = pltpu.roll(found, turn, 1) if turn else found
-                total = jnp.where(lax.div(lane, per_tile) == t, moved[t : t + 1], total)
-            block = place_ref[0] ^ k
+                value = found[t][o]
+                moved = pltpu.roll(value, turn, 1) if turn else value
+                total = jnp.where(lax.div(lane, per_tile) == t, moved[0:1], total)
             if joined:
-                side = joined
-                outs[0][pl.ds(block * side + (place_ref[1] ^ a), 1), 0, :] = total[:, :blk]
+                outs[0][pl.ds(k * joined + (place_ref[1] ^ a), 1), 0, :] = total[:, :blk]
             else:
-                outs[o][pl.ds(block, 1), 0, :] = total[:, :blk]
-
-
-def compare(place, sets, plan, joined, sizes):
-    groups, halves, half, cap, blk = sizes
-    n_sets = len(sets)
-    flat = [piece for one in sets for piece in one]
-    rows, width = groups * blk, flat[0].shape[1]
-    tile = rows // TILES
+                outs[o][k, :, :] = total[:, :blk]
+
+
+def order(place, found, starts, joined, sizes):
+    groups, halves, half, cap, blk = sizes
     vmem = pl.BlockSpec(memory_space=pltpu.VMEM)
-    combos = sum(len(cols) for _, cols in plan) * TILES * (TILES + 1) // 2
     if joined:
         out_shape = [jax.ShapeDtypeStruct((groups * joined, 1, blk), jnp.float32)]
     else:
-        out_shape = [jax.ShapeDtypeStruct((groups, 1, blk), jnp.float32)] * len(plan)
+        out_shape = [jax.ShapeDtypeStruct((groups, 1, blk), jnp.float32)] * len(starts)
     return pl.pallas_call(
-        functools.partial(compare_kernel, sizes, plan, n_sets, joined),
+        functools.partial(order_kernel, sizes, starts, joined),
         out_shape=out_shape,
-        in_specs=[pl.BlockSpec(memory_space=pltpu.SMEM)] + [vmem] * len(flat),
+        in_specs=[pl.BlockSpec(memory_space=pltpu.SMEM)] + [vmem] * TILES,
         out_specs=[vmem] * len(out_shape),
-        scratch_shapes=[
-            pltpu.VMEM((n_sets * rows, 128), jnp.float32),
-            pltpu.VMEM((len(plan), 8, tile), jnp.float32),
-            pltpu.VMEM((len(plan), 8, tile), jnp.float32),
-            pltpu.VMEM((width, tile), jnp.bfloat16),
-            pltpu.VMEM((len(plan), 8, tile), jnp.float32),
-        ],
-        compiler_params=pltpu.CompilerParams(vmem_limit_bytes=48 * 1024 * 1024),
-        cost_estimate=pl.CostEstimate(
-            flops=2 * combos * tile * tile * width, bytes_accessed=2 * n_sets * rows * width, transcendentals=0
-        ),
-    )(place, *flat)
+    )(place, *found)
 
 
 def unpack_kernel(sizes, dest_ref, back_ref, out_ref):
@@ -296,7 +330,7 @@
         out_shape=jax.ShapeDtypeStruct(dest.shape, jnp.float32),
         in_specs=[vmem] * 2,
         out_specs=vmem,
-        compiler_params=pltpu.CompilerParams(vmem_limit_bytes=48 * 1024 * 1024),
+        compiler_params=pltpu.CompilerParams(vmem_limit_bytes=VMEM_LIMIT),
     )(dest, back)
 
 
@@ -321,26 +355,32 @@
     offsets, pairs = cover(members)
     here = lax.axis_index("mem").astype(jnp.int32)
     place = jnp.stack([here // side, here % side])
-    packed = pack(place, embeddings, cluster, rank, sizes)
+    packed = pack(embeddings, cluster, rank, sizes)
     dest, sends = packed[0], packed[1:]
 
-    own = [sends[0]]
-    for k in range(1, groups):
-        send = sends[k]
-        if k > 2:
-            send, own[k - 1] = lax.optimization_barrier((send, own[k - 1]))
-        own.append(swap(send, k, 0))
-    held = {0: own}
-    for d in offsets[1:]:
-        core_bit = d & ~side
-        via = core_bit if d & side and core_bit in held else 0
-        held[d] = [swap(piece, 0, d ^ via) for piece in held[via]]
+    columns = [[b * side + spot for b in range(groups)] for spot in range(side)]
+    held = {d: [] for d in offsets}
+    for t in range(TILES):
+        send = sends[t]
+        if t:
+            send, held[0][t - 1] = lax.optimization_barrier((send, held[0][t - 1]))
+        held[0].append(
+            lax.all_to_all(
+                send, "mem", split_axis=0, concat_axis=0, tiled=True, axis_index_groups=columns
+            )
+        )
+    for t in range(TILES):
+        for d in offsets[1:]:
+            core_bit = side
+            via = d ^ core_bit if d & core_bit and d ^ core_bit in held else 0
+            held[d].append(swap(held[via][t], 0, d ^ via))
 
     index = {d: i for i, d in enumerate(offsets)}
     starts = sorted({a for a, _ in pairs.values()})
     plan = [(index[a], [index[b] for _, (e, b) in sorted(pairs.items()) if e == a]) for a in starts]
     joined = side if all(a < side for a in starts) else 0
-    found = compare(place, [held[d] for d in offsets], plan, joined, sizes)
+    found = [compare([held[d] for d in offsets], plan, t, sizes) for t in range(TILES)]
+    found = order(place, found, starts, joined, sizes)
     if joined:
         back = found[0]
     else:

time: 94.5 us -> 118 us (1.25)
  blocking collectives: 12 us -> 45.1 us
  waiting for transfers between devices: 35.6 us -> 21.1 us
  Pallas kernels: 21.4 us -> 23.9 us
  local copies, waits for them, and re-layouts: 4.27 us -> 5.49 us
    all_to_all x0 -> x2, blocking collectives: none -> 33.6 us  [on_device(): lax.all_to_all(send, 'mem', split_axis=0, concat_axis=0, tiled=True, axis...]
    ppermute x19 -> x16, waiting for transfers between devices: 35.6 us -> 13.7 us  [swap(): lax.ppermute(value, ('grp', 'mem'), [(i, i ^ mask) for i in range(devices)])]
    all_to_all x0 -> x2, waiting for transfers between devices: none -> 7.41 us  [on_device(): lax.all_to_all(send, 'mem', split_axis=0, concat_axis=0, tiled=True, axis...]
    ppermute x19 -> x16, starting transfers between devices: 20.8 us -> 13.5 us  [swap(): lax.ppermute(value, ('grp', 'mem'), [(i, i ^ mask) for i in range(devices)])]
    all_to_all x0 -> x2, starting transfers between devices: none -> 7.1 us  [on_device(): lax.all_to_all(send, 'mem', split_axis=0, concat_axis=0, tiled=True, axis...]
    pallas_call x1 -> x5, Pallas kernels: 15.5 us -> 18.3 us  [the longest x4 16.8 us: compare(): pl.pallas_call(functools.partial(compare_kernel, sizes, plan, n_sets, t),...]
    unnamed x18 -> x22, local copies, waits for them, and re-layouts: 4.27 us -> 5.49 us
  transfers between devices with their start and end apart: 19 -> 18, of which waited for: 8 -> 5; matrix products, arithmetic and copies ran while one was open for 0% -> 1% of each run, Pallas kernels for 0% -> 9%
where the time goes in v3:
time: 118 us; the launch traced here: 117 us
  blocking collectives  45.1 us (38%)
  Pallas kernels  23.9 us (20%)
  waiting for transfers between devices  21.1 us (18%)
  starting transfers between devices  20.6 us (17%)
  local copies, waits for them, and re-layouts  5.49 us (5%)
    all_to_all x2, blocking collectives, on_device(): lax.all_to_all(send, 'mem', split_axis=0, concat_axis=0, tiled=True, axis...  33.6 us
    pallas_call x4, Pallas kernels, compare(): pl.pallas_call(functools.partial(compare_kernel, sizes, plan, n_sets, t),...  16.8 us
    ppermute x16, waiting for transfers between devices, swap(): lax.ppermute(value, ('grp', 'mem'), [(i, i ^ mask) for i in range(devices)])  13.7 us
    ppermute x16, starting transfers between devices, swap(): lax.ppermute(value, ('grp', 'mem'), [(i, i ^ mask) for i in range(devices)])  13.5 us
    all_to_all x1, blocking collectives, on_device(): back = lax.all_to_all(back, 'mem', split_axis=0, concat_axis=0, tiled=True)  11.5 us
    all_to_all x2, waiting for transfers between devices, on_device(): lax.all_to_all(send, 'mem', split_axis=0, concat_axis=0, tiled=True, axis...  7.41 us
    all_to_all x2, starting transfers between devices, on_device(): lax.all_to_all(send, 'mem', split_axis=0, concat_axis=0, tiled=True, axis...  7.1 us
    unnamed x22, local copies, waits for them, and re-layouts  5.49 us
  transfers between devices with their start and end apart: 18, of which 5 were waited for; matrix products, arithmetic and copies ran while one was open for 1% of the time, Pallas kernels for 9%

profile of v3, /device:TPU:0, one launch (start us, length us, event | category | flops | bytes accessed | tf_op | source)
XLA Modules:
  0.0 117.0 jit_solution(6605135903253808459)
XLA Ops:
  0.0 1.4 %copy-done = bf16[1024,768]{1,0:T(8,128)(2,1)S(1)} copy-done((bf16[1024,768]{1,0:T(8,128)(2,1)S(1)}, bf16[1024,768]{1,0:T(8,128)(2,1)}, u32[]{:S(2)}) %copy-start) | copy-done | bytes 1572888
  2.8 4.6 %shard_map.37 = (s32[1,1024]{1,0:T(1,128)S(1)}, bf16[320,768]{1,0:T(8,128)(2,1)S(1)}, bf16[256,768]{1,0:T(8,128)(2,1)S(1)}, bf16[256,768]{1,0:T(8,128)(2,1)}, bf16[256,768]{1,0:T(8,128)(2,1)}) custom-call(bf16[1024,768]{1,0:T(8,128)(2,1)S(1)} %copy-done, s32[1,1024]{1,0:T(1,128)S(1)} %bitcast.37, s32[1,1024]{1,0:T(1,128)S(1)} %bitcast.38), custom_call_target="tpu_custom_call" | custom-call | tf_op jit(solution)/shard_map/pallas_call | solution.py:163
  7.4 19.9 %all_to_all.52 = bf16[4,80,768]{2,1,0:T(8,128)(2,1)S(1)} all-to-all(bf16[4,80,768]{2,1,0:T(8,128)(2,1)S(1)} %bitcast.20), channel_id=1, replica_groups={{0,2,4,6},{1,3,5,7},{8,10,12,14},{9,11,13,15},{16,18,20,22},{17,19,21,2..., dimensions={0} | all-to-all | bytes 983040 | tf_op jit(solution)/shard_map/all_to_all | solution.py:368
  27.3 13.7 %all_to_all.53 = bf16[4,64,768]{2,1,0:T(8,128)(2,1)S(1)} all-to-all(bf16[4,64,768]{2,1,0:T(8,128)(2,1)S(1)} %bitcast.36), channel_id=1, replica_groups={{0,2,4,6},{1,3,5,7},{8,10,12,14},{9,11,13,15},{16,18,20,22},{17,19,21,2..., dimensions={0} | all-to-all | bytes 786432 | tf_op jit(solution)/shard_map/all_to_all | solution.py:368
  41.0 3.5 %all-to-all-start.2 = ((bf16[4,64,768]{2,1,0:T(8,128)(2,1)}), bf16[4,64,768]{2,1,0:T(8,128)(2,1)S(1)}, u32[]{:S(2)}, u32[]{:S(2)}) async-start(bf16[4,64,768]{2,1,0:T(8,128)(2,1)} %bitcast.8), calls=%async_computation.2 | async-start | bytes 786432 | tf_op jit(solution)/shard_map/all_to_all | solution.py:368
  44.5 1.6 %collective-permute-start.2 = (bf16[320,768]{1,0:T(8,128)(2,1)S(1)}, bf16[320,768]{1,0:T(8,128)(2,1)S(1)}, u32[]{:S(2)}, u32[]{:S(2)}) collective-permute-start(bf16[320,768]{1,0:T(8,128)(2,1)S(1)} %bitcast.13), channel_id=1, source_target_pairs={{0,16},{1,17},{2,18},{3,19},{4,20},{5,21},{6,22},{7,23},{8,24},{9,... | collective-permute-start | bytes 1474568 | tf_op jit(solution)/shard_map/ppermute | solution.py:353
  46.0 1.5 %collective-permute-start = (bf16[320,768]{1,0:T(8,128)(2,1)S(1)}, bf16[320,768]{1,0:T(8,128)(2,1)S(1)}, u32[]{:S(2)}, u32[]{:S(2)}) collective-permute-start(bf16[320,768]{1,0:T(8,128)(2,1)S(1)} %bitcast.14), channel_id=1, source_target_pairs={{0,1},{1,0},{2,3},{3,2},{4,5},{5,4},{6,7},{7,6},{8,9},{9,8},{10,11... | collective-permute-start | bytes 1474568 | tf_op jit(solution)/shard_map/ppermute | solution.py:353
  47.5 7.4 %all-to-all-done.2 = bf16[4,64,768]{2,1,0:T(8,128)(2,1)S(1)} async-done(((bf16[4,64,768]{2,1,0:T(8,128)(2,1)}), bf16[4,64,768]{2,1,0:T(8,128)(2,1)S(1)}, u32[]{:S(2)}, u32[]{:S(2)}) %all-to-all-start.2) | async-done | bytes 393248 | tf_op jit(solution)/shard_map/all_to_all | solution.py:368
  55.0 3.6 %all-to-all-start.3 = ((bf16[4,64,768]{2,1,0:T(8,128)(2,1)}), bf16[4,64,768]{2,1,0:T(8,128)(2,1)S(1)}, u32[]{:S(2)}, u32[]{:S(2)}) async-start(bf16[4,64,768]{2,1,0:T(8,128)(2,1)} %bitcast.10), calls=%async_computation.3 | async-start | bytes 786432 | tf_op jit(solution)/shard_map/all_to_all | solution.py:368
  58.6 1.6 %collective-permute-start.6 = (bf16[256,768]{1,0:T(8,128)(2,1)S(1)}, bf16[256,768]{1,0:T(8,128)(2,1)S(1)}, u32[]{:S(2)}, u32[]{:S(2)}) collective-permute-start(bf16[256,768]{1,0:T(8,128)(2,1)S(1)} %bitcast.21), channel_id=1, source_target_pairs={{0,16},{1,17},{2,18},{3,19},{4,20},{5,21},{6,22},{7,23},{8,24},{9,... | collective-permute-start | bytes 1179656 | tf_op jit(solution)/shard_map/ppermute | solution.py:353
  60.2 1.5 %collective-permute-start.4 = (bf16[256,768]{1,0:T(8,128)(2,1)S(1)}, bf16[256,768]{1,0:T(8,128)(2,1)S(1)}, u32[]{:S(2)}, u32[]{:S(2)}) collective-permute-start(bf16[256,768]{1,0:T(8,128)(2,1)S(1)} %bitcast.22), channel_id=1, source_target_pairs={{0,1},{1,0},{2,3},{3,2},{4,5},{5,4},{6,7},{7,6},{8,9},{9,8},{10,11... | collective-permute-start | bytes 1179656 | tf_op jit(solution)/shard_map/ppermute | solution.py:353
  62.7 6.6 %collective-permute-done.6.refs_7_.refs_10_.refs_13_ = bf16[256,768]{1,0:T(8,128)(2,1)S(1)} collective-permute-done((bf16[256,768]{1,0:T(8,128)(2,1)S(1)}, bf16[256,768]{1,0:T(8,128)(2,1)S(1)}, u32[]{:S(2)}, u32[]{:S(2)}) %collective-permute-start.6) | collective-permute-done | bytes 393248 | tf_op jit(solution)/shard_map/ppermute | solution.py:353
  70.1 2.5 %collective-permute-start.8 = (bf16[256,768]{1,0:T(8,128)(2,1)S(1)}, bf16[256,768]{1,0:T(8,128)(2,1)}, u32[]{:S(2)}, u32[]{:S(2)}) collective-permute-start(bf16[256,768]{1,0:T(8,128)(2,1)S(1)} %bitcast.28), channel_id=1, source_target_pairs={{0,1},{1,0},{2,3},{3,2},{4,5},{5,4},{6,7},{7,6},{8,9},{9,8},{10,11... | collective-permute-start | bytes 1179656 | tf_op jit(solution)/shard_map/ppermute | solution.py:353
  73.4 1.8 %collective-permute-start.14 = (bf16[256,768]{1,0:T(8,128)(2,1)S(1)}, bf16[256,768]{1,0:T(8,128)(2,1)}, u32[]{:S(2)}, u32[]{:S(2)}) collective-permute-start(bf16[256,768]{1,0:T(8,128)(2,1)S(1)} %bitcast.32), channel_id=1, source_target_pairs={{0,16},{1,17},{2,18},{3,19},{4,20},{5,21},{6,22},{7,23},{8,24},{9,... | collective-permute-start | bytes 1179656 | tf_op jit(solution)/shard_map/ppermute | solution.py:353
  76.4 1.8 %collective-permute-start.12 = (bf16[256,768]{1,0:T(8,128)(2,1)S(1)}, bf16[256,768]{1,0:T(8,128)(2,1)S(1)}, u32[]{:S(2)}, u32[]{:S(2)}) collective-permute-start(bf16[256,768]{1,0:T(8,128)(2,1)S(1)} %bitcast.33), channel_id=1, source_target_pairs={{0,1},{1,0},{2,3},{3,2},{4,5},{5,4},{6,7},{7,6},{8,9},{9,8},{10,11... | collective-permute-start | bytes 1179656 | tf_op jit(solution)/shard_map/ppermute | solution.py:353
  78.2 4.5 %collective-permute-done.8.refs_5_.refs_6_ = bf16[256,768]{1,0:T(8,128)(2,1)} collective-permute-done((bf16[256,768]{1,0:T(8,128)(2,1)S(1)}, bf16[256,768]{1,0:T(8,128)(2,1)}, u32[]{:S(2)}, u32[]{:S(2)}) %collective-permute-start.8) | collective-permute-done | bytes 393248 | tf_op jit(solution)/shard_map/ppermute | solution.py:353
  82.7 2.1 %collective-permute-done.14.refs_15_ = bf16[256,768]{1,0:T(8,128)(2,1)} collective-permute-done((bf16[256,768]{1,0:T(8,128)(2,1)S(1)}, bf16[256,768]{1,0:T(8,128)(2,1)}, u32[]{:S(2)}, u32[]{:S(2)}) %collective-permute-start.14) | collective-permute-done | bytes 393248 | tf_op jit(solution)/shard_map/ppermute | solution.py:353
  84.9 2.5 %shard_map.38.refs_0_ = f32[2,8,256]{2,1,0:T(8,128)S(1)} custom-call(bf16[320,768]{1,0:T(8,128)(2,1)S(1)} %bitcast.16, bf16[320,768]{1,0:T(8,128)(2,1)S(1)} %collective-permute-done.refs_1_.refs_2_.refs_3_.refs_4_, bf16[320,768]{1,0:T(8,128)(2,1)S(1)} %collective-permute-done.1.refs_2_.refs_4_.refs_6_.refs_8_, ...), custom_call_target="tpu_custom_call" | custom-call | flops 805306368 | bytes 1966080 | tf_op jit(solution)/shard_map/pallas_call | solution.py:250
  87.4 3.5 %shard_map.39.refs_1_ = f32[2,8,256]{2,1,0:T(8,128)S(1)} custom-call(bf16[320,768]{1,0:T(8,128)(2,1)S(1)} %bitcast.17, bf16[256,768]{1,0:T(8,128)(2,1)S(1)} %bitcast.24, bf16[320,768]{1,0:T(8,128)(2,1)S(1)} %collective-permute-done.refs_1_.refs_2_.refs_3_.refs_4_, bf16[256,768]{1,0:T(8,128)(2,1)S(1)} %copy-done.8, ...), custom_call_target="tpu_custom_call" | custom-call | flops 1610612736 | bytes 3932160 | tf_op jit(solution)/shard_map/pallas_call | solution.py:250
  91.0 4.9 %shard_map.40.refs_2_ = f32[2,8,256]{2,1,0:T(8,128)S(1)} custom-call(bf16[320,768]{1,0:T(8,128)(2,1)S(1)} %bitcast.18, bf16[256,768]{1,0:T(8,128)(2,1)S(1)} %bitcast.25, bf16[256,768]{1,0:T(8,128)(2,1)S(1)} %bitcast.30, bf16[320,768]{1,0:T(8,128)(2,1)S(1)} %collective-permute-done.refs_1_.refs_2_.refs_3_.refs_4_, bf16[256,768]{1,0:T(8,128)(2,1)S(1)} %copy-done.8, ...), custom_call_target="tpu_custom_call" | custom-call | flops 2415919104 | bytes 5898240 | tf_op jit(solution)/shard_map/pallas_call | solution.py:250
  96.5 5.8 %shard_map.41.refs_3_ = f32[2,8,256]{2,1,0:T(8,128)S(1)} custom-call(bf16[320,768]{1,0:T(8,128)(2,1)S(1)} %bitcast.19, bf16[256,768]{1,0:T(8,128)(2,1)S(1)} %bitcast.26, bf16[256,768]{1,0:T(8,128)(2,1)S(1)} %bitcast.31, bf16[256,768]{1,0:T(8,128)(2,1)S(1)} %bitcast.35, bf16[320,768]{1,0:T(8,128)(2,1)S(1)} %collective-permute-done.refs_1_.refs_2_.refs_3_.refs_4_, ...), custom_call_target="tpu_custom_call" | custom-call | flops 3221225472 | bytes 7864320 | tf_op jit(solution)/shard_map/pallas_call | solution.py:250
  102.9 1.5 %shard_map.42 = f32[8,1,256]{2,1,0:T(1,128)} custom-call(s32[2]{0:T(128)} %pad_add_fusion.place_ref, f32[2,8,256]{2,1,0:T(8,128)} %copy-done.1, f32[2,8,256]{2,1,0:T(8,128)} %copy-done.2, f32[2,8,256]{2,1,0:T(8,128)} %copy-done.3, f32[2,8,256]{2,1,0:T(8,128)} %copy-done.4), custom_call_target="tpu_custom_call" | custom-call | tf_op jit(solution)/shard_map/pallas_call | solution.py:295
  104.4 11.5 %all_to_all.54.back_ref = f32[8,1,256]{2,1,0:T(1,128)S(1)} all-to-all(f32[8,1,256]{2,1,0:T(1,128)} %shard_map.42), channel_id=1, replica_groups=mesh['grp'=4,'mem'=8] {'mem'}, dimensions={0} | all-to-all | bytes 16384 | tf_op jit(solution)/shard_map/all_to_all | solution.py:401
  115.9 1.1 shard_map.43
  (45 shorter events, 6.3 us)
Async XLA Ops:
  0.0 1.4 %copy-start = (bf16[1024,768]{1,0:T(8,128)(2,1)S(1)}, bf16[1024,768]{1,0:T(8,128)(2,1)}, u32[]{:S(2)}) copy-start(bf16[1024,768]{1,0:T(8,128)(2,1)} %emb_hbm.1) | copy-start | bytes 4718596
  41.0 14.0 %all-to-all-start.2 = ((bf16[4,64,768]{2,1,0:T(8,128)(2,1)}), bf16[4,64,768]{2,1,0:T(8,128)(2,1)S(1)}, u32[]{:S(2)}, u32[]{:S(2)}) async-start(bf16[4,64,768]{2,1,0:T(8,128)(2,1)} %bitcast.8), calls=%async_computation.2 | async-start | bytes 786432 | tf_op jit(solution)/shard_map/all_to_all | solution.py:368
  44.5 17.2 %collective-permute-start.2 = (bf16[320,768]{1,0:T(8,128)(2,1)S(1)}, bf16[320,768]{1,0:T(8,128)(2,1)S(1)}, u32[]{:S(2)}, u32[]{:S(2)}) collective-permute-start(bf16[320,768]{1,0:T(8,128)(2,1)S(1)} %bitcast.13), channel_id=1, source_target_pairs={{0,16},{1,17},{2,18},{3,19},{4,20},{5,21},{6,22},{7,23},{8,24},{9,... | collective-permute-start | bytes 1474568 | tf_op jit(solution)/shard_map/ppermute | solution.py:353
  46.0 15.7 %collective-permute-start = (bf16[320,768]{1,0:T(8,128)(2,1)S(1)}, bf16[320,768]{1,0:T(8,128)(2,1)S(1)}, u32[]{:S(2)}, u32[]{:S(2)}) collective-permute-start(bf16[320,768]{1,0:T(8,128)(2,1)S(1)} %bitcast.14), channel_id=1, source_target_pairs={{0,1},{1,0},{2,3},{3,2},{4,5},{5,4},{6,7},{7,6},{8,9},{9,8},{10,11... | collective-permute-start | bytes 1474568 | tf_op jit(solution)/shard_map/ppermute | solution.py:353
  47.5 14.7 %collective-permute-start.1 = (bf16[320,768]{1,0:T(8,128)(2,1)S(1)}, bf16[320,768]{1,0:T(8,128)(2,1)S(1)}, u32[]{:S(2)}, u32[]{:S(2)}) collective-permute-start(bf16[320,768]{1,0:T(8,128)(2,1)S(1)} %bitcast.15), channel_id=1, source_target_pairs={{0,8},{1,9},{2,10},{3,11},{4,12},{5,13},{6,14},{7,15},{8,0},{9,1},... | collective-permute-start | bytes 1474568 | tf_op jit(solution)/shard_map/ppermute | solution.py:353
  55.0 18.5 %all-to-all-start.3 = ((bf16[4,64,768]{2,1,0:T(8,128)(2,1)}), bf16[4,64,768]{2,1,0:T(8,128)(2,1)S(1)}, u32[]{:S(2)}, u32[]{:S(2)}) async-start(bf16[4,64,768]{2,1,0:T(8,128)(2,1)} %bitcast.10), calls=%async_computation.3 | async-start | bytes 786432 | tf_op jit(solution)/shard_map/all_to_all | solution.py:368
  58.6 10.8 %collective-permute-start.6 = (bf16[256,768]{1,0:T(8,128)(2,1)S(1)}, bf16[256,768]{1,0:T(8,128)(2,1)S(1)}, u32[]{:S(2)}, u32[]{:S(2)}) collective-permute-start(bf16[256,768]{1,0:T(8,128)(2,1)S(1)} %bitcast.21), channel_id=1, source_target_pairs={{0,16},{1,17},{2,18},{3,19},{4,20},{5,21},{6,22},{7,23},{8,24},{9,... | collective-permute-start | bytes 1179656 | tf_op jit(solution)/shard_map/ppermute | solution.py:353
  60.2 9.2 %collective-permute-start.4 = (bf16[256,768]{1,0:T(8,128)(2,1)S(1)}, bf16[256,768]{1,0:T(8,128)(2,1)S(1)}, u32[]{:S(2)}, u32[]{:S(2)}) collective-permute-start(bf16[256,768]{1,0:T(8,128)(2,1)S(1)} %bitcast.22), channel_id=1, source_target_pairs={{0,1},{1,0},{2,3},{3,2},{4,5},{5,4},{6,7},{7,6},{8,9},{9,8},{10,11... | collective-permute-start | bytes 1179656 | tf_op jit(solution)/shard_map/ppermute | solution.py:353
  61.7 11.0 %collective-permute-start.5 = (bf16[256,768]{1,0:T(8,128)(2,1)S(1)}, bf16[256,768]{1,0:T(8,128)(2,1)S(1)}, u32[]{:S(2)}, u32[]{:S(2)}) collective-permute-start(bf16[256,768]{1,0:T(8,128)(2,1)S(1)} %bitcast.23), channel_id=1, source_target_pairs={{0,8},{1,9},{2,10},{3,11},{4,12},{5,13},{6,14},{7,15},{8,0},{9,1},... | collective-permute-start | bytes 1179656 | tf_op jit(solution)/shard_map/ppermute | solution.py:353
  61.7 13.6 %collective-permute-start.3 = (bf16[320,768]{1,0:T(8,128)(2,1)S(1)}, bf16[320,768]{1,0:T(8,128)(2,1)}, u32[]{:S(2)}, u32[]{:S(2)}) collective-permute-start(bf16[320,768]{1,0:T(8,128)(2,1)S(1)} %collective-permute-done.2.refs_3_.refs_6_.refs_9_.refs_12_), channel_id=1, source_target_pairs={{0,8},{1,9},{2,10},{3,11},{4,12},{5,13},{6,14},{7,15},{8,0},{9,1},... | collective-permute-start | bytes 1474568 | tf_op jit(solution)/shard_map/ppermute | solution.py:353
  62.2 13.5 %collective-permute-start.10 = (bf16[256,768]{1,0:T(8,128)(2,1)S(1)}, bf16[256,768]{1,0:T(8,128)(2,1)}, u32[]{:S(2)}, u32[]{:S(2)}) collective-permute-start(bf16[256,768]{1,0:T(8,128)(2,1)S(1)} %bitcast.27), channel_id=1, source_target_pairs={{0,16},{1,17},{2,18},{3,19},{4,20},{5,21},{6,22},{7,23},{8,24},{9,... | collective-permute-start | bytes 1179656 | tf_op jit(solution)/shard_map/ppermute | solution.py:353
  69.4 7.0 %collective-permute-start.7 = (bf16[256,768]{1,0:T(8,128)(2,1)S(1)}, bf16[256,768]{1,0:T(8,128)(2,1)}, u32[]{:S(2)}, u32[]{:S(2)}) collective-permute-start(bf16[256,768]{1,0:T(8,128)(2,1)S(1)} %collective-permute-done.6.refs_7_.refs_10_.refs_13_), channel_id=1, source_target_pairs={{0,8},{1,9},{2,10},{3,11},{4,12},{5,13},{6,14},{7,15},{8,0},{9,1},... | collective-permute-start | bytes 1179656 | tf_op jit(solution)/shard_map/ppermute | solution.py:353
  70.1 12.6 %collective-permute-start.8 = (bf16[256,768]{1,0:T(8,128)(2,1)S(1)}, bf16[256,768]{1,0:T(8,128)(2,1)}, u32[]{:S(2)}, u32[]{:S(2)}) collective-permute-start(bf16[256,768]{1,0:T(8,128)(2,1)S(1)} %bitcast.28), channel_id=1, source_target_pairs={{0,1},{1,0},{2,3},{3,2},{4,5},{5,4},{6,7},{7,6},{8,9},{9,8},{10,11... | collective-permute-start | bytes 1179656 | tf_op jit(solution)/shard_map/ppermute | solution.py:353
  72.7 0.8 copy-start.9
  73.4 11.4 %collective-permute-start.14 = (bf16[256,768]{1,0:T(8,128)(2,1)S(1)}, bf16[256,768]{1,0:T(8,128)(2,1)}, u32[]{:S(2)}, u32[]{:S(2)}) collective-permute-start(bf16[256,768]{1,0:T(8,128)(2,1)S(1)} %bitcast.32), channel_id=1, source_target_pairs={{0,16},{1,17},{2,18},{3,19},{4,20},{5,21},{6,22},{7,23},{8,24},{9,... | collective-permute-start | bytes 1179656 | tf_op jit(solution)/shard_map/ppermute | solution.py:353
  75.3 15.7 %collective-permute-start.9 = (bf16[256,768]{1,0:T(8,128)(2,1)S(1)}, bf16[256,768]{1,0:T(8,128)(2,1)}, u32[]{:S(2)}, u32[]{:S(2)}) collective-permute-start(bf16[256,768]{1,0:T(8,128)(2,1)S(1)} %bitcast.29), channel_id=1, source_target_pairs={{0,8},{1,9},{2,10},{3,11},{4,12},{5,13},{6,14},{7,15},{8,0},{9,1},... | collective-permute-start | bytes 1179656 | tf_op jit(solution)/shard_map/ppermute | solution.py:353
  75.7 15.3 %collective-permute-start.11 = (bf16[256,768]{1,0:T(8,128)(2,1)}, bf16[256,768]{1,0:T(8,128)(2,1)}, u32[]{:S(2)}, u32[]{:S(2)}) collective-permute-start(bf16[256,768]{1,0:T(8,128)(2,1)} %collective-permute-done.10.refs_11_.refs_14_), channel_id=1, source_target_pairs={{0,8},{1,9},{2,10},{3,11},{4,12},{5,13},{6,14},{7,15},{8,0},{9,1},... | collective-permute-start | bytes 1179656 | tf_op jit(solution)/shard_map/ppermute | solution.py:353
  75.8 11.6 %copy-start.8 = (bf16[256,768]{1,0:T(8,128)(2,1)S(1)}, bf16[256,768]{1,0:T(8,128)(2,1)}, u32[]{:S(2)}) copy-start(bf16[256,768]{1,0:T(8,128)(2,1)} %copy-done.7) | copy-start | bytes 1179652
  75.8 11.6 %copy-start.10 = (bf16[256,768]{1,0:T(8,128)(2,1)S(1)}, bf16[256,768]{1,0:T(8,128)(2,1)}, u32[]{:S(2)}) copy-start(bf16[256,768]{1,0:T(8,128)(2,1)} %copy-done.9) | copy-start | bytes 1179652
  76.4 20.1 %collective-permute-start.12 = (bf16[256,768]{1,0:T(8,128)(2,1)S(1)}, bf16[256,768]{1,0:T(8,128)(2,1)S(1)}, u32[]{:S(2)}, u32[]{:S(2)}) collective-permute-start(bf16[256,768]{1,0:T(8,128)(2,1)S(1)} %bitcast.33), channel_id=1, source_target_pairs={{0,1},{1,0},{2,3},{3,2},{4,5},{5,4},{6,7},{7,6},{8,9},{9,8},{10,11... | collective-permute-start | bytes 1179656 | tf_op jit(solution)/shard_map/ppermute | solution.py:353
  82.7 13.7 %collective-permute-start.13 = (bf16[256,768]{1,0:T(8,128)(2,1)S(1)}, bf16[256,768]{1,0:T(8,128)(2,1)S(1)}, u32[]{:S(2)}, u32[]{:S(2)}) collective-permute-start(bf16[256,768]{1,0:T(8,128)(2,1)S(1)} %bitcast.34), channel_id=1, source_target_pairs={{0,8},{1,9},{2,10},{3,11},{4,12},{5,13},{6,14},{7,15},{8,0},{9,1},... | collective-permute-start | bytes 1179656 | tf_op jit(solution)/shard_map/ppermute | solution.py:353
  84.9 11.6 %collective-permute-start.15 = (bf16[256,768]{1,0:T(8,128)(2,1)}, bf16[256,768]{1,0:T(8,128)(2,1)S(1)}, u32[]{:S(2)}, u32[]{:S(2)}) collective-permute-start(bf16[256,768]{1,0:T(8,128)(2,1)} %collective-permute-done.14.refs_15_), channel_id=1, source_target_pairs={{0,8},{1,9},{2,10},{3,11},{4,12},{5,13},{6,14},{7,15},{8,0},{9,1},... | collective-permute-start | bytes 1179656 | tf_op jit(solution)/shard_map/ppermute | solution.py:353
  87.4 3.5 %copy-start.1 = (f32[2,8,256]{2,1,0:T(8,128)}, f32[2,8,256]{2,1,0:T(8,128)S(1)}, u32[]{:S(2)}) copy-start(f32[2,8,256]{2,1,0:T(8,128)S(1)} %shard_map.38.refs_0_) | copy-start | bytes 49156
  91.0 4.9 %copy-start.2 = (f32[2,8,256]{2,1,0:T(8,128)}, f32[2,8,256]{2,1,0:T(8,128)S(1)}, u32[]{:S(2)}) copy-start(f32[2,8,256]{2,1,0:T(8,128)S(1)} %shard_map.39.refs_1_) | copy-start | bytes 49156
  (5 other events, 3.3 us)

commit v4 on v2

--- a/solution.py
+++ b/solution.py
@@ -11,6 +11,8 @@
 TILES = 4
 LABEL_ROWS = 16
 FAR = 1.0e9
+PACK_VMEM = 60 * 1024 * 1024
+COMPARE_VMEM = 24 * 1024 * 1024
 NT = (((1,), (1,)), ((), ()))
 TN = (((0,), (0,)), ((), ()))
 
@@ -140,16 +142,18 @@
             pltpu.VMEM((1, rows), jnp.int32),
             pltpu.SemaphoreType.DMA((2 + rows // 256,)),
         ],
-        compiler_params=pltpu.CompilerParams(vmem_limit_bytes=48 * 1024 * 1024),
+        compiler_params=pltpu.CompilerParams(vmem_limit_bytes=PACK_VMEM),
     )(place, embeddings, cluster.reshape(1, rows), rank.reshape(1, rows))
 
 
-def compare_kernel(sizes, plan, n_sets, joined, place_ref, *refs):
+def compare_kernel(sizes, jobs, names, joined, has_prev, place_ref, *refs):
     groups, halves, half, cap, blk = sizes
-    blocks = [refs[i * groups : (i + 1) * groups] for i in range(n_sets)]
-    n_out = 1 if joined else len(plan)
-    outs = refs[n_sets * groups : n_sets * groups + n_out]
-    key_col, key_row, low_row, turned, best = refs[n_sets * groups + n_out :]
+    block = dict(zip(names, refs))
+    refs = refs[len(names) :]
+    prev = None
+    if has_prev:
+        prev, refs = refs[0], refs[1:]
+    outs, (key_col, key_row, low_row, turned, best) = refs[:-5], refs[-5:]
     rows = groups * blk
     per_tile = blk // TILES
     tile = rows // TILES
@@ -165,16 +169,17 @@
         1.0,
         jnp.where(weight_row == 1, cap_all, jnp.where(weight_row == 2, float(half), 0.0)),
     ).astype(jnp.bfloat16)
-    for i in range(n_sets):
-        for k in range(groups):
-            key_col[pl.ds((i * groups + k) * blk, blk), :] = lax.dot_general(
-                blocks[i][k][blk : blk + LABEL_ROWS, 0:blk], weights, TN, preferred_element_type=jnp.float32
-            )
-    for o, (a, _) in enumerate(plan):
+    needed = sorted({piece for _, pieces in jobs for piece in pieces})
+    key_at = {piece: n * blk for n, piece in enumerate(needed)}
+    for piece in needed:
+        key_col[pl.ds(key_at[piece], blk), :] = lax.dot_general(
+            block[piece][blk : blk + LABEL_ROWS, 0:blk], weights, TN, preferred_element_type=jnp.float32
+        )
+    for o, (a, _) in enumerate(jobs):
         rest = jnp.zeros((LABEL_ROWS, tile), jnp.float32)
         code = jnp.zeros((LABEL_ROWS, tile), jnp.float32)
         for k in range(groups):
-            label = blocks[a][k][blk : blk + LABEL_ROWS, tile : 3 * tile].astype(jnp.float32)
+            label = block[a, k][blk : blk + LABEL_ROWS, tile : 3 * tile].astype(jnp.float32)
             rest = jnp.where(from_block == k, label[:, :tile], rest)
             code = jnp.where(from_block == k, label[:, tile:], code)
         low = code * cap_all
@@ -183,87 +188,95 @@
         key_row[o] = key[0:8]
         low_row[o] = low[0:8]
 
-    def tile_of(i, t):
-        at = pl.ds(pl.multiple_of(t * per_tile, per_tile), per_tile)
-        return [blocks[i][k][at, :] for k in range(groups)]
-
-    for o, (a, cols) in enumerate(plan):
-
-        def one_tile(t, _, a=a, cols=cols, o=o):
-            turned[...] = jnp.concatenate(tile_of(a, t), axis=0).T
+    def part_of(ref, base, t):
+        return ref[pl.ds(pl.multiple_of(base + t * per_tile, per_tile), per_tile), :]
+
+    best[...] = prev[...] if has_prev else jnp.full(best.shape, -1.0, jnp.float32)
+    for o, (a, pieces) in enumerate(jobs):
+
+        def one_tile(t, _, a=a, pieces=pieces, o=o):
+            turned[...] = jnp.concatenate(
+                [part_of(block[a, k], 0, t) for k in range(groups)], axis=0
+            ).T
             mine = key_row[o, pl.ds(t, 1), :]
             floor = low_row[o, pl.ds(t, 1), :]
 
             def one_col(s, acc):
-                theirs = []
-                pieces = []
-                for b in cols:
-                    pieces += tile_of(b, s)
-                    for k in range(groups):
-                        at = pl.multiple_of((b * groups + k) * blk + s * per_tile, per_tile)
-                        theirs.append(key_col[pl.ds(at, per_tile), :])
+                theirs = [part_of(key_col, key_at[piece], s) for piece in pieces]
                 theirs = jnp.concatenate(theirs, axis=0)
                 theirs = jnp.concatenate([theirs] * (tile // 128), axis=1)
                 sims = jnp.dot(
-                    jnp.concatenate(pieces, axis=0), turned[...], preferred_element_type=jnp.float32
+                    jnp.concatenate([part_of(block[piece], 0, s) for piece in pieces], axis=0),
+                    turned[...],
+                    preferred_element_type=jnp.float32,
                 )
                 keep = (theirs >= floor) & (theirs < mine)
                 sims = jnp.where(keep, sims, -1.0)
-                top = jnp.max(sims.reshape(len(cols) * tile // 8, 8, tile), axis=0)
+                top = jnp.max(sims.reshape(len(pieces) * per_tile // 8, 8, tile), axis=0)
                 return jnp.maximum(acc, top)
 
             acc = lax.fori_loop(0, t + 1, one_col, jnp.full((8, tile), -1.0, jnp.float32))
-            best[o, pl.ds(t, 1), :] = jnp.max(acc, axis=0, keepdims=True)
+            best[a, pl.ds(t, 1), :] = jnp.maximum(
+                best[a, pl.ds(t, 1), :], jnp.max(acc, axis=0, keepdims=True)
+            )
             return 0
 
         lax.fori_loop(0, TILES, one_tile, 0)
 
+    if not has_prev:
+        outs[0][...] = best[...]
+        return
     lane = lax.broadcasted_iota(jnp.int32, (1, tile), 1)
-    for o, (a, _) in enumerate(plan):
-        found = best[o]
+    for o, (a, _) in enumerate(jobs):
+        found = best[a]
         for k in range(groups):
             total = jnp.full((1, tile), -1.0, jnp.float32)
             for t in range(TILES):
                 turn = ((t - k) * per_tile) % tile
                 moved = pltpu.roll(found, turn, 1) if turn else found
                 total = jnp.where(lax.div(lane, per_tile) == t, moved[t : t + 1], total)
-            block = place_ref[0] ^ k
+            at = place_ref[0] ^ k
             if joined:
-                side = joined
-                outs[0][pl.ds(block * side + (place_ref[1] ^ a), 1), 0, :] = total[:, :blk]
+                outs[0][pl.ds(at * joined + (place_ref[1] ^ a), 1), 0, :] = total[:, :blk]
             else:
-                outs[o][pl.ds(block, 1), 0, :] = total[:, :blk]
-
-
-def compare(place, sets, plan, joined, sizes):
+                outs[o][pl.ds(at, 1), 0, :] = total[:, :blk]
+
+
+def compare(place, blocks, jobs, prev, joined, n_sets, sizes):
     groups, halves, half, cap, blk = sizes
-    n_sets = len(sets)
-    flat = [piece for one in sets for piece in one]
-    rows, width = groups * blk, flat[0].shape[1]
-    tile = rows // TILES
+    names = {piece for _, pieces in jobs for piece in pieces}
+    names |= {(a, k) for a, _ in jobs for k in range(groups)}
+    names = sorted(names)
+    width = blocks[0, 0].shape[1]
+    tile = groups * blk // TILES
     vmem = pl.BlockSpec(memory_space=pltpu.VMEM)
-    combos = sum(len(cols) for _, cols in plan) * TILES * (TILES + 1) // 2
-    if joined:
+    steps = TILES * (TILES + 1) // 2
+    work = sum(len(pieces) for _, pieces in jobs) * steps * (blk // TILES) * tile * width
+    if prev is None:
+        out_shape = [jax.ShapeDtypeStruct((n_sets, 8, tile), jnp.float32)]
+    elif joined:
         out_shape = [jax.ShapeDtypeStruct((groups * joined, 1, blk), jnp.float32)]
     else:
-        out_shape = [jax.ShapeDtypeStruct((groups, 1, blk), jnp.float32)] * len(plan)
+        out_shape = [jax.ShapeDtypeStruct((groups, 1, blk), jnp.float32)] * len(jobs)
+    operands = [place] + [blocks[piece] for piece in names] + ([] if prev is None else [prev])
+    needed = {piece for _, pieces in jobs for piece in pieces}
     return pl.pallas_call(
-        functools.partial(compare_kernel, sizes, plan, n_sets, joined),
+        functools.partial(compare_kernel, sizes, jobs, names, joined, prev is not None),
         out_shape=out_shape,
-        in_specs=[pl.BlockSpec(memory_space=pltpu.SMEM)] + [vmem] * len(flat),
+        in_specs=[pl.BlockSpec(memory_space=pltpu.SMEM)] + [vmem] * (len(operands) - 1),
         out_specs=[vmem] * len(out_shape),
         scratch_shapes=[
-            pltpu.VMEM((n_sets * rows, 128), jnp.float32),
-            pltpu.VMEM((len(plan), 8, tile), jnp.float32),
-            pltpu.VMEM((len(plan), 8, tile), jnp.float32),
+            pltpu.VMEM((len(needed) * blk, 128), jnp.float32),
+            pltpu.VMEM((len(jobs), 8, tile), jnp.float32),
+            pltpu.VMEM((len(jobs), 8, tile), jnp.float32),
             pltpu.VMEM((width, tile), jnp.bfloat16),
-            pltpu.VMEM((len(plan), 8, tile), jnp.float32),
+            pltpu.VMEM((n_sets, 8, tile), jnp.float32),
         ],
-        compiler_params=pltpu.CompilerParams(vmem_limit_bytes=48 * 1024 * 1024),
+        compiler_params=pltpu.CompilerParams(vmem_limit_bytes=COMPARE_VMEM),
         cost_estimate=pl.CostEstimate(
-            flops=2 * combos * tile * tile * width, bytes_accessed=2 * n_sets * rows * width, transcendentals=0
+            flops=2 * work, bytes_accessed=2 * len(names) * blk * width, transcendentals=0
         ),
-    )(place, *flat)
+    )(*operands)
 
 
 def unpack_kernel(sizes, dest_ref, back_ref, out_ref):
@@ -296,7 +309,7 @@
         out_shape=jax.ShapeDtypeStruct(dest.shape, jnp.float32),
         in_specs=[vmem] * 2,
         out_specs=vmem,
-        compiler_params=pltpu.CompilerParams(vmem_limit_bytes=48 * 1024 * 1024),
+        compiler_params=pltpu.CompilerParams(vmem_limit_bytes=COMPARE_VMEM),
     )(dest, back)
 
 
@@ -325,22 +338,47 @@
     dest, sends = packed[0], packed[1:]
 
     own = [sends[0]]
+    first_hop = swap(own[0], 0, members // 2)
     for k in range(1, groups):
         send = sends[k]
-        if k > 2:
-            send, own[k - 1] = lax.optimization_barrier((send, own[k - 1]))
+        if k == 3:
+            send, first_hop = lax.optimization_barrier((send, first_hop))
+        elif k > 3:
+            send, own[k - 2] = lax.optimization_barrier((send, own[k - 2]))
         own.append(swap(send, k, 0))
+    last = groups - 1
+    hop = {}
+    for d in offsets[1:]:
+        via = d ^ side if d & side and d ^ side in offsets else 0
+        hop[d] = via
+    near = [d for d in offsets[1:] if hop[d] == 0]
+    far = [d for d in offsets[1:] if hop[d] != 0]
     held = {0: own}
-    for d in offsets[1:]:
-        core_bit = d & ~side
-        via = core_bit if d & side and core_bit in held else 0
-        held[d] = [swap(piece, 0, d ^ via) for piece in held[via]]
+    for d in near:
+        held[d] = [
+            first_hop if d == members // 2 and k == 0 else swap(own[k], 0, d) for k in range(groups)
+        ]
+    for d in far:
+        held[d] = [swap(piece, 0, d ^ hop[d]) for piece in held[hop[d]][:last]]
 
     index = {d: i for i, d in enumerate(offsets)}
     starts = sorted({a for a, _ in pairs.values()})
-    plan = [(index[a], [index[b] for _, (e, b) in sorted(pairs.items()) if e == a]) for a in starts]
+    early, late = [], []
+    for a in starts:
+        cols = [index[b] for _, (e, b) in sorted(pairs.items()) if e == a]
+        pieces = [(b, k) for b in cols for k in range(groups)]
+        if a == 0:
+            soon = [(b, k) for b, k in pieces if b == 0 or k < last]
+            early.append((0, soon))
+            pieces = [piece for piece in pieces if piece not in soon]
+        late.append((index[a], pieces))
     joined = side if all(a < side for a in starts) else 0
-    found = compare(place, [held[d] for d in offsets], plan, joined, sizes)
+    blocks = {(index[d], k): piece for d in offsets for k, piece in enumerate(held[d])}
+    prev = compare(place, blocks, early, None, 0, len(offsets), sizes)[0]
+    for d in far:
+        piece, prev = lax.optimization_barrier((held[hop[d]][last], prev))
+        blocks[index[d], last] = swap(piece, 0, d ^ hop[d])
+    found = compare(place, blocks, late, prev, joined, len(offsets), sizes)
     if joined:
         back = found[0]
     else:

time: 94.5 us -> 91.7 us (0.970)
  waiting for transfers between devices: 35.6 us -> 28.2 us
  blocking collectives: 12 us -> 15.8 us
  local copies, waits for them, and re-layouts: 4.27 us -> 1.01 us
  Pallas kernels: 21.4 us -> 24.5 us
    ppermute x19, waiting for transfers between devices: 35.6 us -> 28.2 us  [swap(): lax.ppermute(value, ('grp', 'mem'), [(i, i ^ mask) for i in range(devices)])]
    all_to_all x1, blocking collectives: 12 us -> 15.8 us  [on_device(): back = lax.all_to_all(back, 'mem', split_axis=0, concat_axis=0, tiled=True)]
    unnamed x18 -> x6, local copies, waits for them, and re-layouts: 4.27 us -> 1.01 us
    pallas_call x1 -> x2, Pallas kernels: 15.5 us -> 17.6 us  [compare(): pl.pallas_call(functools.partial(compare_kernel, sizes, jobs, names, join...]
    pallas_call x1, Pallas kernels: 4.82 us -> 5.81 us  [pack(): pl.pallas_call(functools.partial(pack_kernel, sizes), out_shape=out_shape...]
  transfers between devices with their start and end apart: 19 -> 19, of which waited for: 8 -> 6; matrix products, arithmetic and copies ran while one was open for 0% -> 0% of each run, Pallas kernels for 0% -> 8%
where the time goes in v4:
time: 91.7 us; the launch traced here: 91.5 us
  waiting for transfers between devices  28.2 us (31%)
  Pallas kernels  24.5 us (27%)
  starting transfers between devices  21.4 us (23%)
  blocking collectives  15.8 us (17%)
  local copies, waits for them, and re-layouts  1.01 us (1%)
    ppermute x19, waiting for transfers between devices, swap(): lax.ppermute(value, ('grp', 'mem'), [(i, i ^ mask) for i in range(devices)])  28.2 us
    ppermute x19, starting transfers between devices, swap(): lax.ppermute(value, ('grp', 'mem'), [(i, i ^ mask) for i in range(devices)])  21.4 us
    pallas_call x2, Pallas kernels, compare(): pl.pallas_call(functools.partial(compare_kernel, sizes, jobs, names, join...  17.6 us
    all_to_all x1, blocking collectives, on_device(): back = lax.all_to_all(back, 'mem', split_axis=0, concat_axis=0, tiled=True)  15.8 us
    pallas_call x1, Pallas kernels, pack(): pl.pallas_call(functools.partial(pack_kernel, sizes), out_shape=out_shape...  5.81 us
  transfers between devices with their start and end apart: 19, of which 6 were waited for; matrix products, arithmetic and copies ran while one was open for 0% of the time, Pallas kernels for 8%

profile of v4, /device:TPU:0, one launch (start us, length us, event | category | flops | bytes accessed | tf_op | source)
XLA Modules:
  0.0 91.5 jit_solution(6391913344463357423)
XLA Ops:
  0.0 0.6 pad_add_fusion.place_ref
  0.6 5.8 %shard_map.37 = (s32[1,1024]{1,0:T(1,128)}, bf16[272,768]{1,0:T(8,128)(2,1)}, bf16[272,768]{1,0:T(8,128)(2,1)}, bf16[272,768]{1,0:T(8,128)(2,1)}, bf16[272,768]{1,0:T(8,128)(2,1)}) custom-call(s32[2]{0:T(128)} %pad_add_fusion.place_ref, bf16[1024,768]{1,0:T(8,128)(2,1)} %emb_hbm.1, s32[1,1024]{1,0:T(1,128)} %bitcast.5, s32[1,1024]{1,0:T(1,128)} %bitcast.6), custom_call_target="tpu_custom_call" | custom-call | tf_op jit(solution)/shard_map/pallas_call | solution.py:134
  6.4 3.1 %collective-permute-start = (bf16[272,768]{1,0:T(8,128)(2,1)}, bf16[272,768]{1,0:T(8,128)(2,1)S(1)}, u32[]{:S(2)}, u32[]{:S(2)}) collective-permute-start(bf16[272,768]{1,0:T(8,128)(2,1)} %get-tuple-element.16), channel_id=1, source_target_pairs={{0,2},{1,3},{2,0},{3,1},{4,6},{5,7},{6,4},{7,5},{8,10},{9,11},{10,... | collective-permute-start | bytes 1253384 | tf_op jit(solution)/shard_map/ppermute | solution.py:332
  9.5 2.6 %collective-permute-start.1 = (bf16[272,768]{1,0:T(8,128)(2,1)}, bf16[272,768]{1,0:T(8,128)(2,1)S(1)}, u32[]{:S(2)}, u32[]{:S(2)}) collective-permute-start(bf16[272,768]{1,0:T(8,128)(2,1)} %get-tuple-element.17), channel_id=1, source_target_pairs={{0,4},{1,5},{2,6},{3,7},{4,0},{5,1},{6,2},{7,3},{8,12},{9,13},{10,... | collective-permute-start | bytes 1253384 | tf_op jit(solution)/shard_map/ppermute | solution.py:332
  12.1 1.5 %collective-permute-start.4 = (bf16[272,768]{1,0:T(8,128)(2,1)}, bf16[272,768]{1,0:T(8,128)(2,1)S(1)}, u32[]{:S(2)}, u32[]{:S(2)}) collective-permute-start(bf16[272,768]{1,0:T(8,128)(2,1)} %get-tuple-element.15.refs_0_), channel_id=1, source_target_pairs={{0,1},{1,0},{2,3},{3,2},{4,5},{5,4},{6,7},{7,6},{8,9},{9,8},{10,11... | collective-permute-start | bytes 1253384 | tf_op jit(solution)/shard_map/ppermute | solution.py:332
  13.6 1.5 %collective-permute-start.2 = (bf16[272,768]{1,0:T(8,128)(2,1)}, bf16[272,768]{1,0:T(8,128)(2,1)S(1)}, u32[]{:S(2)}, u32[]{:S(2)}) collective-permute-start(bf16[272,768]{1,0:T(8,128)(2,1)} %get-tuple-element.15.refs_0_), channel_id=1, source_target_pairs={{0,16},{1,17},{2,18},{3,19},{4,20},{5,21},{6,22},{7,23},{8,24},{9,... | collective-permute-start | bytes 1253384 | tf_op jit(solution)/shard_map/ppermute | solution.py:332
  15.1 13.1 %collective-permute-done.refs_1_ = bf16[272,768]{1,0:T(8,128)(2,1)S(1)} collective-permute-done((bf16[272,768]{1,0:T(8,128)(2,1)}, bf16[272,768]{1,0:T(8,128)(2,1)S(1)}, u32[]{:S(2)}, u32[]{:S(2)}) %collective-permute-start) | collective-permute-done | bytes 417824 | tf_op jit(solution)/shard_map/ppermute | solution.py:332
  28.2 1.7 %collective-permute-start.12 = (bf16[272,768]{1,0:T(8,128)(2,1)S(1)}, bf16[272,768]{1,0:T(8,128)(2,1)S(1)}, u32[]{:S(2)}, u32[]{:S(2)}) collective-permute-start(bf16[272,768]{1,0:T(8,128)(2,1)S(1)} %collective-permute-done.refs_1_), channel_id=1, source_target_pairs={{0,16},{1,17},{2,18},{3,19},{4,20},{5,21},{6,22},{7,23},{8,24},{9,... | collective-permute-start | bytes 1253384 | tf_op jit(solution)/shard_map/ppermute | solution.py:332
  29.8 0.9 collective-permute-done.1.refs_2_
  30.7 1.5 %collective-permute-start.5 = (bf16[272,768]{1,0:T(8,128)(2,1)S(1)}, bf16[272,768]{1,0:T(8,128)(2,1)S(1)}, u32[]{:S(2)}, u32[]{:S(2)}) collective-permute-start(bf16[272,768]{1,0:T(8,128)(2,1)S(1)} %collective-permute-done.refs_1_), channel_id=1, source_target_pairs={{0,1},{1,0},{2,3},{3,2},{4,5},{5,4},{6,7},{7,6},{8,9},{9,8},{10,11... | collective-permute-start | bytes 1253384 | tf_op jit(solution)/shard_map/ppermute | solution.py:332
  32.2 1.5 %collective-permute-start.13 = (bf16[272,768]{1,0:T(8,128)(2,1)S(1)}, bf16[272,768]{1,0:T(8,128)(2,1)S(1)}, u32[]{:S(2)}, u32[]{:S(2)}) collective-permute-start(bf16[272,768]{1,0:T(8,128)(2,1)S(1)} %collective-permute-done.1.refs_2_), channel_id=1, source_target_pairs={{0,16},{1,17},{2,18},{3,19},{4,20},{5,21},{6,22},{7,23},{8,24},{9,... | collective-permute-start | bytes 1253384 | tf_op jit(solution)/shard_map/ppermute | solution.py:332
  33.7 7.0 %collective-permute-done.12.refs_11_.refs_13_ = bf16[272,768]{1,0:T(8,128)(2,1)S(1)} collective-permute-done((bf16[272,768]{1,0:T(8,128)(2,1)S(1)}, bf16[272,768]{1,0:T(8,128)(2,1)S(1)}, u32[]{:S(2)}, u32[]{:S(2)}) %collective-permute-start.12) | collective-permute-done | bytes 417824 | tf_op jit(solution)/shard_map/ppermute | solution.py:332
  40.7 2.6 %collective-permute-start.3 = (bf16[272,768]{1,0:T(8,128)(2,1)}, bf16[272,768]{1,0:T(8,128)(2,1)S(1)}, u32[]{:S(2)}, u32[]{:S(2)}) collective-permute-start(bf16[272,768]{1,0:T(8,128)(2,1)} %get-tuple-element.19), channel_id=1, source_target_pairs={{0,6},{1,7},{2,4},{3,5},{4,2},{5,3},{6,0},{7,1},{8,14},{9,15},{10,... | collective-permute-start | bytes 1253384 | tf_op jit(solution)/shard_map/ppermute | solution.py:332
  43.4 1.5 %collective-permute-start.6 = (bf16[272,768]{1,0:T(8,128)(2,1)S(1)}, bf16[272,768]{1,0:T(8,128)(2,1)S(1)}, u32[]{:S(2)}, u32[]{:S(2)}) collective-permute-start(bf16[272,768]{1,0:T(8,128)(2,1)S(1)} %collective-permute-done.1.refs_2_), channel_id=1, source_target_pairs={{0,1},{1,0},{2,3},{3,2},{4,5},{5,4},{6,7},{7,6},{8,9},{9,8},{10,11... | collective-permute-start | bytes 1253384 | tf_op jit(solution)/shard_map/ppermute | solution.py:332
  44.9 3.0 %collective-permute-done.13.refs_12_.refs_14_ = bf16[272,768]{1,0:T(8,128)(2,1)S(1)} collective-permute-done((bf16[272,768]{1,0:T(8,128)(2,1)S(1)}, bf16[272,768]{1,0:T(8,128)(2,1)S(1)}, u32[]{:S(2)}, u32[]{:S(2)}) %collective-permute-start.13) | collective-permute-done | bytes 417824 | tf_op jit(solution)/shard_map/ppermute | solution.py:332
  48.5 2.5 %collective-permute-done.3.refs_3_ = bf16[272,768]{1,0:T(8,128)(2,1)S(1)} collective-permute-done((bf16[272,768]{1,0:T(8,128)(2,1)}, bf16[272,768]{1,0:T(8,128)(2,1)S(1)}, u32[]{:S(2)}, u32[]{:S(2)}) %collective-permute-start.3) | collective-permute-done | bytes 417824 | tf_op jit(solution)/shard_map/ppermute | solution.py:332
  51.0 1.5 %collective-permute-start.14 = (bf16[272,768]{1,0:T(8,128)(2,1)S(1)}, bf16[272,768]{1,0:T(8,128)(2,1)S(1)}, u32[]{:S(2)}, u32[]{:S(2)}) collective-permute-start(bf16[272,768]{1,0:T(8,128)(2,1)S(1)} %collective-permute-done.3.refs_3_), channel_id=1, source_target_pairs={{0,16},{1,17},{2,18},{3,19},{4,20},{5,21},{6,22},{7,23},{8,24},{9,... | collective-permute-start | bytes 1253384 | tf_op jit(solution)/shard_map/ppermute | solution.py:332
  52.5 1.6 %collective-permute-start.7 = (bf16[272,768]{1,0:T(8,128)(2,1)S(1)}, bf16[272,768]{1,0:T(8,128)(2,1)S(1)}, u32[]{:S(2)}, u32[]{:S(2)}) collective-permute-start(bf16[272,768]{1,0:T(8,128)(2,1)S(1)} %collective-permute-done.3.refs_3_), channel_id=1, source_target_pairs={{0,1},{1,0},{2,3},{3,2},{4,5},{5,4},{6,7},{7,6},{8,9},{9,8},{10,11... | collective-permute-start | bytes 1253384 | tf_op jit(solution)/shard_map/ppermute | solution.py:332
  54.2 1.0 %copy-done.2 = bf16[272,768]{1,0:T(8,128)(2,1)S(1)} copy-done((bf16[272,768]{1,0:T(8,128)(2,1)S(1)}, bf16[272,768]{1,0:T(8,128)(2,1)}, u32[]{:S(2)}) %copy-start.2) | copy-done | bytes 417816
  55.1 7.6 %shard_map.38.refs_20_ = f32[5,8,256]{2,1,0:T(8,128)S(1)} custom-call(s32[2]{0:T(128)S(1)} %copy-done.1, bf16[272,768]{1,0:T(8,128)(2,1)S(1)} %copy-done.2, bf16[272,768]{1,0:T(8,128)(2,1)S(1)} %collective-permute-done.refs_1_, bf16[272,768]{1,0:T(8,128)(2,1)S(1)} %collective-permute-done.1.refs_2_, bf16[272,768]{1,0:T(8,128)(2,1)S(1)} %collective-permute-done.3.refs_3_, ...), custom_call_target="tpu_custom_call" | custom-call | flops 4026531840 | bytes 6291456 | tf_op jit(solution)/shard_map/pallas_call | solution.py:263
  63.0 1.6 %collective-permute-done.7.refs_7_ = bf16[272,768]{1,0:T(8,128)(2,1)S(1)} collective-permute-done((bf16[272,768]{1,0:T(8,128)(2,1)S(1)}, bf16[272,768]{1,0:T(8,128)(2,1)S(1)}, u32[]{:S(2)}, u32[]{:S(2)}) %collective-permute-start.7) | collective-permute-done | bytes 417824 | tf_op jit(solution)/shard_map/ppermute | solution.py:332
  64.6 10.0 %shard_map.39 = f32[8,1,256]{2,1,0:T(1,128)S(1)} custom-call(s32[2]{0:T(128)S(1)} %copy-done.1, bf16[272,768]{1,0:T(8,128)(2,1)S(1)} %copy-done.2, bf16[272,768]{1,0:T(8,128)(2,1)S(1)} %collective-permute-done.refs_1_, bf16[272,768]{1,0:T(8,128)(2,1)S(1)} %collective-permute-done.1.refs_2_, bf16[272,768]{1,0:T(8,128)(2,1)S(1)} %collective-permute-done.3.refs_3_, ...), custom_call_target="tpu_custom_call" | custom-call | flops 4026531840 | bytes 7864320 | tf_op jit(solution)/shard_map/pallas_call | solution.py:263
  74.6 15.8 %all_to_all.5.back_ref = f32[8,1,256]{2,1,0:T(1,128)S(1)} all-to-all(f32[8,1,256]{2,1,0:T(1,128)S(1)} %shard_map.39), channel_id=1, replica_groups=mesh['grp'=4,'mem'=8] {'mem'}, dimensions={0} | all-to-all | bytes 16384 | tf_op jit(solution)/shard_map/all_to_all | solution.py:399
  90.4 1.1 %shard_map.40 = f32[1,1024]{1,0:T(1,128)} custom-call(s32[1,1024]{1,0:T(1,128)S(1)} %copy-done, f32[8,1,256]{2,1,0:T(1,128)S(1)} %all_to_all.5.back_ref), custom_call_target="tpu_custom_call" | custom-call | tf_op jit(solution)/shard_map/pallas_call | solution.py:307
  (26 shorter events, 0.8 us)
Async XLA Ops:
  0.6 53.6 %copy-start.1 = (s32[2]{0:T(128)S(1)}, s32[2]{0:T(128)}, u32[]{:S(2)}) copy-start(s32[2]{0:T(128)} %pad_add_fusion.place_ref) | copy-start | bytes 28
  6.4 21.8 %collective-permute-start = (bf16[272,768]{1,0:T(8,128)(2,1)}, bf16[272,768]{1,0:T(8,128)(2,1)S(1)}, u32[]{:S(2)}, u32[]{:S(2)}) collective-permute-start(bf16[272,768]{1,0:T(8,128)(2,1)} %get-tuple-element.16), channel_id=1, source_target_pairs={{0,2},{1,3},{2,0},{3,1},{4,6},{5,7},{6,4},{7,5},{8,10},{9,11},{10,... | collective-permute-start | bytes 1253384 | tf_op jit(solution)/shard_map/ppermute | solution.py:332
  9.5 21.2 %collective-permute-start.1 = (bf16[272,768]{1,0:T(8,128)(2,1)}, bf16[272,768]{1,0:T(8,128)(2,1)S(1)}, u32[]{:S(2)}, u32[]{:S(2)}) collective-permute-start(bf16[272,768]{1,0:T(8,128)(2,1)} %get-tuple-element.17), channel_id=1, source_target_pairs={{0,4},{1,5},{2,6},{3,7},{4,0},{5,1},{6,2},{7,3},{8,12},{9,13},{10,... | collective-permute-start | bytes 1253384 | tf_op jit(solution)/shard_map/ppermute | solution.py:332
  12.1 18.6 %collective-permute-start.8 = (bf16[272,768]{1,0:T(8,128)(2,1)}, bf16[272,768]{1,0:T(8,128)(2,1)S(1)}, u32[]{:S(2)}, u32[]{:S(2)}) collective-permute-start(bf16[272,768]{1,0:T(8,128)(2,1)} %get-tuple-element.15.refs_0_), channel_id=1, source_target_pairs={{0,8},{1,9},{2,10},{3,11},{4,12},{5,13},{6,14},{7,15},{8,0},{9,1},... | collective-permute-start | bytes 1253384 | tf_op jit(solution)/shard_map/ppermute | solution.py:332
  12.1 20.2 %collective-permute-start.4 = (bf16[272,768]{1,0:T(8,128)(2,1)}, bf16[272,768]{1,0:T(8,128)(2,1)S(1)}, u32[]{:S(2)}, u32[]{:S(2)}) collective-permute-start(bf16[272,768]{1,0:T(8,128)(2,1)} %get-tuple-element.15.refs_0_), channel_id=1, source_target_pairs={{0,1},{1,0},{2,3},{3,2},{4,5},{5,4},{6,7},{7,6},{8,9},{9,8},{10,11... | collective-permute-start | bytes 1253384 | tf_op jit(solution)/shard_map/ppermute | solution.py:332
  13.6 20.1 %collective-permute-start.2 = (bf16[272,768]{1,0:T(8,128)(2,1)}, bf16[272,768]{1,0:T(8,128)(2,1)S(1)}, u32[]{:S(2)}, u32[]{:S(2)}) collective-permute-start(bf16[272,768]{1,0:T(8,128)(2,1)} %get-tuple-element.15.refs_0_), channel_id=1, source_target_pairs={{0,16},{1,17},{2,18},{3,19},{4,20},{5,21},{6,22},{7,23},{8,24},{9,... | collective-permute-start | bytes 1253384 | tf_op jit(solution)/shard_map/ppermute | solution.py:332
  28.2 12.6 %collective-permute-start.12 = (bf16[272,768]{1,0:T(8,128)(2,1)S(1)}, bf16[272,768]{1,0:T(8,128)(2,1)S(1)}, u32[]{:S(2)}, u32[]{:S(2)}) collective-permute-start(bf16[272,768]{1,0:T(8,128)(2,1)S(1)} %collective-permute-done.refs_1_), channel_id=1, source_target_pairs={{0,16},{1,17},{2,18},{3,19},{4,20},{5,21},{6,22},{7,23},{8,24},{9,... | collective-permute-start | bytes 1253384 | tf_op jit(solution)/shard_map/ppermute | solution.py:332
  30.7 12.7 %collective-permute-start.9 = (bf16[272,768]{1,0:T(8,128)(2,1)S(1)}, bf16[272,768]{1,0:T(8,128)(2,1)S(1)}, u32[]{:S(2)}, u32[]{:S(2)}) collective-permute-start(bf16[272,768]{1,0:T(8,128)(2,1)S(1)} %collective-permute-done.refs_1_), channel_id=1, source_target_pairs={{0,8},{1,9},{2,10},{3,11},{4,12},{5,13},{6,14},{7,15},{8,0},{9,1},... | collective-permute-start | bytes 1253384 | tf_op jit(solution)/shard_map/ppermute | solution.py:332
  30.7 14.2 %collective-permute-start.5 = (bf16[272,768]{1,0:T(8,128)(2,1)S(1)}, bf16[272,768]{1,0:T(8,128)(2,1)S(1)}, u32[]{:S(2)}, u32[]{:S(2)}) collective-permute-start(bf16[272,768]{1,0:T(8,128)(2,1)S(1)} %collective-permute-done.refs_1_), channel_id=1, source_target_pairs={{0,1},{1,0},{2,3},{3,2},{4,5},{5,4},{6,7},{7,6},{8,9},{9,8},{10,11... | collective-permute-start | bytes 1253384 | tf_op jit(solution)/shard_map/ppermute | solution.py:332
  32.2 15.7 %collective-permute-start.13 = (bf16[272,768]{1,0:T(8,128)(2,1)S(1)}, bf16[272,768]{1,0:T(8,128)(2,1)S(1)}, u32[]{:S(2)}, u32[]{:S(2)}) collective-permute-start(bf16[272,768]{1,0:T(8,128)(2,1)S(1)} %collective-permute-done.1.refs_2_), channel_id=1, source_target_pairs={{0,16},{1,17},{2,18},{3,19},{4,20},{5,21},{6,22},{7,23},{8,24},{9,... | collective-permute-start | bytes 1253384 | tf_op jit(solution)/shard_map/ppermute | solution.py:332
  33.7 14.2 %collective-permute-start.10 = (bf16[272,768]{1,0:T(8,128)(2,1)S(1)}, bf16[272,768]{1,0:T(8,128)(2,1)S(1)}, u32[]{:S(2)}, u32[]{:S(2)}) collective-permute-start(bf16[272,768]{1,0:T(8,128)(2,1)S(1)} %collective-permute-done.1.refs_2_), channel_id=1, source_target_pairs={{0,8},{1,9},{2,10},{3,11},{4,12},{5,13},{6,14},{7,15},{8,0},{9,1},... | collective-permute-start | bytes 1253384 | tf_op jit(solution)/shard_map/ppermute | solution.py:332
  40.7 10.3 %collective-permute-start.3 = (bf16[272,768]{1,0:T(8,128)(2,1)}, bf16[272,768]{1,0:T(8,128)(2,1)S(1)}, u32[]{:S(2)}, u32[]{:S(2)}) collective-permute-start(bf16[272,768]{1,0:T(8,128)(2,1)} %get-tuple-element.19), channel_id=1, source_target_pairs={{0,6},{1,7},{2,4},{3,5},{4,2},{5,3},{6,0},{7,1},{8,14},{9,15},{10,... | collective-permute-start | bytes 1253384 | tf_op jit(solution)/shard_map/ppermute | solution.py:332
  43.4 9.1 %collective-permute-start.6 = (bf16[272,768]{1,0:T(8,128)(2,1)S(1)}, bf16[272,768]{1,0:T(8,128)(2,1)S(1)}, u32[]{:S(2)}, u32[]{:S(2)}) collective-permute-start(bf16[272,768]{1,0:T(8,128)(2,1)S(1)} %collective-permute-done.1.refs_2_), channel_id=1, source_target_pairs={{0,1},{1,0},{2,3},{3,2},{4,5},{5,4},{6,7},{7,6},{8,9},{9,8},{10,11... | collective-permute-start | bytes 1253384 | tf_op jit(solution)/shard_map/ppermute | solution.py:332
  44.9 7.6 %collective-permute-start.15 = (bf16[272,768]{1,0:T(8,128)(2,1)S(1)}, bf16[272,768]{1,0:T(8,128)(2,1)S(1)}, u32[]{:S(2)}, u32[]{:S(2)}) collective-permute-start(bf16[272,768]{1,0:T(8,128)(2,1)S(1)} %collective-permute-done.2.refs_10_.refs_12_), channel_id=1, source_target_pairs={{0,8},{1,9},{2,10},{3,11},{4,12},{5,13},{6,14},{7,15},{8,0},{9,1},... | collective-permute-start | bytes 1253384 | tf_op jit(solution)/shard_map/ppermute | solution.py:332
  47.9 6.2 %collective-permute-start.16 = (bf16[272,768]{1,0:T(8,128)(2,1)S(1)}, bf16[272,768]{1,0:T(8,128)(2,1)S(1)}, u32[]{:S(2)}, u32[]{:S(2)}) collective-permute-start(bf16[272,768]{1,0:T(8,128)(2,1)S(1)} %collective-permute-done.12.refs_11_.refs_13_), channel_id=1, source_target_pairs={{0,8},{1,9},{2,10},{3,11},{4,12},{5,13},{6,14},{7,15},{8,0},{9,1},... | collective-permute-start | bytes 1253384 | tf_op jit(solution)/shard_map/ppermute | solution.py:332
  47.9 6.2 %collective-permute-start.17 = (bf16[272,768]{1,0:T(8,128)(2,1)S(1)}, bf16[272,768]{1,0:T(8,128)(2,1)S(1)}, u32[]{:S(2)}, u32[]{:S(2)}) collective-permute-start(bf16[272,768]{1,0:T(8,128)(2,1)S(1)} %collective-permute-done.13.refs_12_.refs_14_), channel_id=1, source_target_pairs={{0,8},{1,9},{2,10},{3,11},{4,12},{5,13},{6,14},{7,15},{8,0},{9,1},... | collective-permute-start | bytes 1253384 | tf_op jit(solution)/shard_map/ppermute | solution.py:332
  51.0 11.8 %collective-permute-start.14 = (bf16[272,768]{1,0:T(8,128)(2,1)S(1)}, bf16[272,768]{1,0:T(8,128)(2,1)S(1)}, u32[]{:S(2)}, u32[]{:S(2)}) collective-permute-start(bf16[272,768]{1,0:T(8,128)(2,1)S(1)} %collective-permute-done.3.refs_3_), channel_id=1, source_target_pairs={{0,16},{1,17},{2,18},{3,19},{4,20},{5,21},{6,22},{7,23},{8,24},{9,... | collective-permute-start | bytes 1253384 | tf_op jit(solution)/shard_map/ppermute | solution.py:332
  52.5 10.5 %collective-permute-start.11 = (bf16[272,768]{1,0:T(8,128)(2,1)S(1)}, bf16[272,768]{1,0:T(8,128)(2,1)S(1)}, u32[]{:S(2)}, u32[]{:S(2)}) collective-permute-start(bf16[272,768]{1,0:T(8,128)(2,1)S(1)} %collective-permute-done.3.refs_3_), channel_id=1, source_target_pairs={{0,8},{1,9},{2,10},{3,11},{4,12},{5,13},{6,14},{7,15},{8,0},{9,1},... | collective-permute-start | bytes 1253384 | tf_op jit(solution)/shard_map/ppermute | solution.py:332
  52.5 12.1 %collective-permute-start.7 = (bf16[272,768]{1,0:T(8,128)(2,1)S(1)}, bf16[272,768]{1,0:T(8,128)(2,1)S(1)}, u32[]{:S(2)}, u32[]{:S(2)}) collective-permute-start(bf16[272,768]{1,0:T(8,128)(2,1)S(1)} %collective-permute-done.3.refs_3_), channel_id=1, source_target_pairs={{0,1},{1,0},{2,3},{3,2},{4,5},{5,4},{6,7},{7,6},{8,9},{9,8},{10,11... | collective-permute-start | bytes 1253384 | tf_op jit(solution)/shard_map/ppermute | solution.py:332
  54.1 1.0 %copy-start.2 = (bf16[272,768]{1,0:T(8,128)(2,1)S(1)}, bf16[272,768]{1,0:T(8,128)(2,1)}, u32[]{:S(2)}) copy-start(bf16[272,768]{1,0:T(8,128)(2,1)} %get-tuple-element.15.refs_0_) | copy-start | bytes 1253380
  62.7 27.6 %copy-start = (s32[1,1024]{1,0:T(1,128)S(1)}, s32[1,1024]{1,0:T(1,128)}, u32[]{:S(2)}) copy-start(s32[1,1024]{1,0:T(1,128)} %get-tuple-element.14.dest_ref) | copy-start | bytes 12292
  62.8 1.8 %collective-permute-start.18 = (bf16[272,768]{1,0:T(8,128)(2,1)S(1)}, bf16[272,768]{1,0:T(8,128)(2,1)S(1)}, u32[]{:S(2)}, u32[]{:S(2)}) collective-permute-start(bf16[272,768]{1,0:T(8,128)(2,1)S(1)} %collective-permute-done.14.refs_15_), channel_id=1, source_target_pairs={{0,8},{1,9},{2,10},{3,11},{4,12},{5,13},{6,14},{7,15},{8,0},{9,1},... | collective-permute-start | bytes 1253384 | tf_op jit(solution)/shard_map/ppermute | solution.py:332

commit v5 on v4

--- a/solution.py
+++ b/solution.py
@@ -39,7 +39,7 @@
     return offsets, pairs
 
 
-def pack_kernel(sizes, place_ref, emb_hbm, cluster_hbm, rank_hbm, *refs):
+def pack_kernel(sizes, emb_hbm, cluster_hbm, rank_hbm, *refs):
     groups, halves, half, cap, blk = sizes
     dest_ref, sends = refs[0], refs[1 : 1 + groups]
     emb_ref, cluster_ref, rank_ref, sems = refs[1 + groups :]
@@ -80,7 +80,7 @@
         places.append(jnp.where(mine >= 0, mine * cap + position.astype(jnp.int32), -1))
     dest = jnp.concatenate(places, axis=1)
     dest_ref[...] = dest
-    dest = jnp.where(dest >= 0, dest ^ (place_ref[0] * blk), -1)
+    dest = jnp.where(dest >= 0, dest ^ (lax.axis_index("mem") // (halves // 2 // groups) * blk), -1)
 
     units_of = []
     for j in range(rows // step):
@@ -124,7 +124,7 @@
         sends[k][blk : blk + LABEL_ROWS, :] = jnp.concatenate(parts, axis=1).astype(jnp.bfloat16)
 
 
-def pack(place, embeddings, cluster, rank, sizes):
+def pack(embeddings, cluster, rank, sizes):
     groups, halves, half, cap, blk = sizes
     rows, width = embeddings.shape
     vmem = pl.BlockSpec(memory_space=pltpu.VMEM)
@@ -134,7 +134,7 @@
     return pl.pallas_call(
         functools.partial(pack_kernel, sizes),
         out_shape=out_shape,
-        in_specs=[pl.BlockSpec(memory_space=pltpu.SMEM), hbm, hbm, hbm],
+        in_specs=[hbm, hbm, hbm],
         out_specs=[vmem] * len(out_shape),
         scratch_shapes=[
             pltpu.VMEM((rows, width), jnp.bfloat16),
@@ -143,13 +143,14 @@
             pltpu.SemaphoreType.DMA((2 + rows // 256,)),
         ],
         compiler_params=pltpu.CompilerParams(vmem_limit_bytes=PACK_VMEM),
-    )(place, embeddings, cluster.reshape(1, rows), rank.reshape(1, rows))
-
-
-def compare_kernel(sizes, jobs, names, joined, has_prev, place_ref, *refs):
+    )(embeddings, cluster.reshape(1, rows), rank.reshape(1, rows))
+
+
+def compare_kernel(sizes, jobs, names, spots, joined, has_prev, *refs):
     groups, halves, half, cap, blk = sizes
-    block = dict(zip(names, refs))
+    array = dict(zip(names, refs))
     refs = refs[len(names) :]
+    block = {piece: (array[name], at * (blk + LABEL_ROWS)) for piece, (name, at) in spots.items()}
     prev = None
     if has_prev:
         prev, refs = refs[0], refs[1:]
@@ -171,15 +172,20 @@
     ).astype(jnp.bfloat16)
     needed = sorted({piece for _, pieces in jobs for piece in pieces})
     key_at = {piece: n * blk for n, piece in enumerate(needed)}
+
+    def label_of(piece):
+        ref, base = block[piece]
+        return ref[base + blk : base + blk + LABEL_ROWS, :]
+
     for piece in needed:
         key_col[pl.ds(key_at[piece], blk), :] = lax.dot_general(
-            block[piece][blk : blk + LABEL_ROWS, 0:blk], weights, TN, preferred_element_type=jnp.float32
+            label_of(piece)[:, 0:blk], weights, TN, preferred_element_type=jnp.float32
         )
     for o, (a, _) in enumerate(jobs):
         rest = jnp.zeros((LABEL_ROWS, tile), jnp.float32)
         code = jnp.zeros((LABEL_ROWS, tile), jnp.float32)
         for k in range(groups):
-            label = block[a, k][blk : blk + LABEL_ROWS, tile : 3 * tile].astype(jnp.float32)
+            label = label_of((a, k))[:, tile : 3 * tile].astype(jnp.float32)
             rest = jnp.where(from_block == k, label[:, :tile], rest)
             code = jnp.where(from_block == k, label[:, tile:], code)
         low = code * cap_all
@@ -196,7 +202,7 @@
 
         def one_tile(t, _, a=a, pieces=pieces, o=o):
             turned[...] = jnp.concatenate(
-                [part_of(block[a, k], 0, t) for k in range(groups)], axis=0
+                [part_of(*block[a, k], t) for k in range(groups)], axis=0
             ).T
             mine = key_row[o, pl.ds(t, 1), :]
             floor = low_row[o, pl.ds(t, 1), :]
@@ -206,7 +212,7 @@
                 theirs = jnp.concatenate(theirs, axis=0)
                 theirs = jnp.concatenate([theirs] * (tile // 128), axis=1)
                 sims = jnp.dot(
-                    jnp.concatenate([part_of(block[piece], 0, s) for piece in pieces], axis=0),
+                    jnp.concatenate([part_of(*block[piece], s) for piece in pieces], axis=0),
                     turned[...],
                     preferred_element_type=jnp.float32,
                 )
@@ -227,6 +233,8 @@
         outs[0][...] = best[...]
         return
     lane = lax.broadcasted_iota(jnp.int32, (1, tile), 1)
+    side = halves // 2 // groups
+    here = lax.axis_index("mem")
     for o, (a, _) in enumerate(jobs):
         found = best[a]
         for k in range(groups):
@@ -235,19 +243,28 @@
                 turn = ((t - k) * per_tile) % tile
                 moved = pltpu.roll(found, turn, 1) if turn else found
                 total = jnp.where(lax.div(lane, per_tile) == t, moved[t : t + 1], total)
-            at = place_ref[0] ^ k
+            at = (here // side) ^ k
             if joined:
-                outs[0][pl.ds(at * joined + (place_ref[1] ^ a), 1), 0, :] = total[:, :blk]
+                outs[0][pl.ds(at * joined + ((here % side) ^ a), 1), 0, :] = total[:, :blk]
             else:
                 outs[o][pl.ds(at, 1), 0, :] = total[:, :blk]
 
 
-def compare(place, blocks, jobs, prev, joined, n_sets, sizes):
+def compare(blocks, jobs, prev, joined, n_sets, sizes):
     groups, halves, half, cap, blk = sizes
-    names = {piece for _, pieces in jobs for piece in pieces}
-    names |= {(a, k) for a, _ in jobs for k in range(groups)}
-    names = sorted(names)
-    width = blocks[0, 0].shape[1]
+    used = {piece for _, pieces in jobs for piece in pieces}
+    used |= {(a, k) for a, _ in jobs for k in range(groups)}
+    spots = {}
+    arrays = {}
+    for piece in sorted(used):
+        value, at = blocks[piece]
+        name = next((n for n, v in arrays.items() if v is value), None)
+        if name is None:
+            name = len(arrays)
+            arrays[name] = value
+        spots[piece] = (name, at)
+    names = list(arrays)
+    width = arrays[0].shape[1]
     tile = groups * blk // TILES
     vmem = pl.BlockSpec(memory_space=pltpu.VMEM)
     steps = TILES * (TILES + 1) // 2
@@ -258,12 +275,12 @@
         out_shape = [jax.ShapeDtypeStruct((groups * joined, 1, blk), jnp.float32)]
     else:
         out_shape = [jax.ShapeDtypeStruct((groups, 1, blk), jnp.float32)] * len(jobs)
-    operands = [place] + [blocks[piece] for piece in names] + ([] if prev is None else [prev])
+    operands = list(arrays.values()) + ([] if prev is None else [prev])
     needed = {piece for _, pieces in jobs for piece in pieces}
     return pl.pallas_call(
-        functools.partial(compare_kernel, sizes, jobs, names, joined, prev is not None),
+        functools.partial(compare_kernel, sizes, jobs, names, spots, joined, prev is not None),
         out_shape=out_shape,
-        in_specs=[pl.BlockSpec(memory_space=pltpu.SMEM)] + [vmem] * (len(operands) - 1),
+        in_specs=[vmem] * len(operands),
         out_specs=[vmem] * len(out_shape),
         scratch_shapes=[
             pltpu.VMEM((len(needed) * blk, 128), jnp.float32),
@@ -274,9 +291,27 @@
         ],
         compiler_params=pltpu.CompilerParams(vmem_limit_bytes=COMPARE_VMEM),
         cost_estimate=pl.CostEstimate(
-            flops=2 * work, bytes_accessed=2 * len(names) * blk * width, transcendentals=0
+            flops=2 * work, bytes_accessed=2 * len(used) * blk * width, transcendentals=0
         ),
     )(*operands)
+
+
+def join_kernel(first_ref, second_ref, out_ref):
+    rows = first_ref.shape[0]
+    out_ref[:rows, :] = first_ref[...]
+    out_ref[rows:, :] = second_ref[...]
+
+
+def join(first, second):
+    rows, width = first.shape
+    vmem = pl.BlockSpec(memory_space=pltpu.VMEM)
+    return pl.pallas_call(
+        join_kernel,
+        out_shape=jax.ShapeDtypeStruct((2 * rows, width), first.dtype),
+        in_specs=[vmem, vmem],
+        out_specs=vmem,
+        compiler_params=pltpu.CompilerParams(vmem_limit_bytes=COMPARE_VMEM),
+    )(first, second)
 
 
 def unpack_kernel(sizes, dest_ref, back_ref, out_ref):
@@ -332,34 +367,44 @@
         return lax.ppermute(value, ("grp", "mem"), [(i, i ^ mask) for i in range(devices)])
 
     offsets, pairs = cover(members)
-    here = lax.axis_index("mem").astype(jnp.int32)
-    place = jnp.stack([here // side, here % side])
-    packed = pack(place, embeddings, cluster, rank, sizes)
+    packed = pack(embeddings, cluster, rank, sizes)
     dest, sends = packed[0], packed[1:]
 
-    own = [sends[0]]
-    first_hop = swap(own[0], 0, members // 2)
-    for k in range(1, groups):
-        send = sends[k]
-        if k == 3:
-            send, first_hop = lax.optimization_barrier((send, first_hop))
-        elif k > 3:
-            send, own[k - 2] = lax.optimization_barrier((send, own[k - 2]))
-        own.append(swap(send, k, 0))
     last = groups - 1
-    hop = {}
-    for d in offsets[1:]:
-        via = d ^ side if d & side and d ^ side in offsets else 0
-        hop[d] = via
-    near = [d for d in offsets[1:] if hop[d] == 0]
-    far = [d for d in offsets[1:] if hop[d] != 0]
-    held = {0: own}
+    far = [d for d in offsets if d & side and d != side and d ^ side in offsets]
+    near = [d for d in offsets[1:] if d not in far]
+    lead = far[0] ^ side if far else near[0]
+    held = {0: [sends[0]]}
     for d in near:
-        held[d] = [
-            first_hop if d == members // 2 and k == 0 else swap(own[k], 0, d) for k in range(groups)
-        ]
+        held[d] = [swap(sends[0], 0, d)]
     for d in far:
-        held[d] = [swap(piece, 0, d ^ hop[d]) for piece in held[hop[d]][:last]]
+        held[d] = [swap(held[d ^ side][0], 0, side)]
+    after = held[lead][0]
+    for k in range(1, groups, 2):
+        if k > 1:
+            send, after = lax.optimization_barrier((sends[k], after))
+        else:
+            send = sends[k]
+        mine = swap(send, k, 0)
+        if k < last:
+            also = swap(sends[k + 1], k + 1, 0)
+            if k == 1:
+                mine, also, *firsts = lax.optimization_barrier(
+                    (mine, also, *(held[d][0] for d in near))
+                )
+                for d, first in zip(near, firsts):
+                    held[d] = [first]
+            mine = join(mine, also)
+            after = mine
+        held[0].append(mine)
+        for d in near:
+            held[d].append(swap(mine, 0, d))
+    for spot in range(1, len(held[0]) - 1):
+        for d in far:
+            piece, held[0][spot + 1] = lax.optimization_barrier(
+                (held[d ^ side][spot], held[0][spot + 1])
+            )
+            held[d].append(swap(piece, 0, side))
 
     index = {d: i for i, d in enumerate(offsets)}
     starts = sorted({a for a, _ in pairs.values()})
@@ -373,12 +418,17 @@
             pieces = [piece for piece in pieces if piece not in soon]
         late.append((index[a], pieces))
     joined = side if all(a < side for a in starts) else 0
-    blocks = {(index[d], k): piece for d in offsets for k, piece in enumerate(held[d])}
-    prev = compare(place, blocks, early, None, 0, len(offsets), sizes)[0]
+    blocks = {}
+    for d in offsets:
+        for k in range(groups):
+            spot = (k + 1) // 2
+            if spot < len(held[d]):
+                blocks[index[d], k] = (held[d][spot], 1 - k % 2 if 0 < k < last else 0)
+    prev = compare(blocks, early, None, 0, len(offsets), sizes)[0]
     for d in far:
-        piece, prev = lax.optimization_barrier((held[hop[d]][last], prev))
-        blocks[index[d], last] = swap(piece, 0, d ^ hop[d])
-    found = compare(place, blocks, late, prev, joined, len(offsets), sizes)
+        piece, prev = lax.optimization_barrier((held[d ^ side][-1], prev))
+        blocks[index[d], last] = (swap(piece, 0, side), 0)
+    found = compare(blocks, late, prev, joined, len(offsets), sizes)
     if joined:
         back = found[0]
     else:
@@ -393,7 +443,7 @@
         for spot in range(side):
             value = near_of[spot]
             for mine in range(1, side):
-                value = jnp.where(place[1] == mine, near_of[spot ^ mine], value)
+                value = jnp.where(lax.axis_index("mem") % side == mine, near_of[spot ^ mine], value)
             rows_of.append(value)
         back = jnp.stack(rows_of, axis=1).reshape(groups * side, 1, blk)
     back = lax.all_to_all(back, "mem", split_axis=0, concat_axis=0, tiled=True)

time: 91.7 us -> 84.8 us (0.925)
  waiting for transfers between devices: 28.2 us -> 33.8 us
  blocking collectives: 15.8 us -> 10.3 us
  starting transfers between devices: 21.4 us -> 17.7 us
  Pallas kernels: 24.5 us -> 22.7 us
  local copies, waits for them, and re-layouts: 1.01 us -> 0.01 us
    ppermute x19 -> x15, waiting for transfers between devices: 28.2 us -> 33.8 us  [swap(): lax.ppermute(value, ('grp', 'mem'), [(i, i ^ mask) for i in range(devices)])]
    all_to_all x1, blocking collectives: 15.8 us -> 10.3 us  [on_device(): back = lax.all_to_all(back, 'mem', split_axis=0, concat_axis=0, tiled=True)]
    ppermute x19 -> x15, starting transfers between devices: 21.4 us -> 17.7 us  [swap(): lax.ppermute(value, ('grp', 'mem'), [(i, i ^ mask) for i in range(devices)])]
    pallas_call x2 -> x3, Pallas kernels: 17.6 us -> 16.6 us  [the longest x2 16.5 us: compare(): pl.pallas_call(functools.partial(compare_kernel, sizes, jobs, names, spot...]
    unnamed x6, local copies, waits for them, and re-layouts: 1.01 us -> 0.01 us
  transfers between devices with their start and end apart: 19 -> 15, of which waited for: 6 -> 8; matrix products, arithmetic and copies ran while one was open for 0% -> 0% of each run, Pallas kernels for 8% -> 8%
where the time goes in v5:
time: 84.8 us; the launch traced here: 84.6 us
  waiting for transfers between devices  33.8 us (40%)
  Pallas kernels  22.7 us (27%)
  starting transfers between devices  17.7 us (21%)
  blocking collectives  10.3 us (12%)
    ppermute x15, waiting for transfers between devices, swap(): lax.ppermute(value, ('grp', 'mem'), [(i, i ^ mask) for i in range(devices)])  33.8 us
    ppermute x15, starting transfers between devices, swap(): lax.ppermute(value, ('grp', 'mem'), [(i, i ^ mask) for i in range(devices)])  17.7 us
    pallas_call x2, Pallas kernels, compare(): pl.pallas_call(functools.partial(compare_kernel, sizes, jobs, names, spot...  16.5 us
    all_to_all x1, blocking collectives, on_device(): back = lax.all_to_all(back, 'mem', split_axis=0, concat_axis=0, tiled=True)  10.3 us
    pallas_call x1, Pallas kernels, pack(): pl.pallas_call(functools.partial(pack_kernel, sizes), out_shape=out_shape...  5.08 us
  transfers between devices with their start and end apart: 15, of which 8 were waited for; matrix products, arithmetic and copies ran while one was open for 0% of the time, Pallas kernels for 8%

profile of v5, /device:TPU:0, one launch (start us, length us, event | category | flops | bytes accessed | tf_op | source)
XLA Modules:
  0.0 84.6 jit_solution(5391275922651499014)
XLA Ops:
  0.0 5.1 %shard_map.37 = (s32[1,1024]{1,0:T(1,128)}, bf16[272,768]{1,0:T(8,128)(2,1)}, bf16[272,768]{1,0:T(8,128)(2,1)}, bf16[272,768]{1,0:T(8,128)(2,1)}, bf16[272,768]{1,0:T(8,128)(2,1)}) custom-call(bf16[1024,768]{1,0:T(8,128)(2,1)} %emb_hbm.1, s32[1,1024]{1,0:T(1,128)} %bitcast.3, s32[1,1024]{1,0:T(1,128)} %bitcast.4), custom_call_target="tpu_custom_call" | custom-call | tf_op jit(solution)/shard_map/pallas_call | solution.py:134
  5.1 3.1 %collective-permute-start = (bf16[272,768]{1,0:T(8,128)(2,1)}, bf16[272,768]{1,0:T(8,128)(2,1)S(1)}, u32[]{:S(2)}, u32[]{:S(2)}) collective-permute-start(bf16[272,768]{1,0:T(8,128)(2,1)} %get-tuple-element.22), channel_id=1, source_target_pairs={{0,2},{1,3},{2,0},{3,1},{4,6},{5,7},{6,4},{7,5},{8,10},{9,11},{10,... | collective-permute-start | bytes 1253384 | tf_op jit(solution)/shard_map/ppermute | solution.py:367
  8.2 2.6 %collective-permute-start.1 = (bf16[272,768]{1,0:T(8,128)(2,1)}, bf16[272,768]{1,0:T(8,128)(2,1)S(1)}, u32[]{:S(2)}, u32[]{:S(2)}) collective-permute-start(bf16[272,768]{1,0:T(8,128)(2,1)} %get-tuple-element.23), channel_id=1, source_target_pairs={{0,4},{1,5},{2,6},{3,7},{4,0},{5,1},{6,2},{7,3},{8,12},{9,13},{10,... | collective-permute-start | bytes 1253384 | tf_op jit(solution)/shard_map/ppermute | solution.py:367
  10.8 1.5 %collective-permute-start.4 = (bf16[272,768]{1,0:T(8,128)(2,1)}, bf16[272,768]{1,0:T(8,128)(2,1)S(1)}, u32[]{:S(2)}, u32[]{:S(2)}) collective-permute-start(bf16[272,768]{1,0:T(8,128)(2,1)} %get-tuple-element.21.refs_0_), channel_id=1, source_target_pairs={{0,16},{1,17},{2,18},{3,19},{4,20},{5,21},{6,22},{7,23},{8,24},{9,... | collective-permute-start | bytes 1253384 | tf_op jit(solution)/shard_map/ppermute | solution.py:367
  12.3 1.5 %collective-permute-start.2 = (bf16[272,768]{1,0:T(8,128)(2,1)}, bf16[272,768]{1,0:T(8,128)(2,1)S(1)}, u32[]{:S(2)}, u32[]{:S(2)}) collective-permute-start(bf16[272,768]{1,0:T(8,128)(2,1)} %get-tuple-element.21.refs_0_), channel_id=1, source_target_pairs={{0,1},{1,0},{2,3},{3,2},{4,5},{5,4},{6,7},{7,6},{8,9},{9,8},{10,11... | collective-permute-start | bytes 1253384 | tf_op jit(solution)/shard_map/ppermute | solution.py:367
  13.8 13.1 %collective-permute-done.first_ref = bf16[272,768]{1,0:T(8,128)(2,1)S(1)} collective-permute-done((bf16[272,768]{1,0:T(8,128)(2,1)}, bf16[272,768]{1,0:T(8,128)(2,1)S(1)}, u32[]{:S(2)}, u32[]{:S(2)}) %collective-permute-start) | collective-permute-done | bytes 417824 | tf_op jit(solution)/shard_map/ppermute | solution.py:367
  26.9 2.5 %collective-permute-done.1.second_ref = bf16[272,768]{1,0:T(8,128)(2,1)S(1)} collective-permute-done((bf16[272,768]{1,0:T(8,128)(2,1)}, bf16[272,768]{1,0:T(8,128)(2,1)S(1)}, u32[]{:S(2)}, u32[]{:S(2)}) %collective-permute-start.1) | collective-permute-done | bytes 417824 | tf_op jit(solution)/shard_map/ppermute | solution.py:367
  29.5 1.6 %collective-permute-start.5 = (bf16[544,768]{1,0:T(8,128)(2,1)S(1)}, bf16[544,768]{1,0:T(8,128)(2,1)S(1)}, u32[]{:S(2)}, u32[]{:S(2)}) collective-permute-start(bf16[544,768]{1,0:T(8,128)(2,1)S(1)} %shard_map.38.refs_1_), channel_id=1, source_target_pairs={{0,16},{1,17},{2,18},{3,19},{4,20},{5,21},{6,22},{7,23},{8,24},{9,... | collective-permute-start | bytes 2506760 | tf_op jit(solution)/shard_map/ppermute | solution.py:367
  31.0 2.5 %collective-permute-start.6 = (bf16[272,768]{1,0:T(8,128)(2,1)S(1)}, bf16[272,768]{1,0:T(8,128)(2,1)S(1)}, u32[]{:S(2)}, u32[]{:S(2)}) collective-permute-start(bf16[272,768]{1,0:T(8,128)(2,1)S(1)} %copy-done.2), channel_id=1, source_target_pairs={{0,6},{1,7},{2,4},{3,5},{4,2},{5,3},{6,0},{7,1},{8,14},{9,15},{10,... | collective-permute-start | bytes 1253384 | tf_op jit(solution)/shard_map/ppermute | solution.py:367
  33.5 1.5 %collective-permute-start.7 = (bf16[544,768]{1,0:T(8,128)(2,1)S(1)}, bf16[544,768]{1,0:T(8,128)(2,1)S(1)}, u32[]{:S(2)}, u32[]{:S(2)}) collective-permute-start(bf16[544,768]{1,0:T(8,128)(2,1)S(1)} %shard_map.38.refs_1_), channel_id=1, source_target_pairs={{0,1},{1,0},{2,3},{3,2},{4,5},{5,4},{6,7},{7,6},{8,9},{9,8},{10,11... | collective-permute-start | bytes 2506760 | tf_op jit(solution)/shard_map/ppermute | solution.py:367
  35.0 5.9 %collective-permute-done.6.refs_2_ = bf16[272,768]{1,0:T(8,128)(2,1)S(1)} collective-permute-done((bf16[272,768]{1,0:T(8,128)(2,1)S(1)}, bf16[272,768]{1,0:T(8,128)(2,1)S(1)}, u32[]{:S(2)}, u32[]{:S(2)}) %collective-permute-start.6) | collective-permute-done | bytes 417824 | tf_op jit(solution)/shard_map/ppermute | solution.py:367
  40.9 5.9 %collective-permute-done.5.refs_8_.refs_10_ = bf16[544,768]{1,0:T(8,128)(2,1)S(1)} collective-permute-done((bf16[544,768]{1,0:T(8,128)(2,1)S(1)}, bf16[544,768]{1,0:T(8,128)(2,1)S(1)}, u32[]{:S(2)}, u32[]{:S(2)}) %collective-permute-start.5) | collective-permute-done | bytes 835616 | tf_op jit(solution)/shard_map/ppermute | solution.py:367
  46.8 0.5 collective-permute-start.12
  47.3 1.4 %collective-permute-start.11 = (bf16[272,768]{1,0:T(8,128)(2,1)S(1)}, bf16[272,768]{1,0:T(8,128)(2,1)S(1)}, u32[]{:S(2)}, u32[]{:S(2)}) collective-permute-start(bf16[272,768]{1,0:T(8,128)(2,1)S(1)} %collective-permute-done.6.refs_2_), channel_id=1, source_target_pairs={{0,16},{1,17},{2,18},{3,19},{4,20},{5,21},{6,22},{7,23},{8,24},{9,... | collective-permute-start | bytes 1253384 | tf_op jit(solution)/shard_map/ppermute | solution.py:367
  48.7 1.1 %collective-permute-done.12.refs_9_.refs_12_ = bf16[272,768]{1,0:T(8,128)(2,1)S(1)} collective-permute-done((bf16[272,768]{1,0:T(8,128)(2,1)S(1)}, bf16[272,768]{1,0:T(8,128)(2,1)S(1)}, u32[]{:S(2)}, u32[]{:S(2)}) %collective-permute-start.12) | collective-permute-done | bytes 417824 | tf_op jit(solution)/shard_map/ppermute | solution.py:367
  49.8 0.1 collective-permute-start.10
  49.9 1.4 %collective-permute-start.8 = (bf16[272,768]{1,0:T(8,128)(2,1)S(1)}, bf16[272,768]{1,0:T(8,128)(2,1)S(1)}, u32[]{:S(2)}, u32[]{:S(2)}) collective-permute-start(bf16[272,768]{1,0:T(8,128)(2,1)S(1)} %collective-permute-done.6.refs_2_), channel_id=1, source_target_pairs={{0,1},{1,0},{2,3},{3,2},{4,5},{5,4},{6,7},{7,6},{8,9},{9,8},{10,11... | collective-permute-start | bytes 1253384 | tf_op jit(solution)/shard_map/ppermute | solution.py:367
  51.3 3.6 %collective-permute-done.7.refs_4_ = bf16[544,768]{1,0:T(8,128)(2,1)S(1)} collective-permute-done((bf16[544,768]{1,0:T(8,128)(2,1)S(1)}, bf16[544,768]{1,0:T(8,128)(2,1)S(1)}, u32[]{:S(2)}, u32[]{:S(2)}) %collective-permute-start.7) | collective-permute-done | bytes 835616 | tf_op jit(solution)/shard_map/ppermute | solution.py:367
  54.9 7.1 %shard_map.39.refs_15_ = f32[5,8,256]{2,1,0:T(8,128)S(1)} custom-call(bf16[272,768]{1,0:T(8,128)(2,1)S(1)} %copy-done.1, bf16[544,768]{1,0:T(8,128)(2,1)S(1)} %shard_map.38.refs_1_, bf16[272,768]{1,0:T(8,128)(2,1)S(1)} %collective-permute-done.6.refs_2_, bf16[272,768]{1,0:T(8,128)(2,1)S(1)} %collective-permute-done.2.refs_3_, ...), custom_call_target="tpu_custom_call" | custom-call | flops 4026531840 | bytes 6291456 | tf_op jit(solution)/shard_map/pallas_call | solution.py:280
  62.1 1.4 %collective-permute-done.8.refs_5_ = bf16[272,768]{1,0:T(8,128)(2,1)S(1)} collective-permute-done((bf16[272,768]{1,0:T(8,128)(2,1)S(1)}, bf16[272,768]{1,0:T(8,128)(2,1)S(1)}, u32[]{:S(2)}, u32[]{:S(2)}) %collective-permute-start.8) | collective-permute-done | bytes 417824 | tf_op jit(solution)/shard_map/ppermute | solution.py:367
  63.5 0.3 collective-permute-done.14.refs_14_
  63.8 9.4 %shard_map.40 = f32[8,1,256]{2,1,0:T(1,128)S(1)} custom-call(bf16[272,768]{1,0:T(8,128)(2,1)S(1)} %copy-done.1, bf16[544,768]{1,0:T(8,128)(2,1)S(1)} %shard_map.38.refs_1_, bf16[272,768]{1,0:T(8,128)(2,1)S(1)} %collective-permute-done.6.refs_2_, bf16[272,768]{1,0:T(8,128)(2,1)S(1)} %collective-permute-done.2.refs_3_, ...), custom_call_target="tpu_custom_call" | custom-call | flops 4026531840 | bytes 7864320 | tf_op jit(solution)/shard_map/pallas_call | solution.py:280
  73.3 10.3 %all_to_all.5.back_ref = f32[8,1,256]{2,1,0:T(1,128)S(1)} all-to-all(f32[8,1,256]{2,1,0:T(1,128)S(1)} %shard_map.40), channel_id=1, replica_groups=mesh['grp'=4,'mem'=8] {'mem'}, dimensions={0} | all-to-all | bytes 16384 | tf_op jit(solution)/shard_map/all_to_all | solution.py:449
  83.5 1.1 %shard_map.41 = f32[1,1024]{1,0:T(1,128)} custom-call(s32[1,1024]{1,0:T(1,128)S(1)} %copy-done, f32[8,1,256]{2,1,0:T(1,128)S(1)} %all_to_all.5.back_ref), custom_call_target="tpu_custom_call" | custom-call | tf_op jit(solution)/shard_map/pallas_call | solution.py:342
  (18 shorter events, 0.2 us)
Async XLA Ops:
  5.1 26.0 %copy-start.2 = (bf16[272,768]{1,0:T(8,128)(2,1)S(1)}, bf16[272,768]{1,0:T(8,128)(2,1)}, u32[]{:S(2)}) copy-start(bf16[272,768]{1,0:T(8,128)(2,1)} %get-tuple-element.27) | copy-start | bytes 1253380
  5.1 49.8 %copy-start.1 = (bf16[272,768]{1,0:T(8,128)(2,1)S(1)}, bf16[272,768]{1,0:T(8,128)(2,1)}, u32[]{:S(2)}) copy-start(bf16[272,768]{1,0:T(8,128)(2,1)} %get-tuple-element.21.refs_0_) | copy-start | bytes 1253380
  5.1 21.8 %collective-permute-start = (bf16[272,768]{1,0:T(8,128)(2,1)}, bf16[272,768]{1,0:T(8,128)(2,1)S(1)}, u32[]{:S(2)}, u32[]{:S(2)}) collective-permute-start(bf16[272,768]{1,0:T(8,128)(2,1)} %get-tuple-element.22), channel_id=1, source_target_pairs={{0,2},{1,3},{2,0},{3,1},{4,6},{5,7},{6,4},{7,5},{8,10},{9,11},{10,... | collective-permute-start | bytes 1253384 | tf_op jit(solution)/shard_map/ppermute | solution.py:367
  8.2 21.2 %collective-permute-start.1 = (bf16[272,768]{1,0:T(8,128)(2,1)}, bf16[272,768]{1,0:T(8,128)(2,1)S(1)}, u32[]{:S(2)}, u32[]{:S(2)}) collective-permute-start(bf16[272,768]{1,0:T(8,128)(2,1)} %get-tuple-element.23), channel_id=1, source_target_pairs={{0,4},{1,5},{2,6},{3,7},{4,0},{5,1},{6,2},{7,3},{8,12},{9,13},{10,... | collective-permute-start | bytes 1253384 | tf_op jit(solution)/shard_map/ppermute | solution.py:367
  10.8 18.6 %collective-permute-start.4 = (bf16[272,768]{1,0:T(8,128)(2,1)}, bf16[272,768]{1,0:T(8,128)(2,1)S(1)}, u32[]{:S(2)}, u32[]{:S(2)}) collective-permute-start(bf16[272,768]{1,0:T(8,128)(2,1)} %get-tuple-element.21.refs_0_), channel_id=1, source_target_pairs={{0,16},{1,17},{2,18},{3,19},{4,20},{5,21},{6,22},{7,23},{8,24},{9,... | collective-permute-start | bytes 1253384 | tf_op jit(solution)/shard_map/ppermute | solution.py:367
  12.3 17.1 %collective-permute-start.3 = (bf16[272,768]{1,0:T(8,128)(2,1)}, bf16[272,768]{1,0:T(8,128)(2,1)S(1)}, u32[]{:S(2)}, u32[]{:S(2)}) collective-permute-start(bf16[272,768]{1,0:T(8,128)(2,1)} %get-tuple-element.21.refs_0_), channel_id=1, source_target_pairs={{0,8},{1,9},{2,10},{3,11},{4,12},{5,13},{6,14},{7,15},{8,0},{9,1},... | collective-permute-start | bytes 1253384 | tf_op jit(solution)/shard_map/ppermute | solution.py:367
  12.3 17.1 %collective-permute-start.2 = (bf16[272,768]{1,0:T(8,128)(2,1)}, bf16[272,768]{1,0:T(8,128)(2,1)S(1)}, u32[]{:S(2)}, u32[]{:S(2)}) collective-permute-start(bf16[272,768]{1,0:T(8,128)(2,1)} %get-tuple-element.21.refs_0_), channel_id=1, source_target_pairs={{0,1},{1,0},{2,3},{3,2},{4,5},{5,4},{6,7},{7,6},{8,9},{9,8},{10,11... | collective-permute-start | bytes 1253384 | tf_op jit(solution)/shard_map/ppermute | solution.py:367
  29.5 17.3 %collective-permute-start.5 = (bf16[544,768]{1,0:T(8,128)(2,1)S(1)}, bf16[544,768]{1,0:T(8,128)(2,1)S(1)}, u32[]{:S(2)}, u32[]{:S(2)}) collective-permute-start(bf16[544,768]{1,0:T(8,128)(2,1)S(1)} %shard_map.38.refs_1_), channel_id=1, source_target_pairs={{0,16},{1,17},{2,18},{3,19},{4,20},{5,21},{6,22},{7,23},{8,24},{9,... | collective-permute-start | bytes 2506760 | tf_op jit(solution)/shard_map/ppermute | solution.py:367
  31.0 9.9 %collective-permute-start.6 = (bf16[272,768]{1,0:T(8,128)(2,1)S(1)}, bf16[272,768]{1,0:T(8,128)(2,1)S(1)}, u32[]{:S(2)}, u32[]{:S(2)}) collective-permute-start(bf16[272,768]{1,0:T(8,128)(2,1)S(1)} %copy-done.2), channel_id=1, source_target_pairs={{0,6},{1,7},{2,4},{3,5},{4,2},{5,3},{6,0},{7,1},{8,14},{9,15},{10,... | collective-permute-start | bytes 1253384 | tf_op jit(solution)/shard_map/ppermute | solution.py:367
  33.5 16.4 %collective-permute-start.9 = (bf16[544,768]{1,0:T(8,128)(2,1)S(1)}, bf16[544,768]{1,0:T(8,128)(2,1)S(1)}, u32[]{:S(2)}, u32[]{:S(2)}) collective-permute-start(bf16[544,768]{1,0:T(8,128)(2,1)S(1)} %shard_map.38.refs_1_), channel_id=1, source_target_pairs={{0,8},{1,9},{2,10},{3,11},{4,12},{5,13},{6,14},{7,15},{8,0},{9,1},... | collective-permute-start | bytes 2506760 | tf_op jit(solution)/shard_map/ppermute | solution.py:367
  33.5 21.4 %collective-permute-start.7 = (bf16[544,768]{1,0:T(8,128)(2,1)S(1)}, bf16[544,768]{1,0:T(8,128)(2,1)S(1)}, u32[]{:S(2)}, u32[]{:S(2)}) collective-permute-start(bf16[544,768]{1,0:T(8,128)(2,1)S(1)} %shard_map.38.refs_1_), channel_id=1, source_target_pairs={{0,1},{1,0},{2,3},{3,2},{4,5},{5,4},{6,7},{7,6},{8,9},{9,8},{10,11... | collective-permute-start | bytes 2506760 | tf_op jit(solution)/shard_map/ppermute | solution.py:367
  46.8 8.1 %collective-permute-start.13 = (bf16[544,768]{1,0:T(8,128)(2,1)S(1)}, bf16[544,768]{1,0:T(8,128)(2,1)S(1)}, u32[]{:S(2)}, u32[]{:S(2)}) collective-permute-start(bf16[544,768]{1,0:T(8,128)(2,1)S(1)} %collective-permute-done.5.refs_8_.refs_10_), channel_id=1, source_target_pairs={{0,8},{1,9},{2,10},{3,11},{4,12},{5,13},{6,14},{7,15},{8,0},{9,1},... | collective-permute-start | bytes 2506760 | tf_op jit(solution)/shard_map/ppermute | solution.py:367
  46.8 3.0 %collective-permute-start.12 = (bf16[272,768]{1,0:T(8,128)(2,1)S(1)}, bf16[272,768]{1,0:T(8,128)(2,1)S(1)}, u32[]{:S(2)}, u32[]{:S(2)}) collective-permute-start(bf16[272,768]{1,0:T(8,128)(2,1)S(1)} %collective-permute-done.4.refs_7_.refs_9_), channel_id=1, source_target_pairs={{0,8},{1,9},{2,10},{3,11},{4,12},{5,13},{6,14},{7,15},{8,0},{9,1},... | collective-permute-start | bytes 1253384 | tf_op jit(solution)/shard_map/ppermute | solution.py:367
  47.3 14.7 %collective-permute-start.11 = (bf16[272,768]{1,0:T(8,128)(2,1)S(1)}, bf16[272,768]{1,0:T(8,128)(2,1)S(1)}, u32[]{:S(2)}, u32[]{:S(2)}) collective-permute-start(bf16[272,768]{1,0:T(8,128)(2,1)S(1)} %collective-permute-done.6.refs_2_), channel_id=1, source_target_pairs={{0,16},{1,17},{2,18},{3,19},{4,20},{5,21},{6,22},{7,23},{8,24},{9,... | collective-permute-start | bytes 1253384 | tf_op jit(solution)/shard_map/ppermute | solution.py:367
  49.8 12.3 %collective-permute-start.10 = (bf16[272,768]{1,0:T(8,128)(2,1)S(1)}, bf16[272,768]{1,0:T(8,128)(2,1)S(1)}, u32[]{:S(2)}, u32[]{:S(2)}) collective-permute-start(bf16[272,768]{1,0:T(8,128)(2,1)S(1)} %collective-permute-done.6.refs_2_), channel_id=1, source_target_pairs={{0,8},{1,9},{2,10},{3,11},{4,12},{5,13},{6,14},{7,15},{8,0},{9,1},... | collective-permute-start | bytes 1253384 | tf_op jit(solution)/shard_map/ppermute | solution.py:367
  49.9 13.6 %collective-permute-start.8 = (bf16[272,768]{1,0:T(8,128)(2,1)S(1)}, bf16[272,768]{1,0:T(8,128)(2,1)S(1)}, u32[]{:S(2)}, u32[]{:S(2)}) collective-permute-start(bf16[272,768]{1,0:T(8,128)(2,1)S(1)} %collective-permute-done.6.refs_2_), channel_id=1, source_target_pairs={{0,1},{1,0},{2,3},{3,2},{4,5},{5,4},{6,7},{7,6},{8,9},{9,8},{10,11... | collective-permute-start | bytes 1253384 | tf_op jit(solution)/shard_map/ppermute | solution.py:367
  62.0 21.6 %copy-start = (s32[1,1024]{1,0:T(1,128)S(1)}, s32[1,1024]{1,0:T(1,128)}, u32[]{:S(2)}) copy-start(s32[1,1024]{1,0:T(1,128)} %get-tuple-element.20.dest_ref) | copy-start | bytes 12292
  62.0 1.8 %collective-permute-start.14 = (bf16[272,768]{1,0:T(8,128)(2,1)S(1)}, bf16[272,768]{1,0:T(8,128)(2,1)S(1)}, u32[]{:S(2)}, u32[]{:S(2)}) collective-permute-start(bf16[272,768]{1,0:T(8,128)(2,1)S(1)} %collective-permute-done.11.refs_11_), channel_id=1, source_target_pairs={{0,8},{1,9},{2,10},{3,11},{4,12},{5,13},{6,14},{7,15},{8,0},{9,1},... | collective-permute-start | bytes 1253384 | tf_op jit(solution)/shard_map/ppermute | solution.py:367

commit v6 on v5

--- a/solution.py
+++ b/solution.py
@@ -39,10 +39,10 @@
     return offsets, pairs
 
 
-def pack_kernel(sizes, emb_hbm, cluster_hbm, rank_hbm, *refs):
+def pack_kernel(sizes, ks, emb_hbm, cluster_hbm, rank_hbm, *refs):
     groups, halves, half, cap, blk = sizes
-    dest_ref, sends = refs[0], refs[1 : 1 + groups]
-    emb_ref, cluster_ref, rank_ref, sems = refs[1 + groups :]
+    dest_ref, outs = refs[0], refs[1 : 1 + len(ks)]
+    emb_ref, cluster_ref, rank_ref, stage, sems, out_sems = refs[1 + len(ks) :]
     rows = emb_ref.shape[0]
     step = 256
     loads = [
@@ -107,10 +107,11 @@
     own_tile = label_row == lax.div(label_col, per_tile)
     unit_col = lax.div(label_col, cap).astype(jnp.float32)
     slot = lax.broadcasted_iota(jnp.int32, (blk, rows), 0)
-    width = sends[0].shape[1]
-    for k in range(groups):
+    width = emb_ref.shape[1]
+    leaving = []
+    for n, k in enumerate(ks):
         pick = (slot + k * blk == dest).astype(jnp.float32).astype(jnp.bfloat16)
-        sends[k][0:blk, :] = jnp.dot(pick, unit, preferred_element_type=jnp.float32).astype(
+        stage[n, 0:blk, :] = jnp.dot(pick, unit, preferred_element_type=jnp.float32).astype(
             jnp.bfloat16
         )
         mine = lax.dot_general(labels, pick, NT, preferred_element_type=jnp.float32)
@@ -121,28 +122,36 @@
             parts.append(jnp.dot(line, spread, preferred_element_type=jnp.float32))
         if width > 3 * wide_tile:
             parts.append(jnp.zeros((LABEL_ROWS, width - 3 * wide_tile), jnp.float32))
-        sends[k][blk : blk + LABEL_ROWS, :] = jnp.concatenate(parts, axis=1).astype(jnp.bfloat16)
-
-
-def pack(embeddings, cluster, rank, sizes):
+        stage[n, blk : blk + LABEL_ROWS, :] = jnp.concatenate(parts, axis=1).astype(jnp.bfloat16)
+        leaving.append(pltpu.make_async_copy(stage.at[n], outs[n], out_sems.at[n]))
+        leaving[-1].start()
+    for copy in leaving:
+        copy.wait()
+
+
+def pack(embeddings, cluster, rank, ks, sizes):
     groups, halves, half, cap, blk = sizes
     rows, width = embeddings.shape
-    vmem = pl.BlockSpec(memory_space=pltpu.VMEM)
     hbm = pl.BlockSpec(memory_space=pltpu.HBM)
     out_shape = [jax.ShapeDtypeStruct((1, rows), jnp.int32)]
-    out_shape += [jax.ShapeDtypeStruct((blk + LABEL_ROWS, width), jnp.bfloat16)] * groups
+    out_shape += [jax.ShapeDtypeStruct((blk + LABEL_ROWS, width), jnp.bfloat16)] * len(ks)
     return pl.pallas_call(
-        functools.partial(pack_kernel, sizes),
+        functools.partial(pack_kernel, sizes, ks),
         out_shape=out_shape,
         in_specs=[hbm, hbm, hbm],
-        out_specs=[vmem] * len(out_shape),
+        out_specs=[pl.BlockSpec(memory_space=pltpu.VMEM)] + [hbm] * len(ks),
         scratch_shapes=[
             pltpu.VMEM((rows, width), jnp.bfloat16),
             pltpu.VMEM((1, rows), jnp.int32),
             pltpu.VMEM((1, rows), jnp.int32),
+            pltpu.VMEM((len(ks), blk + LABEL_ROWS, width), jnp.bfloat16),
             pltpu.SemaphoreType.DMA((2 + rows // 256,)),
+            pltpu.SemaphoreType.DMA((len(ks),)),
         ],
         compiler_params=pltpu.CompilerParams(vmem_limit_bytes=PACK_VMEM),
+        cost_estimate=pl.CostEstimate(
+            flops=2 * len(ks) * blk * rows * width, bytes_accessed=4 * rows * width, transcendentals=0
+        ),
     )(embeddings, cluster.reshape(1, rows), rank.reshape(1, rows))
 
 
@@ -194,40 +203,35 @@
         key_row[o] = key[0:8]
         low_row[o] = low[0:8]
 
-    def part_of(ref, base, t):
-        return ref[pl.ds(pl.multiple_of(base + t * per_tile, per_tile), per_tile), :]
+    def rows_of(ref, base, first, last):
+        return ref[base + first * per_tile : base + last * per_tile, :]
 
     best[...] = prev[...] if has_prev else jnp.full(best.shape, -1.0, jnp.float32)
     for o, (a, pieces) in enumerate(jobs):
-
-        def one_tile(t, _, a=a, pieces=pieces, o=o):
-            turned[...] = jnp.concatenate(
-                [part_of(*block[a, k], t) for k in range(groups)], axis=0
+        for t in range(TILES):
+            turned[o, t] = jnp.concatenate(
+                [rows_of(*block[a, k], t, t + 1) for k in range(groups)], axis=0
             ).T
-            mine = key_row[o, pl.ds(t, 1), :]
-            floor = low_row[o, pl.ds(t, 1), :]
-
-            def one_col(s, acc):
-                theirs = [part_of(key_col, key_at[piece], s) for piece in pieces]
+            mine = key_row[o, t : t + 1, :]
+            floor = low_row[o, t : t + 1, :]
+            acc = jnp.full((8, tile), -1.0, jnp.float32)
+            for at in range(0, len(pieces), groups):
+                some = pieces[at : at + groups]
+                theirs = [rows_of(key_col, key_at[piece], 0, t + 1) for piece in some]
                 theirs = jnp.concatenate(theirs, axis=0)
                 theirs = jnp.concatenate([theirs] * (tile // 128), axis=1)
                 sims = jnp.dot(
-                    jnp.concatenate([part_of(*block[piece], s) for piece in pieces], axis=0),
-                    turned[...],
+                    jnp.concatenate([rows_of(*block[piece], 0, t + 1) for piece in some], axis=0),
+                    turned[o, t],
                     preferred_element_type=jnp.float32,
                 )
                 keep = (theirs >= floor) & (theirs < mine)
                 sims = jnp.where(keep, sims, -1.0)
-                top = jnp.max(sims.reshape(len(pieces) * per_tile // 8, 8, tile), axis=0)
-                return jnp.maximum(acc, top)
-
-            acc = lax.fori_loop(0, t + 1, one_col, jnp.full((8, tile), -1.0, jnp.float32))
-            best[a, pl.ds(t, 1), :] = jnp.maximum(
-                best[a, pl.ds(t, 1), :], jnp.max(acc, axis=0, keepdims=True)
+                top = jnp.max(sims.reshape(sims.shape[0] // 8, 8, tile), axis=0)
+                acc = jnp.maximum(acc, top)
+            best[a, t : t + 1, :] = jnp.maximum(
+                best[a, t : t + 1, :], jnp.max(acc, axis=0, keepdims=True)
             )
-            return 0
-
-        lax.fori_loop(0, TILES, one_tile, 0)
 
     if not has_prev:
         outs[0][...] = best[...]
@@ -286,7 +290,7 @@
             pltpu.VMEM((len(needed) * blk, 128), jnp.float32),
             pltpu.VMEM((len(jobs), 8, tile), jnp.float32),
             pltpu.VMEM((len(jobs), 8, tile), jnp.float32),
-            pltpu.VMEM((width, tile), jnp.bfloat16),
+            pltpu.VMEM((len(jobs), TILES, width, tile), jnp.bfloat16),
             pltpu.VMEM((n_sets, 8, tile), jnp.float32),
         ],
         compiler_params=pltpu.CompilerParams(vmem_limit_bytes=COMPARE_VMEM),
@@ -367,8 +371,16 @@
         return lax.ppermute(value, ("grp", "mem"), [(i, i ^ mask) for i in range(devices)])
 
     offsets, pairs = cover(members)
-    packed = pack(embeddings, cluster, rank, sizes)
-    dest, sends = packed[0], packed[1:]
+    sends = [None] * groups
+    first = tuple(range(1, min(3, groups)))
+    dest, *packed = pack(embeddings, cluster, rank, first, sizes)
+    for k, value in zip(first, packed):
+        sends[k] = value
+    rest = tuple(k for k in range(groups) if k not in first)
+    cluster, dest = lax.optimization_barrier((cluster, dest))
+    _, *packed = pack(embeddings, cluster, rank, rest, sizes)
+    for k, value in zip(rest, packed):
+        sends[k] = value
 
     last = groups - 1
     far = [d for d in offsets if d & side and d != side and d ^ side in offsets]
@@ -400,11 +412,14 @@
         for d in near:
             held[d].append(swap(mine, 0, d))
     for spot in range(1, len(held[0]) - 1):
+        values = lax.optimization_barrier(
+            (held[0][spot + 1], *(held[d][spot] for d in near))
+        )
+        held[0][spot + 1] = values[0]
+        for d, value in zip(near, values[1:]):
+            held[d][spot] = value
         for d in far:
-            piece, held[0][spot + 1] = lax.optimization_barrier(
-                (held[d ^ side][spot], held[0][spot + 1])
-            )
-            held[d].append(swap(piece, 0, side))
+            held[d].append(swap(held[d ^ side][spot], 0, side))
 
     index = {d: i for i, d in enumerate(offsets)}
     starts = sorted({a for a, _ in pairs.values()})

time: 84.8 us -> 82.7 us (0.975)
  Pallas kernels: 22.7 us -> 20.6 us
    pallas_call x2, Pallas kernels: 16.5 us -> 10.7 us  [compare(): pl.pallas_call(functools.partial(compare_kernel, sizes, jobs, names, spot...]
    pallas_call x1 -> x2, Pallas kernels: 5.08 us -> 8.73 us  [pack(): pl.pallas_call(functools.partial(pack_kernel, sizes, ks), out_shape=out_s...]
  transfers between devices with their start and end apart: 15 -> 15, of which waited for: 8 -> 9; matrix products, arithmetic and copies ran while one was open for 0% -> 0% of each run, Pallas kernels for 8% -> 12%
where the time goes in v6:
time: 82.7 us; the launch traced here: 82.4 us
  waiting for transfers between devices  33.8 us (41%)
  Pallas kernels  20.6 us (25%)
  starting transfers between devices  16.9 us (20%)
  blocking collectives  11 us (13%)
    ppermute x15, waiting for transfers between devices, swap(): lax.ppermute(value, ('grp', 'mem'), [(i, i ^ mask) for i in range(devices)])  33.8 us
    ppermute x15, starting transfers between devices, swap(): lax.ppermute(value, ('grp', 'mem'), [(i, i ^ mask) for i in range(devices)])  16.9 us
    all_to_all x1, blocking collectives, on_device(): back = lax.all_to_all(back, 'mem', split_axis=0, concat_axis=0, tiled=True)  11 us
    pallas_call x2, Pallas kernels, compare(): pl.pallas_call(functools.partial(compare_kernel, sizes, jobs, names, spot...  10.7 us
    pallas_call x2, Pallas kernels, pack(): pl.pallas_call(functools.partial(pack_kernel, sizes, ks), out_shape=out_s...  8.73 us
  transfers between devices with their start and end apart: 15, of which 9 were waited for; matrix products, arithmetic and copies ran while one was open for 0% of the time, Pallas kernels for 12%

profile of v6, /device:TPU:0, one launch (start us, length us, event | category | flops | bytes accessed | tf_op | source)
XLA Modules:
  0.0 82.4 jit_solution(15470011960272489347)
XLA Ops:
  0.0 4.4 %shard_map.37 = (s32[1,1024]{1,0:T(1,128)}, bf16[272,768]{1,0:T(8,128)(2,1)}, bf16[272,768]{1,0:T(8,128)(2,1)}) custom-call(bf16[1024,768]{1,0:T(8,128)(2,1)} %emb_hbm.3, s32[1,1024]{1,0:T(1,128)} %bitcast.4, s32[1,1024]{1,0:T(1,128)} %bitcast.6), custom_call_target="tpu_custom_call" | custom-call | flops 805306368 | bytes 3145728 | tf_op jit(solution)/shard_map/pallas_call | solution.py:138
  4.4 3.1 %collective-permute-start = (bf16[272,768]{1,0:T(8,128)(2,1)}, bf16[272,768]{1,0:T(8,128)(2,1)S(1)}, u32[]{:S(2)}, u32[]{:S(2)}) collective-permute-start(bf16[272,768]{1,0:T(8,128)(2,1)} %get-tuple-element.28), channel_id=1, source_target_pairs={{0,2},{1,3},{2,0},{3,1},{4,6},{5,7},{6,4},{7,5},{8,10},{9,11},{10,... | collective-permute-start | bytes 1253384 | tf_op jit(solution)/shard_map/ppermute | solution.py:371
  7.5 2.6 %collective-permute-start.1 = (bf16[272,768]{1,0:T(8,128)(2,1)}, bf16[272,768]{1,0:T(8,128)(2,1)S(1)}, u32[]{:S(2)}, u32[]{:S(2)}) collective-permute-start(bf16[272,768]{1,0:T(8,128)(2,1)} %get-tuple-element.29), channel_id=1, source_target_pairs={{0,4},{1,5},{2,6},{3,7},{4,0},{5,1},{6,2},{7,3},{8,12},{9,13},{10,... | collective-permute-start | bytes 1253384 | tf_op jit(solution)/shard_map/ppermute | solution.py:371
  10.1 4.4 %shard_map.38 = (s32[1,1024]{1,0:T(1,128)}, bf16[272,768]{1,0:T(8,128)(2,1)}, bf16[272,768]{1,0:T(8,128)(2,1)}) custom-call(bf16[1024,768]{1,0:T(8,128)(2,1)} %emb_hbm.3, s32[1,1024]{1,0:T(1,128)} %bitcast.5, s32[1,1024]{1,0:T(1,128)} %bitcast.7), custom_call_target="tpu_custom_call" | custom-call | flops 805306368 | bytes 3145728 | tf_op jit(solution)/shard_map/pallas_call | solution.py:138
  14.4 1.6 %collective-permute-start.4 = (bf16[272,768]{1,0:T(8,128)(2,1)}, bf16[272,768]{1,0:T(8,128)(2,1)S(1)}, u32[]{:S(2)}, u32[]{:S(2)}) collective-permute-start(bf16[272,768]{1,0:T(8,128)(2,1)} %get-tuple-element.27.refs_0_), channel_id=1, source_target_pairs={{0,16},{1,17},{2,18},{3,19},{4,20},{5,21},{6,22},{7,23},{8,24},{9,... | collective-permute-start | bytes 1253384 | tf_op jit(solution)/shard_map/ppermute | solution.py:371
  16.0 1.5 %collective-permute-start.2 = (bf16[272,768]{1,0:T(8,128)(2,1)}, bf16[272,768]{1,0:T(8,128)(2,1)S(1)}, u32[]{:S(2)}, u32[]{:S(2)}) collective-permute-start(bf16[272,768]{1,0:T(8,128)(2,1)} %get-tuple-element.27.refs_0_), channel_id=1, source_target_pairs={{0,1},{1,0},{2,3},{3,2},{4,5},{5,4},{6,7},{7,6},{8,9},{9,8},{10,11... | collective-permute-start | bytes 1253384 | tf_op jit(solution)/shard_map/ppermute | solution.py:371
  17.5 8.6 %collective-permute-done.first_ref = bf16[272,768]{1,0:T(8,128)(2,1)S(1)} collective-permute-done((bf16[272,768]{1,0:T(8,128)(2,1)}, bf16[272,768]{1,0:T(8,128)(2,1)S(1)}, u32[]{:S(2)}, u32[]{:S(2)}) %collective-permute-start) | collective-permute-done | bytes 417824 | tf_op jit(solution)/shard_map/ppermute | solution.py:371
  26.2 2.5 %collective-permute-done.1.second_ref = bf16[272,768]{1,0:T(8,128)(2,1)S(1)} collective-permute-done((bf16[272,768]{1,0:T(8,128)(2,1)}, bf16[272,768]{1,0:T(8,128)(2,1)S(1)}, u32[]{:S(2)}, u32[]{:S(2)}) %collective-permute-start.1) | collective-permute-done | bytes 417824 | tf_op jit(solution)/shard_map/ppermute | solution.py:371
  28.8 1.6 %collective-permute-start.8 = (bf16[544,768]{1,0:T(8,128)(2,1)S(1)}, bf16[544,768]{1,0:T(8,128)(2,1)S(1)}, u32[]{:S(2)}, u32[]{:S(2)}) collective-permute-start(bf16[544,768]{1,0:T(8,128)(2,1)S(1)} %shard_map.39.refs_1_), channel_id=1, source_target_pairs={{0,16},{1,17},{2,18},{3,19},{4,20},{5,21},{6,22},{7,23},{8,24},{9,... | collective-permute-start | bytes 2506760 | tf_op jit(solution)/shard_map/ppermute | solution.py:371
  30.3 1.5 %collective-permute-start.6 = (bf16[544,768]{1,0:T(8,128)(2,1)S(1)}, bf16[544,768]{1,0:T(8,128)(2,1)S(1)}, u32[]{:S(2)}, u32[]{:S(2)}) collective-permute-start(bf16[544,768]{1,0:T(8,128)(2,1)S(1)} %shard_map.39.refs_1_), channel_id=1, source_target_pairs={{0,1},{1,0},{2,3},{3,2},{4,5},{5,4},{6,7},{7,6},{8,9},{9,8},{10,11... | collective-permute-start | bytes 2506760 | tf_op jit(solution)/shard_map/ppermute | solution.py:371
  31.8 2.5 %collective-permute-start.5 = (bf16[272,768]{1,0:T(8,128)(2,1)S(1)}, bf16[272,768]{1,0:T(8,128)(2,1)S(1)}, u32[]{:S(2)}, u32[]{:S(2)}) collective-permute-start(bf16[272,768]{1,0:T(8,128)(2,1)S(1)} %copy-done.2), channel_id=1, source_target_pairs={{0,6},{1,7},{2,4},{3,5},{4,2},{5,3},{6,0},{7,1},{8,14},{9,15},{10,... | collective-permute-start | bytes 1253384 | tf_op jit(solution)/shard_map/ppermute | solution.py:371
  34.3 11.2 %collective-permute-done.5.refs_2_ = bf16[272,768]{1,0:T(8,128)(2,1)S(1)} collective-permute-done((bf16[272,768]{1,0:T(8,128)(2,1)S(1)}, bf16[272,768]{1,0:T(8,128)(2,1)S(1)}, u32[]{:S(2)}, u32[]{:S(2)}) %collective-permute-start.5) | collective-permute-done | bytes 417824 | tf_op jit(solution)/shard_map/ppermute | solution.py:371
  45.5 3.1 %collective-permute-done.8.refs_8_.refs_10_ = bf16[544,768]{1,0:T(8,128)(2,1)S(1)} collective-permute-done((bf16[544,768]{1,0:T(8,128)(2,1)S(1)}, bf16[544,768]{1,0:T(8,128)(2,1)S(1)}, u32[]{:S(2)}, u32[]{:S(2)}) %collective-permute-start.8) | collective-permute-done | bytes 835616 | tf_op jit(solution)/shard_map/ppermute | solution.py:371
  48.6 2.7 %collective-permute-done.6.refs_4_ = bf16[544,768]{1,0:T(8,128)(2,1)S(1)} collective-permute-done((bf16[544,768]{1,0:T(8,128)(2,1)S(1)}, bf16[544,768]{1,0:T(8,128)(2,1)S(1)}, u32[]{:S(2)}, u32[]{:S(2)}) %collective-permute-start.6) | collective-permute-done | bytes 835616 | tf_op jit(solution)/shard_map/ppermute | solution.py:371
  51.3 0.5 collective-permute-start.12
  51.8 0.5 collective-permute-start.11
  52.4 1.5 %collective-permute-start.9 = (bf16[272,768]{1,0:T(8,128)(2,1)S(1)}, bf16[272,768]{1,0:T(8,128)(2,1)S(1)}, u32[]{:S(2)}, u32[]{:S(2)}) collective-permute-start(bf16[272,768]{1,0:T(8,128)(2,1)S(1)} %collective-permute-done.5.refs_2_), channel_id=1, source_target_pairs={{0,1},{1,0},{2,3},{3,2},{4,5},{5,4},{6,7},{7,6},{8,9},{9,8},{10,11... | collective-permute-start | bytes 1253384 | tf_op jit(solution)/shard_map/ppermute | solution.py:371
  54.3 5.5 %shard_map.40.refs_15_ = f32[5,8,256]{2,1,0:T(8,128)S(1)} custom-call(bf16[272,768]{1,0:T(8,128)(2,1)S(1)} %copy-done.1, bf16[544,768]{1,0:T(8,128)(2,1)S(1)} %shard_map.39.refs_1_, bf16[272,768]{1,0:T(8,128)(2,1)S(1)} %collective-permute-done.5.refs_2_, bf16[272,768]{1,0:T(8,128)(2,1)S(1)} %collective-permute-done.2.refs_3_, ...), custom_call_target="tpu_custom_call" | custom-call | flops 4026531840 | bytes 6291456 | tf_op jit(solution)/shard_map/pallas_call | solution.py:284
  59.8 3.5 %collective-permute-done.11.refs_11_ = bf16[272,768]{1,0:T(8,128)(2,1)S(1)} collective-permute-done((bf16[272,768]{1,0:T(8,128)(2,1)S(1)}, bf16[272,768]{1,0:T(8,128)(2,1)S(1)}, u32[]{:S(2)}, u32[]{:S(2)}) %collective-permute-start.11) | collective-permute-done | bytes 417824 | tf_op jit(solution)/shard_map/ppermute | solution.py:371
  63.4 1.0 %collective-permute-done.9.refs_5_ = bf16[272,768]{1,0:T(8,128)(2,1)S(1)} collective-permute-done((bf16[272,768]{1,0:T(8,128)(2,1)S(1)}, bf16[272,768]{1,0:T(8,128)(2,1)S(1)}, u32[]{:S(2)}, u32[]{:S(2)}) %collective-permute-start.9) | collective-permute-done | bytes 417824 | tf_op jit(solution)/shard_map/ppermute | solution.py:371
  64.4 0.7 collective-permute-done.14.refs_14_
  65.1 5.2 %shard_map.41 = f32[8,1,256]{2,1,0:T(1,128)S(1)} custom-call(bf16[272,768]{1,0:T(8,128)(2,1)S(1)} %copy-done.1, bf16[544,768]{1,0:T(8,128)(2,1)S(1)} %shard_map.39.refs_1_, bf16[272,768]{1,0:T(8,128)(2,1)S(1)} %collective-permute-done.5.refs_2_, bf16[272,768]{1,0:T(8,128)(2,1)S(1)} %collective-permute-done.2.refs_3_, ...), custom_call_target="tpu_custom_call" | custom-call | flops 4026531840 | bytes 7864320 | tf_op jit(solution)/shard_map/pallas_call | solution.py:284
  70.3 11.0 %all_to_all.5.back_ref = f32[8,1,256]{2,1,0:T(1,128)S(1)} all-to-all(f32[8,1,256]{2,1,0:T(1,128)S(1)} %shard_map.41), channel_id=1, replica_groups=mesh['grp'=4,'mem'=8] {'mem'}, dimensions={0} | all-to-all | bytes 16384 | tf_op jit(solution)/shard_map/all_to_all | solution.py:464
  81.3 1.1 %shard_map.42 = f32[1,1024]{1,0:T(1,128)} custom-call(s32[1,1024]{1,0:T(1,128)S(1)} %copy-done, f32[8,1,256]{2,1,0:T(1,128)S(1)} %all_to_all.5.back_ref), custom_call_target="tpu_custom_call" | custom-call | tf_op jit(solution)/shard_map/pallas_call | solution.py:346
  (19 shorter events, 0.5 us)
Async XLA Ops:
  4.4 21.8 %collective-permute-start = (bf16[272,768]{1,0:T(8,128)(2,1)}, bf16[272,768]{1,0:T(8,128)(2,1)S(1)}, u32[]{:S(2)}, u32[]{:S(2)}) collective-permute-start(bf16[272,768]{1,0:T(8,128)(2,1)} %get-tuple-element.28), channel_id=1, source_target_pairs={{0,2},{1,3},{2,0},{3,1},{4,6},{5,7},{6,4},{7,5},{8,10},{9,11},{10,... | collective-permute-start | bytes 1253384 | tf_op jit(solution)/shard_map/ppermute | solution.py:371
  7.5 21.2 %collective-permute-start.1 = (bf16[272,768]{1,0:T(8,128)(2,1)}, bf16[272,768]{1,0:T(8,128)(2,1)S(1)}, u32[]{:S(2)}, u32[]{:S(2)}) collective-permute-start(bf16[272,768]{1,0:T(8,128)(2,1)} %get-tuple-element.29), channel_id=1, source_target_pairs={{0,4},{1,5},{2,6},{3,7},{4,0},{5,1},{6,2},{7,3},{8,12},{9,13},{10,... | collective-permute-start | bytes 1253384 | tf_op jit(solution)/shard_map/ppermute | solution.py:371
  14.4 17.4 %copy-start.2 = (bf16[272,768]{1,0:T(8,128)(2,1)S(1)}, bf16[272,768]{1,0:T(8,128)(2,1)}, u32[]{:S(2)}) copy-start(bf16[272,768]{1,0:T(8,128)(2,1)} %get-tuple-element.33) | copy-start | bytes 1253380
  14.4 39.8 %copy-start.1 = (bf16[272,768]{1,0:T(8,128)(2,1)S(1)}, bf16[272,768]{1,0:T(8,128)(2,1)}, u32[]{:S(2)}) copy-start(bf16[272,768]{1,0:T(8,128)(2,1)} %get-tuple-element.27.refs_0_) | copy-start | bytes 1253380
  14.4 14.2 %collective-permute-start.4 = (bf16[272,768]{1,0:T(8,128)(2,1)}, bf16[272,768]{1,0:T(8,128)(2,1)S(1)}, u32[]{:S(2)}, u32[]{:S(2)}) collective-permute-start(bf16[272,768]{1,0:T(8,128)(2,1)} %get-tuple-element.27.refs_0_), channel_id=1, source_target_pairs={{0,16},{1,17},{2,18},{3,19},{4,20},{5,21},{6,22},{7,23},{8,24},{9,... | collective-permute-start | bytes 1253384 | tf_op jit(solution)/shard_map/ppermute | solution.py:371
  16.0 12.7 %collective-permute-start.3 = (bf16[272,768]{1,0:T(8,128)(2,1)}, bf16[272,768]{1,0:T(8,128)(2,1)S(1)}, u32[]{:S(2)}, u32[]{:S(2)}) collective-permute-start(bf16[272,768]{1,0:T(8,128)(2,1)} %get-tuple-element.27.refs_0_), channel_id=1, source_target_pairs={{0,8},{1,9},{2,10},{3,11},{4,12},{5,13},{6,14},{7,15},{8,0},{9,1},... | collective-permute-start | bytes 1253384 | tf_op jit(solution)/shard_map/ppermute | solution.py:371
  16.0 12.7 %collective-permute-start.2 = (bf16[272,768]{1,0:T(8,128)(2,1)}, bf16[272,768]{1,0:T(8,128)(2,1)S(1)}, u32[]{:S(2)}, u32[]{:S(2)}) collective-permute-start(bf16[272,768]{1,0:T(8,128)(2,1)} %get-tuple-element.27.refs_0_), channel_id=1, source_target_pairs={{0,1},{1,0},{2,3},{3,2},{4,5},{5,4},{6,7},{7,6},{8,9},{9,8},{10,11... | collective-permute-start | bytes 1253384 | tf_op jit(solution)/shard_map/ppermute | solution.py:371
  28.8 19.9 %collective-permute-start.8 = (bf16[544,768]{1,0:T(8,128)(2,1)S(1)}, bf16[544,768]{1,0:T(8,128)(2,1)S(1)}, u32[]{:S(2)}, u32[]{:S(2)}) collective-permute-start(bf16[544,768]{1,0:T(8,128)(2,1)S(1)} %shard_map.39.refs_1_), channel_id=1, source_target_pairs={{0,16},{1,17},{2,18},{3,19},{4,20},{5,21},{6,22},{7,23},{8,24},{9,... | collective-permute-start | bytes 2506760 | tf_op jit(solution)/shard_map/ppermute | solution.py:371
  30.3 18.3 %collective-permute-start.7 = (bf16[544,768]{1,0:T(8,128)(2,1)S(1)}, bf16[544,768]{1,0:T(8,128)(2,1)S(1)}, u32[]{:S(2)}, u32[]{:S(2)}) collective-permute-start(bf16[544,768]{1,0:T(8,128)(2,1)S(1)} %shard_map.39.refs_1_), channel_id=1, source_target_pairs={{0,8},{1,9},{2,10},{3,11},{4,12},{5,13},{6,14},{7,15},{8,0},{9,1},... | collective-permute-start | bytes 2506760 | tf_op jit(solution)/shard_map/ppermute | solution.py:371
  30.3 21.0 %collective-permute-start.6 = (bf16[544,768]{1,0:T(8,128)(2,1)S(1)}, bf16[544,768]{1,0:T(8,128)(2,1)S(1)}, u32[]{:S(2)}, u32[]{:S(2)}) collective-permute-start(bf16[544,768]{1,0:T(8,128)(2,1)S(1)} %shard_map.39.refs_1_), channel_id=1, source_target_pairs={{0,1},{1,0},{2,3},{3,2},{4,5},{5,4},{6,7},{7,6},{8,9},{9,8},{10,11... | collective-permute-start | bytes 2506760 | tf_op jit(solution)/shard_map/ppermute | solution.py:371
  31.8 13.7 %collective-permute-start.5 = (bf16[272,768]{1,0:T(8,128)(2,1)S(1)}, bf16[272,768]{1,0:T(8,128)(2,1)S(1)}, u32[]{:S(2)}, u32[]{:S(2)}) collective-permute-start(bf16[272,768]{1,0:T(8,128)(2,1)S(1)} %copy-done.2), channel_id=1, source_target_pairs={{0,6},{1,7},{2,4},{3,5},{4,2},{5,3},{6,0},{7,1},{8,14},{9,15},{10,... | collective-permute-start | bytes 1253384 | tf_op jit(solution)/shard_map/ppermute | solution.py:371
  51.3 3.0 %collective-permute-start.13 = (bf16[544,768]{1,0:T(8,128)(2,1)S(1)}, bf16[544,768]{1,0:T(8,128)(2,1)S(1)}, u32[]{:S(2)}, u32[]{:S(2)}) collective-permute-start(bf16[544,768]{1,0:T(8,128)(2,1)S(1)} %collective-permute-done.8.refs_8_.refs_10_), channel_id=1, source_target_pairs={{0,8},{1,9},{2,10},{3,11},{4,12},{5,13},{6,14},{7,15},{8,0},{9,1},... | collective-permute-start | bytes 2506760 | tf_op jit(solution)/shard_map/ppermute | solution.py:371
  51.3 3.0 %collective-permute-start.12 = (bf16[272,768]{1,0:T(8,128)(2,1)S(1)}, bf16[272,768]{1,0:T(8,128)(2,1)S(1)}, u32[]{:S(2)}, u32[]{:S(2)}) collective-permute-start(bf16[272,768]{1,0:T(8,128)(2,1)S(1)} %collective-permute-done.4.refs_7_.refs_9_), channel_id=1, source_target_pairs={{0,8},{1,9},{2,10},{3,11},{4,12},{5,13},{6,14},{7,15},{8,0},{9,1},... | collective-permute-start | bytes 1253384 | tf_op jit(solution)/shard_map/ppermute | solution.py:371
  51.8 11.6 %collective-permute-start.11 = (bf16[272,768]{1,0:T(8,128)(2,1)S(1)}, bf16[272,768]{1,0:T(8,128)(2,1)S(1)}, u32[]{:S(2)}, u32[]{:S(2)}) collective-permute-start(bf16[272,768]{1,0:T(8,128)(2,1)S(1)} %collective-permute-done.5.refs_2_), channel_id=1, source_target_pairs={{0,16},{1,17},{2,18},{3,19},{4,20},{5,21},{6,22},{7,23},{8,24},{9,... | collective-permute-start | bytes 1253384 | tf_op jit(solution)/shard_map/ppermute | solution.py:371
  52.4 11.0 %collective-permute-start.10 = (bf16[272,768]{1,0:T(8,128)(2,1)S(1)}, bf16[272,768]{1,0:T(8,128)(2,1)S(1)}, u32[]{:S(2)}, u32[]{:S(2)}) collective-permute-start(bf16[272,768]{1,0:T(8,128)(2,1)S(1)} %collective-permute-done.5.refs_2_), channel_id=1, source_target_pairs={{0,8},{1,9},{2,10},{3,11},{4,12},{5,13},{6,14},{7,15},{8,0},{9,1},... | collective-permute-start | bytes 1253384 | tf_op jit(solution)/shard_map/ppermute | solution.py:371
  52.4 12.1 %collective-permute-start.9 = (bf16[272,768]{1,0:T(8,128)(2,1)S(1)}, bf16[272,768]{1,0:T(8,128)(2,1)S(1)}, u32[]{:S(2)}, u32[]{:S(2)}) collective-permute-start(bf16[272,768]{1,0:T(8,128)(2,1)S(1)} %collective-permute-done.5.refs_2_), channel_id=1, source_target_pairs={{0,1},{1,0},{2,3},{3,2},{4,5},{5,4},{6,7},{7,6},{8,9},{9,8},{10,11... | collective-permute-start | bytes 1253384 | tf_op jit(solution)/shard_map/ppermute | solution.py:371
  59.8 21.5 %copy-start = (s32[1,1024]{1,0:T(1,128)S(1)}, s32[1,1024]{1,0:T(1,128)}, u32[]{:S(2)}) copy-start(s32[1,1024]{1,0:T(1,128)} %get-tuple-element.25.dest_ref) | copy-start | bytes 12292
  63.4 1.8 %collective-permute-start.14 = (bf16[272,768]{1,0:T(8,128)(2,1)S(1)}, bf16[272,768]{1,0:T(8,128)(2,1)S(1)}, u32[]{:S(2)}, u32[]{:S(2)}) collective-permute-start(bf16[272,768]{1,0:T(8,128)(2,1)S(1)} %collective-permute-done.11.refs_11_), channel_id=1, source_target_pairs={{0,8},{1,9},{2,10},{3,11},{4,12},{5,13},{6,14},{7,15},{8,0},{9,1},... | collective-permute-start | bytes 1253384 | tf_op jit(solution)/shard_map/ppermute | solution.py:371

commit v7 on v6

--- a/solution.py
+++ b/solution.py
@@ -11,6 +11,7 @@
 TILES = 4
 LABEL_ROWS = 16
 FAR = 1.0e9
+JOIN_FLOPS = 10_000_000_000
 PACK_VMEM = 60 * 1024 * 1024
 COMPARE_VMEM = 24 * 1024 * 1024
 NT = (((1,), (1,)), ((), ()))
@@ -300,22 +301,26 @@
     )(*operands)
 
 
-def join_kernel(first_ref, second_ref, out_ref):
-    rows = first_ref.shape[0]
-    out_ref[:rows, :] = first_ref[...]
-    out_ref[rows:, :] = second_ref[...]
-
-
-def join(first, second):
-    rows, width = first.shape
+def join_kernel(*refs):
+    out_ref, at = refs[-1], 0
+    for ref in refs[:-1]:
+        out_ref[at : at + ref.shape[0], :] = ref[...]
+        at += ref.shape[0]
+
+
+def join(pieces):
+    if len(pieces) == 1:
+        return pieces[0]
+    rows = sum(piece.shape[0] for piece in pieces)
     vmem = pl.BlockSpec(memory_space=pltpu.VMEM)
     return pl.pallas_call(
         join_kernel,
-        out_shape=jax.ShapeDtypeStruct((2 * rows, width), first.dtype),
-        in_specs=[vmem, vmem],
+        out_shape=jax.ShapeDtypeStruct((rows, pieces[0].shape[1]), pieces[0].dtype),
+        in_specs=[vmem] * len(pieces),
         out_specs=vmem,
         compiler_params=pltpu.CompilerParams(vmem_limit_bytes=COMPARE_VMEM),
-    )(first, second)
+        cost_estimate=pl.CostEstimate(flops=JOIN_FLOPS, bytes_accessed=0, transcendentals=0),
+    )(*pieces)
 
 
 def unpack_kernel(sizes, dest_ref, back_ref, out_ref):
@@ -372,77 +377,67 @@
 
     offsets, pairs = cover(members)
     sends = [None] * groups
-    first = tuple(range(1, min(3, groups)))
+    first = (1,)
     dest, *packed = pack(embeddings, cluster, rank, first, sizes)
     for k, value in zip(first, packed):
         sends[k] = value
-    rest = tuple(k for k in range(groups) if k not in first)
+    rest = (2, 0, *range(3, groups))
     cluster, dest = lax.optimization_barrier((cluster, dest))
     _, *packed = pack(embeddings, cluster, rank, rest, sizes)
     for k, value in zip(rest, packed):
         sends[k] = value
 
     last = groups - 1
-    far = [d for d in offsets if d & side and d != side and d ^ side in offsets]
-    near = [d for d in offsets[1:] if d not in far]
-    lead = far[0] ^ side if far else near[0]
-    held = {0: [sends[0]]}
-    for d in near:
-        held[d] = [swap(sends[0], 0, d)]
-    for d in far:
-        held[d] = [swap(held[d ^ side][0], 0, side)]
-    after = held[lead][0]
-    for k in range(1, groups, 2):
-        if k > 1:
-            send, after = lax.optimization_barrier((sends[k], after))
-        else:
-            send = sends[k]
-        mine = swap(send, k, 0)
-        if k < last:
-            also = swap(sends[k + 1], k + 1, 0)
+    across = {0: side}
+    across.update({d: d ^ side for d in offsets if d & side == 0 and d and d ^ side in offsets})
+    near = [d for d in offsets[1:] if d not in across.values()]
+
+    held = {d: [] for d in [0, *near]}
+    for k in range(groups):
+        send = sends[k]
+        if k > 2:
+            send, held[0][k - 2] = lax.optimization_barrier((send, held[0][k - 2]))
+        held[0].append(swap(send, k, 0))
+    for k in range(groups):
+        for d in near:
+            piece = held[0][k]
             if k == 1:
-                mine, also, *firsts = lax.optimization_barrier(
-                    (mine, also, *(held[d][0] for d in near))
-                )
-                for d, first in zip(near, firsts):
-                    held[d] = [first]
-            mine = join(mine, also)
-            after = mine
-        held[0].append(mine)
-        for d in near:
-            held[d].append(swap(mine, 0, d))
-    for spot in range(1, len(held[0]) - 1):
-        values = lax.optimization_barrier(
-            (held[0][spot + 1], *(held[d][spot] for d in near))
-        )
-        held[0][spot + 1] = values[0]
-        for d, value in zip(near, values[1:]):
-            held[d][spot] = value
-        for d in far:
-            held[d].append(swap(held[d ^ side][spot], 0, side))
-
+                piece, held[d][0] = lax.optimization_barrier((piece, held[d][0]))
+            elif k == 2:
+                piece, *values = lax.optimization_barrier((piece, *(held[e][1] for e in near)))
+                for e, value in zip(near, values):
+                    held[e][1] = value
+            held[d].append(swap(piece, 0, d))
     index = {d: i for i, d in enumerate(offsets)}
+    blocks = {(index[d], k): (piece, 0) for d in held for k, piece in enumerate(held[d])}
+
+    def cross(wanted, after):
+        pieces = [held[d][k] for d, k in wanted]
+        pieces[0], *after = lax.optimization_barrier((pieces[0], *after))
+        moved = swap(join(pieces), 0, side)
+        for at, (d, k) in enumerate(wanted):
+            blocks[index[across[d]], k] = (moved, at)
+        return after
+
+    for d in across:
+        cross([(d, k) for k in range(last - 1)], [])
     starts = sorted({a for a, _ in pairs.values()})
     early, late = [], []
     for a in starts:
         cols = [index[b] for _, (e, b) in sorted(pairs.items()) if e == a]
         pieces = [(b, k) for b in cols for k in range(groups)]
         if a == 0:
-            soon = [(b, k) for b, k in pieces if b == 0 or k < last]
-            early.append((0, soon))
-            pieces = [piece for piece in pieces if piece not in soon]
+            ready = {(0, last)} | {(index[d], k) for d in held for k in range(last)}
+            ready |= {(index[d], k) for d in across.values() for k in range(last - 1)}
+            early.append((0, [piece for piece in pieces if piece in ready]))
+            pieces = [piece for piece in pieces if piece not in ready]
         late.append((index[a], pieces))
     joined = side if all(a < side for a in starts) else 0
-    blocks = {}
-    for d in offsets:
-        for k in range(groups):
-            spot = (k + 1) // 2
-            if spot < len(held[d]):
-                blocks[index[d], k] = (held[d][spot], 1 - k % 2 if 0 < k < last else 0)
     prev = compare(blocks, early, None, 0, len(offsets), sizes)[0]
-    for d in far:
-        piece, prev = lax.optimization_barrier((held[d ^ side][-1], prev))
-        blocks[index[d], last] = (swap(piece, 0, side), 0)
+    for d, k in [(0, last - 1), (0, last)] + [
+        (d, k) for k in (last - 1, last) for d in across if d
+    ]:
+        (prev,) = cross([(d, k)], [prev])
     found = compare(blocks, late, prev, joined, len(offsets), sizes)
     if joined:
         back = found[0]

time: 82.7 us -> 88.6 us (1.071)
  blocking collectives: 11 us -> 17.3 us
  waiting for transfers between devices: 33.8 us -> 32.2 us
  local copies, waits for them, and re-layouts: 0.01 us -> 1.02 us
  starting transfers between devices: 16.9 us -> 17.8 us
    all_to_all x1, blocking collectives: 11 us -> 17.3 us  [on_device(): back = lax.all_to_all(back, 'mem', split_axis=0, concat_axis=0, tiled=True)]
    ppermute x15 -> x17, waiting for transfers between devices: 33.8 us -> 32.2 us  [swap(): lax.ppermute(value, ('grp', 'mem'), [(i, i ^ mask) for i in range(devices)])]
    unnamed x6 -> x8, local copies, waits for them, and re-layouts: 0.01 us -> 1.02 us
    ppermute x15 -> x17, starting transfers between devices: 16.9 us -> 17.8 us  [swap(): lax.ppermute(value, ('grp', 'mem'), [(i, i ^ mask) for i in range(devices)])]
  transfers between devices with their start and end apart: 15 -> 17, of which waited for: 9 -> 8; matrix products, arithmetic and copies ran while one was open for 0% -> 0% of each run, Pallas kernels for 12% -> 11%
where the time goes in v7:
time: 88.6 us; the launch traced here: 88.4 us
  waiting for transfers between devices  32.2 us (36%)
  Pallas kernels  20 us (23%)
  starting transfers between devices  17.8 us (20%)
  blocking collectives  17.3 us (20%)
  local copies, waits for them, and re-layouts  1.02 us (1%)
    ppermute x17, waiting for transfers between devices, swap(): lax.ppermute(value, ('grp', 'mem'), [(i, i ^ mask) for i in range(devices)])  32.2 us
    ppermute x17, starting transfers between devices, swap(): lax.ppermute(value, ('grp', 'mem'), [(i, i ^ mask) for i in range(devices)])  17.8 us
    all_to_all x1, blocking collectives, on_device(): back = lax.all_to_all(back, 'mem', split_axis=0, concat_axis=0, tiled=True)  17.3 us
    pallas_call x2, Pallas kernels, compare(): pl.pallas_call(functools.partial(compare_kernel, sizes, jobs, names, spot...  10.1 us
    pallas_call x2, Pallas kernels, pack(): pl.pallas_call(functools.partial(pack_kernel, sizes, ks), out_shape=out_s...  8.73 us
  transfers between devices with their start and end apart: 17, of which 8 were waited for; matrix products, arithmetic and copies ran while one was open for 0% of the time, Pallas kernels for 11%

profile of v7, /device:TPU:0, one launch (start us, length us, event | category | flops | bytes accessed | tf_op | source)
XLA Modules:
  0.0 88.4 jit_solution(5780848312597357876)
XLA Ops:
  0.0 3.7 %shard_map.37 = (s32[1,1024]{1,0:T(1,128)}, bf16[272,768]{1,0:T(8,128)(2,1)}) custom-call(bf16[1024,768]{1,0:T(8,128)(2,1)} %emb_hbm.3, s32[1,1024]{1,0:T(1,128)} %bitcast.4, s32[1,1024]{1,0:T(1,128)} %bitcast.6), custom_call_target="tpu_custom_call" | custom-call | flops 402653184 | bytes 3145728 | tf_op jit(solution)/shard_map/pallas_call | solution.py:139
  3.7 3.1 %collective-permute-start = (bf16[272,768]{1,0:T(8,128)(2,1)}, bf16[272,768]{1,0:T(8,128)(2,1)S(1)}, u32[]{:S(2)}, u32[]{:S(2)}) collective-permute-start(bf16[272,768]{1,0:T(8,128)(2,1)} %get-tuple-element.37), channel_id=1, source_target_pairs={{0,2},{1,3},{2,0},{3,1},{4,6},{5,7},{6,4},{7,5},{8,10},{9,11},{10,... | collective-permute-start | bytes 1253384 | tf_op jit(solution)/shard_map/ppermute | solution.py:376
  6.8 5.0 %shard_map.38 = (s32[1,1024]{1,0:T(1,128)}, bf16[272,768]{1,0:T(8,128)(2,1)}, bf16[272,768]{1,0:T(8,128)(2,1)}, bf16[272,768]{1,0:T(8,128)(2,1)}) custom-call(bf16[1024,768]{1,0:T(8,128)(2,1)} %emb_hbm.3, s32[1,1024]{1,0:T(1,128)} %bitcast.5, s32[1,1024]{1,0:T(1,128)} %bitcast.7), custom_call_target="tpu_custom_call" | custom-call | flops 1207959552 | bytes 3145728 | tf_op jit(solution)/shard_map/pallas_call | solution.py:139
  11.8 1.6 %collective-permute-start.5 = (bf16[272,768]{1,0:T(8,128)(2,1)}, bf16[272,768]{1,0:T(8,128)(2,1)S(1)}, u32[]{:S(2)}, u32[]{:S(2)}) collective-permute-start(bf16[272,768]{1,0:T(8,128)(2,1)} %get-tuple-element.35.refs_0_), channel_id=1, source_target_pairs={{0,16},{1,17},{2,18},{3,19},{4,20},{5,21},{6,22},{7,23},{8,24},{9,... | collective-permute-start | bytes 1253384 | tf_op jit(solution)/shard_map/ppermute | solution.py:376
  13.4 1.5 %collective-permute-start.3 = (bf16[272,768]{1,0:T(8,128)(2,1)}, bf16[272,768]{1,0:T(8,128)(2,1)S(1)}, u32[]{:S(2)}, u32[]{:S(2)}) collective-permute-start(bf16[272,768]{1,0:T(8,128)(2,1)} %get-tuple-element.35.refs_0_), channel_id=1, source_target_pairs={{0,1},{1,0},{2,3},{3,2},{4,5},{5,4},{6,7},{7,6},{8,9},{9,8},{10,11... | collective-permute-start | bytes 1253384 | tf_op jit(solution)/shard_map/ppermute | solution.py:376
  14.9 2.6 %collective-permute-start.1 = (bf16[272,768]{1,0:T(8,128)(2,1)}, bf16[272,768]{1,0:T(8,128)(2,1)S(1)}, u32[]{:S(2)}, u32[]{:S(2)}) collective-permute-start(bf16[272,768]{1,0:T(8,128)(2,1)} %get-tuple-element.39), channel_id=1, source_target_pairs={{0,4},{1,5},{2,6},{3,7},{4,0},{5,1},{6,2},{7,3},{8,12},{9,13},{10,... | collective-permute-start | bytes 1253384 | tf_op jit(solution)/shard_map/ppermute | solution.py:376
  17.5 5.7 %collective-permute-done.5.refs_0_.refs_8_.refs_11_ = bf16[272,768]{1,0:T(8,128)(2,1)S(1)} collective-permute-done((bf16[272,768]{1,0:T(8,128)(2,1)}, bf16[272,768]{1,0:T(8,128)(2,1)S(1)}, u32[]{:S(2)}, u32[]{:S(2)}) %collective-permute-start.5) | collective-permute-done | bytes 417824 | tf_op jit(solution)/shard_map/ppermute | solution.py:376
  23.2 1.5 %collective-permute-start.6 = (bf16[272,768]{1,0:T(8,128)(2,1)S(1)}, bf16[272,768]{1,0:T(8,128)(2,1)S(1)}, u32[]{:S(2)}, u32[]{:S(2)}) collective-permute-start(bf16[272,768]{1,0:T(8,128)(2,1)S(1)} %collective-permute-done.refs_1_), channel_id=1, source_target_pairs={{0,16},{1,17},{2,18},{3,19},{4,20},{5,21},{6,22},{7,23},{8,24},{9,... | collective-permute-start | bytes 1253384 | tf_op jit(solution)/shard_map/ppermute | solution.py:376
  24.7 1.5 %collective-permute-start.4 = (bf16[272,768]{1,0:T(8,128)(2,1)S(1)}, bf16[272,768]{1,0:T(8,128)(2,1)S(1)}, u32[]{:S(2)}, u32[]{:S(2)}) collective-permute-start(bf16[272,768]{1,0:T(8,128)(2,1)S(1)} %collective-permute-done.refs_1_), channel_id=1, source_target_pairs={{0,1},{1,0},{2,3},{3,2},{4,5},{5,4},{6,7},{7,6},{8,9},{9,8},{10,11... | collective-permute-start | bytes 1253384 | tf_op jit(solution)/shard_map/ppermute | solution.py:376
  26.2 1.0 %copy-done.1 = bf16[272,768]{1,0:T(8,128)(2,1)S(1)} copy-done((bf16[272,768]{1,0:T(8,128)(2,1)S(1)}, bf16[272,768]{1,0:T(8,128)(2,1)}, u32[]{:S(2)}) %copy-start.1) | copy-done | bytes 417816
  27.4 8.1 %collective-permute-done.1.refs_2_ = bf16[272,768]{1,0:T(8,128)(2,1)S(1)} collective-permute-done((bf16[272,768]{1,0:T(8,128)(2,1)}, bf16[272,768]{1,0:T(8,128)(2,1)S(1)}, u32[]{:S(2)}, u32[]{:S(2)}) %collective-permute-start.1) | collective-permute-done | bytes 417824 | tf_op jit(solution)/shard_map/ppermute | solution.py:376
  35.7 2.6 %collective-permute-start.2 = (bf16[272,768]{1,0:T(8,128)(2,1)S(1)}, bf16[272,768]{1,0:T(8,128)(2,1)S(1)}, u32[]{:S(2)}, u32[]{:S(2)}) collective-permute-start(bf16[272,768]{1,0:T(8,128)(2,1)S(1)} %copy-done.3), channel_id=1, source_target_pairs={{0,6},{1,7},{2,4},{3,5},{4,2},{5,3},{6,0},{7,1},{8,14},{9,15},{10,... | collective-permute-start | bytes 1253384 | tf_op jit(solution)/shard_map/ppermute | solution.py:376
  38.8 0.6 collective-permute-start.7
  39.4 10.3 %collective-permute-done.2.refs_3_ = bf16[272,768]{1,0:T(8,128)(2,1)S(1)} collective-permute-done((bf16[272,768]{1,0:T(8,128)(2,1)S(1)}, bf16[272,768]{1,0:T(8,128)(2,1)S(1)}, u32[]{:S(2)}, u32[]{:S(2)}) %collective-permute-start.2) | collective-permute-done | bytes 417824 | tf_op jit(solution)/shard_map/ppermute | solution.py:376
  49.6 0.6 collective-permute-start.14
  50.8 4.4 %shard_map.41.refs_18_ = f32[5,8,256]{2,1,0:T(8,128)S(1)} custom-call(bf16[272,768]{1,0:T(8,128)(2,1)S(1)} %copy-done.2, bf16[272,768]{1,0:T(8,128)(2,1)S(1)} %collective-permute-done.refs_1_, bf16[272,768]{1,0:T(8,128)(2,1)S(1)} %collective-permute-done.1.refs_2_, bf16[272,768]{1,0:T(8,128)(2,1)S(1)} %collective-permute-done.2.refs_3_, ...), custom_call_target="tpu_custom_call" | custom-call | flops 3523215360 | bytes 5505024 | tf_op jit(solution)/shard_map/pallas_call | solution.py:285
  55.2 5.5 %collective-permute-done.14.refs_14_ = bf16[272,768]{1,0:T(8,128)(2,1)S(1)} collective-permute-done((bf16[272,768]{1,0:T(8,128)(2,1)S(1)}, bf16[272,768]{1,0:T(8,128)(2,1)S(1)}, u32[]{:S(2)}, u32[]{:S(2)}) %collective-permute-start.14) | collective-permute-done | bytes 417824 | tf_op jit(solution)/shard_map/ppermute | solution.py:376
  61.8 0.7 collective-permute-done.16.refs_17_
  62.5 0.6 collective-permute-done.15.refs_16_
  63.1 0.6 collective-permute-done.13.refs_10_
  63.7 0.6 collective-permute-done.12.refs_9_
  64.3 5.7 %shard_map.42 = f32[8,1,256]{2,1,0:T(1,128)S(1)} custom-call(bf16[272,768]{1,0:T(8,128)(2,1)S(1)} %copy-done.2, bf16[272,768]{1,0:T(8,128)(2,1)S(1)} %collective-permute-done.refs_1_, bf16[272,768]{1,0:T(8,128)(2,1)S(1)} %collective-permute-done.1.refs_2_, bf16[272,768]{1,0:T(8,128)(2,1)S(1)} %collective-permute-done.2.refs_3_, ...), custom_call_target="tpu_custom_call" | custom-call | flops 4529848320 | bytes 7864320 | tf_op jit(solution)/shard_map/pallas_call | solution.py:285
  70.0 17.3 %all_to_all.5.back_ref = f32[8,1,256]{2,1,0:T(1,128)S(1)} all-to-all(f32[8,1,256]{2,1,0:T(1,128)S(1)} %shard_map.42), channel_id=1, replica_groups=mesh['grp'=4,'mem'=8] {'mem'}, dimensions={0} | all-to-all | bytes 16384 | tf_op jit(solution)/shard_map/all_to_all | solution.py:459
  87.3 1.1 %shard_map.43 = f32[1,1024]{1,0:T(1,128)} custom-call(s32[1,1024]{1,0:T(1,128)S(1)} %copy-done, f32[8,1,256]{2,1,0:T(1,128)S(1)} %all_to_all.5.back_ref), custom_call_target="tpu_custom_call" | custom-call | tf_op jit(solution)/shard_map/pallas_call | solution.py:351
  (26 shorter events, 2.4 us)
Async XLA Ops:
  3.7 13.8 %collective-permute-start = (bf16[272,768]{1,0:T(8,128)(2,1)}, bf16[272,768]{1,0:T(8,128)(2,1)S(1)}, u32[]{:S(2)}, u32[]{:S(2)}) collective-permute-start(bf16[272,768]{1,0:T(8,128)(2,1)} %get-tuple-element.37), channel_id=1, source_target_pairs={{0,2},{1,3},{2,0},{3,1},{4,6},{5,7},{6,4},{7,5},{8,10},{9,11},{10,... | collective-permute-start | bytes 1253384 | tf_op jit(solution)/shard_map/ppermute | solution.py:376
  11.8 11.4 %collective-permute-start.5 = (bf16[272,768]{1,0:T(8,128)(2,1)}, bf16[272,768]{1,0:T(8,128)(2,1)S(1)}, u32[]{:S(2)}, u32[]{:S(2)}) collective-permute-start(bf16[272,768]{1,0:T(8,128)(2,1)} %get-tuple-element.35.refs_0_), channel_id=1, source_target_pairs={{0,16},{1,17},{2,18},{3,19},{4,20},{5,21},{6,22},{7,23},{8,24},{9,... | collective-permute-start | bytes 1253384 | tf_op jit(solution)/shard_map/ppermute | solution.py:376
  13.4 11.3 %collective-permute-start.3 = (bf16[272,768]{1,0:T(8,128)(2,1)}, bf16[272,768]{1,0:T(8,128)(2,1)S(1)}, u32[]{:S(2)}, u32[]{:S(2)}) collective-permute-start(bf16[272,768]{1,0:T(8,128)(2,1)} %get-tuple-element.35.refs_0_), channel_id=1, source_target_pairs={{0,1},{1,0},{2,3},{3,2},{4,5},{5,4},{6,7},{7,6},{8,9},{9,8},{10,11... | collective-permute-start | bytes 1253384 | tf_op jit(solution)/shard_map/ppermute | solution.py:376
  14.9 20.6 %collective-permute-start.1 = (bf16[272,768]{1,0:T(8,128)(2,1)}, bf16[272,768]{1,0:T(8,128)(2,1)S(1)}, u32[]{:S(2)}, u32[]{:S(2)}) collective-permute-start(bf16[272,768]{1,0:T(8,128)(2,1)} %get-tuple-element.39), channel_id=1, source_target_pairs={{0,4},{1,5},{2,6},{3,7},{4,0},{5,1},{6,2},{7,3},{8,12},{9,13},{10,... | collective-permute-start | bytes 1253384 | tf_op jit(solution)/shard_map/ppermute | solution.py:376
  23.2 12.3 %collective-permute-start.6 = (bf16[272,768]{1,0:T(8,128)(2,1)S(1)}, bf16[272,768]{1,0:T(8,128)(2,1)S(1)}, u32[]{:S(2)}, u32[]{:S(2)}) collective-permute-start(bf16[272,768]{1,0:T(8,128)(2,1)S(1)} %collective-permute-done.refs_1_), channel_id=1, source_target_pairs={{0,16},{1,17},{2,18},{3,19},{4,20},{5,21},{6,22},{7,23},{8,24},{9,... | collective-permute-start | bytes 1253384 | tf_op jit(solution)/shard_map/ppermute | solution.py:376
  24.7 10.8 %collective-permute-start.4 = (bf16[272,768]{1,0:T(8,128)(2,1)S(1)}, bf16[272,768]{1,0:T(8,128)(2,1)S(1)}, u32[]{:S(2)}, u32[]{:S(2)}) collective-permute-start(bf16[272,768]{1,0:T(8,128)(2,1)S(1)} %collective-permute-done.refs_1_), channel_id=1, source_target_pairs={{0,1},{1,0},{2,3},{3,2},{4,5},{5,4},{6,7},{7,6},{8,9},{9,8},{10,11... | collective-permute-start | bytes 1253384 | tf_op jit(solution)/shard_map/ppermute | solution.py:376
  26.2 1.0 %copy-start.1 = (bf16[272,768]{1,0:T(8,128)(2,1)S(1)}, bf16[272,768]{1,0:T(8,128)(2,1)}, u32[]{:S(2)}) copy-start(bf16[272,768]{1,0:T(8,128)(2,1)} %get-tuple-element.35.refs_0_) | copy-start | bytes 1253380
  27.3 8.4 %copy-start.3 = (bf16[272,768]{1,0:T(8,128)(2,1)S(1)}, bf16[272,768]{1,0:T(8,128)(2,1)}, u32[]{:S(2)}) copy-start(bf16[272,768]{1,0:T(8,128)(2,1)} %get-tuple-element.40) | copy-start | bytes 1253380
  27.3 23.5 %copy-start.2 = (bf16[272,768]{1,0:T(8,128)(2,1)S(1)}, bf16[272,768]{1,0:T(8,128)(2,1)}, u32[]{:S(2)}) copy-start(bf16[272,768]{1,0:T(8,128)(2,1)} %get-tuple-element.35.refs_0_) | copy-start | bytes 1253380
  27.3 23.5 %collective-permute-start.9 = (bf16[544,768]{1,0:T(8,128)(2,1)S(1)}, bf16[544,768]{1,0:T(8,128)(2,1)S(1)}, u32[]{:S(2)}, u32[]{:S(2)}) collective-permute-start(bf16[544,768]{1,0:T(8,128)(2,1)S(1)} %shard_map.39), channel_id=1, source_target_pairs={{0,8},{1,9},{2,10},{3,11},{4,12},{5,13},{6,14},{7,15},{8,0},{9,1},... | collective-permute-start | bytes 2506760 | tf_op jit(solution)/shard_map/ppermute | solution.py:376
  35.6 15.2 %collective-permute-start.11 = (bf16[544,768]{1,0:T(8,128)(2,1)S(1)}, bf16[544,768]{1,0:T(8,128)(2,1)S(1)}, u32[]{:S(2)}, u32[]{:S(2)}) collective-permute-start(bf16[544,768]{1,0:T(8,128)(2,1)S(1)} %shard_map.40), channel_id=1, source_target_pairs={{0,8},{1,9},{2,10},{3,11},{4,12},{5,13},{6,14},{7,15},{8,0},{9,1},... | collective-permute-start | bytes 2506760 | tf_op jit(solution)/shard_map/ppermute | solution.py:376
  35.7 14.0 %collective-permute-start.2 = (bf16[272,768]{1,0:T(8,128)(2,1)S(1)}, bf16[272,768]{1,0:T(8,128)(2,1)S(1)}, u32[]{:S(2)}, u32[]{:S(2)}) collective-permute-start(bf16[272,768]{1,0:T(8,128)(2,1)S(1)} %copy-done.3), channel_id=1, source_target_pairs={{0,6},{1,7},{2,4},{3,5},{4,2},{5,3},{6,0},{7,1},{8,14},{9,15},{10,... | collective-permute-start | bytes 1253384 | tf_op jit(solution)/shard_map/ppermute | solution.py:376
  38.3 12.0 %collective-permute-start.10 = (bf16[272,768]{1,0:T(8,128)(2,1)S(1)}, bf16[272,768]{1,0:T(8,128)(2,1)S(1)}, u32[]{:S(2)}, u32[]{:S(2)}) collective-permute-start(bf16[272,768]{1,0:T(8,128)(2,1)S(1)} %collective-permute-done.1.refs_2_), channel_id=1, source_target_pairs={{0,16},{1,17},{2,18},{3,19},{4,20},{5,21},{6,22},{7,23},{8,24},{9,... | collective-permute-start | bytes 1253384 | tf_op jit(solution)/shard_map/ppermute | solution.py:376
  38.8 12.0 %collective-permute-start.7 = (bf16[272,768]{1,0:T(8,128)(2,1)S(1)}, bf16[272,768]{1,0:T(8,128)(2,1)S(1)}, u32[]{:S(2)}, u32[]{:S(2)}) collective-permute-start(bf16[272,768]{1,0:T(8,128)(2,1)S(1)} %collective-permute-done.1.refs_2_), channel_id=1, source_target_pairs={{0,1},{1,0},{2,3},{3,2},{4,5},{5,4},{6,7},{7,6},{8,9},{9,8},{10,11... | collective-permute-start | bytes 1253384 | tf_op jit(solution)/shard_map/ppermute | solution.py:376
  49.6 11.1 %collective-permute-start.14 = (bf16[272,768]{1,0:T(8,128)(2,1)S(1)}, bf16[272,768]{1,0:T(8,128)(2,1)S(1)}, u32[]{:S(2)}, u32[]{:S(2)}) collective-permute-start(bf16[272,768]{1,0:T(8,128)(2,1)S(1)} %collective-permute-done.2.refs_3_), channel_id=1, source_target_pairs={{0,16},{1,17},{2,18},{3,19},{4,20},{5,21},{6,22},{7,23},{8,24},{9,... | collective-permute-start | bytes 1253384 | tf_op jit(solution)/shard_map/ppermute | solution.py:376
  50.2 11.6 %collective-permute-start.8 = (bf16[272,768]{1,0:T(8,128)(2,1)S(1)}, bf16[272,768]{1,0:T(8,128)(2,1)S(1)}, u32[]{:S(2)}, u32[]{:S(2)}) collective-permute-start(bf16[272,768]{1,0:T(8,128)(2,1)S(1)} %collective-permute-done.2.refs_3_), channel_id=1, source_target_pairs={{0,1},{1,0},{2,3},{3,2},{4,5},{5,4},{6,7},{7,6},{8,9},{9,8},{10,11... | collective-permute-start | bytes 1253384 | tf_op jit(solution)/shard_map/ppermute | solution.py:376
  55.2 32.1 %copy-start = (s32[1,1024]{1,0:T(1,128)S(1)}, s32[1,1024]{1,0:T(1,128)}, u32[]{:S(2)}) copy-start(s32[1,1024]{1,0:T(1,128)} %get-tuple-element.33.dest_ref) | copy-start | bytes 12292
  60.8 1.8 %collective-permute-start.16 = (bf16[272,768]{1,0:T(8,128)(2,1)S(1)}, bf16[272,768]{1,0:T(8,128)(2,1)S(1)}, u32[]{:S(2)}, u32[]{:S(2)}) collective-permute-start(bf16[272,768]{1,0:T(8,128)(2,1)S(1)} %collective-permute-done.14.refs_14_), channel_id=1, source_target_pairs={{0,8},{1,9},{2,10},{3,11},{4,12},{5,13},{6,14},{7,15},{8,0},{9,1},... | collective-permute-start | bytes 1253384 | tf_op jit(solution)/shard_map/ppermute | solution.py:376
  60.8 2.4 %collective-permute-start.15 = (bf16[272,768]{1,0:T(8,128)(2,1)S(1)}, bf16[272,768]{1,0:T(8,128)(2,1)S(1)}, u32[]{:S(2)}, u32[]{:S(2)}) collective-permute-start(bf16[272,768]{1,0:T(8,128)(2,1)S(1)} %collective-permute-done.10.refs_10_.refs_13_), channel_id=1, source_target_pairs={{0,8},{1,9},{2,10},{3,11},{4,12},{5,13},{6,14},{7,15},{8,0},{9,1},... | collective-permute-start | bytes 1253384 | tf_op jit(solution)/shard_map/ppermute | solution.py:376
  61.3 2.4 %collective-permute-start.13 = (bf16[272,768]{1,0:T(8,128)(2,1)S(1)}, bf16[272,768]{1,0:T(8,128)(2,1)S(1)}, u32[]{:S(2)}, u32[]{:S(2)}) collective-permute-start(bf16[272,768]{1,0:T(8,128)(2,1)S(1)} %collective-permute-done.2.refs_3_), channel_id=1, source_target_pairs={{0,8},{1,9},{2,10},{3,11},{4,12},{5,13},{6,14},{7,15},{8,0},{9,1},... | collective-permute-start | bytes 1253384 | tf_op jit(solution)/shard_map/ppermute | solution.py:376
  61.3 3.0 %collective-permute-start.12 = (bf16[272,768]{1,0:T(8,128)(2,1)S(1)}, bf16[272,768]{1,0:T(8,128)(2,1)S(1)}, u32[]{:S(2)}, u32[]{:S(2)}) collective-permute-start(bf16[272,768]{1,0:T(8,128)(2,1)S(1)} %collective-permute-done.1.refs_2_), channel_id=1, source_target_pairs={{0,8},{1,9},{2,10},{3,11},{4,12},{5,13},{6,14},{7,15},{8,0},{9,1},... | collective-permute-start | bytes 1253384 | tf_op jit(solution)/shard_map/ppermute | solution.py:376

commit v8 on v6

--- a/solution.py
+++ b/solution.py
@@ -39,10 +39,12 @@
     return offsets, pairs
 
 
-def pack_kernel(sizes, ks, emb_hbm, cluster_hbm, rank_hbm, *refs):
+def pack_kernel(sizes, ks, labelled, emb_hbm, cluster_hbm, rank_hbm, *refs):
     groups, halves, half, cap, blk = sizes
-    dest_ref, outs = refs[0], refs[1 : 1 + len(ks)]
-    emb_ref, cluster_ref, rank_ref, stage, sems, out_sems = refs[1 + len(ks) :]
+    outs, refs = refs[: len(ks)], refs[len(ks) :]
+    if labelled:
+        dest_ref, key_ref, *refs = refs
+    emb_ref, cluster_ref, rank_ref, stage, sems, out_sems = refs
     rows = emb_ref.shape[0]
     step = 256
     loads = [
@@ -79,8 +81,12 @@
         carry = carry + jnp.sum(hit, axis=1, keepdims=True)
         places.append(jnp.where(mine >= 0, mine * cap + position.astype(jnp.int32), -1))
     dest = jnp.concatenate(places, axis=1)
-    dest_ref[...] = dest
-    dest = jnp.where(dest >= 0, dest ^ (lax.axis_index("mem") // (halves // 2 // groups) * blk), -1)
+    if labelled:
+        dest_ref[...] = dest
+    members = halves // 2
+    side = members // groups
+    here = lax.axis_index("mem") // side
+    dest = jnp.where(dest >= 0, dest ^ (here * blk), -1)
 
     units_of = []
     for j in range(rows // step):
@@ -95,56 +101,47 @@
         field == 0, safe_rank - which * half, jnp.where(field == 1, parity + 1, 0)
     )
     labels = jnp.where(alive, labels, 0).astype(jnp.float32).astype(jnp.bfloat16)
-    per_tile = blk // TILES
-    wide_tile = groups * per_tile
-    spread = (
-        lax.broadcasted_iota(jnp.int32, (blk, wide_tile), 0) % per_tile
-        == lax.broadcasted_iota(jnp.int32, (blk, wide_tile), 1) % per_tile
-    )
-    spread = spread.astype(jnp.float32).astype(jnp.bfloat16)
-    label_row = lax.broadcasted_iota(jnp.int32, (LABEL_ROWS, blk), 0)
-    label_col = lax.broadcasted_iota(jnp.int32, (LABEL_ROWS, blk), 1)
-    own_tile = label_row == lax.div(label_col, per_tile)
-    unit_col = lax.div(label_col, cap).astype(jnp.float32)
+    unit_of = lax.div(lax.broadcasted_iota(jnp.int32, (1, blk), 1), cap).astype(jnp.float32)
     slot = lax.broadcasted_iota(jnp.int32, (blk, rows), 0)
-    width = emb_ref.shape[1]
     leaving = []
-    for n, k in enumerate(ks):
+    for k in (*ks, *(k for k in range(groups) if labelled and k not in ks)):
         pick = (slot + k * blk == dest).astype(jnp.float32).astype(jnp.bfloat16)
-        stage[n, 0:blk, :] = jnp.dot(pick, unit, preferred_element_type=jnp.float32).astype(
-            jnp.bfloat16
-        )
-        mine = lax.dot_general(labels, pick, NT, preferred_element_type=jnp.float32)
-        plain = jnp.where(label_row == 2, unit_col, mine)
-        parts = [plain] + [jnp.zeros_like(plain)] * ((wide_tile - blk) // blk)
-        for f in range(2):
-            line = jnp.where(own_tile, mine[f : f + 1, :], 0.0).astype(jnp.bfloat16)
-            parts.append(jnp.dot(line, spread, preferred_element_type=jnp.float32))
-        if width > 3 * wide_tile:
-            parts.append(jnp.zeros((LABEL_ROWS, width - 3 * wide_tile), jnp.float32))
-        stage[n, blk : blk + LABEL_ROWS, :] = jnp.concatenate(parts, axis=1).astype(jnp.bfloat16)
-        leaving.append(pltpu.make_async_copy(stage.at[n], outs[n], out_sems.at[n]))
-        leaving[-1].start()
+        if labelled:
+            mine = lax.dot_general(labels, pick, NT, preferred_element_type=jnp.float32)
+            key = mine[0:1] + float(half) * unit_of + float(halves * half) * mine[1:2]
+            for p in range(groups):
+                for y in range(side):
+                    key_ref[pl.ds(p * members + (here ^ k) * side + y, 1), :] = key
+        if k in ks:
+            n = ks.index(k)
+            stage[n] = jnp.dot(pick, unit, preferred_element_type=jnp.float32).astype(jnp.bfloat16)
+            leaving.append(pltpu.make_async_copy(stage.at[n], outs[n], out_sems.at[n]))
+            leaving[-1].start()
     for copy in leaving:
         copy.wait()
 
 
-def pack(embeddings, cluster, rank, ks, sizes):
+def pack(embeddings, cluster, rank, ks, labelled, sizes):
     groups, halves, half, cap, blk = sizes
     rows, width = embeddings.shape
     hbm = pl.BlockSpec(memory_space=pltpu.HBM)
-    out_shape = [jax.ShapeDtypeStruct((1, rows), jnp.int32)]
-    out_shape += [jax.ShapeDtypeStruct((blk + LABEL_ROWS, width), jnp.bfloat16)] * len(ks)
+    vmem = pl.BlockSpec(memory_space=pltpu.VMEM)
+    out_shape = [jax.ShapeDtypeStruct((blk, width), jnp.bfloat16)] * len(ks)
+    out_specs = [hbm] * len(ks)
+    if labelled:
+        out_shape.append(jax.ShapeDtypeStruct((1, rows), jnp.int32))
+        out_shape.append(jax.ShapeDtypeStruct((groups * halves // 2, blk), jnp.float32))
+        out_specs += [vmem, vmem]
     return pl.pallas_call(
-        functools.partial(pack_kernel, sizes, ks),
+        functools.partial(pack_kernel, sizes, ks, labelled),
         out_shape=out_shape,
         in_specs=[hbm, hbm, hbm],
-        out_specs=[pl.BlockSpec(memory_space=pltpu.VMEM)] + [hbm] * len(ks),
+        out_specs=out_specs,
         scratch_shapes=[
             pltpu.VMEM((rows, width), jnp.bfloat16),
             pltpu.VMEM((1, rows), jnp.int32),
             pltpu.VMEM((1, rows), jnp.int32),
-            pltpu.VMEM((len(ks), blk + LABEL_ROWS, width), jnp.bfloat16),
+            pltpu.VMEM((len(ks), blk, width), jnp.bfloat16),
             pltpu.SemaphoreType.DMA((2 + rows // 256,)),
             pltpu.SemaphoreType.DMA((len(ks),)),
         ],
@@ -155,11 +152,11 @@
     )(embeddings, cluster.reshape(1, rows), rank.reshape(1, rows))
 
 
-def compare_kernel(sizes, jobs, names, spots, joined, has_prev, *refs):
+def compare_kernel(sizes, jobs, names, spots, offsets, joined, has_prev, label_ref, *refs):
     groups, halves, half, cap, blk = sizes
     array = dict(zip(names, refs))
     refs = refs[len(names) :]
-    block = {piece: (array[name], at * (blk + LABEL_ROWS)) for piece, (name, at) in spots.items()}
+    block = {piece: (array[name], at * blk) for piece, (name, at) in spots.items()}
     prev = None
     if has_prev:
         prev, refs = refs[0], refs[1:]
@@ -169,39 +166,42 @@
     tile = rows // TILES
     cap_all = float(halves * half)
 
-    lane = lax.broadcasted_iota(jnp.int32, (LABEL_ROWS, tile), 1)
-    line = lax.broadcasted_iota(jnp.int32, (LABEL_ROWS, tile), 0)
-    from_block = lax.div(lane, per_tile)
-    which = line * (halves // TILES) + lax.div(lane - from_block * per_tile, cap)
+    members = halves // 2
+    side = members // groups
+    across, along = lax.axis_index("grp"), lax.axis_index("mem")
+
+    def keys_of(piece):
+        i, k = piece
+        row = (across ^ (offsets[i] // side)) * members
+        row += ((along // side) ^ k) * side + ((along % side) ^ (offsets[i] % side))
+        return label_ref[pl.ds(row, 1), :]
+
     weight_row = lax.broadcasted_iota(jnp.int32, (LABEL_ROWS, 128), 0)
-    weights = jnp.where(
-        weight_row == 0,
-        1.0,
-        jnp.where(weight_row == 1, cap_all, jnp.where(weight_row == 2, float(half), 0.0)),
-    ).astype(jnp.bfloat16)
+    weights = jnp.where(weight_row == 0, 1.0, jnp.where(weight_row == 1, float(half), 0.0))
+    weights = weights.astype(jnp.bfloat16)
+    field = lax.broadcasted_iota(jnp.int32, (LABEL_ROWS, blk), 0)
     needed = sorted({piece for _, pieces in jobs for piece in pieces})
     key_at = {piece: n * blk for n, piece in enumerate(needed)}
-
-    def label_of(piece):
-        ref, base = block[piece]
-        return ref[base + blk : base + blk + LABEL_ROWS, :]
-
     for piece in needed:
+        key = keys_of(piece)
+        high = jnp.floor(key * (1.0 / half))
+        split = jnp.where(field == 0, key - high * half, jnp.where(field == 1, high, 0.0))
         key_col[pl.ds(key_at[piece], blk), :] = lax.dot_general(
-            label_of(piece)[:, 0:blk], weights, TN, preferred_element_type=jnp.float32
+            split.astype(jnp.bfloat16), weights, TN, preferred_element_type=jnp.float32
         )
+    lane = lax.div(lax.broadcasted_iota(jnp.int32, (1, tile), 1), per_tile)
     for o, (a, _) in enumerate(jobs):
-        rest = jnp.zeros((LABEL_ROWS, tile), jnp.float32)
-        code = jnp.zeros((LABEL_ROWS, tile), jnp.float32)
-        for k in range(groups):
-            label = label_of((a, k))[:, tile : 3 * tile].astype(jnp.float32)
-            rest = jnp.where(from_block == k, label[:, :tile], rest)
-            code = jnp.where(from_block == k, label[:, tile:], code)
-        low = code * cap_all
-        key = low + (which * half).astype(jnp.float32) + rest
-        low = jnp.where(code > 0.5, low, FAR)
-        key_row[o] = key[0:8]
-        low_row[o] = low[0:8]
+        keys = [keys_of((a, k)) for k in range(groups)]
+        keys = [jnp.concatenate([key] * (tile // blk), axis=1) for key in keys]
+        for t in range(TILES):
+            line = jnp.zeros((1, tile), jnp.float32)
+            for k in range(groups):
+                turn = ((k - t) * per_tile) % tile
+                moved = pltpu.roll(keys[k], turn, 1) if turn else keys[k]
+                line = jnp.where(lane == k, moved, line)
+            low = jnp.floor(line * (1.0 / cap_all)) * cap_all
+            key_row[o, t : t + 1, :] = line
+            low_row[o, t : t + 1, :] = jnp.where(low > 0.5, low, FAR)
 
     def rows_of(ref, base, first, last):
         return ref[base + first * per_tile : base + last * per_tile, :]
@@ -236,9 +236,6 @@
     if not has_prev:
         outs[0][...] = best[...]
         return
-    lane = lax.broadcasted_iota(jnp.int32, (1, tile), 1)
-    side = halves // 2 // groups
-    here = lax.axis_index("mem")
     for o, (a, _) in enumerate(jobs):
         found = best[a]
         for k in range(groups):
@@ -246,16 +243,17 @@
             for t in range(TILES):
                 turn = ((t - k) * per_tile) % tile
                 moved = pltpu.roll(found, turn, 1) if turn else found
-                total = jnp.where(lax.div(lane, per_tile) == t, moved[t : t + 1], total)
-            at = (here // side) ^ k
+                total = jnp.where(lane == t, moved[t : t + 1], total)
+            at = (along // side) ^ k
             if joined:
-                outs[0][pl.ds(at * joined + ((here % side) ^ a), 1), 0, :] = total[:, :blk]
+                outs[0][pl.ds(at * joined + ((along % side) ^ a), 1), 0, :] = total[:, :blk]
             else:
                 outs[o][pl.ds(at, 1), 0, :] = total[:, :blk]
 
 
-def compare(blocks, jobs, prev, joined, n_sets, sizes):
+def compare(labels, blocks, jobs, prev, joined, offsets, sizes):
     groups, halves, half, cap, blk = sizes
+    n_sets = len(offsets)
     used = {piece for _, pieces in jobs for piece in pieces}
     used |= {(a, k) for a, _ in jobs for k in range(groups)}
     spots = {}
@@ -279,10 +277,12 @@
         out_shape = [jax.ShapeDtypeStruct((groups * joined, 1, blk), jnp.float32)]
     else:
         out_shape = [jax.ShapeDtypeStruct((groups, 1, blk), jnp.float32)] * len(jobs)
-    operands = list(arrays.values()) + ([] if prev is None else [prev])
+    operands = [labels] + list(arrays.values()) + ([] if prev is None else [prev])
     needed = {piece for _, pieces in jobs for piece in pieces}
     return pl.pallas_call(
-        functools.partial(compare_kernel, sizes, jobs, names, spots, joined, prev is not None),
+        functools.partial(
+            compare_kernel, sizes, jobs, names, spots, offsets, joined, prev is not None
+        ),
         out_shape=out_shape,
         in_specs=[vmem] * len(operands),
         out_specs=[vmem] * len(out_shape),
@@ -373,14 +373,14 @@
     offsets, pairs = cover(members)
     sends = [None] * groups
     first = tuple(range(1, min(3, groups)))
-    dest, *packed = pack(embeddings, cluster, rank, first, sizes)
-    for k, value in zip(first, packed):
+    for k, value in zip(first, pack(embeddings, cluster, rank, first, False, sizes)):
         sends[k] = value
     rest = tuple(k for k in range(groups) if k not in first)
-    cluster, dest = lax.optimization_barrier((cluster, dest))
-    _, *packed = pack(embeddings, cluster, rank, rest, sizes)
+    cluster, sends[1] = lax.optimization_barrier((cluster, sends[1]))
+    *packed, dest, labels = pack(embeddings, cluster, rank, rest, True, sizes)
     for k, value in zip(rest, packed):
         sends[k] = value
+    labels = lax.all_to_all(labels, ("grp", "mem"), split_axis=0, concat_axis=0, tiled=True)
 
     last = groups - 1
     far = [d for d in offsets if d & side and d != side and d ^ side in offsets]
@@ -401,11 +401,11 @@
         if k < last:
             also = swap(sends[k + 1], k + 1, 0)
             if k == 1:
-                mine, also, *firsts = lax.optimization_barrier(
-                    (mine, also, *(held[d][0] for d in near))
+                mine, also, labels, *firsts = lax.optimization_barrier(
+                    (mine, also, labels, *(held[d][0] for d in near))
                 )
-                for d, first in zip(near, firsts):
-                    held[d] = [first]
+                for d, value in zip(near, firsts):
+                    held[d] = [value]
             mine = join(mine, also)
             after = mine
         held[0].append(mine)
@@ -422,6 +422,16 @@
             held[d].append(swap(held[d ^ side][spot], 0, side))
 
     index = {d: i for i, d in enumerate(offsets)}
+    blocks = {}
+
+    def note():
+        for d in offsets:
+            for spot, value in enumerate(held[d]):
+                ks = [0] if spot == 0 else [k for k in (2 * spot - 1, 2 * spot) if k < groups]
+                for at, k in enumerate(ks):
+                    blocks[index[d], k] = (value, at)
+
+    note()
     starts = sorted({a for a, _ in pairs.values()})
     early, late = [], []
     for a in starts:
@@ -433,17 +443,12 @@
             pieces = [piece for piece in pieces if piece not in soon]
         late.append((index[a], pieces))
     joined = side if all(a < side for a in starts) else 0
-    blocks = {}
-    for d in offsets:
-        for k in range(groups):
-            spot = (k + 1) // 2
-            if spot < len(held[d]):
-                blocks[index[d], k] = (held[d][spot], 1 - k % 2 if 0 < k < last else 0)
-    prev = compare(blocks, early, None, 0, len(offsets), sizes)[0]
+    prev = compare(labels, blocks, early, None, 0, offsets, sizes)[0]
     for d in far:
         piece, prev = lax.optimization_barrier((held[d ^ side][-1], prev))
-        blocks[index[d], last] = (swap(piece, 0, side), 0)
-    found = compare(blocks, late, prev, joined, len(offsets), sizes)
+        held[d].append(swap(piece, 0, side))
+    note()
+    found = compare(labels, blocks, late, prev, joined, offsets, sizes)
     if joined:
         back = found[0]
     else:

time: 82.7 us -> 80.7 us (0.976)
  waiting for transfers between devices: 33.8 us -> 22.1 us
  blocking collectives: 11 us -> 22.4 us
  starting transfers between devices: 16.9 us -> 14.9 us
    all_to_all x0 -> x1, blocking collectives: none -> 12 us  [on_device(): lax.all_to_all(labels, ('grp', 'mem'), split_axis=0, concat_axis=0, tiled...]
    ppermute x15, waiting for transfers between devices: 33.8 us -> 22.1 us  [swap(): lax.ppermute(value, ('grp', 'mem'), [(i, i ^ mask) for i in range(devices)])]
    ppermute x15, starting transfers between devices: 16.9 us -> 14.9 us  [swap(): lax.ppermute(value, ('grp', 'mem'), [(i, i ^ mask) for i in range(devices)])]
    pallas_call x2, Pallas kernels: 8.73 us -> 7.52 us  [pack(): pl.pallas_call(functools.partial(pack_kernel, sizes, ks, labelled), out_s...]
  transfers between devices with their start and end apart: 15 -> 15, of which waited for: 9 -> 6; matrix products, arithmetic and copies ran while one was open for 0% -> 1% of each run, Pallas kernels for 12% -> 12%
where the time goes in v8:
time: 80.7 us; the launch traced here: 80.4 us
  blocking collectives  22.4 us (28%)
  waiting for transfers between devices  22.1 us (27%)
  Pallas kernels  20.1 us (25%)
  starting transfers between devices  14.9 us (18%)
  local copies, waits for them, and re-layouts  0.81 us (1%)
    ppermute x15, waiting for transfers between devices, swap(): lax.ppermute(value, ('grp', 'mem'), [(i, i ^ mask) for i in range(devices)])  22.1 us
    ppermute x15, starting transfers between devices, swap(): lax.ppermute(value, ('grp', 'mem'), [(i, i ^ mask) for i in range(devices)])  14.9 us
    all_to_all x1, blocking collectives, on_device(): lax.all_to_all(labels, ('grp', 'mem'), split_axis=0, concat_axis=0, tiled...  12 us
    pallas_call x2, Pallas kernels, compare(): pl.pallas_call(functools.partial(compare_kernel, sizes, jobs, names, spot...  11.4 us
    all_to_all x1, blocking collectives, on_device(): back = lax.all_to_all(back, 'mem', split_axis=0, concat_axis=0, tiled=True)  10.4 us
    pallas_call x2, Pallas kernels, pack(): pl.pallas_call(functools.partial(pack_kernel, sizes, ks, labelled), out_s...  7.52 us
  transfers between devices with their start and end apart: 15, of which 6 were waited for; matrix products, arithmetic and copies ran while one was open for 1% of the time, Pallas kernels for 12%

profile of v8, /device:TPU:0, one launch (start us, length us, event | category | flops | bytes accessed | tf_op | source)
XLA Modules:
  0.0 80.4 jit_solution(14882233622643961949)
XLA Ops:
  0.0 3.3 %shard_map.37 = (bf16[256,768]{1,0:T(8,128)(2,1)}, bf16[256,768]{1,0:T(8,128)(2,1)}) custom-call(bf16[1024,768]{1,0:T(8,128)(2,1)} %emb_hbm.3, s32[1,1024]{1,0:T(1,128)} %bitcast.11, s32[1,1024]{1,0:T(1,128)} %bitcast.13), custom_call_target="tpu_custom_call" | custom-call | flops 805306368 | bytes 3145728 | tf_op jit(solution)/shard_map/pallas_call | solution.py:135
  3.3 3.1 %collective-permute-start = (bf16[256,768]{1,0:T(8,128)(2,1)}, bf16[256,768]{1,0:T(8,128)(2,1)S(1)}, u32[]{:S(2)}, u32[]{:S(2)}) collective-permute-start(bf16[256,768]{1,0:T(8,128)(2,1)} %get-tuple-element.29), channel_id=1, source_target_pairs={{0,2},{1,3},{2,0},{3,1},{4,6},{5,7},{6,4},{7,5},{8,10},{9,11},{10,... | collective-permute-start | bytes 1179656 | tf_op jit(solution)/shard_map/ppermute | solution.py:371
  6.4 2.6 %collective-permute-start.1 = (bf16[256,768]{1,0:T(8,128)(2,1)}, bf16[256,768]{1,0:T(8,128)(2,1)S(1)}, u32[]{:S(2)}, u32[]{:S(2)}) collective-permute-start(bf16[256,768]{1,0:T(8,128)(2,1)} %get-tuple-element.30), channel_id=1, source_target_pairs={{0,4},{1,5},{2,6},{3,7},{4,0},{5,1},{6,2},{7,3},{8,12},{9,13},{10,... | collective-permute-start | bytes 1179656 | tf_op jit(solution)/shard_map/ppermute | solution.py:371
  9.0 4.2 %shard_map.38 = (bf16[256,768]{1,0:T(8,128)(2,1)}, bf16[256,768]{1,0:T(8,128)(2,1)}, s32[1,1024]{1,0:T(1,128)}, f32[32,256]{1,0:T(8,128)}) custom-call(bf16[1024,768]{1,0:T(8,128)(2,1)} %emb_hbm.3, s32[1,1024]{1,0:T(1,128)} %bitcast.12, s32[1,1024]{1,0:T(1,128)} %bitcast.14), custom_call_target="tpu_custom_call" | custom-call | flops 805306368 | bytes 3145728 | tf_op jit(solution)/shard_map/pallas_call | solution.py:135
  13.2 1.6 %collective-permute-start.4 = (bf16[256,768]{1,0:T(8,128)(2,1)}, bf16[256,768]{1,0:T(8,128)(2,1)S(1)}, u32[]{:S(2)}, u32[]{:S(2)}) collective-permute-start(bf16[256,768]{1,0:T(8,128)(2,1)} %get-tuple-element.32.refs_0_), channel_id=1, source_target_pairs={{0,16},{1,17},{2,18},{3,19},{4,20},{5,21},{6,22},{7,23},{8,24},{9,... | collective-permute-start | bytes 1179656 | tf_op jit(solution)/shard_map/ppermute | solution.py:371
  14.8 1.5 %collective-permute-start.2 = (bf16[256,768]{1,0:T(8,128)(2,1)}, bf16[256,768]{1,0:T(8,128)(2,1)S(1)}, u32[]{:S(2)}, u32[]{:S(2)}) collective-permute-start(bf16[256,768]{1,0:T(8,128)(2,1)} %get-tuple-element.32.refs_0_), channel_id=1, source_target_pairs={{0,1},{1,0},{2,3},{3,2},{4,5},{5,4},{6,7},{7,6},{8,9},{9,8},{10,11... | collective-permute-start | bytes 1179656 | tf_op jit(solution)/shard_map/ppermute | solution.py:371
  16.3 0.8 copy.4
  17.1 12.0 %all_to_all.17 = f32[32,1,256]{2,1,0:T(1,128)S(1)} all-to-all(f32[32,1,256]{2,1,0:T(1,128)S(1)} %copy.4), channel_id=1, replica_groups=mesh['grp'=4,'mem'=8] {'grp','mem'}, dimensions={0} | all-to-all | bytes 65536 | tf_op jit(solution)/shard_map/all_to_all | solution.py:383
  29.2 0.6 collective-permute-start.8
  29.8 0.6 collective-permute-start.6
  30.4 2.4 %collective-permute-start.5 = (bf16[256,768]{1,0:T(8,128)(2,1)S(1)}, bf16[256,768]{1,0:T(8,128)(2,1)S(1)}, u32[]{:S(2)}, u32[]{:S(2)}) collective-permute-start(bf16[256,768]{1,0:T(8,128)(2,1)S(1)} %copy-done.2), channel_id=1, source_target_pairs={{0,6},{1,7},{2,4},{3,5},{4,2},{5,3},{6,0},{7,1},{8,14},{9,15},{10,... | collective-permute-start | bytes 1179656 | tf_op jit(solution)/shard_map/ppermute | solution.py:371
  32.9 10.7 %collective-permute-done.5.refs_2_ = bf16[256,768]{1,0:T(8,128)(2,1)S(1)} collective-permute-done((bf16[256,768]{1,0:T(8,128)(2,1)S(1)}, bf16[256,768]{1,0:T(8,128)(2,1)S(1)}, u32[]{:S(2)}, u32[]{:S(2)}) %collective-permute-start.5) | collective-permute-done | bytes 393248 | tf_op jit(solution)/shard_map/ppermute | solution.py:371
  43.6 5.1 %collective-permute-done.8.refs_8_.refs_10_ = bf16[512,768]{1,0:T(8,128)(2,1)S(1)} collective-permute-done((bf16[512,768]{1,0:T(8,128)(2,1)S(1)}, bf16[512,768]{1,0:T(8,128)(2,1)S(1)}, u32[]{:S(2)}, u32[]{:S(2)}) %collective-permute-start.8) | collective-permute-done | bytes 786464 | tf_op jit(solution)/shard_map/ppermute | solution.py:371
  48.6 1.1 %collective-permute-done.6.refs_4_ = bf16[512,768]{1,0:T(8,128)(2,1)S(1)} collective-permute-done((bf16[512,768]{1,0:T(8,128)(2,1)S(1)}, bf16[512,768]{1,0:T(8,128)(2,1)S(1)}, u32[]{:S(2)}, u32[]{:S(2)}) %collective-permute-start.6) | collective-permute-done | bytes 786464 | tf_op jit(solution)/shard_map/ppermute | solution.py:371
  49.8 0.5 collective-permute-start.12
  50.3 1.5 %collective-permute-start.11 = (bf16[256,768]{1,0:T(8,128)(2,1)S(1)}, bf16[256,768]{1,0:T(8,128)(2,1)S(1)}, u32[]{:S(2)}, u32[]{:S(2)}) collective-permute-start(bf16[256,768]{1,0:T(8,128)(2,1)S(1)} %collective-permute-done.5.refs_2_), channel_id=1, source_target_pairs={{0,16},{1,17},{2,18},{3,19},{4,20},{5,21},{6,22},{7,23},{8,24},{9,... | collective-permute-start | bytes 1179656 | tf_op jit(solution)/shard_map/ppermute | solution.py:371
  51.8 0.5 collective-permute-start.9
  52.3 0.3 collective-permute-done.12.refs_9_.refs_12_
  52.6 5.8 %shard_map.40.refs_15_ = f32[5,8,256]{2,1,0:T(8,128)S(1)} custom-call(f32[32,256]{1,0:T(8,128)S(1)} %bitcast.8, bf16[256,768]{1,0:T(8,128)(2,1)S(1)} %copy-done.1, bf16[512,768]{1,0:T(8,128)(2,1)S(1)} %shard_map.39.refs_1_, bf16[256,768]{1,0:T(8,128)(2,1)S(1)} %collective-permute-done.5.refs_2_, bf16[256,768]{1,0:T(8,128)(2,1)S(1)} %collective-permute-done.2.refs_3_, ...), custom_call_target="tpu_custom_call" | custom-call | flops 4026531840 | bytes 6291456 | tf_op jit(solution)/shard_map/pallas_call | solution.py:282
  58.5 2.8 %collective-permute-done.11.refs_11_ = bf16[256,768]{1,0:T(8,128)(2,1)S(1)} collective-permute-done((bf16[256,768]{1,0:T(8,128)(2,1)S(1)}, bf16[256,768]{1,0:T(8,128)(2,1)S(1)}, u32[]{:S(2)}, u32[]{:S(2)}) %collective-permute-start.11) | collective-permute-done | bytes 393248 | tf_op jit(solution)/shard_map/ppermute | solution.py:371
  61.3 2.0 %collective-permute-done.9.refs_5_ = bf16[256,768]{1,0:T(8,128)(2,1)S(1)} collective-permute-done((bf16[256,768]{1,0:T(8,128)(2,1)S(1)}, bf16[256,768]{1,0:T(8,128)(2,1)S(1)}, u32[]{:S(2)}, u32[]{:S(2)}) %collective-permute-start.9) | collective-permute-done | bytes 393248 | tf_op jit(solution)/shard_map/ppermute | solution.py:371
  63.3 5.6 %shard_map.41 = f32[8,1,256]{2,1,0:T(1,128)S(1)} custom-call(f32[32,256]{1,0:T(8,128)S(1)} %bitcast.9, bf16[256,768]{1,0:T(8,128)(2,1)S(1)} %copy-done.1, bf16[512,768]{1,0:T(8,128)(2,1)S(1)} %shard_map.39.refs_1_, bf16[256,768]{1,0:T(8,128)(2,1)S(1)} %collective-permute-done.5.refs_2_, bf16[256,768]{1,0:T(8,128)(2,1)S(1)} %collective-permute-done.2.refs_3_, ...), custom_call_target="tpu_custom_call" | custom-call | flops 4026531840 | bytes 7864320 | tf_op jit(solution)/shard_map/pallas_call | solution.py:282
  68.9 10.4 %all_to_all.18.back_ref = f32[8,1,256]{2,1,0:T(1,128)S(1)} all-to-all(f32[8,1,256]{2,1,0:T(1,128)S(1)} %shard_map.41), channel_id=1, replica_groups=mesh['grp'=4,'mem'=8] {'mem'}, dimensions={0} | all-to-all | bytes 16384 | tf_op jit(solution)/shard_map/all_to_all | solution.py:469
  79.3 1.1 %shard_map.42 = f32[1,1024]{1,0:T(1,128)} custom-call(s32[1,1024]{1,0:T(1,128)S(1)} %copy-done, f32[8,1,256]{2,1,0:T(1,128)S(1)} %all_to_all.18.back_ref), custom_call_target="tpu_custom_call" | custom-call | tf_op jit(solution)/shard_map/pallas_call | solution.py:346
  (22 shorter events, 0.1 us)
Async XLA Ops:
  3.3 25.8 %collective-permute-start = (bf16[256,768]{1,0:T(8,128)(2,1)}, bf16[256,768]{1,0:T(8,128)(2,1)S(1)}, u32[]{:S(2)}, u32[]{:S(2)}) collective-permute-start(bf16[256,768]{1,0:T(8,128)(2,1)} %get-tuple-element.29), channel_id=1, source_target_pairs={{0,2},{1,3},{2,0},{3,1},{4,6},{5,7},{6,4},{7,5},{8,10},{9,11},{10,... | collective-permute-start | bytes 1179656 | tf_op jit(solution)/shard_map/ppermute | solution.py:371
  6.4 22.7 %collective-permute-start.1 = (bf16[256,768]{1,0:T(8,128)(2,1)}, bf16[256,768]{1,0:T(8,128)(2,1)S(1)}, u32[]{:S(2)}, u32[]{:S(2)}) collective-permute-start(bf16[256,768]{1,0:T(8,128)(2,1)} %get-tuple-element.30), channel_id=1, source_target_pairs={{0,4},{1,5},{2,6},{3,7},{4,0},{5,1},{6,2},{7,3},{8,12},{9,13},{10,... | collective-permute-start | bytes 1179656 | tf_op jit(solution)/shard_map/ppermute | solution.py:371
  13.2 17.2 %copy-start.2 = (bf16[256,768]{1,0:T(8,128)(2,1)S(1)}, bf16[256,768]{1,0:T(8,128)(2,1)}, u32[]{:S(2)}) copy-start(bf16[256,768]{1,0:T(8,128)(2,1)} %get-tuple-element.37) | copy-start | bytes 1179652
  13.2 39.4 %copy-start.1 = (bf16[256,768]{1,0:T(8,128)(2,1)S(1)}, bf16[256,768]{1,0:T(8,128)(2,1)}, u32[]{:S(2)}) copy-start(bf16[256,768]{1,0:T(8,128)(2,1)} %get-tuple-element.32.refs_0_) | copy-start | bytes 1179652
  13.2 15.9 %collective-permute-start.4 = (bf16[256,768]{1,0:T(8,128)(2,1)}, bf16[256,768]{1,0:T(8,128)(2,1)S(1)}, u32[]{:S(2)}, u32[]{:S(2)}) collective-permute-start(bf16[256,768]{1,0:T(8,128)(2,1)} %get-tuple-element.32.refs_0_), channel_id=1, source_target_pairs={{0,16},{1,17},{2,18},{3,19},{4,20},{5,21},{6,22},{7,23},{8,24},{9,... | collective-permute-start | bytes 1179656 | tf_op jit(solution)/shard_map/ppermute | solution.py:371
  14.8 14.3 %collective-permute-start.3 = (bf16[256,768]{1,0:T(8,128)(2,1)}, bf16[256,768]{1,0:T(8,128)(2,1)S(1)}, u32[]{:S(2)}, u32[]{:S(2)}) collective-permute-start(bf16[256,768]{1,0:T(8,128)(2,1)} %get-tuple-element.32.refs_0_), channel_id=1, source_target_pairs={{0,8},{1,9},{2,10},{3,11},{4,12},{5,13},{6,14},{7,15},{8,0},{9,1},... | collective-permute-start | bytes 1179656 | tf_op jit(solution)/shard_map/ppermute | solution.py:371
  14.8 14.4 %collective-permute-start.2 = (bf16[256,768]{1,0:T(8,128)(2,1)}, bf16[256,768]{1,0:T(8,128)(2,1)S(1)}, u32[]{:S(2)}, u32[]{:S(2)}) collective-permute-start(bf16[256,768]{1,0:T(8,128)(2,1)} %get-tuple-element.32.refs_0_), channel_id=1, source_target_pairs={{0,1},{1,0},{2,3},{3,2},{4,5},{5,4},{6,7},{7,6},{8,9},{9,8},{10,11... | collective-permute-start | bytes 1179656 | tf_op jit(solution)/shard_map/ppermute | solution.py:371
  29.2 19.4 %collective-permute-start.8 = (bf16[512,768]{1,0:T(8,128)(2,1)S(1)}, bf16[512,768]{1,0:T(8,128)(2,1)S(1)}, u32[]{:S(2)}, u32[]{:S(2)}) collective-permute-start(bf16[512,768]{1,0:T(8,128)(2,1)S(1)} %shard_map.39.refs_1_), channel_id=1, source_target_pairs={{0,16},{1,17},{2,18},{3,19},{4,20},{5,21},{6,22},{7,23},{8,24},{9,... | collective-permute-start | bytes 2359304 | tf_op jit(solution)/shard_map/ppermute | solution.py:371
  29.8 18.8 %collective-permute-start.7 = (bf16[512,768]{1,0:T(8,128)(2,1)S(1)}, bf16[512,768]{1,0:T(8,128)(2,1)S(1)}, u32[]{:S(2)}, u32[]{:S(2)}) collective-permute-start(bf16[512,768]{1,0:T(8,128)(2,1)S(1)} %shard_map.39.refs_1_), channel_id=1, source_target_pairs={{0,8},{1,9},{2,10},{3,11},{4,12},{5,13},{6,14},{7,15},{8,0},{9,1},... | collective-permute-start | bytes 2359304 | tf_op jit(solution)/shard_map/ppermute | solution.py:371
  29.8 20.0 %collective-permute-start.6 = (bf16[512,768]{1,0:T(8,128)(2,1)S(1)}, bf16[512,768]{1,0:T(8,128)(2,1)S(1)}, u32[]{:S(2)}, u32[]{:S(2)}) collective-permute-start(bf16[512,768]{1,0:T(8,128)(2,1)S(1)} %shard_map.39.refs_1_), channel_id=1, source_target_pairs={{0,1},{1,0},{2,3},{3,2},{4,5},{5,4},{6,7},{7,6},{8,9},{9,8},{10,11... | collective-permute-start | bytes 2359304 | tf_op jit(solution)/shard_map/ppermute | solution.py:371
  30.4 13.2 %collective-permute-start.5 = (bf16[256,768]{1,0:T(8,128)(2,1)S(1)}, bf16[256,768]{1,0:T(8,128)(2,1)S(1)}, u32[]{:S(2)}, u32[]{:S(2)}) collective-permute-start(bf16[256,768]{1,0:T(8,128)(2,1)S(1)} %copy-done.2), channel_id=1, source_target_pairs={{0,6},{1,7},{2,4},{3,5},{4,2},{5,3},{6,0},{7,1},{8,14},{9,15},{10,... | collective-permute-start | bytes 1179656 | tf_op jit(solution)/shard_map/ppermute | solution.py:371
  49.8 2.9 %collective-permute-start.13 = (bf16[512,768]{1,0:T(8,128)(2,1)S(1)}, bf16[512,768]{1,0:T(8,128)(2,1)S(1)}, u32[]{:S(2)}, u32[]{:S(2)}) collective-permute-start(bf16[512,768]{1,0:T(8,128)(2,1)S(1)} %collective-permute-done.8.refs_8_.refs_10_), channel_id=1, source_target_pairs={{0,8},{1,9},{2,10},{3,11},{4,12},{5,13},{6,14},{7,15},{8,0},{9,1},... | collective-permute-start | bytes 2359304 | tf_op jit(solution)/shard_map/ppermute | solution.py:371
  49.8 2.8 %collective-permute-start.12 = (bf16[256,768]{1,0:T(8,128)(2,1)S(1)}, bf16[256,768]{1,0:T(8,128)(2,1)S(1)}, u32[]{:S(2)}, u32[]{:S(2)}) collective-permute-start(bf16[256,768]{1,0:T(8,128)(2,1)S(1)} %collective-permute-done.4.refs_7_.refs_9_), channel_id=1, source_target_pairs={{0,8},{1,9},{2,10},{3,11},{4,12},{5,13},{6,14},{7,15},{8,0},{9,1},... | collective-permute-start | bytes 1179656 | tf_op jit(solution)/shard_map/ppermute | solution.py:371
  50.3 11.0 %collective-permute-start.11 = (bf16[256,768]{1,0:T(8,128)(2,1)S(1)}, bf16[256,768]{1,0:T(8,128)(2,1)S(1)}, u32[]{:S(2)}, u32[]{:S(2)}) collective-permute-start(bf16[256,768]{1,0:T(8,128)(2,1)S(1)} %collective-permute-done.5.refs_2_), channel_id=1, source_target_pairs={{0,16},{1,17},{2,18},{3,19},{4,20},{5,21},{6,22},{7,23},{8,24},{9,... | collective-permute-start | bytes 1179656 | tf_op jit(solution)/shard_map/ppermute | solution.py:371
  51.8 9.5 %collective-permute-start.10 = (bf16[256,768]{1,0:T(8,128)(2,1)S(1)}, bf16[256,768]{1,0:T(8,128)(2,1)S(1)}, u32[]{:S(2)}, u32[]{:S(2)}) collective-permute-start(bf16[256,768]{1,0:T(8,128)(2,1)S(1)} %collective-permute-done.5.refs_2_), channel_id=1, source_target_pairs={{0,8},{1,9},{2,10},{3,11},{4,12},{5,13},{6,14},{7,15},{8,0},{9,1},... | collective-permute-start | bytes 1179656 | tf_op jit(solution)/shard_map/ppermute | solution.py:371
  51.8 11.5 %collective-permute-start.9 = (bf16[256,768]{1,0:T(8,128)(2,1)S(1)}, bf16[256,768]{1,0:T(8,128)(2,1)S(1)}, u32[]{:S(2)}, u32[]{:S(2)}) collective-permute-start(bf16[256,768]{1,0:T(8,128)(2,1)S(1)} %collective-permute-done.5.refs_2_), channel_id=1, source_target_pairs={{0,1},{1,0},{2,3},{3,2},{4,5},{5,4},{6,7},{7,6},{8,9},{9,8},{10,11... | collective-permute-start | bytes 1179656 | tf_op jit(solution)/shard_map/ppermute | solution.py:371
  58.5 20.9 %copy-start = (s32[1,1024]{1,0:T(1,128)S(1)}, s32[1,1024]{1,0:T(1,128)}, u32[]{:S(2)}) copy-start(s32[1,1024]{1,0:T(1,128)} %get-tuple-element.28.dest_ref) | copy-start | bytes 12292
  61.3 2.0 %collective-permute-start.14 = (bf16[256,768]{1,0:T(8,128)(2,1)S(1)}, bf16[256,768]{1,0:T(8,128)(2,1)S(1)}, u32[]{:S(2)}, u32[]{:S(2)}) collective-permute-start(bf16[256,768]{1,0:T(8,128)(2,1)S(1)} %collective-permute-done.11.refs_11_), channel_id=1, source_target_pairs={{0,8},{1,9},{2,10},{3,11},{4,12},{5,13},{6,14},{7,15},{8,0},{9,1},... | collective-permute-start | bytes 1179656 | tf_op jit(solution)/shard_map/ppermute | solution.py:371

commit v9 on v8

--- a/solution.py
+++ b/solution.py
@@ -111,7 +111,7 @@
             key = mine[0:1] + float(half) * unit_of + float(halves * half) * mine[1:2]
             for p in range(groups):
                 for y in range(side):
-                    key_ref[pl.ds(p * members + (here ^ k) * side + y, 1), :] = key
+                    key_ref[pl.ds(p * members + (here ^ k) * side + y, 1), 0, :] = key
         if k in ks:
             n = ks.index(k)
             stage[n] = jnp.dot(pick, unit, preferred_element_type=jnp.float32).astype(jnp.bfloat16)
@@ -130,7 +130,7 @@
     out_specs = [hbm] * len(ks)
     if labelled:
         out_shape.append(jax.ShapeDtypeStruct((1, rows), jnp.int32))
-        out_shape.append(jax.ShapeDtypeStruct((groups * halves // 2, blk), jnp.float32))
+        out_shape.append(jax.ShapeDtypeStruct((groups * halves // 2, 1, blk), jnp.float32))
         out_specs += [vmem, vmem]
     return pl.pallas_call(
         functools.partial(pack_kernel, sizes, ks, labelled),
@@ -174,7 +174,7 @@
         i, k = piece
         row = (across ^ (offsets[i] // side)) * members
         row += ((along // side) ^ k) * side + ((along % side) ^ (offsets[i] % side))
-        return label_ref[pl.ds(row, 1), :]
+        return label_ref[pl.ds(row, 1), 0, :]
 
     weight_row = lax.broadcasted_iota(jnp.int32, (LABEL_ROWS, 128), 0)
     weights = jnp.where(weight_row == 0, 1.0, jnp.where(weight_row == 1, float(half), 0.0))
@@ -380,7 +380,6 @@
     *packed, dest, labels = pack(embeddings, cluster, rank, rest, True, sizes)
     for k, value in zip(rest, packed):
         sends[k] = value
-    labels = lax.all_to_all(labels, ("grp", "mem"), split_axis=0, concat_axis=0, tiled=True)
 
     last = groups - 1
     far = [d for d in offsets if d & side and d != side and d ^ side in offsets]
@@ -401,22 +400,26 @@
         if k < last:
             also = swap(sends[k + 1], k + 1, 0)
             if k == 1:
-                mine, also, labels, *firsts = lax.optimization_barrier(
-                    (mine, also, labels, *(held[d][0] for d in near))
+                mine, also, *firsts = lax.optimization_barrier(
+                    (mine, also, *(held[d][0] for d in near))
                 )
                 for d, value in zip(near, firsts):
                     held[d] = [value]
             mine = join(mine, also)
+            if k == 1:
+                mine, labels = lax.optimization_barrier((mine, labels))
+                labels = lax.all_to_all(
+                    labels, ("grp", "mem"), split_axis=0, concat_axis=0, tiled=True
+                )
             after = mine
         held[0].append(mine)
         for d in near:
             held[d].append(swap(mine, 0, d))
     for spot in range(1, len(held[0]) - 1):
-        values = lax.optimization_barrier(
-            (held[0][spot + 1], *(held[d][spot] for d in near))
+        held[0][spot + 1], labels, *values = lax.optimization_barrier(
+            (held[0][spot + 1], labels, *(held[d][spot] for d in near))
         )
-        held[0][spot + 1] = values[0]
-        for d, value in zip(near, values[1:]):
+        for d, value in zip(near, values):
             held[d][spot] = value
         for d in far:
             held[d].append(swap(held[d ^ side][spot], 0, side))

time: 80.7 us -> 80.4 us (level)
  waiting for transfers between devices: 22.1 us -> 14.4 us
  blocking collectives: 22.4 us -> 27.7 us
  starting transfers between devices: 14.9 us -> 17.9 us
    ppermute x15, waiting for transfers between devices: 22.1 us -> 14.4 us  [swap(): lax.ppermute(value, ('grp', 'mem'), [(i, i ^ mask) for i in range(devices)])]
    all_to_all x1, blocking collectives: 12 us -> 17.7 us  [on_device(): lax.all_to_all(labels, ('grp', 'mem'), split_axis=0, concat_axis=0, tiled...]
    ppermute x15, starting transfers between devices: 14.9 us -> 17.9 us  [swap(): lax.ppermute(value, ('grp', 'mem'), [(i, i ^ mask) for i in range(devices)])]
  transfers between devices with their start and end apart: 15 -> 15, of which waited for: 6 -> 4; matrix products, arithmetic and copies ran while one was open for 1% -> 0% of each run, Pallas kernels for 12% -> 13%
where the time goes in v9:
time: 80.4 us; the launch traced here: 80.1 us
  blocking collectives  27.7 us (34%)
  Pallas kernels  20.1 us (25%)
  starting transfers between devices  17.9 us (22%)
  waiting for transfers between devices  14.4 us (18%)
    ppermute x15, starting transfers between devices, swap(): lax.ppermute(value, ('grp', 'mem'), [(i, i ^ mask) for i in range(devices)])  17.9 us
    all_to_all x1, blocking collectives, on_device(): lax.all_to_all(labels, ('grp', 'mem'), split_axis=0, concat_axis=0, tiled...  17.7 us
    ppermute x15, waiting for transfers between devices, swap(): lax.ppermute(value, ('grp', 'mem'), [(i, i ^ mask) for i in range(devices)])  14.4 us
    pallas_call x2, Pallas kernels, compare(): pl.pallas_call(functools.partial(compare_kernel, sizes, jobs, names, spot...  11.4 us
    all_to_all x1, blocking collectives, on_device(): back = lax.all_to_all(back, 'mem', split_axis=0, concat_axis=0, tiled=True)  9.93 us
    pallas_call x2, Pallas kernels, pack(): pl.pallas_call(functools.partial(pack_kernel, sizes, ks, labelled), out_s...  7.54 us
  transfers between devices with their start and end apart: 15, of which 4 were waited for; matrix products, arithmetic and copies ran while one was open for 0% of the time, Pallas kernels for 13%

profile of v9, /device:TPU:0, one launch (start us, length us, event | category | flops | bytes accessed | tf_op | source)
XLA Modules:
  0.0 80.1 jit_solution(7739453686809712705)
XLA Ops:
  0.0 3.3 %shard_map.37 = (bf16[256,768]{1,0:T(8,128)(2,1)}, bf16[256,768]{1,0:T(8,128)(2,1)}) custom-call(bf16[1024,768]{1,0:T(8,128)(2,1)} %emb_hbm.3, s32[1,1024]{1,0:T(1,128)} %bitcast.4, s32[1,1024]{1,0:T(1,128)} %bitcast.6), custom_call_target="tpu_custom_call" | custom-call | flops 805306368 | bytes 3145728 | tf_op jit(solution)/shard_map/pallas_call | solution.py:135
  3.3 3.1 %collective-permute-start = (bf16[256,768]{1,0:T(8,128)(2,1)}, bf16[256,768]{1,0:T(8,128)(2,1)S(1)}, u32[]{:S(2)}, u32[]{:S(2)}) collective-permute-start(bf16[256,768]{1,0:T(8,128)(2,1)} %get-tuple-element.32), channel_id=1, source_target_pairs={{0,2},{1,3},{2,0},{3,1},{4,6},{5,7},{6,4},{7,5},{8,10},{9,11},{10,... | collective-permute-start | bytes 1179656 | tf_op jit(solution)/shard_map/ppermute | solution.py:371
  6.4 2.6 %collective-permute-start.1 = (bf16[256,768]{1,0:T(8,128)(2,1)}, bf16[256,768]{1,0:T(8,128)(2,1)S(1)}, u32[]{:S(2)}, u32[]{:S(2)}) collective-permute-start(bf16[256,768]{1,0:T(8,128)(2,1)} %get-tuple-element.33), channel_id=1, source_target_pairs={{0,4},{1,5},{2,6},{3,7},{4,0},{5,1},{6,2},{7,3},{8,12},{9,13},{10,... | collective-permute-start | bytes 1179656 | tf_op jit(solution)/shard_map/ppermute | solution.py:371
  9.0 4.2 %shard_map.38 = (bf16[256,768]{1,0:T(8,128)(2,1)}, bf16[256,768]{1,0:T(8,128)(2,1)}, s32[1,1024]{1,0:T(1,128)}, f32[32,1,256]{2,1,0:T(1,128)}) custom-call(bf16[1024,768]{1,0:T(8,128)(2,1)} %emb_hbm.3, s32[1,1024]{1,0:T(1,128)} %bitcast.5, s32[1,1024]{1,0:T(1,128)} %bitcast.7), custom_call_target="tpu_custom_call" | custom-call | flops 805306368 | bytes 3145728 | tf_op jit(solution)/shard_map/pallas_call | solution.py:135
  13.3 1.6 %collective-permute-start.4 = (bf16[256,768]{1,0:T(8,128)(2,1)}, bf16[256,768]{1,0:T(8,128)(2,1)S(1)}, u32[]{:S(2)}, u32[]{:S(2)}) collective-permute-start(bf16[256,768]{1,0:T(8,128)(2,1)} %get-tuple-element.34.refs_0_), channel_id=1, source_target_pairs={{0,16},{1,17},{2,18},{3,19},{4,20},{5,21},{6,22},{7,23},{8,24},{9,... | collective-permute-start | bytes 1179656 | tf_op jit(solution)/shard_map/ppermute | solution.py:371
  14.8 1.5 %collective-permute-start.2 = (bf16[256,768]{1,0:T(8,128)(2,1)}, bf16[256,768]{1,0:T(8,128)(2,1)S(1)}, u32[]{:S(2)}, u32[]{:S(2)}) collective-permute-start(bf16[256,768]{1,0:T(8,128)(2,1)} %get-tuple-element.34.refs_0_), channel_id=1, source_target_pairs={{0,1},{1,0},{2,3},{3,2},{4,5},{5,4},{6,7},{7,6},{8,9},{9,8},{10,11... | collective-permute-start | bytes 1179656 | tf_op jit(solution)/shard_map/ppermute | solution.py:371
  16.3 7.7 %collective-permute-done.first_ref = bf16[256,768]{1,0:T(8,128)(2,1)S(1)} collective-permute-done((bf16[256,768]{1,0:T(8,128)(2,1)}, bf16[256,768]{1,0:T(8,128)(2,1)S(1)}, u32[]{:S(2)}, u32[]{:S(2)}) %collective-permute-start) | collective-permute-done | bytes 393248 | tf_op jit(solution)/shard_map/ppermute | solution.py:371
  24.1 2.5 %collective-permute-done.1.second_ref = bf16[256,768]{1,0:T(8,128)(2,1)S(1)} collective-permute-done((bf16[256,768]{1,0:T(8,128)(2,1)}, bf16[256,768]{1,0:T(8,128)(2,1)S(1)}, u32[]{:S(2)}, u32[]{:S(2)}) %collective-permute-start.1) | collective-permute-done | bytes 393248 | tf_op jit(solution)/shard_map/ppermute | solution.py:371
  26.6 0.1 shard_map.39.refs_1_
  26.7 1.5 %collective-permute-start.8 = (bf16[512,768]{1,0:T(8,128)(2,1)S(1)}, bf16[512,768]{1,0:T(8,128)(2,1)S(1)}, u32[]{:S(2)}, u32[]{:S(2)}) collective-permute-start(bf16[512,768]{1,0:T(8,128)(2,1)S(1)} %shard_map.39.refs_1_), channel_id=1, source_target_pairs={{0,16},{1,17},{2,18},{3,19},{4,20},{5,21},{6,22},{7,23},{8,24},{9,... | collective-permute-start | bytes 2359304 | tf_op jit(solution)/shard_map/ppermute | solution.py:371
  28.2 1.5 %collective-permute-start.6 = (bf16[512,768]{1,0:T(8,128)(2,1)S(1)}, bf16[512,768]{1,0:T(8,128)(2,1)S(1)}, u32[]{:S(2)}, u32[]{:S(2)}) collective-permute-start(bf16[512,768]{1,0:T(8,128)(2,1)S(1)} %shard_map.39.refs_1_), channel_id=1, source_target_pairs={{0,1},{1,0},{2,3},{3,2},{4,5},{5,4},{6,7},{7,6},{8,9},{9,8},{10,11... | collective-permute-start | bytes 2359304 | tf_op jit(solution)/shard_map/ppermute | solution.py:371
  29.7 2.5 %collective-permute-start.5 = (bf16[256,768]{1,0:T(8,128)(2,1)S(1)}, bf16[256,768]{1,0:T(8,128)(2,1)S(1)}, u32[]{:S(2)}, u32[]{:S(2)}) collective-permute-start(bf16[256,768]{1,0:T(8,128)(2,1)S(1)} %copy-done.3), channel_id=1, source_target_pairs={{0,6},{1,7},{2,4},{3,5},{4,2},{5,3},{6,0},{7,1},{8,14},{9,15},{10,... | collective-permute-start | bytes 1179656 | tf_op jit(solution)/shard_map/ppermute | solution.py:371
  32.2 17.7 %all_to_all.10.label_ref = f32[32,1,256]{2,1,0:T(1,128)S(1)} all-to-all(f32[32,1,256]{2,1,0:T(1,128)S(1)} %copy-done.2), channel_id=1, replica_groups=mesh['grp'=4,'mem'=8] {'grp','mem'}, dimensions={0} | all-to-all | bytes 65536 | tf_op jit(solution)/shard_map/all_to_all | solution.py:411
  50.0 0.1 collective-permute-start.13
  50.1 0.5 collective-permute-start.12
  50.5 1.4 %collective-permute-start.11 = (bf16[256,768]{1,0:T(8,128)(2,1)S(1)}, bf16[256,768]{1,0:T(8,128)(2,1)S(1)}, u32[]{:S(2)}, u32[]{:S(2)}) collective-permute-start(bf16[256,768]{1,0:T(8,128)(2,1)S(1)} %collective-permute-done.5.refs_2_), channel_id=1, source_target_pairs={{0,16},{1,17},{2,18},{3,19},{4,20},{5,21},{6,22},{7,23},{8,24},{9,... | collective-permute-start | bytes 1179656 | tf_op jit(solution)/shard_map/ppermute | solution.py:371
  52.0 1.6 %collective-permute-start.9 = (bf16[256,768]{1,0:T(8,128)(2,1)S(1)}, bf16[256,768]{1,0:T(8,128)(2,1)S(1)}, u32[]{:S(2)}, u32[]{:S(2)}) collective-permute-start(bf16[256,768]{1,0:T(8,128)(2,1)S(1)} %collective-permute-done.5.refs_2_), channel_id=1, source_target_pairs={{0,1},{1,0},{2,3},{3,2},{4,5},{5,4},{6,7},{7,6},{8,9},{9,8},{10,11... | collective-permute-start | bytes 1179656 | tf_op jit(solution)/shard_map/ppermute | solution.py:371
  53.5 5.8 %shard_map.40.refs_15_ = f32[5,8,256]{2,1,0:T(8,128)S(1)} custom-call(f32[32,1,256]{2,1,0:T(1,128)S(1)} %all_to_all.10.label_ref, bf16[256,768]{1,0:T(8,128)(2,1)S(1)} %copy-done.1, bf16[512,768]{1,0:T(8,128)(2,1)S(1)} %shard_map.39.refs_1_, bf16[256,768]{1,0:T(8,128)(2,1)S(1)} %collective-permute-done.5.refs_2_, ...), custom_call_target="tpu_custom_call" | custom-call | flops 4026531840 | bytes 6291456 | tf_op jit(solution)/shard_map/pallas_call | solution.py:282
  59.4 0.0 copy-start
  59.4 2.3 %collective-permute-done.11.refs_11_ = bf16[256,768]{1,0:T(8,128)(2,1)S(1)} collective-permute-done((bf16[256,768]{1,0:T(8,128)(2,1)S(1)}, bf16[256,768]{1,0:T(8,128)(2,1)S(1)}, u32[]{:S(2)}, u32[]{:S(2)}) %collective-permute-start.11) | collective-permute-done | bytes 393248 | tf_op jit(solution)/shard_map/ppermute | solution.py:371
  61.6 1.8 %collective-permute-done.9.refs_5_ = bf16[256,768]{1,0:T(8,128)(2,1)S(1)} collective-permute-done((bf16[256,768]{1,0:T(8,128)(2,1)S(1)}, bf16[256,768]{1,0:T(8,128)(2,1)S(1)}, u32[]{:S(2)}, u32[]{:S(2)}) %collective-permute-start.9) | collective-permute-done | bytes 393248 | tf_op jit(solution)/shard_map/ppermute | solution.py:371
  63.5 5.6 %shard_map.41 = f32[8,1,256]{2,1,0:T(1,128)S(1)} custom-call(f32[32,1,256]{2,1,0:T(1,128)S(1)} %all_to_all.10.label_ref, bf16[256,768]{1,0:T(8,128)(2,1)S(1)} %copy-done.1, bf16[512,768]{1,0:T(8,128)(2,1)S(1)} %shard_map.39.refs_1_, bf16[256,768]{1,0:T(8,128)(2,1)S(1)} %collective-permute-done.5.refs_2_, ...), custom_call_target="tpu_custom_call" | custom-call | flops 4026531840 | bytes 7864320 | tf_op jit(solution)/shard_map/pallas_call | solution.py:282
  69.1 9.9 %all_to_all.11.back_ref = f32[8,1,256]{2,1,0:T(1,128)S(1)} all-to-all(f32[8,1,256]{2,1,0:T(1,128)S(1)} %shard_map.41), channel_id=1, replica_groups=mesh['grp'=4,'mem'=8] {'mem'}, dimensions={0} | all-to-all | bytes 16384 | tf_op jit(solution)/shard_map/all_to_all | solution.py:472
  79.1 1.1 %shard_map.42 = f32[1,1024]{1,0:T(1,128)} custom-call(s32[1,1024]{1,0:T(1,128)S(1)} %copy-done, f32[8,1,256]{2,1,0:T(1,128)S(1)} %all_to_all.11.back_ref), custom_call_target="tpu_custom_call" | custom-call | tf_op jit(solution)/shard_map/pallas_call | solution.py:346
  (22 shorter events, 0.1 us)
Async XLA Ops:
  3.3 20.7 %collective-permute-start = (bf16[256,768]{1,0:T(8,128)(2,1)}, bf16[256,768]{1,0:T(8,128)(2,1)S(1)}, u32[]{:S(2)}, u32[]{:S(2)}) collective-permute-start(bf16[256,768]{1,0:T(8,128)(2,1)} %get-tuple-element.32), channel_id=1, source_target_pairs={{0,2},{1,3},{2,0},{3,1},{4,6},{5,7},{6,4},{7,5},{8,10},{9,11},{10,... | collective-permute-start | bytes 1179656 | tf_op jit(solution)/shard_map/ppermute | solution.py:371
  6.4 20.2 %collective-permute-start.1 = (bf16[256,768]{1,0:T(8,128)(2,1)}, bf16[256,768]{1,0:T(8,128)(2,1)S(1)}, u32[]{:S(2)}, u32[]{:S(2)}) collective-permute-start(bf16[256,768]{1,0:T(8,128)(2,1)} %get-tuple-element.33), channel_id=1, source_target_pairs={{0,4},{1,5},{2,6},{3,7},{4,0},{5,1},{6,2},{7,3},{8,12},{9,13},{10,... | collective-permute-start | bytes 1179656 | tf_op jit(solution)/shard_map/ppermute | solution.py:371
  13.2 16.5 %copy-start.3 = (bf16[256,768]{1,0:T(8,128)(2,1)S(1)}, bf16[256,768]{1,0:T(8,128)(2,1)}, u32[]{:S(2)}) copy-start(bf16[256,768]{1,0:T(8,128)(2,1)} %get-tuple-element.39) | copy-start | bytes 1179652
  13.2 19.0 %copy-start.2 = (f32[32,1,256]{2,1,0:T(1,128)S(1)}, f32[32,1,256]{2,1,0:T(1,128)}, u32[]{:S(2)}) copy-start(f32[32,1,256]{2,1,0:T(1,128)} %get-tuple-element.40) | copy-start | bytes 98308
  13.3 40.3 %copy-start.1 = (bf16[256,768]{1,0:T(8,128)(2,1)S(1)}, bf16[256,768]{1,0:T(8,128)(2,1)}, u32[]{:S(2)}) copy-start(bf16[256,768]{1,0:T(8,128)(2,1)} %get-tuple-element.34.refs_0_) | copy-start | bytes 1179652
  13.3 13.3 %collective-permute-start.4 = (bf16[256,768]{1,0:T(8,128)(2,1)}, bf16[256,768]{1,0:T(8,128)(2,1)S(1)}, u32[]{:S(2)}, u32[]{:S(2)}) collective-permute-start(bf16[256,768]{1,0:T(8,128)(2,1)} %get-tuple-element.34.refs_0_), channel_id=1, source_target_pairs={{0,16},{1,17},{2,18},{3,19},{4,20},{5,21},{6,22},{7,23},{8,24},{9,... | collective-permute-start | bytes 1179656 | tf_op jit(solution)/shard_map/ppermute | solution.py:371
  14.8 11.8 %collective-permute-start.3 = (bf16[256,768]{1,0:T(8,128)(2,1)}, bf16[256,768]{1,0:T(8,128)(2,1)S(1)}, u32[]{:S(2)}, u32[]{:S(2)}) collective-permute-start(bf16[256,768]{1,0:T(8,128)(2,1)} %get-tuple-element.34.refs_0_), channel_id=1, source_target_pairs={{0,8},{1,9},{2,10},{3,11},{4,12},{5,13},{6,14},{7,15},{8,0},{9,1},... | collective-permute-start | bytes 1179656 | tf_op jit(solution)/shard_map/ppermute | solution.py:371
  14.8 11.8 %collective-permute-start.2 = (bf16[256,768]{1,0:T(8,128)(2,1)}, bf16[256,768]{1,0:T(8,128)(2,1)S(1)}, u32[]{:S(2)}, u32[]{:S(2)}) collective-permute-start(bf16[256,768]{1,0:T(8,128)(2,1)} %get-tuple-element.34.refs_0_), channel_id=1, source_target_pairs={{0,1},{1,0},{2,3},{3,2},{4,5},{5,4},{6,7},{7,6},{8,9},{9,8},{10,11... | collective-permute-start | bytes 1179656 | tf_op jit(solution)/shard_map/ppermute | solution.py:371
  26.7 23.3 %collective-permute-start.8 = (bf16[512,768]{1,0:T(8,128)(2,1)S(1)}, bf16[512,768]{1,0:T(8,128)(2,1)S(1)}, u32[]{:S(2)}, u32[]{:S(2)}) collective-permute-start(bf16[512,768]{1,0:T(8,128)(2,1)S(1)} %shard_map.39.refs_1_), channel_id=1, source_target_pairs={{0,16},{1,17},{2,18},{3,19},{4,20},{5,21},{6,22},{7,23},{8,24},{9,... | collective-permute-start | bytes 2359304 | tf_op jit(solution)/shard_map/ppermute | solution.py:371
  28.2 21.7 %collective-permute-start.7 = (bf16[512,768]{1,0:T(8,128)(2,1)S(1)}, bf16[512,768]{1,0:T(8,128)(2,1)S(1)}, u32[]{:S(2)}, u32[]{:S(2)}) collective-permute-start(bf16[512,768]{1,0:T(8,128)(2,1)S(1)} %shard_map.39.refs_1_), channel_id=1, source_target_pairs={{0,8},{1,9},{2,10},{3,11},{4,12},{5,13},{6,14},{7,15},{8,0},{9,1},... | collective-permute-start | bytes 2359304 | tf_op jit(solution)/shard_map/ppermute | solution.py:371
  28.2 21.7 %collective-permute-start.6 = (bf16[512,768]{1,0:T(8,128)(2,1)S(1)}, bf16[512,768]{1,0:T(8,128)(2,1)S(1)}, u32[]{:S(2)}, u32[]{:S(2)}) collective-permute-start(bf16[512,768]{1,0:T(8,128)(2,1)S(1)} %shard_map.39.refs_1_), channel_id=1, source_target_pairs={{0,1},{1,0},{2,3},{3,2},{4,5},{5,4},{6,7},{7,6},{8,9},{9,8},{10,11... | collective-permute-start | bytes 2359304 | tf_op jit(solution)/shard_map/ppermute | solution.py:371
  29.7 20.2 %collective-permute-start.5 = (bf16[256,768]{1,0:T(8,128)(2,1)S(1)}, bf16[256,768]{1,0:T(8,128)(2,1)S(1)}, u32[]{:S(2)}, u32[]{:S(2)}) collective-permute-start(bf16[256,768]{1,0:T(8,128)(2,1)S(1)} %copy-done.3), channel_id=1, source_target_pairs={{0,6},{1,7},{2,4},{3,5},{4,2},{5,3},{6,0},{7,1},{8,14},{9,15},{10,... | collective-permute-start | bytes 1179656 | tf_op jit(solution)/shard_map/ppermute | solution.py:371
  50.0 3.6 %collective-permute-start.13 = (bf16[512,768]{1,0:T(8,128)(2,1)S(1)}, bf16[512,768]{1,0:T(8,128)(2,1)S(1)}, u32[]{:S(2)}, u32[]{:S(2)}) collective-permute-start(bf16[512,768]{1,0:T(8,128)(2,1)S(1)} %collective-permute-done.8.refs_8_.refs_10_), channel_id=1, source_target_pairs={{0,8},{1,9},{2,10},{3,11},{4,12},{5,13},{6,14},{7,15},{8,0},{9,1},... | collective-permute-start | bytes 2359304 | tf_op jit(solution)/shard_map/ppermute | solution.py:371
  50.1 3.4 %collective-permute-start.12 = (bf16[256,768]{1,0:T(8,128)(2,1)S(1)}, bf16[256,768]{1,0:T(8,128)(2,1)S(1)}, u32[]{:S(2)}, u32[]{:S(2)}) collective-permute-start(bf16[256,768]{1,0:T(8,128)(2,1)S(1)} %collective-permute-done.4.refs_7_.refs_9_), channel_id=1, source_target_pairs={{0,8},{1,9},{2,10},{3,11},{4,12},{5,13},{6,14},{7,15},{8,0},{9,1},... | collective-permute-start | bytes 1179656 | tf_op jit(solution)/shard_map/ppermute | solution.py:371
  50.5 11.1 %collective-permute-start.11 = (bf16[256,768]{1,0:T(8,128)(2,1)S(1)}, bf16[256,768]{1,0:T(8,128)(2,1)S(1)}, u32[]{:S(2)}, u32[]{:S(2)}) collective-permute-start(bf16[256,768]{1,0:T(8,128)(2,1)S(1)} %collective-permute-done.5.refs_2_), channel_id=1, source_target_pairs={{0,16},{1,17},{2,18},{3,19},{4,20},{5,21},{6,22},{7,23},{8,24},{9,... | collective-permute-start | bytes 1179656 | tf_op jit(solution)/shard_map/ppermute | solution.py:371
  52.0 9.7 %collective-permute-start.10 = (bf16[256,768]{1,0:T(8,128)(2,1)S(1)}, bf16[256,768]{1,0:T(8,128)(2,1)S(1)}, u32[]{:S(2)}, u32[]{:S(2)}) collective-permute-start(bf16[256,768]{1,0:T(8,128)(2,1)S(1)} %collective-permute-done.5.refs_2_), channel_id=1, source_target_pairs={{0,8},{1,9},{2,10},{3,11},{4,12},{5,13},{6,14},{7,15},{8,0},{9,1},... | collective-permute-start | bytes 1179656 | tf_op jit(solution)/shard_map/ppermute | solution.py:371
  52.0 11.5 %collective-permute-start.9 = (bf16[256,768]{1,0:T(8,128)(2,1)S(1)}, bf16[256,768]{1,0:T(8,128)(2,1)S(1)}, u32[]{:S(2)}, u32[]{:S(2)}) collective-permute-start(bf16[256,768]{1,0:T(8,128)(2,1)S(1)} %collective-permute-done.5.refs_2_), channel_id=1, source_target_pairs={{0,1},{1,0},{2,3},{3,2},{4,5},{5,4},{6,7},{7,6},{8,9},{9,8},{10,11... | collective-permute-start | bytes 1179656 | tf_op jit(solution)/shard_map/ppermute | solution.py:371
  59.4 19.7 %copy-start = (s32[1,1024]{1,0:T(1,128)S(1)}, s32[1,1024]{1,0:T(1,128)}, u32[]{:S(2)}) copy-start(s32[1,1024]{1,0:T(1,128)} %get-tuple-element.30.dest_ref) | copy-start | bytes 12292
  61.6 1.9 %collective-permute-start.14 = (bf16[256,768]{1,0:T(8,128)(2,1)S(1)}, bf16[256,768]{1,0:T(8,128)(2,1)S(1)}, u32[]{:S(2)}, u32[]{:S(2)}) collective-permute-start(bf16[256,768]{1,0:T(8,128)(2,1)S(1)} %collective-permute-done.11.refs_11_), channel_id=1, source_target_pairs={{0,8},{1,9},{2,10},{3,11},{4,12},{5,13},{6,14},{7,15},{8,0},{9,1},... | collective-permute-start | bytes 1179656 | tf_op jit(solution)/shard_map/ppermute | solution.py:371

commit v10 on v9

--- a/solution.py
+++ b/solution.py
@@ -152,7 +152,7 @@
     )(embeddings, cluster.reshape(1, rows), rank.reshape(1, rows))
 
 
-def compare_kernel(sizes, jobs, names, spots, offsets, joined, has_prev, label_ref, *refs):
+def compare_kernel(sizes, jobs, names, spots, offsets, starts, joined, has_prev, label_ref, *refs):
     groups, halves, half, cap, blk = sizes
     array = dict(zip(names, refs))
     refs = refs[len(names) :]
@@ -160,7 +160,7 @@
     prev = None
     if has_prev:
         prev, refs = refs[0], refs[1:]
-    outs, (key_col, key_row, low_row, turned, best) = refs[:-5], refs[-5:]
+    outs, (key_col, turned, best) = refs[:-3], refs[-3:]
     rows = groups * blk
     per_tile = blk // TILES
     tile = rows // TILES
@@ -180,7 +180,7 @@
     weights = jnp.where(weight_row == 0, 1.0, jnp.where(weight_row == 1, float(half), 0.0))
     weights = weights.astype(jnp.bfloat16)
     field = lax.broadcasted_iota(jnp.int32, (LABEL_ROWS, blk), 0)
-    needed = sorted({piece for _, pieces in jobs for piece in pieces})
+    needed = sorted({piece for *_, pieces in jobs for piece in pieces})
     key_at = {piece: n * blk for n, piece in enumerate(needed)}
     for piece in needed:
         key = keys_of(piece)
@@ -190,53 +190,70 @@
             split.astype(jnp.bfloat16), weights, TN, preferred_element_type=jnp.float32
         )
     lane = lax.div(lax.broadcasted_iota(jnp.int32, (1, tile), 1), per_tile)
-    for o, (a, _) in enumerate(jobs):
-        keys = [keys_of((a, k)) for k in range(groups)]
+
+    def floor_of(key):
+        low = jnp.floor(key * (1.0 / cap_all)) * cap_all
+        return jnp.where(low > 0.5, low, FAR)
+
+    def lines_of(a, ks):
+        keys = [keys_of((a, k)) if k in ks else jnp.zeros((1, blk), jnp.float32) for k in range(groups)]
         keys = [jnp.concatenate([key] * (tile // blk), axis=1) for key in keys]
+        lines = []
         for t in range(TILES):
             line = jnp.zeros((1, tile), jnp.float32)
             for k in range(groups):
                 turn = ((k - t) * per_tile) % tile
                 moved = pltpu.roll(keys[k], turn, 1) if turn else keys[k]
                 line = jnp.where(lane == k, moved, line)
-            low = jnp.floor(line * (1.0 / cap_all)) * cap_all
-            key_row[o, t : t + 1, :] = line
-            low_row[o, t : t + 1, :] = jnp.where(low > 0.5, low, FAR)
+            lines.append(line)
+        return lines
 
     def rows_of(ref, base, first, last):
         return ref[base + first * per_tile : base + last * per_tile, :]
 
     best[...] = prev[...] if has_prev else jnp.full(best.shape, -1.0, jnp.float32)
-    for o, (a, pieces) in enumerate(jobs):
+
+    def search(a, row, queries, mine, pieces, last, spot):
+        width = mine.shape[1]
+        turned[spot, :, 0:width] = jnp.concatenate(queries, axis=0).T
+        floor = floor_of(mine)
+        acc = jnp.full((8, width), -1.0, jnp.float32)
+        for at in range(0, len(pieces), groups):
+            some = pieces[at : at + groups]
+            theirs = [rows_of(key_col, key_at[piece], 0, last) for piece in some]
+            theirs = jnp.concatenate(theirs, axis=0)
+            theirs = jnp.concatenate([theirs] * (width // 128), axis=1)
+            sims = jnp.dot(
+                jnp.concatenate([rows_of(*block[piece], 0, last) for piece in some], axis=0),
+                turned[spot, :, 0:width],
+                preferred_element_type=jnp.float32,
+            )
+            keep = (theirs >= floor) & (theirs < mine)
+            sims = jnp.where(keep, sims, -1.0)
+            top = jnp.max(sims.reshape(sims.shape[0] // 8, 8, width), axis=0)
+            acc = jnp.maximum(acc, top)
+        best[a, row : row + 1, 0:width] = jnp.maximum(
+            best[a, row : row + 1, 0:width], jnp.max(acc, axis=0, keepdims=True)
+        )
+
+    spot = 0
+    for a, whole, ks, pieces in jobs:
+        if whole:
+            (k,) = ks
+            queries = [rows_of(*block[a, k], 0, TILES)]
+            search(a, TILES, queries, keys_of((a, k)), pieces, TILES, spot)
+            spot += 1
+            continue
+        lines = lines_of(a, ks)
         for t in range(TILES):
-            turned[o, t] = jnp.concatenate(
-                [rows_of(*block[a, k], t, t + 1) for k in range(groups)], axis=0
-            ).T
-            mine = key_row[o, t : t + 1, :]
-            floor = low_row[o, t : t + 1, :]
-            acc = jnp.full((8, tile), -1.0, jnp.float32)
-            for at in range(0, len(pieces), groups):
-                some = pieces[at : at + groups]
-                theirs = [rows_of(key_col, key_at[piece], 0, t + 1) for piece in some]
-                theirs = jnp.concatenate(theirs, axis=0)
-                theirs = jnp.concatenate([theirs] * (tile // 128), axis=1)
-                sims = jnp.dot(
-                    jnp.concatenate([rows_of(*block[piece], 0, t + 1) for piece in some], axis=0),
-                    turned[o, t],
-                    preferred_element_type=jnp.float32,
-                )
-                keep = (theirs >= floor) & (theirs < mine)
-                sims = jnp.where(keep, sims, -1.0)
-                top = jnp.max(sims.reshape(sims.shape[0] // 8, 8, tile), axis=0)
-                acc = jnp.maximum(acc, top)
-            best[a, t : t + 1, :] = jnp.maximum(
-                best[a, t : t + 1, :], jnp.max(acc, axis=0, keepdims=True)
-            )
-
-    if not has_prev:
+            queries = [rows_of(*block[a, k if k in ks else ks[0]], t, t + 1) for k in range(groups)]
+            search(a, t, queries, lines[t], pieces, t + 1, spot)
+            spot += 1
+
+    if not starts:
         outs[0][...] = best[...]
         return
-    for o, (a, _) in enumerate(jobs):
+    for o, a in enumerate(starts):
         found = best[a]
         for k in range(groups):
             total = jnp.full((1, tile), -1.0, jnp.float32)
@@ -244,6 +261,8 @@
                 turn = ((t - k) * per_tile) % tile
                 moved = pltpu.roll(found, turn, 1) if turn else found
                 total = jnp.where(lane == t, moved[t : t + 1], total)
+            if any(a == e and whole and k in ks for e, whole, ks, _ in jobs):
+                total = jnp.maximum(total, found[TILES : TILES + 1])
             at = (along // side) ^ k
             if joined:
                 outs[0][pl.ds(at * joined + ((along % side) ^ a), 1), 0, :] = total[:, :blk]
@@ -251,11 +270,12 @@
                 outs[o][pl.ds(at, 1), 0, :] = total[:, :blk]
 
 
-def compare(labels, blocks, jobs, prev, joined, offsets, sizes):
+def compare(labels, blocks, jobs, prev, starts, joined, offsets, sizes):
     groups, halves, half, cap, blk = sizes
     n_sets = len(offsets)
-    used = {piece for _, pieces in jobs for piece in pieces}
-    used |= {(a, k) for a, _ in jobs for k in range(groups)}
+    used = {piece for *_, pieces in jobs for piece in pieces}
+    used |= {(a, k) for a, _, ks, _ in jobs for k in ks}
+    searches = sum(1 if whole else TILES for _, whole, _, _ in jobs)
     spots = {}
     arrays = {}
     for piece in sorted(used):
@@ -269,33 +289,32 @@
     width = arrays[0].shape[1]
     tile = groups * blk // TILES
     vmem = pl.BlockSpec(memory_space=pltpu.VMEM)
-    steps = TILES * (TILES + 1) // 2
-    work = sum(len(pieces) for _, pieces in jobs) * steps * (blk // TILES) * tile * width
-    if prev is None:
+    work = blk * tile * width * sum(
+        len(pieces) * (1.0 if whole else (TILES + 1) / 2 / TILES) for _, whole, _, pieces in jobs
+    )
+    if not starts:
         out_shape = [jax.ShapeDtypeStruct((n_sets, 8, tile), jnp.float32)]
     elif joined:
         out_shape = [jax.ShapeDtypeStruct((groups * joined, 1, blk), jnp.float32)]
     else:
-        out_shape = [jax.ShapeDtypeStruct((groups, 1, blk), jnp.float32)] * len(jobs)
+        out_shape = [jax.ShapeDtypeStruct((groups, 1, blk), jnp.float32)] * len(starts)
     operands = [labels] + list(arrays.values()) + ([] if prev is None else [prev])
-    needed = {piece for _, pieces in jobs for piece in pieces}
+    needed = {piece for *_, pieces in jobs for piece in pieces}
     return pl.pallas_call(
         functools.partial(
-            compare_kernel, sizes, jobs, names, spots, offsets, joined, prev is not None
+            compare_kernel, sizes, jobs, names, spots, offsets, starts, joined, prev is not None
         ),
         out_shape=out_shape,
         in_specs=[vmem] * len(operands),
         out_specs=[vmem] * len(out_shape),
         scratch_shapes=[
             pltpu.VMEM((len(needed) * blk, 128), jnp.float32),
-            pltpu.VMEM((len(jobs), 8, tile), jnp.float32),
-            pltpu.VMEM((len(jobs), 8, tile), jnp.float32),
-            pltpu.VMEM((len(jobs), TILES, width, tile), jnp.bfloat16),
+            pltpu.VMEM((searches, width, tile), jnp.bfloat16),
             pltpu.VMEM((n_sets, 8, tile), jnp.float32),
         ],
         compiler_params=pltpu.CompilerParams(vmem_limit_bytes=COMPARE_VMEM),
         cost_estimate=pl.CostEstimate(
-            flops=2 * work, bytes_accessed=2 * len(used) * blk * width, transcendentals=0
+            flops=int(2 * work), bytes_accessed=2 * len(used) * blk * width, transcendentals=0
         ),
     )(*operands)
 
@@ -417,11 +436,14 @@
             held[d].append(swap(mine, 0, d))
     for spot in range(1, len(held[0]) - 1):
         held[0][spot + 1], labels, *values = lax.optimization_barrier(
-            (held[0][spot + 1], labels, *(held[d][spot] for d in near))
+            (held[0][spot + 1], labels, *(held[d][0] for d in far), *(held[d][spot] for d in near))
         )
+        for d in far:
+            held[d][0] = values.pop(0)
         for d, value in zip(near, values):
             held[d][spot] = value
-        for d in far:
+    for d in far:
+        for spot in range(1, len(held[0]) - 1):
             held[d].append(swap(held[d ^ side][spot], 0, side))
 
     index = {d: i for i, d in enumerate(offsets)}
@@ -436,22 +458,32 @@
 
     note()
     starts = sorted({a for a, _ in pairs.values()})
-    early, late = [], []
+    every = tuple(range(groups))
+    early, middle, late = [], [], []
     for a in starts:
         cols = [index[b] for _, (e, b) in sorted(pairs.items()) if e == a]
-        pieces = [(b, k) for b in cols for k in range(groups)]
+        pieces = [(b, k) for b in cols for k in every]
+        soon = [(b, k) for b, k in pieces if k < last]
         if a == 0:
-            soon = [(b, k) for b, k in pieces if b == 0 or k < last]
-            early.append((0, soon))
-            pieces = [piece for piece in pieces if piece not in soon]
-        late.append((index[a], pieces))
+            slow = {(index[d], k) for d in far for k in range(1, last)} | {(index[side], last)}
+            ready = [piece for piece in pieces if piece in soon or piece[0] == 0]
+            early.append((0, False, every, [piece for piece in ready if piece not in slow]))
+            middle.append((0, False, every, [piece for piece in pieces if piece in slow]))
+            done = early[-1][-1] + middle[-1][-1]
+            late.append((0, False, every, [piece for piece in pieces if piece not in done]))
+        else:
+            middle.append((index[a], False, every[:-1], soon))
+            late.append((index[a], False, every, [piece for piece in pieces if piece not in soon]))
+            late.append((index[a], True, (last,), soon))
+    order = [index[a] for a in starts]
     joined = side if all(a < side for a in starts) else 0
-    prev = compare(labels, blocks, early, None, 0, offsets, sizes)[0]
+    prev = compare(labels, blocks, early, None, (), 0, offsets, sizes)[0]
+    prev = compare(labels, blocks, middle, prev, (), 0, offsets, sizes)[0]
     for d in far:
         piece, prev = lax.optimization_barrier((held[d ^ side][-1], prev))
         held[d].append(swap(piece, 0, side))
     note()
-    found = compare(labels, blocks, late, prev, joined, offsets, sizes)
+    found = compare(labels, blocks, late, prev, order, joined, offsets, sizes)
     if joined:
         back = found[0]
     else:

time: 80.4 us -> 78.3 us (0.974)
  waiting for transfers between devices: 14.4 us -> 12 us
    ppermute x15, waiting for transfers between devices: 14.4 us -> 12 us  [swap(): lax.ppermute(value, ('grp', 'mem'), [(i, i ^ mask) for i in range(devices)])]
    pallas_call x2 -> x3, Pallas kernels: 11.4 us -> 11.5 us  [compare(): pl.pallas_call(functools.partial(compare_kernel, sizes, jobs, names, spot...]
  transfers between devices with their start and end apart: 15 -> 15, of which waited for: 4 -> 5; matrix products, arithmetic and copies ran while one was open for 0% -> 0% of each run, Pallas kernels for 13% -> 16%
where the time goes in v10:
time: 78.3 us; the launch traced here: 78.1 us
  blocking collectives  27.6 us (35%)
  Pallas kernels  20.1 us (26%)
  starting transfers between devices  18.1 us (23%)
  waiting for transfers between devices  12 us (15%)
    ppermute x15, starting transfers between devices, swap(): lax.ppermute(value, ('grp', 'mem'), [(i, i ^ mask) for i in range(devices)])  18.1 us
    all_to_all x1, blocking collectives, on_device(): lax.all_to_all(labels, ('grp', 'mem'), split_axis=0, concat_axis=0, tiled...  17.8 us
    ppermute x15, waiting for transfers between devices, swap(): lax.ppermute(value, ('grp', 'mem'), [(i, i ^ mask) for i in range(devices)])  12 us
    pallas_call x3, Pallas kernels, compare(): pl.pallas_call(functools.partial(compare_kernel, sizes, jobs, names, spot...  11.5 us
    all_to_all x1, blocking collectives, on_device(): back = lax.all_to_all(back, 'mem', split_axis=0, concat_axis=0, tiled=True)  9.87 us
    pallas_call x2, Pallas kernels, pack(): pl.pallas_call(functools.partial(pack_kernel, sizes, ks, labelled), out_s...  7.54 us
  transfers between devices with their start and end apart: 15, of which 5 were waited for; matrix products, arithmetic and copies ran while one was open for 0% of the time, Pallas kernels for 16%

profile of v10, /device:TPU:0, one launch (start us, length us, event | category | flops | bytes accessed | tf_op | source)
XLA Modules:
  0.0 78.1 jit_solution(13380866841066458028)
XLA Ops:
  0.0 3.3 %shard_map.37 = (bf16[256,768]{1,0:T(8,128)(2,1)}, bf16[256,768]{1,0:T(8,128)(2,1)}) custom-call(bf16[1024,768]{1,0:T(8,128)(2,1)} %emb_hbm.3, s32[1,1024]{1,0:T(1,128)} %bitcast.4, s32[1,1024]{1,0:T(1,128)} %bitcast.6), custom_call_target="tpu_custom_call" | custom-call | flops 805306368 | bytes 3145728 | tf_op jit(solution)/shard_map/pallas_call | solution.py:135
  3.3 3.1 %collective-permute-start = (bf16[256,768]{1,0:T(8,128)(2,1)}, bf16[256,768]{1,0:T(8,128)(2,1)S(1)}, u32[]{:S(2)}, u32[]{:S(2)}) collective-permute-start(bf16[256,768]{1,0:T(8,128)(2,1)} %get-tuple-element.33), channel_id=1, source_target_pairs={{0,2},{1,3},{2,0},{3,1},{4,6},{5,7},{6,4},{7,5},{8,10},{9,11},{10,... | collective-permute-start | bytes 1179656 | tf_op jit(solution)/shard_map/ppermute | solution.py:390
  6.4 2.6 %collective-permute-start.1 = (bf16[256,768]{1,0:T(8,128)(2,1)}, bf16[256,768]{1,0:T(8,128)(2,1)S(1)}, u32[]{:S(2)}, u32[]{:S(2)}) collective-permute-start(bf16[256,768]{1,0:T(8,128)(2,1)} %get-tuple-element.34), channel_id=1, source_target_pairs={{0,4},{1,5},{2,6},{3,7},{4,0},{5,1},{6,2},{7,3},{8,12},{9,13},{10,... | collective-permute-start | bytes 1179656 | tf_op jit(solution)/shard_map/ppermute | solution.py:390
  9.0 4.2 %shard_map.38 = (bf16[256,768]{1,0:T(8,128)(2,1)}, bf16[256,768]{1,0:T(8,128)(2,1)}, s32[1,1024]{1,0:T(1,128)}, f32[32,1,256]{2,1,0:T(1,128)}) custom-call(bf16[1024,768]{1,0:T(8,128)(2,1)} %emb_hbm.3, s32[1,1024]{1,0:T(1,128)} %bitcast.5, s32[1,1024]{1,0:T(1,128)} %bitcast.7), custom_call_target="tpu_custom_call" | custom-call | flops 805306368 | bytes 3145728 | tf_op jit(solution)/shard_map/pallas_call | solution.py:135
  13.3 1.6 %collective-permute-start.4 = (bf16[256,768]{1,0:T(8,128)(2,1)}, bf16[256,768]{1,0:T(8,128)(2,1)S(1)}, u32[]{:S(2)}, u32[]{:S(2)}) collective-permute-start(bf16[256,768]{1,0:T(8,128)(2,1)} %get-tuple-element.35.refs_0_), channel_id=1, source_target_pairs={{0,16},{1,17},{2,18},{3,19},{4,20},{5,21},{6,22},{7,23},{8,24},{9,... | collective-permute-start | bytes 1179656 | tf_op jit(solution)/shard_map/ppermute | solution.py:390
  14.8 1.5 %collective-permute-start.2 = (bf16[256,768]{1,0:T(8,128)(2,1)}, bf16[256,768]{1,0:T(8,128)(2,1)S(1)}, u32[]{:S(2)}, u32[]{:S(2)}) collective-permute-start(bf16[256,768]{1,0:T(8,128)(2,1)} %get-tuple-element.35.refs_0_), channel_id=1, source_target_pairs={{0,1},{1,0},{2,3},{3,2},{4,5},{5,4},{6,7},{7,6},{8,9},{9,8},{10,11... | collective-permute-start | bytes 1179656 | tf_op jit(solution)/shard_map/ppermute | solution.py:390
  16.3 7.7 %collective-permute-done.first_ref = bf16[256,768]{1,0:T(8,128)(2,1)S(1)} collective-permute-done((bf16[256,768]{1,0:T(8,128)(2,1)}, bf16[256,768]{1,0:T(8,128)(2,1)S(1)}, u32[]{:S(2)}, u32[]{:S(2)}) %collective-permute-start) | collective-permute-done | bytes 393248 | tf_op jit(solution)/shard_map/ppermute | solution.py:390
  24.1 2.5 %collective-permute-done.1.second_ref = bf16[256,768]{1,0:T(8,128)(2,1)S(1)} collective-permute-done((bf16[256,768]{1,0:T(8,128)(2,1)}, bf16[256,768]{1,0:T(8,128)(2,1)S(1)}, u32[]{:S(2)}, u32[]{:S(2)}) %collective-permute-start.1) | collective-permute-done | bytes 393248 | tf_op jit(solution)/shard_map/ppermute | solution.py:390
  26.7 1.5 %collective-permute-start.9 = (bf16[512,768]{1,0:T(8,128)(2,1)S(1)}, bf16[512,768]{1,0:T(8,128)(2,1)S(1)}, u32[]{:S(2)}, u32[]{:S(2)}) collective-permute-start(bf16[512,768]{1,0:T(8,128)(2,1)S(1)} %shard_map.39.refs_1_), channel_id=1, source_target_pairs={{0,16},{1,17},{2,18},{3,19},{4,20},{5,21},{6,22},{7,23},{8,24},{9,... | collective-permute-start | bytes 2359304 | tf_op jit(solution)/shard_map/ppermute | solution.py:390
  28.2 1.5 %collective-permute-start.7 = (bf16[512,768]{1,0:T(8,128)(2,1)S(1)}, bf16[512,768]{1,0:T(8,128)(2,1)S(1)}, u32[]{:S(2)}, u32[]{:S(2)}) collective-permute-start(bf16[512,768]{1,0:T(8,128)(2,1)S(1)} %shard_map.39.refs_1_), channel_id=1, source_target_pairs={{0,1},{1,0},{2,3},{3,2},{4,5},{5,4},{6,7},{7,6},{8,9},{9,8},{10,11... | collective-permute-start | bytes 2359304 | tf_op jit(solution)/shard_map/ppermute | solution.py:390
  29.7 0.2 collective-permute-start.6
  30.0 2.5 %collective-permute-start.5 = (bf16[256,768]{1,0:T(8,128)(2,1)S(1)}, bf16[256,768]{1,0:T(8,128)(2,1)S(1)}, u32[]{:S(2)}, u32[]{:S(2)}) collective-permute-start(bf16[256,768]{1,0:T(8,128)(2,1)S(1)} %copy-done.3), channel_id=1, source_target_pairs={{0,6},{1,7},{2,4},{3,5},{4,2},{5,3},{6,0},{7,1},{8,14},{9,15},{10,... | collective-permute-start | bytes 1179656 | tf_op jit(solution)/shard_map/ppermute | solution.py:390
  32.4 17.8 %all_to_all.10.label_ref = f32[32,1,256]{2,1,0:T(1,128)S(1)} all-to-all(f32[32,1,256]{2,1,0:T(1,128)S(1)} %copy-done.2), channel_id=1, replica_groups=mesh['grp'=4,'mem'=8] {'grp','mem'}, dimensions={0} | all-to-all | bytes 65536 | tf_op jit(solution)/shard_map/all_to_all | solution.py:430
  50.3 0.1 collective-permute-start.13
  50.4 0.5 collective-permute-start.11
  50.8 1.4 %collective-permute-start.12 = (bf16[256,768]{1,0:T(8,128)(2,1)S(1)}, bf16[256,768]{1,0:T(8,128)(2,1)S(1)}, u32[]{:S(2)}, u32[]{:S(2)}) collective-permute-start(bf16[256,768]{1,0:T(8,128)(2,1)S(1)} %collective-permute-done.5.refs_2_), channel_id=1, source_target_pairs={{0,16},{1,17},{2,18},{3,19},{4,20},{5,21},{6,22},{7,23},{8,24},{9,... | collective-permute-start | bytes 1179656 | tf_op jit(solution)/shard_map/ppermute | solution.py:390
  52.3 1.6 %collective-permute-start.10 = (bf16[256,768]{1,0:T(8,128)(2,1)S(1)}, bf16[256,768]{1,0:T(8,128)(2,1)S(1)}, u32[]{:S(2)}, u32[]{:S(2)}) collective-permute-start(bf16[256,768]{1,0:T(8,128)(2,1)S(1)} %collective-permute-done.5.refs_2_), channel_id=1, source_target_pairs={{0,1},{1,0},{2,3},{3,2},{4,5},{5,4},{6,7},{7,6},{8,9},{9,8},{10,11... | collective-permute-start | bytes 1179656 | tf_op jit(solution)/shard_map/ppermute | solution.py:390
  53.8 4.2 %shard_map.40.refs_12_ = f32[5,8,256]{2,1,0:T(8,128)S(1)} custom-call(f32[32,1,256]{2,1,0:T(1,128)S(1)} %all_to_all.10.label_ref, bf16[256,768]{1,0:T(8,128)(2,1)S(1)} %copy-done, bf16[512,768]{1,0:T(8,128)(2,1)S(1)} %shard_map.39.refs_1_, bf16[256,768]{1,0:T(8,128)(2,1)S(1)} %collective-permute-done.5.refs_2_, ...), custom_call_target="tpu_custom_call" | custom-call | flops 880803840 | bytes 5505024 | tf_op jit(solution)/shard_map/pallas_call | solution.py:303
  58.0 3.9 %shard_map.41.refs_15_ = f32[5,8,256]{2,1,0:T(8,128)S(1)} custom-call(f32[32,1,256]{2,1,0:T(1,128)S(1)} %all_to_all.10.label_ref, bf16[256,768]{1,0:T(8,128)(2,1)S(1)} %copy-done, bf16[512,768]{1,0:T(8,128)(2,1)S(1)} %shard_map.39.refs_1_, bf16[256,768]{1,0:T(8,128)(2,1)S(1)} %collective-permute-done.5.refs_2_, ...), custom_call_target="tpu_custom_call" | custom-call | flops 754974720 | bytes 6684672 | tf_op jit(solution)/shard_map/pallas_call | solution.py:303
  62.0 1.1 %collective-permute-done.10.refs_5_ = bf16[256,768]{1,0:T(8,128)(2,1)S(1)} collective-permute-done((bf16[256,768]{1,0:T(8,128)(2,1)S(1)}, bf16[256,768]{1,0:T(8,128)(2,1)S(1)}, u32[]{:S(2)}, u32[]{:S(2)}) %collective-permute-start.10) | collective-permute-done | bytes 393248 | tf_op jit(solution)/shard_map/ppermute | solution.py:390
  63.1 0.6 collective-permute-done.14.refs_14_
  63.7 3.4 %shard_map.42 = f32[8,1,256]{2,1,0:T(1,128)S(1)} custom-call(f32[32,1,256]{2,1,0:T(1,128)S(1)} %all_to_all.10.label_ref, bf16[256,768]{1,0:T(8,128)(2,1)S(1)} %copy-done, bf16[512,768]{1,0:T(8,128)(2,1)S(1)} %shard_map.39.refs_1_, bf16[256,768]{1,0:T(8,128)(2,1)S(1)} %collective-permute-done.5.refs_2_, bf16[256,768]{1,0:T(8,128)(2,1)S(1)} %collective-permute-done.2.refs_3_, ...), custom_call_target="tpu_custom_call" | custom-call | flops 1283457024 | bytes 7864320 | tf_op jit(solution)/shard_map/pallas_call | solution.py:303
  67.1 9.9 %all_to_all.11.back_ref = f32[8,1,256]{2,1,0:T(1,128)S(1)} all-to-all(f32[8,1,256]{2,1,0:T(1,128)S(1)} %shard_map.42), channel_id=1, replica_groups=mesh['grp'=4,'mem'=8] {'mem'}, dimensions={0} | all-to-all | bytes 16384 | tf_op jit(solution)/shard_map/all_to_all | solution.py:504
  77.0 1.1 %shard_map.43 = f32[1,1024]{1,0:T(1,128)} custom-call(s32[1,1024]{1,0:T(1,128)S(1)} %copy-done.1, f32[8,1,256]{2,1,0:T(1,128)S(1)} %all_to_all.11.back_ref), custom_call_target="tpu_custom_call" | custom-call | tf_op jit(solution)/shard_map/pallas_call | solution.py:365
  (23 shorter events, 0.2 us)
Async XLA Ops:
  3.3 20.7 %collective-permute-start = (bf16[256,768]{1,0:T(8,128)(2,1)}, bf16[256,768]{1,0:T(8,128)(2,1)S(1)}, u32[]{:S(2)}, u32[]{:S(2)}) collective-permute-start(bf16[256,768]{1,0:T(8,128)(2,1)} %get-tuple-element.33), channel_id=1, source_target_pairs={{0,2},{1,3},{2,0},{3,1},{4,6},{5,7},{6,4},{7,5},{8,10},{9,11},{10,... | collective-permute-start | bytes 1179656 | tf_op jit(solution)/shard_map/ppermute | solution.py:390
  6.4 20.2 %collective-permute-start.1 = (bf16[256,768]{1,0:T(8,128)(2,1)}, bf16[256,768]{1,0:T(8,128)(2,1)S(1)}, u32[]{:S(2)}, u32[]{:S(2)}) collective-permute-start(bf16[256,768]{1,0:T(8,128)(2,1)} %get-tuple-element.34), channel_id=1, source_target_pairs={{0,4},{1,5},{2,6},{3,7},{4,0},{5,1},{6,2},{7,3},{8,12},{9,13},{10,... | collective-permute-start | bytes 1179656 | tf_op jit(solution)/shard_map/ppermute | solution.py:390
  13.2 16.7 %copy-start.3 = (bf16[256,768]{1,0:T(8,128)(2,1)S(1)}, bf16[256,768]{1,0:T(8,128)(2,1)}, u32[]{:S(2)}) copy-start(bf16[256,768]{1,0:T(8,128)(2,1)} %get-tuple-element.40) | copy-start | bytes 1179652
  13.2 19.2 %copy-start.2 = (f32[32,1,256]{2,1,0:T(1,128)S(1)}, f32[32,1,256]{2,1,0:T(1,128)}, u32[]{:S(2)}) copy-start(f32[32,1,256]{2,1,0:T(1,128)} %get-tuple-element.41) | copy-start | bytes 98308
  13.3 40.6 %copy-start = (bf16[256,768]{1,0:T(8,128)(2,1)S(1)}, bf16[256,768]{1,0:T(8,128)(2,1)}, u32[]{:S(2)}) copy-start(bf16[256,768]{1,0:T(8,128)(2,1)} %get-tuple-element.35.refs_0_) | copy-start | bytes 1179652
  13.3 13.3 %collective-permute-start.4 = (bf16[256,768]{1,0:T(8,128)(2,1)}, bf16[256,768]{1,0:T(8,128)(2,1)S(1)}, u32[]{:S(2)}, u32[]{:S(2)}) collective-permute-start(bf16[256,768]{1,0:T(8,128)(2,1)} %get-tuple-element.35.refs_0_), channel_id=1, source_target_pairs={{0,16},{1,17},{2,18},{3,19},{4,20},{5,21},{6,22},{7,23},{8,24},{9,... | collective-permute-start | bytes 1179656 | tf_op jit(solution)/shard_map/ppermute | solution.py:390
  14.8 11.8 %collective-permute-start.3 = (bf16[256,768]{1,0:T(8,128)(2,1)}, bf16[256,768]{1,0:T(8,128)(2,1)S(1)}, u32[]{:S(2)}, u32[]{:S(2)}) collective-permute-start(bf16[256,768]{1,0:T(8,128)(2,1)} %get-tuple-element.35.refs_0_), channel_id=1, source_target_pairs={{0,8},{1,9},{2,10},{3,11},{4,12},{5,13},{6,14},{7,15},{8,0},{9,1},... | collective-permute-start | bytes 1179656 | tf_op jit(solution)/shard_map/ppermute | solution.py:390
  14.8 11.8 %collective-permute-start.2 = (bf16[256,768]{1,0:T(8,128)(2,1)}, bf16[256,768]{1,0:T(8,128)(2,1)S(1)}, u32[]{:S(2)}, u32[]{:S(2)}) collective-permute-start(bf16[256,768]{1,0:T(8,128)(2,1)} %get-tuple-element.35.refs_0_), channel_id=1, source_target_pairs={{0,1},{1,0},{2,3},{3,2},{4,5},{5,4},{6,7},{7,6},{8,9},{9,8},{10,11... | collective-permute-start | bytes 1179656 | tf_op jit(solution)/shard_map/ppermute | solution.py:390
  26.7 23.6 %collective-permute-start.9 = (bf16[512,768]{1,0:T(8,128)(2,1)S(1)}, bf16[512,768]{1,0:T(8,128)(2,1)S(1)}, u32[]{:S(2)}, u32[]{:S(2)}) collective-permute-start(bf16[512,768]{1,0:T(8,128)(2,1)S(1)} %shard_map.39.refs_1_), channel_id=1, source_target_pairs={{0,16},{1,17},{2,18},{3,19},{4,20},{5,21},{6,22},{7,23},{8,24},{9,... | collective-permute-start | bytes 2359304 | tf_op jit(solution)/shard_map/ppermute | solution.py:390
  28.2 22.0 %collective-permute-start.8 = (bf16[512,768]{1,0:T(8,128)(2,1)S(1)}, bf16[512,768]{1,0:T(8,128)(2,1)S(1)}, u32[]{:S(2)}, u32[]{:S(2)}) collective-permute-start(bf16[512,768]{1,0:T(8,128)(2,1)S(1)} %shard_map.39.refs_1_), channel_id=1, source_target_pairs={{0,8},{1,9},{2,10},{3,11},{4,12},{5,13},{6,14},{7,15},{8,0},{9,1},... | collective-permute-start | bytes 2359304 | tf_op jit(solution)/shard_map/ppermute | solution.py:390
  28.2 22.0 %collective-permute-start.7 = (bf16[512,768]{1,0:T(8,128)(2,1)S(1)}, bf16[512,768]{1,0:T(8,128)(2,1)S(1)}, u32[]{:S(2)}, u32[]{:S(2)}) collective-permute-start(bf16[512,768]{1,0:T(8,128)(2,1)S(1)} %shard_map.39.refs_1_), channel_id=1, source_target_pairs={{0,1},{1,0},{2,3},{3,2},{4,5},{5,4},{6,7},{7,6},{8,9},{9,8},{10,11... | collective-permute-start | bytes 2359304 | tf_op jit(solution)/shard_map/ppermute | solution.py:390
  29.7 20.5 %collective-permute-start.6 = (bf16[256,768]{1,0:T(8,128)(2,1)S(1)}, bf16[256,768]{1,0:T(8,128)(2,1)S(1)}, u32[]{:S(2)}, u32[]{:S(2)}) collective-permute-start(bf16[256,768]{1,0:T(8,128)(2,1)S(1)} %collective-permute-done.4.refs_7_.refs_8_.refs_9_), channel_id=1, source_target_pairs={{0,8},{1,9},{2,10},{3,11},{4,12},{5,13},{6,14},{7,15},{8,0},{9,1},... | collective-permute-start | bytes 1179656 | tf_op jit(solution)/shard_map/ppermute | solution.py:390
  30.0 20.3 %collective-permute-start.5 = (bf16[256,768]{1,0:T(8,128)(2,1)S(1)}, bf16[256,768]{1,0:T(8,128)(2,1)S(1)}, u32[]{:S(2)}, u32[]{:S(2)}) collective-permute-start(bf16[256,768]{1,0:T(8,128)(2,1)S(1)} %copy-done.3), channel_id=1, source_target_pairs={{0,6},{1,7},{2,4},{3,5},{4,2},{5,3},{6,0},{7,1},{8,14},{9,15},{10,... | collective-permute-start | bytes 1179656 | tf_op jit(solution)/shard_map/ppermute | solution.py:390
  50.3 7.8 %collective-permute-start.13 = (bf16[512,768]{1,0:T(8,128)(2,1)S(1)}, bf16[512,768]{1,0:T(8,128)(2,1)S(1)}, u32[]{:S(2)}, u32[]{:S(2)}) collective-permute-start(bf16[512,768]{1,0:T(8,128)(2,1)S(1)} %collective-permute-done.9.refs_8_.refs_9_.refs_10_), channel_id=1, source_target_pairs={{0,8},{1,9},{2,10},{3,11},{4,12},{5,13},{6,14},{7,15},{8,0},{9,1},... | collective-permute-start | bytes 2359304 | tf_op jit(solution)/shard_map/ppermute | solution.py:390
  50.4 7.6 %collective-permute-start.11 = (bf16[256,768]{1,0:T(8,128)(2,1)S(1)}, bf16[256,768]{1,0:T(8,128)(2,1)S(1)}, u32[]{:S(2)}, u32[]{:S(2)}) collective-permute-start(bf16[256,768]{1,0:T(8,128)(2,1)S(1)} %collective-permute-done.5.refs_2_), channel_id=1, source_target_pairs={{0,8},{1,9},{2,10},{3,11},{4,12},{5,13},{6,14},{7,15},{8,0},{9,1},... | collective-permute-start | bytes 1179656 | tf_op jit(solution)/shard_map/ppermute | solution.py:390
  50.8 11.1 %collective-permute-start.12 = (bf16[256,768]{1,0:T(8,128)(2,1)S(1)}, bf16[256,768]{1,0:T(8,128)(2,1)S(1)}, u32[]{:S(2)}, u32[]{:S(2)}) collective-permute-start(bf16[256,768]{1,0:T(8,128)(2,1)S(1)} %collective-permute-done.5.refs_2_), channel_id=1, source_target_pairs={{0,16},{1,17},{2,18},{3,19},{4,20},{5,21},{6,22},{7,23},{8,24},{9,... | collective-permute-start | bytes 1179656 | tf_op jit(solution)/shard_map/ppermute | solution.py:390
  52.3 10.9 %collective-permute-start.10 = (bf16[256,768]{1,0:T(8,128)(2,1)S(1)}, bf16[256,768]{1,0:T(8,128)(2,1)S(1)}, u32[]{:S(2)}, u32[]{:S(2)}) collective-permute-start(bf16[256,768]{1,0:T(8,128)(2,1)S(1)} %collective-permute-done.5.refs_2_), channel_id=1, source_target_pairs={{0,1},{1,0},{2,3},{3,2},{4,5},{5,4},{6,7},{7,6},{8,9},{9,8},{10,11... | collective-permute-start | bytes 1179656 | tf_op jit(solution)/shard_map/ppermute | solution.py:390
  61.9 15.1 %copy-start.1 = (s32[1,1024]{1,0:T(1,128)S(1)}, s32[1,1024]{1,0:T(1,128)}, u32[]{:S(2)}) copy-start(s32[1,1024]{1,0:T(1,128)} %get-tuple-element.31.dest_ref) | copy-start | bytes 12292
  61.9 1.7 %collective-permute-start.14 = (bf16[256,768]{1,0:T(8,128)(2,1)S(1)}, bf16[256,768]{1,0:T(8,128)(2,1)S(1)}, u32[]{:S(2)}, u32[]{:S(2)}) collective-permute-start(bf16[256,768]{1,0:T(8,128)(2,1)S(1)} %collective-permute-done.12.refs_11_), channel_id=1, source_target_pairs={{0,8},{1,9},{2,10},{3,11},{4,12},{5,13},{6,14},{7,15},{8,0},{9,1},... | collective-permute-start | bytes 1179656 | tf_op jit(solution)/shard_map/ppermute | solution.py:390

commit v11 on v10

--- a/solution.py
+++ b/solution.py
@@ -399,6 +399,7 @@
     *packed, dest, labels = pack(embeddings, cluster, rank, rest, True, sizes)
     for k, value in zip(rest, packed):
         sends[k] = value
+    labels = lax.all_to_all(labels, ("grp", "mem"), split_axis=0, concat_axis=0, tiled=True)
 
     last = groups - 1
     far = [d for d in offsets if d & side and d != side and d ^ side in offsets]
@@ -419,24 +420,19 @@
         if k < last:
             also = swap(sends[k + 1], k + 1, 0)
             if k == 1:
-                mine, also, *firsts = lax.optimization_barrier(
-                    (mine, also, *(held[d][0] for d in near))
+                mine, also, labels, *firsts = lax.optimization_barrier(
+                    (mine, also, labels, *(held[d][0] for d in near))
                 )
                 for d, value in zip(near, firsts):
                     held[d] = [value]
             mine = join(mine, also)
-            if k == 1:
-                mine, labels = lax.optimization_barrier((mine, labels))
-                labels = lax.all_to_all(
-                    labels, ("grp", "mem"), split_axis=0, concat_axis=0, tiled=True
-                )
             after = mine
         held[0].append(mine)
         for d in near:
             held[d].append(swap(mine, 0, d))
     for spot in range(1, len(held[0]) - 1):
-        held[0][spot + 1], labels, *values = lax.optimization_barrier(
-            (held[0][spot + 1], labels, *(held[d][0] for d in far), *(held[d][spot] for d in near))
+        held[0][spot + 1], *values = lax.optimization_barrier(
+            (held[0][spot + 1], *(held[d][0] for d in far), *(held[d][spot] for d in near))
         )
         for d in far:
             held[d][0] = values.pop(0)

time: 78.3 us -> 78.6 us (level)
  waiting for transfers between devices: 12 us -> 19.3 us
  blocking collectives: 27.6 us -> 23.5 us
  starting transfers between devices: 18.1 us -> 15.2 us
    ppermute x15, waiting for transfers between devices: 12 us -> 19.3 us  [swap(): lax.ppermute(value, ('grp', 'mem'), [(i, i ^ mask) for i in range(devices)])]
    all_to_all x1, blocking collectives: 17.8 us -> 12.8 us  [on_device(): lax.all_to_all(labels, ('grp', 'mem'), split_axis=0, concat_axis=0, tiled...]
    ppermute x15, starting transfers between devices: 18.1 us -> 15.2 us  [swap(): lax.ppermute(value, ('grp', 'mem'), [(i, i ^ mask) for i in range(devices)])]
    all_to_all x1, blocking collectives: 9.87 us -> 10.8 us  [on_device(): back = lax.all_to_all(back, 'mem', split_axis=0, concat_axis=0, tiled=True)]
  transfers between devices with their start and end apart: 15 -> 15, of which waited for: 5 -> 6; matrix products, arithmetic and copies ran while one was open for 0% -> 0% of each run, Pallas kernels for 16% -> 16%
where the time goes in v11:
time: 78.6 us; the launch traced here: 78.3 us
  blocking collectives  23.5 us (30%)
  Pallas kernels  20.1 us (26%)
  waiting for transfers between devices  19.3 us (25%)
  starting transfers between devices  15.2 us (19%)
    ppermute x15, waiting for transfers between devices, swap(): lax.ppermute(value, ('grp', 'mem'), [(i, i ^ mask) for i in range(devices)])  19.3 us
    ppermute x15, starting transfers between devices, swap(): lax.ppermute(value, ('grp', 'mem'), [(i, i ^ mask) for i in range(devices)])  15.2 us
    all_to_all x1, blocking collectives, on_device(): lax.all_to_all(labels, ('grp', 'mem'), split_axis=0, concat_axis=0, tiled...  12.8 us
    pallas_call x3, Pallas kernels, compare(): pl.pallas_call(functools.partial(compare_kernel, sizes, jobs, names, spot...  11.5 us
    all_to_all x1, blocking collectives, on_device(): back = lax.all_to_all(back, 'mem', split_axis=0, concat_axis=0, tiled=True)  10.8 us
    pallas_call x2, Pallas kernels, pack(): pl.pallas_call(functools.partial(pack_kernel, sizes, ks, labelled), out_s...  7.52 us
  transfers between devices with their start and end apart: 15, of which 6 were waited for; matrix products, arithmetic and copies ran while one was open for 0% of the time, Pallas kernels for 16%

profile of v11, /device:TPU:0, one launch (start us, length us, event | category | flops | bytes accessed | tf_op | source)
XLA Modules:
  0.0 78.3 jit_solution(17779926647255143120)
XLA Ops:
  0.0 3.3 %shard_map.37 = (bf16[256,768]{1,0:T(8,128)(2,1)}, bf16[256,768]{1,0:T(8,128)(2,1)}) custom-call(bf16[1024,768]{1,0:T(8,128)(2,1)} %emb_hbm.3, s32[1,1024]{1,0:T(1,128)} %bitcast.4, s32[1,1024]{1,0:T(1,128)} %bitcast.6), custom_call_target="tpu_custom_call" | custom-call | flops 805306368 | bytes 3145728 | tf_op jit(solution)/shard_map/pallas_call | solution.py:135
  3.3 3.1 %collective-permute-start = (bf16[256,768]{1,0:T(8,128)(2,1)}, bf16[256,768]{1,0:T(8,128)(2,1)S(1)}, u32[]{:S(2)}, u32[]{:S(2)}) collective-permute-start(bf16[256,768]{1,0:T(8,128)(2,1)} %get-tuple-element.30), channel_id=1, source_target_pairs={{0,2},{1,3},{2,0},{3,1},{4,6},{5,7},{6,4},{7,5},{8,10},{9,11},{10,... | collective-permute-start | bytes 1179656 | tf_op jit(solution)/shard_map/ppermute | solution.py:390
  6.4 2.6 %collective-permute-start.1 = (bf16[256,768]{1,0:T(8,128)(2,1)}, bf16[256,768]{1,0:T(8,128)(2,1)S(1)}, u32[]{:S(2)}, u32[]{:S(2)}) collective-permute-start(bf16[256,768]{1,0:T(8,128)(2,1)} %get-tuple-element.31), channel_id=1, source_target_pairs={{0,4},{1,5},{2,6},{3,7},{4,0},{5,1},{6,2},{7,3},{8,12},{9,13},{10,... | collective-permute-start | bytes 1179656 | tf_op jit(solution)/shard_map/ppermute | solution.py:390
  9.0 4.2 %shard_map.38 = (bf16[256,768]{1,0:T(8,128)(2,1)}, bf16[256,768]{1,0:T(8,128)(2,1)}, s32[1,1024]{1,0:T(1,128)}, f32[32,1,256]{2,1,0:T(1,128)}) custom-call(bf16[1024,768]{1,0:T(8,128)(2,1)} %emb_hbm.3, s32[1,1024]{1,0:T(1,128)} %bitcast.5, s32[1,1024]{1,0:T(1,128)} %bitcast.7), custom_call_target="tpu_custom_call" | custom-call | flops 805306368 | bytes 3145728 | tf_op jit(solution)/shard_map/pallas_call | solution.py:135
  13.2 1.5 %collective-permute-start.4 = (bf16[256,768]{1,0:T(8,128)(2,1)}, bf16[256,768]{1,0:T(8,128)(2,1)S(1)}, u32[]{:S(2)}, u32[]{:S(2)}) collective-permute-start(bf16[256,768]{1,0:T(8,128)(2,1)} %get-tuple-element.33.refs_0_), channel_id=1, source_target_pairs={{0,16},{1,17},{2,18},{3,19},{4,20},{5,21},{6,22},{7,23},{8,24},{9,... | collective-permute-start | bytes 1179656 | tf_op jit(solution)/shard_map/ppermute | solution.py:390
  14.8 1.5 %collective-permute-start.2 = (bf16[256,768]{1,0:T(8,128)(2,1)}, bf16[256,768]{1,0:T(8,128)(2,1)S(1)}, u32[]{:S(2)}, u32[]{:S(2)}) collective-permute-start(bf16[256,768]{1,0:T(8,128)(2,1)} %get-tuple-element.33.refs_0_), channel_id=1, source_target_pairs={{0,1},{1,0},{2,3},{3,2},{4,5},{5,4},{6,7},{7,6},{8,9},{9,8},{10,11... | collective-permute-start | bytes 1179656 | tf_op jit(solution)/shard_map/ppermute | solution.py:390
  16.3 12.8 %all_to_all.10.label_ref = f32[32,1,256]{2,1,0:T(1,128)S(1)} all-to-all(f32[32,1,256]{2,1,0:T(1,128)} %get-tuple-element.32), channel_id=1, replica_groups=mesh['grp'=4,'mem'=8] {'grp','mem'}, dimensions={0} | all-to-all | bytes 65536 | tf_op jit(solution)/shard_map/all_to_all | solution.py:402
  29.2 0.6 collective-permute-start.9
  29.8 0.6 collective-permute-start.7
  30.6 2.4 %collective-permute-start.5 = (bf16[256,768]{1,0:T(8,128)(2,1)S(1)}, bf16[256,768]{1,0:T(8,128)(2,1)S(1)}, u32[]{:S(2)}, u32[]{:S(2)}) collective-permute-start(bf16[256,768]{1,0:T(8,128)(2,1)S(1)} %copy-done.2), channel_id=1, source_target_pairs={{0,6},{1,7},{2,4},{3,5},{4,2},{5,3},{6,0},{7,1},{8,14},{9,15},{10,... | collective-permute-start | bytes 1179656 | tf_op jit(solution)/shard_map/ppermute | solution.py:390
  33.1 10.8 %collective-permute-done.5.refs_2_ = bf16[256,768]{1,0:T(8,128)(2,1)S(1)} collective-permute-done((bf16[256,768]{1,0:T(8,128)(2,1)S(1)}, bf16[256,768]{1,0:T(8,128)(2,1)S(1)}, u32[]{:S(2)}, u32[]{:S(2)}) %collective-permute-start.5) | collective-permute-done | bytes 393248 | tf_op jit(solution)/shard_map/ppermute | solution.py:390
  43.9 4.8 %collective-permute-done.9.refs_8_.refs_9_.refs_10_ = bf16[512,768]{1,0:T(8,128)(2,1)S(1)} collective-permute-done((bf16[512,768]{1,0:T(8,128)(2,1)S(1)}, bf16[512,768]{1,0:T(8,128)(2,1)S(1)}, u32[]{:S(2)}, u32[]{:S(2)}) %collective-permute-start.9) | collective-permute-done | bytes 786464 | tf_op jit(solution)/shard_map/ppermute | solution.py:390
  48.6 1.1 %collective-permute-done.7.refs_4_ = bf16[512,768]{1,0:T(8,128)(2,1)S(1)} collective-permute-done((bf16[512,768]{1,0:T(8,128)(2,1)S(1)}, bf16[512,768]{1,0:T(8,128)(2,1)S(1)}, u32[]{:S(2)}, u32[]{:S(2)}) %collective-permute-start.7) | collective-permute-done | bytes 786464 | tf_op jit(solution)/shard_map/ppermute | solution.py:390
  49.8 0.5 collective-permute-start.11
  50.3 1.5 %collective-permute-start.12 = (bf16[256,768]{1,0:T(8,128)(2,1)S(1)}, bf16[256,768]{1,0:T(8,128)(2,1)S(1)}, u32[]{:S(2)}, u32[]{:S(2)}) collective-permute-start(bf16[256,768]{1,0:T(8,128)(2,1)S(1)} %collective-permute-done.5.refs_2_), channel_id=1, source_target_pairs={{0,16},{1,17},{2,18},{3,19},{4,20},{5,21},{6,22},{7,23},{8,24},{9,... | collective-permute-start | bytes 1179656 | tf_op jit(solution)/shard_map/ppermute | solution.py:390
  51.8 0.5 collective-permute-start.10
  52.3 4.2 %shard_map.40.refs_12_ = f32[5,8,256]{2,1,0:T(8,128)S(1)} custom-call(f32[32,1,256]{2,1,0:T(1,128)S(1)} %all_to_all.10.label_ref, bf16[256,768]{1,0:T(8,128)(2,1)S(1)} %copy-done, bf16[512,768]{1,0:T(8,128)(2,1)S(1)} %shard_map.39.refs_1_, bf16[256,768]{1,0:T(8,128)(2,1)S(1)} %collective-permute-done.5.refs_2_, ...), custom_call_target="tpu_custom_call" | custom-call | flops 880803840 | bytes 5505024 | tf_op jit(solution)/shard_map/pallas_call | solution.py:303
  56.5 3.9 %shard_map.41.refs_15_ = f32[5,8,256]{2,1,0:T(8,128)S(1)} custom-call(f32[32,1,256]{2,1,0:T(1,128)S(1)} %all_to_all.10.label_ref, bf16[256,768]{1,0:T(8,128)(2,1)S(1)} %copy-done, bf16[512,768]{1,0:T(8,128)(2,1)S(1)} %shard_map.39.refs_1_, bf16[256,768]{1,0:T(8,128)(2,1)S(1)} %collective-permute-done.5.refs_2_, ...), custom_call_target="tpu_custom_call" | custom-call | flops 754974720 | bytes 6684672 | tf_op jit(solution)/shard_map/pallas_call | solution.py:303
  60.4 0.9 %collective-permute-done.12.refs_11_ = bf16[256,768]{1,0:T(8,128)(2,1)S(1)} collective-permute-done((bf16[256,768]{1,0:T(8,128)(2,1)S(1)}, bf16[256,768]{1,0:T(8,128)(2,1)S(1)}, u32[]{:S(2)}, u32[]{:S(2)}) %collective-permute-start.12) | collective-permute-done | bytes 393248 | tf_op jit(solution)/shard_map/ppermute | solution.py:390
  61.3 1.2 %collective-permute-done.10.refs_5_ = bf16[256,768]{1,0:T(8,128)(2,1)S(1)} collective-permute-done((bf16[256,768]{1,0:T(8,128)(2,1)S(1)}, bf16[256,768]{1,0:T(8,128)(2,1)S(1)}, u32[]{:S(2)}, u32[]{:S(2)}) %collective-permute-start.10) | collective-permute-done | bytes 393248 | tf_op jit(solution)/shard_map/ppermute | solution.py:390
  62.5 0.5 collective-permute-done.14.refs_14_
  63.0 3.4 %shard_map.42 = f32[8,1,256]{2,1,0:T(1,128)S(1)} custom-call(f32[32,1,256]{2,1,0:T(1,128)S(1)} %all_to_all.10.label_ref, bf16[256,768]{1,0:T(8,128)(2,1)S(1)} %copy-done, bf16[512,768]{1,0:T(8,128)(2,1)S(1)} %shard_map.39.refs_1_, bf16[256,768]{1,0:T(8,128)(2,1)S(1)} %collective-permute-done.5.refs_2_, bf16[256,768]{1,0:T(8,128)(2,1)S(1)} %collective-permute-done.2.refs_3_, ...), custom_call_target="tpu_custom_call" | custom-call | flops 1283457024 | bytes 7864320 | tf_op jit(solution)/shard_map/pallas_call | solution.py:303
  66.4 10.8 %all_to_all.11.back_ref = f32[8,1,256]{2,1,0:T(1,128)S(1)} all-to-all(f32[8,1,256]{2,1,0:T(1,128)S(1)} %shard_map.42), channel_id=1, replica_groups=mesh['grp'=4,'mem'=8] {'mem'}, dimensions={0} | all-to-all | bytes 16384 | tf_op jit(solution)/shard_map/all_to_all | solution.py:500
  77.2 1.1 %shard_map.43 = f32[1,1024]{1,0:T(1,128)} custom-call(s32[1,1024]{1,0:T(1,128)S(1)} %copy-done.1, f32[8,1,256]{2,1,0:T(1,128)S(1)} %all_to_all.11.back_ref), custom_call_target="tpu_custom_call" | custom-call | tf_op jit(solution)/shard_map/pallas_call | solution.py:365
  (21 shorter events, 0.3 us)
Async XLA Ops:
  3.3 25.8 %collective-permute-start = (bf16[256,768]{1,0:T(8,128)(2,1)}, bf16[256,768]{1,0:T(8,128)(2,1)S(1)}, u32[]{:S(2)}, u32[]{:S(2)}) collective-permute-start(bf16[256,768]{1,0:T(8,128)(2,1)} %get-tuple-element.30), channel_id=1, source_target_pairs={{0,2},{1,3},{2,0},{3,1},{4,6},{5,7},{6,4},{7,5},{8,10},{9,11},{10,... | collective-permute-start | bytes 1179656 | tf_op jit(solution)/shard_map/ppermute | solution.py:390
  6.4 22.7 %collective-permute-start.1 = (bf16[256,768]{1,0:T(8,128)(2,1)}, bf16[256,768]{1,0:T(8,128)(2,1)S(1)}, u32[]{:S(2)}, u32[]{:S(2)}) collective-permute-start(bf16[256,768]{1,0:T(8,128)(2,1)} %get-tuple-element.31), channel_id=1, source_target_pairs={{0,4},{1,5},{2,6},{3,7},{4,0},{5,1},{6,2},{7,3},{8,12},{9,13},{10,... | collective-permute-start | bytes 1179656 | tf_op jit(solution)/shard_map/ppermute | solution.py:390
  13.2 17.4 %copy-start.2 = (bf16[256,768]{1,0:T(8,128)(2,1)S(1)}, bf16[256,768]{1,0:T(8,128)(2,1)}, u32[]{:S(2)}) copy-start(bf16[256,768]{1,0:T(8,128)(2,1)} %get-tuple-element.38) | copy-start | bytes 1179652
  13.2 39.1 %copy-start = (bf16[256,768]{1,0:T(8,128)(2,1)S(1)}, bf16[256,768]{1,0:T(8,128)(2,1)}, u32[]{:S(2)}) copy-start(bf16[256,768]{1,0:T(8,128)(2,1)} %get-tuple-element.33.refs_0_) | copy-start | bytes 1179652
  13.2 15.9 %collective-permute-start.4 = (bf16[256,768]{1,0:T(8,128)(2,1)}, bf16[256,768]{1,0:T(8,128)(2,1)S(1)}, u32[]{:S(2)}, u32[]{:S(2)}) collective-permute-start(bf16[256,768]{1,0:T(8,128)(2,1)} %get-tuple-element.33.refs_0_), channel_id=1, source_target_pairs={{0,16},{1,17},{2,18},{3,19},{4,20},{5,21},{6,22},{7,23},{8,24},{9,... | collective-permute-start | bytes 1179656 | tf_op jit(solution)/shard_map/ppermute | solution.py:390
  14.8 14.3 %collective-permute-start.3 = (bf16[256,768]{1,0:T(8,128)(2,1)}, bf16[256,768]{1,0:T(8,128)(2,1)S(1)}, u32[]{:S(2)}, u32[]{:S(2)}) collective-permute-start(bf16[256,768]{1,0:T(8,128)(2,1)} %get-tuple-element.33.refs_0_), channel_id=1, source_target_pairs={{0,8},{1,9},{2,10},{3,11},{4,12},{5,13},{6,14},{7,15},{8,0},{9,1},... | collective-permute-start | bytes 1179656 | tf_op jit(solution)/shard_map/ppermute | solution.py:390
  14.8 14.3 %collective-permute-start.2 = (bf16[256,768]{1,0:T(8,128)(2,1)}, bf16[256,768]{1,0:T(8,128)(2,1)S(1)}, u32[]{:S(2)}, u32[]{:S(2)}) collective-permute-start(bf16[256,768]{1,0:T(8,128)(2,1)} %get-tuple-element.33.refs_0_), channel_id=1, source_target_pairs={{0,1},{1,0},{2,3},{3,2},{4,5},{5,4},{6,7},{7,6},{8,9},{9,8},{10,11... | collective-permute-start | bytes 1179656 | tf_op jit(solution)/shard_map/ppermute | solution.py:390
  29.2 19.4 %collective-permute-start.9 = (bf16[512,768]{1,0:T(8,128)(2,1)S(1)}, bf16[512,768]{1,0:T(8,128)(2,1)S(1)}, u32[]{:S(2)}, u32[]{:S(2)}) collective-permute-start(bf16[512,768]{1,0:T(8,128)(2,1)S(1)} %shard_map.39.refs_1_), channel_id=1, source_target_pairs={{0,16},{1,17},{2,18},{3,19},{4,20},{5,21},{6,22},{7,23},{8,24},{9,... | collective-permute-start | bytes 2359304 | tf_op jit(solution)/shard_map/ppermute | solution.py:390
  29.8 18.8 %collective-permute-start.8 = (bf16[512,768]{1,0:T(8,128)(2,1)S(1)}, bf16[512,768]{1,0:T(8,128)(2,1)S(1)}, u32[]{:S(2)}, u32[]{:S(2)}) collective-permute-start(bf16[512,768]{1,0:T(8,128)(2,1)S(1)} %shard_map.39.refs_1_), channel_id=1, source_target_pairs={{0,8},{1,9},{2,10},{3,11},{4,12},{5,13},{6,14},{7,15},{8,0},{9,1},... | collective-permute-start | bytes 2359304 | tf_op jit(solution)/shard_map/ppermute | solution.py:390
  29.8 20.0 %collective-permute-start.7 = (bf16[512,768]{1,0:T(8,128)(2,1)S(1)}, bf16[512,768]{1,0:T(8,128)(2,1)S(1)}, u32[]{:S(2)}, u32[]{:S(2)}) collective-permute-start(bf16[512,768]{1,0:T(8,128)(2,1)S(1)} %shard_map.39.refs_1_), channel_id=1, source_target_pairs={{0,1},{1,0},{2,3},{3,2},{4,5},{5,4},{6,7},{7,6},{8,9},{9,8},{10,11... | collective-permute-start | bytes 2359304 | tf_op jit(solution)/shard_map/ppermute | solution.py:390
  30.4 2.7 %collective-permute-start.6 = (bf16[256,768]{1,0:T(8,128)(2,1)S(1)}, bf16[256,768]{1,0:T(8,128)(2,1)S(1)}, u32[]{:S(2)}, u32[]{:S(2)}) collective-permute-start(bf16[256,768]{1,0:T(8,128)(2,1)S(1)} %collective-permute-done.4.refs_7_.refs_8_.refs_9_), channel_id=1, source_target_pairs={{0,8},{1,9},{2,10},{3,11},{4,12},{5,13},{6,14},{7,15},{8,0},{9,1},... | collective-permute-start | bytes 1179656 | tf_op jit(solution)/shard_map/ppermute | solution.py:390
  30.6 13.2 %collective-permute-start.5 = (bf16[256,768]{1,0:T(8,128)(2,1)S(1)}, bf16[256,768]{1,0:T(8,128)(2,1)S(1)}, u32[]{:S(2)}, u32[]{:S(2)}) collective-permute-start(bf16[256,768]{1,0:T(8,128)(2,1)S(1)} %copy-done.2), channel_id=1, source_target_pairs={{0,6},{1,7},{2,4},{3,5},{4,2},{5,3},{6,0},{7,1},{8,14},{9,15},{10,... | collective-permute-start | bytes 1179656 | tf_op jit(solution)/shard_map/ppermute | solution.py:390
  49.8 6.8 %collective-permute-start.13 = (bf16[512,768]{1,0:T(8,128)(2,1)S(1)}, bf16[512,768]{1,0:T(8,128)(2,1)S(1)}, u32[]{:S(2)}, u32[]{:S(2)}) collective-permute-start(bf16[512,768]{1,0:T(8,128)(2,1)S(1)} %collective-permute-done.9.refs_8_.refs_9_.refs_10_), channel_id=1, source_target_pairs={{0,8},{1,9},{2,10},{3,11},{4,12},{5,13},{6,14},{7,15},{8,0},{9,1},... | collective-permute-start | bytes 2359304 | tf_op jit(solution)/shard_map/ppermute | solution.py:390
  49.8 6.7 %collective-permute-start.11 = (bf16[256,768]{1,0:T(8,128)(2,1)S(1)}, bf16[256,768]{1,0:T(8,128)(2,1)S(1)}, u32[]{:S(2)}, u32[]{:S(2)}) collective-permute-start(bf16[256,768]{1,0:T(8,128)(2,1)S(1)} %collective-permute-done.5.refs_2_), channel_id=1, source_target_pairs={{0,8},{1,9},{2,10},{3,11},{4,12},{5,13},{6,14},{7,15},{8,0},{9,1},... | collective-permute-start | bytes 1179656 | tf_op jit(solution)/shard_map/ppermute | solution.py:390
  50.3 11.0 %collective-permute-start.12 = (bf16[256,768]{1,0:T(8,128)(2,1)S(1)}, bf16[256,768]{1,0:T(8,128)(2,1)S(1)}, u32[]{:S(2)}, u32[]{:S(2)}) collective-permute-start(bf16[256,768]{1,0:T(8,128)(2,1)S(1)} %collective-permute-done.5.refs_2_), channel_id=1, source_target_pairs={{0,16},{1,17},{2,18},{3,19},{4,20},{5,21},{6,22},{7,23},{8,24},{9,... | collective-permute-start | bytes 1179656 | tf_op jit(solution)/shard_map/ppermute | solution.py:390
  51.8 10.7 %collective-permute-start.10 = (bf16[256,768]{1,0:T(8,128)(2,1)S(1)}, bf16[256,768]{1,0:T(8,128)(2,1)S(1)}, u32[]{:S(2)}, u32[]{:S(2)}) collective-permute-start(bf16[256,768]{1,0:T(8,128)(2,1)S(1)} %collective-permute-done.5.refs_2_), channel_id=1, source_target_pairs={{0,1},{1,0},{2,3},{3,2},{4,5},{5,4},{6,7},{7,6},{8,9},{9,8},{10,11... | collective-permute-start | bytes 1179656 | tf_op jit(solution)/shard_map/ppermute | solution.py:390
  60.4 16.8 %copy-start.1 = (s32[1,1024]{1,0:T(1,128)S(1)}, s32[1,1024]{1,0:T(1,128)}, u32[]{:S(2)}) copy-start(s32[1,1024]{1,0:T(1,128)} %get-tuple-element.29.dest_ref) | copy-start | bytes 12292
  61.3 1.7 %collective-permute-start.14 = (bf16[256,768]{1,0:T(8,128)(2,1)S(1)}, bf16[256,768]{1,0:T(8,128)(2,1)S(1)}, u32[]{:S(2)}, u32[]{:S(2)}) collective-permute-start(bf16[256,768]{1,0:T(8,128)(2,1)S(1)} %collective-permute-done.12.refs_11_), channel_id=1, source_target_pairs={{0,8},{1,9},{2,10},{3,11},{4,12},{5,13},{6,14},{7,15},{8,0},{9,1},... | collective-permute-start | bytes 1179656 | tf_op jit(solution)/shard_map/ppermute | solution.py:390

commit v12 on v11

--- a/solution.py
+++ b/solution.py
@@ -11,6 +11,7 @@
 TILES = 4
 LABEL_ROWS = 16
 FAR = 1.0e9
+WANTED = 20_000_000_000
 PACK_VMEM = 60 * 1024 * 1024
 COMPARE_VMEM = 24 * 1024 * 1024
 NT = (((1,), (1,)), ((), ()))
@@ -39,11 +40,11 @@
     return offsets, pairs
 
 
-def pack_kernel(sizes, ks, labelled, emb_hbm, cluster_hbm, rank_hbm, *refs):
+def pack_kernel(sizes, ks, placed, emb_hbm, cluster_hbm, rank_hbm, *refs):
     groups, halves, half, cap, blk = sizes
     outs, refs = refs[: len(ks)], refs[len(ks) :]
-    if labelled:
-        dest_ref, key_ref, *refs = refs
+    if placed:
+        dest_ref, *refs = refs
     emb_ref, cluster_ref, rank_ref, stage, sems, out_sems = refs
     rows = emb_ref.shape[0]
     step = 256
@@ -81,7 +82,7 @@
         carry = carry + jnp.sum(hit, axis=1, keepdims=True)
         places.append(jnp.where(mine >= 0, mine * cap + position.astype(jnp.int32), -1))
     dest = jnp.concatenate(places, axis=1)
-    if labelled:
+    if placed:
         dest_ref[...] = dest
     members = halves // 2
     side = members // groups
@@ -103,37 +104,37 @@
     labels = jnp.where(alive, labels, 0).astype(jnp.float32).astype(jnp.bfloat16)
     unit_of = lax.div(lax.broadcasted_iota(jnp.int32, (1, blk), 1), cap).astype(jnp.float32)
     slot = lax.broadcasted_iota(jnp.int32, (blk, rows), 0)
+    line = lax.broadcasted_iota(jnp.int32, (LABEL_ROWS, blk), 0)
+    width = emb_ref.shape[1]
     leaving = []
-    for k in (*ks, *(k for k in range(groups) if labelled and k not in ks)):
+    for n, k in enumerate(ks):
         pick = (slot + k * blk == dest).astype(jnp.float32).astype(jnp.bfloat16)
-        if labelled:
-            mine = lax.dot_general(labels, pick, NT, preferred_element_type=jnp.float32)
-            key = mine[0:1] + float(half) * unit_of + float(halves * half) * mine[1:2]
-            for p in range(groups):
-                for y in range(side):
-                    key_ref[pl.ds(p * members + (here ^ k) * side + y, 1), 0, :] = key
-        if k in ks:
-            n = ks.index(k)
-            stage[n] = jnp.dot(pick, unit, preferred_element_type=jnp.float32).astype(jnp.bfloat16)
-            leaving.append(pltpu.make_async_copy(stage.at[n], outs[n], out_sems.at[n]))
-            leaving[-1].start()
+        stage[n, 0:blk, :] = jnp.dot(pick, unit, preferred_element_type=jnp.float32).astype(
+            jnp.bfloat16
+        )
+        mine = lax.dot_general(labels, pick, NT, preferred_element_type=jnp.float32)
+        high = unit_of + float(halves) * mine[1:2]
+        strip = jnp.where(line == 0, mine[0:1], jnp.where(line == 1, high, 0.0))
+        strip = jnp.concatenate([strip, jnp.zeros((LABEL_ROWS, width - blk), jnp.float32)], axis=1)
+        stage[n, blk : blk + LABEL_ROWS, :] = strip.astype(jnp.bfloat16)
+        leaving.append(pltpu.make_async_copy(stage.at[n], outs[n], out_sems.at[n]))
+        leaving[-1].start()
     for copy in leaving:
         copy.wait()
 
 
-def pack(embeddings, cluster, rank, ks, labelled, sizes):
+def pack(embeddings, cluster, rank, ks, placed, sizes):
     groups, halves, half, cap, blk = sizes
     rows, width = embeddings.shape
     hbm = pl.BlockSpec(memory_space=pltpu.HBM)
     vmem = pl.BlockSpec(memory_space=pltpu.VMEM)
-    out_shape = [jax.ShapeDtypeStruct((blk, width), jnp.bfloat16)] * len(ks)
+    out_shape = [jax.ShapeDtypeStruct((blk + LABEL_ROWS, width), jnp.bfloat16)] * len(ks)
     out_specs = [hbm] * len(ks)
-    if labelled:
+    if placed:
         out_shape.append(jax.ShapeDtypeStruct((1, rows), jnp.int32))
-        out_shape.append(jax.ShapeDtypeStruct((groups * halves // 2, 1, blk), jnp.float32))
-        out_specs += [vmem, vmem]
+        out_specs.append(vmem)
     return pl.pallas_call(
-        functools.partial(pack_kernel, sizes, ks, labelled),
+        functools.partial(pack_kernel, sizes, ks, placed),
         out_shape=out_shape,
         in_specs=[hbm, hbm, hbm],
         out_specs=out_specs,
@@ -141,7 +142,7 @@
             pltpu.VMEM((rows, width), jnp.bfloat16),
             pltpu.VMEM((1, rows), jnp.int32),
             pltpu.VMEM((1, rows), jnp.int32),
-            pltpu.VMEM((len(ks), blk, width), jnp.bfloat16),
+            pltpu.VMEM((len(ks), blk + LABEL_ROWS, width), jnp.bfloat16),
             pltpu.SemaphoreType.DMA((2 + rows // 256,)),
             pltpu.SemaphoreType.DMA((len(ks),)),
         ],
@@ -152,7 +153,7 @@
     )(embeddings, cluster.reshape(1, rows), rank.reshape(1, rows))
 
 
-def compare_kernel(sizes, jobs, names, spots, offsets, starts, joined, has_prev, label_ref, *refs):
+def compare_kernel(sizes, jobs, names, spots, starts, joined, has_prev, *refs):
     groups, halves, half, cap, blk = sizes
     array = dict(zip(names, refs))
     refs = refs[len(names) :]
@@ -166,28 +167,26 @@
     tile = rows // TILES
     cap_all = float(halves * half)
 
-    members = halves // 2
-    side = members // groups
-    across, along = lax.axis_index("grp"), lax.axis_index("mem")
+    side = halves // 2 // groups
+    along = lax.axis_index("mem")
+
+    def strip_of(piece):
+        ref, at = block[piece]
+        first = ref.shape[0] - LABEL_ROWS
+        return ref[first : first + LABEL_ROWS, at : at + blk]
 
     def keys_of(piece):
-        i, k = piece
-        row = (across ^ (offsets[i] // side)) * members
-        row += ((along // side) ^ k) * side + ((along % side) ^ (offsets[i] % side))
-        return label_ref[pl.ds(row, 1), 0, :]
+        strip = strip_of(piece).astype(jnp.float32)
+        return strip[0:1] + float(half) * strip[1:2]
 
     weight_row = lax.broadcasted_iota(jnp.int32, (LABEL_ROWS, 128), 0)
     weights = jnp.where(weight_row == 0, 1.0, jnp.where(weight_row == 1, float(half), 0.0))
     weights = weights.astype(jnp.bfloat16)
-    field = lax.broadcasted_iota(jnp.int32, (LABEL_ROWS, blk), 0)
     needed = sorted({piece for *_, pieces in jobs for piece in pieces})
     key_at = {piece: n * blk for n, piece in enumerate(needed)}
     for piece in needed:
-        key = keys_of(piece)
-        high = jnp.floor(key * (1.0 / half))
-        split = jnp.where(field == 0, key - high * half, jnp.where(field == 1, high, 0.0))
         key_col[pl.ds(key_at[piece], blk), :] = lax.dot_general(
-            split.astype(jnp.bfloat16), weights, TN, preferred_element_type=jnp.float32
+            strip_of(piece), weights, TN, preferred_element_type=jnp.float32
         )
     lane = lax.div(lax.broadcasted_iota(jnp.int32, (1, tile), 1), per_tile)
 
@@ -270,7 +269,7 @@
                 outs[o][pl.ds(at, 1), 0, :] = total[:, :blk]
 
 
-def compare(labels, blocks, jobs, prev, starts, joined, offsets, sizes):
+def compare(blocks, jobs, prev, starts, joined, offsets, sizes):
     groups, halves, half, cap, blk = sizes
     n_sets = len(offsets)
     used = {piece for *_, pieces in jobs for piece in pieces}
@@ -298,11 +297,11 @@
         out_shape = [jax.ShapeDtypeStruct((groups * joined, 1, blk), jnp.float32)]
     else:
         out_shape = [jax.ShapeDtypeStruct((groups, 1, blk), jnp.float32)] * len(starts)
-    operands = [labels] + list(arrays.values()) + ([] if prev is None else [prev])
+    operands = list(arrays.values()) + ([] if prev is None else [prev])
     needed = {piece for *_, pieces in jobs for piece in pieces}
     return pl.pallas_call(
         functools.partial(
-            compare_kernel, sizes, jobs, names, spots, offsets, starts, joined, prev is not None
+            compare_kernel, sizes, jobs, names, spots, starts, joined, prev is not None
         ),
         out_shape=out_shape,
         in_specs=[vmem] * len(operands),
@@ -319,22 +318,29 @@
     )(*operands)
 
 
-def join_kernel(first_ref, second_ref, out_ref):
-    rows = first_ref.shape[0]
-    out_ref[:rows, :] = first_ref[...]
-    out_ref[rows:, :] = second_ref[...]
-
-
-def join(first, second):
-    rows, width = first.shape
+def join_kernel(*refs):
+    out_ref, ins = refs[-1], refs[:-1]
+    blk, width = ins[0].shape[0] - LABEL_ROWS, ins[0].shape[1]
+    parts = []
+    for n, ref in enumerate(ins):
+        out_ref[n * blk : (n + 1) * blk, :] = ref[0:blk, :]
+        parts.append(ref[blk : blk + LABEL_ROWS, 0:blk])
+    parts.append(jnp.zeros((LABEL_ROWS, width - len(ins) * blk), jnp.bfloat16))
+    out_ref[len(ins) * blk :, :] = jnp.concatenate(parts, axis=1)
+
+
+def join(pieces, flops):
+    rows, width = pieces[0].shape
+    total = len(pieces) * (rows - LABEL_ROWS) + LABEL_ROWS
     vmem = pl.BlockSpec(memory_space=pltpu.VMEM)
     return pl.pallas_call(
         join_kernel,
-        out_shape=jax.ShapeDtypeStruct((2 * rows, width), first.dtype),
-        in_specs=[vmem, vmem],
+        out_shape=jax.ShapeDtypeStruct((total, width), pieces[0].dtype),
+        in_specs=[vmem] * len(pieces),
         out_specs=vmem,
         compiler_params=pltpu.CompilerParams(vmem_limit_bytes=COMPARE_VMEM),
-    )(first, second)
+        cost_estimate=pl.CostEstimate(flops=flops, bytes_accessed=0, transcendentals=0),
+    )(*pieces)
 
 
 def unpack_kernel(sizes, dest_ref, back_ref, out_ref):
@@ -396,10 +402,9 @@
         sends[k] = value
     rest = tuple(k for k in range(groups) if k not in first)
     cluster, sends[1] = lax.optimization_barrier((cluster, sends[1]))
-    *packed, dest, labels = pack(embeddings, cluster, rank, rest, True, sizes)
+    *packed, dest = pack(embeddings, cluster, rank, rest, True, sizes)
     for k, value in zip(rest, packed):
         sends[k] = value
-    labels = lax.all_to_all(labels, ("grp", "mem"), split_axis=0, concat_axis=0, tiled=True)
 
     last = groups - 1
     far = [d for d in offsets if d & side and d != side and d ^ side in offsets]
@@ -420,13 +425,15 @@
         if k < last:
             also = swap(sends[k + 1], k + 1, 0)
             if k == 1:
-                mine, also, labels, *firsts = lax.optimization_barrier(
-                    (mine, also, labels, *(held[d][0] for d in near))
+                mine, also, *firsts = lax.optimization_barrier(
+                    (mine, also, *(held[d][0] for d in near))
                 )
                 for d, value in zip(near, firsts):
                     held[d] = [value]
-            mine = join(mine, also)
+            mine = join([mine, also], 0)
             after = mine
+        else:
+            mine = join([mine], WANTED)
         held[0].append(mine)
         for d in near:
             held[d].append(swap(mine, 0, d))
@@ -473,13 +480,13 @@
             late.append((index[a], True, (last,), soon))
     order = [index[a] for a in starts]
     joined = side if all(a < side for a in starts) else 0
-    prev = compare(labels, blocks, early, None, (), 0, offsets, sizes)[0]
-    prev = compare(labels, blocks, middle, prev, (), 0, offsets, sizes)[0]
+    prev = compare(blocks, early, None, (), 0, offsets, sizes)[0]
+    prev = compare(blocks, middle, prev, (), 0, offsets, sizes)[0]
     for d in far:
         piece, prev = lax.optimization_barrier((held[d ^ side][-1], prev))
         held[d].append(swap(piece, 0, side))
     note()
-    found = compare(labels, blocks, late, prev, order, joined, offsets, sizes)
+    found = compare(blocks, late, prev, order, joined, offsets, sizes)
     if joined:
         back = found[0]
     else:

time: 78.6 us -> 81.2 us (1.033)
  waiting for transfers between devices: 19.3 us -> 33.1 us
  blocking collectives: 23.5 us -> 9.9 us
  starting transfers between devices: 15.2 us -> 17.1 us
    ppermute x15, waiting for transfers between devices: 19.3 us -> 33.1 us  [swap(): lax.ppermute(value, ('grp', 'mem'), [(i, i ^ mask) for i in range(devices)])]
    all_to_all x1 -> x0, blocking collectives: 12.8 us -> none  [on_device(): lax.all_to_all(labels, ('grp', 'mem'), split_axis=0, concat_axis=0, tiled...]
    ppermute x15, starting transfers between devices: 15.2 us -> 17.1 us  [swap(): lax.ppermute(value, ('grp', 'mem'), [(i, i ^ mask) for i in range(devices)])]
    all_to_all x1, blocking collectives: 10.8 us -> 9.9 us  [on_device(): back = lax.all_to_all(back, 'mem', split_axis=0, concat_axis=0, tiled=True)]
    pallas_call x3 -> x4, Pallas kernels: 7.57 us -> 7.85 us  [the longest x2 7.76 us: pack(): pl.pallas_call(functools.partial(pack_kernel, sizes, ks, placed), out_sha...]
  transfers between devices with their start and end apart: 15 -> 15, of which waited for: 6 -> 8; matrix products, arithmetic and copies ran while one was open for 0% -> 0% of each run, Pallas kernels for 16% -> 15%
where the time goes in v12:
time: 81.2 us; the launch traced here: 80.9 us
  waiting for transfers between devices  33.1 us (41%)
  Pallas kernels  20.7 us (25%)
  starting transfers between devices  17.1 us (21%)
  blocking collectives  9.9 us (12%)
    ppermute x15, waiting for transfers between devices, swap(): lax.ppermute(value, ('grp', 'mem'), [(i, i ^ mask) for i in range(devices)])  33.1 us
    ppermute x15, starting transfers between devices, swap(): lax.ppermute(value, ('grp', 'mem'), [(i, i ^ mask) for i in range(devices)])  17.1 us
    pallas_call x3, Pallas kernels, compare(): pl.pallas_call(functools.partial(compare_kernel, sizes, jobs, names, spot...  11.8 us
    all_to_all x1, blocking collectives, on_device(): back = lax.all_to_all(back, 'mem', split_axis=0, concat_axis=0, tiled=True)  9.9 us
    pallas_call x2, Pallas kernels, pack(): pl.pallas_call(functools.partial(pack_kernel, sizes, ks, placed), out_sha...  7.76 us
  transfers between devices with their start and end apart: 15, of which 8 were waited for; matrix products, arithmetic and copies ran while one was open for 0% of the time, Pallas kernels for 15%

profile of v12, /device:TPU:0, one launch (start us, length us, event | category | flops | bytes accessed | tf_op | source)
XLA Modules:
  0.0 80.9 jit_solution(16468416973029439167)
XLA Ops:
  0.0 3.6 %shard_map.37 = (bf16[272,768]{1,0:T(8,128)(2,1)}, bf16[272,768]{1,0:T(8,128)(2,1)}) custom-call(bf16[1024,768]{1,0:T(8,128)(2,1)} %emb_hbm.3, s32[1,1024]{1,0:T(1,128)} %bitcast.4, s32[1,1024]{1,0:T(1,128)} %bitcast.6), custom_call_target="tpu_custom_call" | custom-call | flops 805306368 | bytes 3145728 | tf_op jit(solution)/shard_map/pallas_call | solution.py:136
  3.6 3.1 %collective-permute-start = (bf16[272,768]{1,0:T(8,128)(2,1)}, bf16[272,768]{1,0:T(8,128)(2,1)S(1)}, u32[]{:S(2)}, u32[]{:S(2)}) collective-permute-start(bf16[272,768]{1,0:T(8,128)(2,1)} %get-tuple-element.29), channel_id=1, source_target_pairs={{0,2},{1,3},{2,0},{3,1},{4,6},{5,7},{6,4},{7,5},{8,10},{9,11},{10,... | collective-permute-start | bytes 1253384 | tf_op jit(solution)/shard_map/ppermute | solution.py:396
  6.7 2.6 %collective-permute-start.1 = (bf16[272,768]{1,0:T(8,128)(2,1)}, bf16[272,768]{1,0:T(8,128)(2,1)S(1)}, u32[]{:S(2)}, u32[]{:S(2)}) collective-permute-start(bf16[272,768]{1,0:T(8,128)(2,1)} %get-tuple-element.30), channel_id=1, source_target_pairs={{0,4},{1,5},{2,6},{3,7},{4,0},{5,1},{6,2},{7,3},{8,12},{9,13},{10,... | collective-permute-start | bytes 1253384 | tf_op jit(solution)/shard_map/ppermute | solution.py:396
  9.3 4.2 %shard_map.38 = (bf16[272,768]{1,0:T(8,128)(2,1)}, bf16[272,768]{1,0:T(8,128)(2,1)}, s32[1,1024]{1,0:T(1,128)}) custom-call(bf16[1024,768]{1,0:T(8,128)(2,1)} %emb_hbm.3, s32[1,1024]{1,0:T(1,128)} %bitcast.5, s32[1,1024]{1,0:T(1,128)} %bitcast.7), custom_call_target="tpu_custom_call" | custom-call | flops 805306368 | bytes 3145728 | tf_op jit(solution)/shard_map/pallas_call | solution.py:136
  13.5 1.6 %collective-permute-start.4 = (bf16[272,768]{1,0:T(8,128)(2,1)}, bf16[272,768]{1,0:T(8,128)(2,1)S(1)}, u32[]{:S(2)}, u32[]{:S(2)}) collective-permute-start(bf16[272,768]{1,0:T(8,128)(2,1)} %get-tuple-element.28.refs_0_), channel_id=1, source_target_pairs={{0,16},{1,17},{2,18},{3,19},{4,20},{5,21},{6,22},{7,23},{8,24},{9,... | collective-permute-start | bytes 1253384 | tf_op jit(solution)/shard_map/ppermute | solution.py:396
  15.0 1.5 %collective-permute-start.2 = (bf16[272,768]{1,0:T(8,128)(2,1)}, bf16[272,768]{1,0:T(8,128)(2,1)S(1)}, u32[]{:S(2)}, u32[]{:S(2)}) collective-permute-start(bf16[272,768]{1,0:T(8,128)(2,1)} %get-tuple-element.28.refs_0_), channel_id=1, source_target_pairs={{0,1},{1,0},{2,3},{3,2},{4,5},{5,4},{6,7},{7,6},{8,9},{9,8},{10,11... | collective-permute-start | bytes 1253384 | tf_op jit(solution)/shard_map/ppermute | solution.py:396
  16.6 8.8 %collective-permute-done.refs_0_ = bf16[272,768]{1,0:T(8,128)(2,1)S(1)} collective-permute-done((bf16[272,768]{1,0:T(8,128)(2,1)}, bf16[272,768]{1,0:T(8,128)(2,1)S(1)}, u32[]{:S(2)}, u32[]{:S(2)}) %collective-permute-start) | collective-permute-done | bytes 417824 | tf_op jit(solution)/shard_map/ppermute | solution.py:396
  25.4 2.5 %collective-permute-done.1.refs_1_ = bf16[272,768]{1,0:T(8,128)(2,1)S(1)} collective-permute-done((bf16[272,768]{1,0:T(8,128)(2,1)}, bf16[272,768]{1,0:T(8,128)(2,1)S(1)}, u32[]{:S(2)}, u32[]{:S(2)}) %collective-permute-start.1) | collective-permute-done | bytes 417824 | tf_op jit(solution)/shard_map/ppermute | solution.py:396
  28.0 2.5 %collective-permute-start.5 = (bf16[272,768]{1,0:T(8,128)(2,1)S(1)}, bf16[272,768]{1,0:T(8,128)(2,1)S(1)}, u32[]{:S(2)}, u32[]{:S(2)}) collective-permute-start(bf16[272,768]{1,0:T(8,128)(2,1)S(1)} %copy-done.2), channel_id=1, source_target_pairs={{0,6},{1,7},{2,4},{3,5},{4,2},{5,3},{6,0},{7,1},{8,14},{9,15},{10,... | collective-permute-start | bytes 1253384 | tf_op jit(solution)/shard_map/ppermute | solution.py:396
  30.5 1.5 %collective-permute-start.9 = (bf16[528,768]{1,0:T(8,128)(2,1)S(1)}, bf16[528,768]{1,0:T(8,128)(2,1)S(1)}, u32[]{:S(2)}, u32[]{:S(2)}) collective-permute-start(bf16[528,768]{1,0:T(8,128)(2,1)S(1)} %shard_map.39.refs_1_), channel_id=1, source_target_pairs={{0,16},{1,17},{2,18},{3,19},{4,20},{5,21},{6,22},{7,23},{8,24},{9,... | collective-permute-start | bytes 2433032 | tf_op jit(solution)/shard_map/ppermute | solution.py:396
  32.0 1.5 %collective-permute-start.7 = (bf16[528,768]{1,0:T(8,128)(2,1)S(1)}, bf16[528,768]{1,0:T(8,128)(2,1)S(1)}, u32[]{:S(2)}, u32[]{:S(2)}) collective-permute-start(bf16[528,768]{1,0:T(8,128)(2,1)S(1)} %shard_map.39.refs_1_), channel_id=1, source_target_pairs={{0,1},{1,0},{2,3},{3,2},{4,5},{5,4},{6,7},{7,6},{8,9},{9,8},{10,11... | collective-permute-start | bytes 2433032 | tf_op jit(solution)/shard_map/ppermute | solution.py:396
  33.8 6.8 %collective-permute-done.5.refs_0_ = bf16[272,768]{1,0:T(8,128)(2,1)S(1)} collective-permute-done((bf16[272,768]{1,0:T(8,128)(2,1)S(1)}, bf16[272,768]{1,0:T(8,128)(2,1)S(1)}, u32[]{:S(2)}, u32[]{:S(2)}) %collective-permute-start.5) | collective-permute-done | bytes 417824 | tf_op jit(solution)/shard_map/ppermute | solution.py:396
  40.7 6.6 %collective-permute-done.9.refs_8_.refs_9_.refs_10_ = bf16[528,768]{1,0:T(8,128)(2,1)S(1)} collective-permute-done((bf16[528,768]{1,0:T(8,128)(2,1)S(1)}, bf16[528,768]{1,0:T(8,128)(2,1)S(1)}, u32[]{:S(2)}, u32[]{:S(2)}) %collective-permute-start.9) | collective-permute-done | bytes 811040 | tf_op jit(solution)/shard_map/ppermute | solution.py:396
  47.2 5.3 %collective-permute-done.7.refs_4_ = bf16[528,768]{1,0:T(8,128)(2,1)S(1)} collective-permute-done((bf16[528,768]{1,0:T(8,128)(2,1)S(1)}, bf16[528,768]{1,0:T(8,128)(2,1)S(1)}, u32[]{:S(2)}, u32[]{:S(2)}) %collective-permute-start.7) | collective-permute-done | bytes 811040 | tf_op jit(solution)/shard_map/ppermute | solution.py:396
  52.5 0.5 collective-permute-start.11
  53.0 0.5 collective-permute-start.12
  53.6 1.5 %collective-permute-start.10 = (bf16[272,768]{1,0:T(8,128)(2,1)S(1)}, bf16[272,768]{1,0:T(8,128)(2,1)S(1)}, u32[]{:S(2)}, u32[]{:S(2)}) collective-permute-start(bf16[272,768]{1,0:T(8,128)(2,1)S(1)} %shard_map.40.refs_2_), channel_id=1, source_target_pairs={{0,1},{1,0},{2,3},{3,2},{4,5},{5,4},{6,7},{7,6},{8,9},{9,8},{10,11... | collective-permute-start | bytes 1253384 | tf_op jit(solution)/shard_map/ppermute | solution.py:396
  55.1 4.3 %shard_map.41.refs_12_ = f32[5,8,256]{2,1,0:T(8,128)S(1)} custom-call(bf16[272,768]{1,0:T(8,128)(2,1)S(1)} %copy-done, bf16[528,768]{1,0:T(8,128)(2,1)S(1)} %shard_map.39.refs_1_, bf16[272,768]{1,0:T(8,128)(2,1)S(1)} %shard_map.40.refs_2_, bf16[272,768]{1,0:T(8,128)(2,1)S(1)} %collective-permute-done.2.refs_3_, ...), custom_call_target="tpu_custom_call" | custom-call | flops 880803840 | bytes 5505024 | tf_op jit(solution)/shard_map/pallas_call | solution.py:302
  59.4 3.9 %shard_map.42.refs_15_ = f32[5,8,256]{2,1,0:T(8,128)S(1)} custom-call(bf16[272,768]{1,0:T(8,128)(2,1)S(1)} %copy-done, bf16[528,768]{1,0:T(8,128)(2,1)S(1)} %shard_map.39.refs_1_, bf16[272,768]{1,0:T(8,128)(2,1)S(1)} %shard_map.40.refs_2_, bf16[272,768]{1,0:T(8,128)(2,1)S(1)} %collective-permute-done.2.refs_3_, ...), custom_call_target="tpu_custom_call" | custom-call | flops 754974720 | bytes 6684672 | tf_op jit(solution)/shard_map/pallas_call | solution.py:302
  63.3 1.3 %collective-permute-done.12.refs_11_ = bf16[272,768]{1,0:T(8,128)(2,1)S(1)} collective-permute-done((bf16[272,768]{1,0:T(8,128)(2,1)S(1)}, bf16[272,768]{1,0:T(8,128)(2,1)S(1)}, u32[]{:S(2)}, u32[]{:S(2)}) %collective-permute-start.12) | collective-permute-done | bytes 417824 | tf_op jit(solution)/shard_map/ppermute | solution.py:396
  64.8 1.5 %collective-permute-done.14.refs_14_ = bf16[272,768]{1,0:T(8,128)(2,1)S(1)} collective-permute-done((bf16[272,768]{1,0:T(8,128)(2,1)S(1)}, bf16[272,768]{1,0:T(8,128)(2,1)S(1)}, u32[]{:S(2)}, u32[]{:S(2)}) %collective-permute-start.14) | collective-permute-done | bytes 417824 | tf_op jit(solution)/shard_map/ppermute | solution.py:396
  66.3 3.6 %shard_map.43 = f32[8,1,256]{2,1,0:T(1,128)S(1)} custom-call(bf16[272,768]{1,0:T(8,128)(2,1)S(1)} %copy-done, bf16[528,768]{1,0:T(8,128)(2,1)S(1)} %shard_map.39.refs_1_, bf16[272,768]{1,0:T(8,128)(2,1)S(1)} %shard_map.40.refs_2_, bf16[272,768]{1,0:T(8,128)(2,1)S(1)} %collective-permute-done.2.refs_3_, bf16[528,768]{1,0:T(8,128)(2,1)S(1)} %collective-permute-done.7.refs_4_, ...), custom_call_target="tpu_custom_call" | custom-call | flops 1283457024 | bytes 7864320 | tf_op jit(solution)/shard_map/pallas_call | solution.py:302
  69.9 9.9 %all_to_all.5.back_ref = f32[8,1,256]{2,1,0:T(1,128)S(1)} all-to-all(f32[8,1,256]{2,1,0:T(1,128)S(1)} %shard_map.43), channel_id=1, replica_groups=mesh['grp'=4,'mem'=8] {'mem'}, dimensions={0} | all-to-all | bytes 16384 | tf_op jit(solution)/shard_map/all_to_all | solution.py:507
  79.8 1.1 %shard_map.44 = f32[1,1024]{1,0:T(1,128)} custom-call(s32[1,1024]{1,0:T(1,128)S(1)} %copy-done.1, f32[8,1,256]{2,1,0:T(1,128)S(1)} %all_to_all.5.back_ref), custom_call_target="tpu_custom_call" | custom-call | tf_op jit(solution)/shard_map/pallas_call | solution.py:371
  (21 shorter events, 0.6 us)
Async XLA Ops:
  3.6 21.8 %collective-permute-start = (bf16[272,768]{1,0:T(8,128)(2,1)}, bf16[272,768]{1,0:T(8,128)(2,1)S(1)}, u32[]{:S(2)}, u32[]{:S(2)}) collective-permute-start(bf16[272,768]{1,0:T(8,128)(2,1)} %get-tuple-element.29), channel_id=1, source_target_pairs={{0,2},{1,3},{2,0},{3,1},{4,6},{5,7},{6,4},{7,5},{8,10},{9,11},{10,... | collective-permute-start | bytes 1253384 | tf_op jit(solution)/shard_map/ppermute | solution.py:396
  6.7 21.2 %collective-permute-start.1 = (bf16[272,768]{1,0:T(8,128)(2,1)}, bf16[272,768]{1,0:T(8,128)(2,1)S(1)}, u32[]{:S(2)}, u32[]{:S(2)}) collective-permute-start(bf16[272,768]{1,0:T(8,128)(2,1)} %get-tuple-element.30), channel_id=1, source_target_pairs={{0,4},{1,5},{2,6},{3,7},{4,0},{5,1},{6,2},{7,3},{8,12},{9,13},{10,... | collective-permute-start | bytes 1253384 | tf_op jit(solution)/shard_map/ppermute | solution.py:396
  13.5 14.5 %copy-start.2 = (bf16[272,768]{1,0:T(8,128)(2,1)S(1)}, bf16[272,768]{1,0:T(8,128)(2,1)}, u32[]{:S(2)}) copy-start(bf16[272,768]{1,0:T(8,128)(2,1)} %get-tuple-element.34) | copy-start | bytes 1253380
  13.5 14.4 %collective-permute-start.4 = (bf16[272,768]{1,0:T(8,128)(2,1)}, bf16[272,768]{1,0:T(8,128)(2,1)S(1)}, u32[]{:S(2)}, u32[]{:S(2)}) collective-permute-start(bf16[272,768]{1,0:T(8,128)(2,1)} %get-tuple-element.28.refs_0_), channel_id=1, source_target_pairs={{0,16},{1,17},{2,18},{3,19},{4,20},{5,21},{6,22},{7,23},{8,24},{9,... | collective-permute-start | bytes 1253384 | tf_op jit(solution)/shard_map/ppermute | solution.py:396
  15.0 12.9 %collective-permute-start.3 = (bf16[272,768]{1,0:T(8,128)(2,1)}, bf16[272,768]{1,0:T(8,128)(2,1)S(1)}, u32[]{:S(2)}, u32[]{:S(2)}) collective-permute-start(bf16[272,768]{1,0:T(8,128)(2,1)} %get-tuple-element.28.refs_0_), channel_id=1, source_target_pairs={{0,8},{1,9},{2,10},{3,11},{4,12},{5,13},{6,14},{7,15},{8,0},{9,1},... | collective-permute-start | bytes 1253384 | tf_op jit(solution)/shard_map/ppermute | solution.py:396
  15.0 12.9 %collective-permute-start.2 = (bf16[272,768]{1,0:T(8,128)(2,1)}, bf16[272,768]{1,0:T(8,128)(2,1)S(1)}, u32[]{:S(2)}, u32[]{:S(2)}) collective-permute-start(bf16[272,768]{1,0:T(8,128)(2,1)} %get-tuple-element.28.refs_0_), channel_id=1, source_target_pairs={{0,1},{1,0},{2,3},{3,2},{4,5},{5,4},{6,7},{7,6},{8,9},{9,8},{10,11... | collective-permute-start | bytes 1253384 | tf_op jit(solution)/shard_map/ppermute | solution.py:396
  28.0 27.1 %copy-start = (bf16[272,768]{1,0:T(8,128)(2,1)S(1)}, bf16[272,768]{1,0:T(8,128)(2,1)}, u32[]{:S(2)}) copy-start(bf16[272,768]{1,0:T(8,128)(2,1)} %get-tuple-element.28.refs_0_) | copy-start | bytes 1253380
  28.0 12.6 %collective-permute-start.5 = (bf16[272,768]{1,0:T(8,128)(2,1)S(1)}, bf16[272,768]{1,0:T(8,128)(2,1)S(1)}, u32[]{:S(2)}, u32[]{:S(2)}) collective-permute-start(bf16[272,768]{1,0:T(8,128)(2,1)S(1)} %copy-done.2), channel_id=1, source_target_pairs={{0,6},{1,7},{2,4},{3,5},{4,2},{5,3},{6,0},{7,1},{8,14},{9,15},{10,... | collective-permute-start | bytes 1253384 | tf_op jit(solution)/shard_map/ppermute | solution.py:396
  30.5 16.7 %collective-permute-start.9 = (bf16[528,768]{1,0:T(8,128)(2,1)S(1)}, bf16[528,768]{1,0:T(8,128)(2,1)S(1)}, u32[]{:S(2)}, u32[]{:S(2)}) collective-permute-start(bf16[528,768]{1,0:T(8,128)(2,1)S(1)} %shard_map.39.refs_1_), channel_id=1, source_target_pairs={{0,16},{1,17},{2,18},{3,19},{4,20},{5,21},{6,22},{7,23},{8,24},{9,... | collective-permute-start | bytes 2433032 | tf_op jit(solution)/shard_map/ppermute | solution.py:396
  32.0 15.2 %collective-permute-start.8 = (bf16[528,768]{1,0:T(8,128)(2,1)S(1)}, bf16[528,768]{1,0:T(8,128)(2,1)S(1)}, u32[]{:S(2)}, u32[]{:S(2)}) collective-permute-start(bf16[528,768]{1,0:T(8,128)(2,1)S(1)} %shard_map.39.refs_1_), channel_id=1, source_target_pairs={{0,8},{1,9},{2,10},{3,11},{4,12},{5,13},{6,14},{7,15},{8,0},{9,1},... | collective-permute-start | bytes 2433032 | tf_op jit(solution)/shard_map/ppermute | solution.py:396
  32.0 20.5 %collective-permute-start.7 = (bf16[528,768]{1,0:T(8,128)(2,1)S(1)}, bf16[528,768]{1,0:T(8,128)(2,1)S(1)}, u32[]{:S(2)}, u32[]{:S(2)}) collective-permute-start(bf16[528,768]{1,0:T(8,128)(2,1)S(1)} %shard_map.39.refs_1_), channel_id=1, source_target_pairs={{0,1},{1,0},{2,3},{3,2},{4,5},{5,4},{6,7},{7,6},{8,9},{9,8},{10,11... | collective-permute-start | bytes 2433032 | tf_op jit(solution)/shard_map/ppermute | solution.py:396
  33.6 7.1 %collective-permute-start.6 = (bf16[272,768]{1,0:T(8,128)(2,1)S(1)}, bf16[272,768]{1,0:T(8,128)(2,1)S(1)}, u32[]{:S(2)}, u32[]{:S(2)}) collective-permute-start(bf16[272,768]{1,0:T(8,128)(2,1)S(1)} %collective-permute-done.4.refs_7_.refs_8_.refs_9_), channel_id=1, source_target_pairs={{0,8},{1,9},{2,10},{3,11},{4,12},{5,13},{6,14},{7,15},{8,0},{9,1},... | collective-permute-start | bytes 1253384 | tf_op jit(solution)/shard_map/ppermute | solution.py:396
  52.5 6.9 %collective-permute-start.13 = (bf16[528,768]{1,0:T(8,128)(2,1)S(1)}, bf16[528,768]{1,0:T(8,128)(2,1)S(1)}, u32[]{:S(2)}, u32[]{:S(2)}) collective-permute-start(bf16[528,768]{1,0:T(8,128)(2,1)S(1)} %collective-permute-done.9.refs_8_.refs_9_.refs_10_), channel_id=1, source_target_pairs={{0,8},{1,9},{2,10},{3,11},{4,12},{5,13},{6,14},{7,15},{8,0},{9,1},... | collective-permute-start | bytes 2433032 | tf_op jit(solution)/shard_map/ppermute | solution.py:396
  52.5 6.9 %collective-permute-start.11 = (bf16[272,768]{1,0:T(8,128)(2,1)S(1)}, bf16[272,768]{1,0:T(8,128)(2,1)S(1)}, u32[]{:S(2)}, u32[]{:S(2)}) collective-permute-start(bf16[272,768]{1,0:T(8,128)(2,1)S(1)} %shard_map.40.refs_2_), channel_id=1, source_target_pairs={{0,8},{1,9},{2,10},{3,11},{4,12},{5,13},{6,14},{7,15},{8,0},{9,1},... | collective-permute-start | bytes 1253384 | tf_op jit(solution)/shard_map/ppermute | solution.py:396
  53.0 11.6 %collective-permute-start.12 = (bf16[272,768]{1,0:T(8,128)(2,1)S(1)}, bf16[272,768]{1,0:T(8,128)(2,1)S(1)}, u32[]{:S(2)}, u32[]{:S(2)}) collective-permute-start(bf16[272,768]{1,0:T(8,128)(2,1)S(1)} %shard_map.40.refs_2_), channel_id=1, source_target_pairs={{0,16},{1,17},{2,18},{3,19},{4,20},{5,21},{6,22},{7,23},{8,24},{9,... | collective-permute-start | bytes 1253384 | tf_op jit(solution)/shard_map/ppermute | solution.py:396
  53.6 11.3 %collective-permute-start.10 = (bf16[272,768]{1,0:T(8,128)(2,1)S(1)}, bf16[272,768]{1,0:T(8,128)(2,1)S(1)}, u32[]{:S(2)}, u32[]{:S(2)}) collective-permute-start(bf16[272,768]{1,0:T(8,128)(2,1)S(1)} %shard_map.40.refs_2_), channel_id=1, source_target_pairs={{0,1},{1,0},{2,3},{3,2},{4,5},{5,4},{6,7},{7,6},{8,9},{9,8},{10,11... | collective-permute-start | bytes 1253384 | tf_op jit(solution)/shard_map/ppermute | solution.py:396
  63.3 16.6 %copy-start.1 = (s32[1,1024]{1,0:T(1,128)S(1)}, s32[1,1024]{1,0:T(1,128)}, u32[]{:S(2)}) copy-start(s32[1,1024]{1,0:T(1,128)} %get-tuple-element.27.dest_ref) | copy-start | bytes 12292
  64.6 1.8 %collective-permute-start.14 = (bf16[272,768]{1,0:T(8,128)(2,1)S(1)}, bf16[272,768]{1,0:T(8,128)(2,1)S(1)}, u32[]{:S(2)}, u32[]{:S(2)}) collective-permute-start(bf16[272,768]{1,0:T(8,128)(2,1)S(1)} %collective-permute-done.12.refs_11_), channel_id=1, source_target_pairs={{0,8},{1,9},{2,10},{3,11},{4,12},{5,13},{6,14},{7,15},{8,0},{9,1},... | collective-permute-start | bytes 1253384 | tf_op jit(solution)/shard_map/ppermute | solution.py:396

commit v13 on v12

--- a/solution.py
+++ b/solution.py
@@ -413,8 +413,6 @@
     held = {0: [sends[0]]}
     for d in near:
         held[d] = [swap(sends[0], 0, d)]
-    for d in far:
-        held[d] = [swap(held[d ^ side][0], 0, side)]
     after = held[lead][0]
     for k in range(1, groups, 2):
         if k > 1:
@@ -435,19 +433,24 @@
         else:
             mine = join([mine], WANTED)
         held[0].append(mine)
+    spots = len(held[0])
+    for spot in range(1, spots):
         for d in near:
-            held[d].append(swap(mine, 0, d))
-    for spot in range(1, len(held[0]) - 1):
-        held[0][spot + 1], *values = lax.optimization_barrier(
-            (held[0][spot + 1], *(held[d][0] for d in far), *(held[d][spot] for d in near))
-        )
-        for d in far:
-            held[d][0] = values.pop(0)
-        for d, value in zip(near, values):
-            held[d][spot] = value
+            if d != side:
+                held[d].append(swap(held[0][spot], 0, d))
+    end, side_hop = held[0][-1], held[near[0]]
+    for spot in range(1, spots):
+        piece, end = lax.optimization_barrier((held[0][spot], end))
+        if spot == spots - 1:
+            piece, side_hop[spot - 1] = lax.optimization_barrier((piece, side_hop[spot - 1]))
+        held[side].append(swap(piece, 0, side))
     for d in far:
-        for spot in range(1, len(held[0]) - 1):
-            held[d].append(swap(held[d ^ side][spot], 0, side))
+        held[d] = []
+        for spot in range(spots - 1):
+            piece, side_hop[spots - 2] = lax.optimization_barrier(
+                (held[d ^ side][spot], side_hop[spots - 2])
+            )
+            held[d].append(swap(piece, 0, side))
 
     index = {d: i for i, d in enumerate(offsets)}
     blocks = {}
@@ -468,7 +471,7 @@
         pieces = [(b, k) for b in cols for k in every]
         soon = [(b, k) for b, k in pieces if k < last]
         if a == 0:
-            slow = {(index[d], k) for d in far for k in range(1, last)} | {(index[side], last)}
+            slow = {(index[d], k) for d in far for k in range(last)} | {(index[side], last)}
             ready = [piece for piece in pieces if piece in soon or piece[0] == 0]
             early.append((0, False, every, [piece for piece in ready if piece not in slow]))
             middle.append((0, False, every, [piece for piece in pieces if piece in slow]))

time: 81.2 us -> 78.8 us (0.970)
  waiting for transfers between devices: 33.1 us -> 30.1 us
  blocking collectives: 9.9 us -> 11.1 us
    ppermute x15, waiting for transfers between devices: 33.1 us -> 30.1 us  [swap(): lax.ppermute(value, ('grp', 'mem'), [(i, i ^ mask) for i in range(devices)])]
    all_to_all x1, blocking collectives: 9.9 us -> 11.1 us  [on_device(): back = lax.all_to_all(back, 'mem', split_axis=0, concat_axis=0, tiled=True)]
  transfers between devices with their start and end apart: 15 -> 15, of which waited for: 8 -> 8; matrix products, arithmetic and copies ran while one was open for 0% -> 0% of each run, Pallas kernels for 15% -> 16%
where the time goes in v13:
time: 78.8 us; the launch traced here: 78.5 us
  waiting for transfers between devices  30.1 us (38%)
  Pallas kernels  20.7 us (26%)
  starting transfers between devices  16.5 us (21%)
  blocking collectives  11.1 us (14%)
    ppermute x15, waiting for transfers between devices, swap(): lax.ppermute(value, ('grp', 'mem'), [(i, i ^ mask) for i in range(devices)])  30.1 us
    ppermute x15, starting transfers between devices, swap(): lax.ppermute(value, ('grp', 'mem'), [(i, i ^ mask) for i in range(devices)])  16.5 us
    pallas_call x3, Pallas kernels, compare(): pl.pallas_call(functools.partial(compare_kernel, sizes, jobs, names, spot...  11.7 us
    all_to_all x1, blocking collectives, on_device(): back = lax.all_to_all(back, 'mem', split_axis=0, concat_axis=0, tiled=True)  11.1 us
    pallas_call x2, Pallas kernels, pack(): pl.pallas_call(functools.partial(pack_kernel, sizes, ks, placed), out_sha...  7.76 us
  transfers between devices with their start and end apart: 15, of which 8 were waited for; matrix products, arithmetic and copies ran while one was open for 0% of the time, Pallas kernels for 16%

profile of v13, /device:TPU:0, one launch (start us, length us, event | category | flops | bytes accessed | tf_op | source)
XLA Modules:
  0.0 78.5 jit_solution(16237571983835449713)
XLA Ops:
  0.0 3.6 %shard_map.37 = (bf16[272,768]{1,0:T(8,128)(2,1)}, bf16[272,768]{1,0:T(8,128)(2,1)}) custom-call(bf16[1024,768]{1,0:T(8,128)(2,1)} %emb_hbm.3, s32[1,1024]{1,0:T(1,128)} %bitcast.4, s32[1,1024]{1,0:T(1,128)} %bitcast.6), custom_call_target="tpu_custom_call" | custom-call | flops 805306368 | bytes 3145728 | tf_op jit(solution)/shard_map/pallas_call | solution.py:136
  3.6 3.1 %collective-permute-start = (bf16[272,768]{1,0:T(8,128)(2,1)}, bf16[272,768]{1,0:T(8,128)(2,1)S(1)}, u32[]{:S(2)}, u32[]{:S(2)}) collective-permute-start(bf16[272,768]{1,0:T(8,128)(2,1)} %get-tuple-element.31), channel_id=1, source_target_pairs={{0,2},{1,3},{2,0},{3,1},{4,6},{5,7},{6,4},{7,5},{8,10},{9,11},{10,... | collective-permute-start | bytes 1253384 | tf_op jit(solution)/shard_map/ppermute | solution.py:396
  6.7 2.6 %collective-permute-start.1 = (bf16[272,768]{1,0:T(8,128)(2,1)}, bf16[272,768]{1,0:T(8,128)(2,1)S(1)}, u32[]{:S(2)}, u32[]{:S(2)}) collective-permute-start(bf16[272,768]{1,0:T(8,128)(2,1)} %get-tuple-element.32), channel_id=1, source_target_pairs={{0,4},{1,5},{2,6},{3,7},{4,0},{5,1},{6,2},{7,3},{8,12},{9,13},{10,... | collective-permute-start | bytes 1253384 | tf_op jit(solution)/shard_map/ppermute | solution.py:396
  9.3 4.2 %shard_map.38 = (bf16[272,768]{1,0:T(8,128)(2,1)}, bf16[272,768]{1,0:T(8,128)(2,1)}, s32[1,1024]{1,0:T(1,128)}) custom-call(bf16[1024,768]{1,0:T(8,128)(2,1)} %emb_hbm.3, s32[1,1024]{1,0:T(1,128)} %bitcast.5, s32[1,1024]{1,0:T(1,128)} %bitcast.7), custom_call_target="tpu_custom_call" | custom-call | flops 805306368 | bytes 3145728 | tf_op jit(solution)/shard_map/pallas_call | solution.py:136
  13.5 1.6 %collective-permute-start.4 = (bf16[272,768]{1,0:T(8,128)(2,1)}, bf16[272,768]{1,0:T(8,128)(2,1)S(1)}, u32[]{:S(2)}, u32[]{:S(2)}) collective-permute-start(bf16[272,768]{1,0:T(8,128)(2,1)} %get-tuple-element.30.refs_0_), channel_id=1, source_target_pairs={{0,16},{1,17},{2,18},{3,19},{4,20},{5,21},{6,22},{7,23},{8,24},{9,... | collective-permute-start | bytes 1253384 | tf_op jit(solution)/shard_map/ppermute | solution.py:396
  15.0 1.5 %collective-permute-start.2 = (bf16[272,768]{1,0:T(8,128)(2,1)}, bf16[272,768]{1,0:T(8,128)(2,1)S(1)}, u32[]{:S(2)}, u32[]{:S(2)}) collective-permute-start(bf16[272,768]{1,0:T(8,128)(2,1)} %get-tuple-element.30.refs_0_), channel_id=1, source_target_pairs={{0,1},{1,0},{2,3},{3,2},{4,5},{5,4},{6,7},{7,6},{8,9},{9,8},{10,11... | collective-permute-start | bytes 1253384 | tf_op jit(solution)/shard_map/ppermute | solution.py:396
  16.6 8.8 %collective-permute-done.refs_0_ = bf16[272,768]{1,0:T(8,128)(2,1)S(1)} collective-permute-done((bf16[272,768]{1,0:T(8,128)(2,1)}, bf16[272,768]{1,0:T(8,128)(2,1)S(1)}, u32[]{:S(2)}, u32[]{:S(2)}) %collective-permute-start) | collective-permute-done | bytes 417824 | tf_op jit(solution)/shard_map/ppermute | solution.py:396
  25.4 2.5 %collective-permute-done.1.refs_1_ = bf16[272,768]{1,0:T(8,128)(2,1)S(1)} collective-permute-done((bf16[272,768]{1,0:T(8,128)(2,1)}, bf16[272,768]{1,0:T(8,128)(2,1)S(1)}, u32[]{:S(2)}, u32[]{:S(2)}) %collective-permute-start.1) | collective-permute-done | bytes 417824 | tf_op jit(solution)/shard_map/ppermute | solution.py:396
  28.0 2.5 %collective-permute-start.5 = (bf16[272,768]{1,0:T(8,128)(2,1)S(1)}, bf16[272,768]{1,0:T(8,128)(2,1)S(1)}, u32[]{:S(2)}, u32[]{:S(2)}) collective-permute-start(bf16[272,768]{1,0:T(8,128)(2,1)S(1)} %copy-done.2), channel_id=1, source_target_pairs={{0,6},{1,7},{2,4},{3,5},{4,2},{5,3},{6,0},{7,1},{8,14},{9,15},{10,... | collective-permute-start | bytes 1253384 | tf_op jit(solution)/shard_map/ppermute | solution.py:396
  30.5 1.5 %collective-permute-start.7 = (bf16[528,768]{1,0:T(8,128)(2,1)S(1)}, bf16[528,768]{1,0:T(8,128)(2,1)S(1)}, u32[]{:S(2)}, u32[]{:S(2)}) collective-permute-start(bf16[528,768]{1,0:T(8,128)(2,1)S(1)} %shard_map.39.refs_1_), channel_id=1, source_target_pairs={{0,1},{1,0},{2,3},{3,2},{4,5},{5,4},{6,7},{7,6},{8,9},{9,8},{10,11... | collective-permute-start | bytes 2433032 | tf_op jit(solution)/shard_map/ppermute | solution.py:396
  32.1 1.5 %collective-permute-start.6 = (bf16[528,768]{1,0:T(8,128)(2,1)S(1)}, bf16[528,768]{1,0:T(8,128)(2,1)S(1)}, u32[]{:S(2)}, u32[]{:S(2)}) collective-permute-start(bf16[528,768]{1,0:T(8,128)(2,1)S(1)} %shard_map.39.refs_1_), channel_id=1, source_target_pairs={{0,16},{1,17},{2,18},{3,19},{4,20},{5,21},{6,22},{7,23},{8,24},{9,... | collective-permute-start | bytes 2433032 | tf_op jit(solution)/shard_map/ppermute | solution.py:396
  33.5 7.1 %collective-permute-done.5.refs_0_ = bf16[272,768]{1,0:T(8,128)(2,1)S(1)} collective-permute-done((bf16[272,768]{1,0:T(8,128)(2,1)S(1)}, bf16[272,768]{1,0:T(8,128)(2,1)S(1)}, u32[]{:S(2)}, u32[]{:S(2)}) %collective-permute-start.5) | collective-permute-done | bytes 417824 | tf_op jit(solution)/shard_map/ppermute | solution.py:396
  40.7 6.5 %collective-permute-done.7.refs_4_ = bf16[528,768]{1,0:T(8,128)(2,1)S(1)} collective-permute-done((bf16[528,768]{1,0:T(8,128)(2,1)S(1)}, bf16[528,768]{1,0:T(8,128)(2,1)S(1)}, u32[]{:S(2)}, u32[]{:S(2)}) %collective-permute-start.7) | collective-permute-done | bytes 811040 | tf_op jit(solution)/shard_map/ppermute | solution.py:396
  47.2 1.2 %collective-permute-done.6.refs_8_.refs_9_.refs_10_ = bf16[528,768]{1,0:T(8,128)(2,1)S(1)} collective-permute-done((bf16[528,768]{1,0:T(8,128)(2,1)S(1)}, bf16[528,768]{1,0:T(8,128)(2,1)S(1)}, u32[]{:S(2)}, u32[]{:S(2)}) %collective-permute-start.6) | collective-permute-done | bytes 811040 | tf_op jit(solution)/shard_map/ppermute | solution.py:396
  48.5 0.5 collective-permute-start.12
  49.0 1.1 %collective-permute-start.11 = (bf16[272,768]{1,0:T(8,128)(2,1)S(1)}, bf16[272,768]{1,0:T(8,128)(2,1)S(1)}, u32[]{:S(2)}, u32[]{:S(2)}) collective-permute-start(bf16[272,768]{1,0:T(8,128)(2,1)S(1)} %shard_map.40.refs_2_), channel_id=1, source_target_pairs={{0,16},{1,17},{2,18},{3,19},{4,20},{5,21},{6,22},{7,23},{8,24},{9,... | collective-permute-start | bytes 1253384 | tf_op jit(solution)/shard_map/ppermute | solution.py:396
  50.6 4.0 %shard_map.41.refs_12_ = f32[5,8,256]{2,1,0:T(8,128)S(1)} custom-call(bf16[272,768]{1,0:T(8,128)(2,1)S(1)} %copy-done, bf16[528,768]{1,0:T(8,128)(2,1)S(1)} %shard_map.39.refs_1_, bf16[272,768]{1,0:T(8,128)(2,1)S(1)} %shard_map.40.refs_2_, bf16[272,768]{1,0:T(8,128)(2,1)S(1)} %collective-permute-done.2.refs_3_, ...), custom_call_target="tpu_custom_call" | custom-call | flops 817889280 | bytes 5111808 | tf_op jit(solution)/shard_map/pallas_call | solution.py:302
  54.7 4.1 %shard_map.42.refs_15_ = f32[5,8,256]{2,1,0:T(8,128)S(1)} custom-call(bf16[272,768]{1,0:T(8,128)(2,1)S(1)} %copy-done, bf16[528,768]{1,0:T(8,128)(2,1)S(1)} %shard_map.39.refs_1_, bf16[272,768]{1,0:T(8,128)(2,1)S(1)} %shard_map.40.refs_2_, bf16[272,768]{1,0:T(8,128)(2,1)S(1)} %collective-permute-done.2.refs_3_, ...), custom_call_target="tpu_custom_call" | custom-call | flops 817889280 | bytes 6684672 | tf_op jit(solution)/shard_map/pallas_call | solution.py:302
  58.8 2.2 %collective-permute-done.11.refs_11_ = bf16[272,768]{1,0:T(8,128)(2,1)S(1)} collective-permute-done((bf16[272,768]{1,0:T(8,128)(2,1)S(1)}, bf16[272,768]{1,0:T(8,128)(2,1)S(1)}, u32[]{:S(2)}, u32[]{:S(2)}) %collective-permute-start.11) | collective-permute-done | bytes 417824 | tf_op jit(solution)/shard_map/ppermute | solution.py:396
  61.0 0.9 %collective-permute-done.8.refs_5_ = bf16[272,768]{1,0:T(8,128)(2,1)S(1)} collective-permute-done((bf16[272,768]{1,0:T(8,128)(2,1)S(1)}, bf16[272,768]{1,0:T(8,128)(2,1)S(1)}, u32[]{:S(2)}, u32[]{:S(2)}) %collective-permute-start.8) | collective-permute-done | bytes 417824 | tf_op jit(solution)/shard_map/ppermute | solution.py:396
  61.9 0.9 %collective-permute-done.14.refs_14_ = bf16[272,768]{1,0:T(8,128)(2,1)S(1)} collective-permute-done((bf16[272,768]{1,0:T(8,128)(2,1)S(1)}, bf16[272,768]{1,0:T(8,128)(2,1)S(1)}, u32[]{:S(2)}, u32[]{:S(2)}) %collective-permute-start.14) | collective-permute-done | bytes 417824 | tf_op jit(solution)/shard_map/ppermute | solution.py:396
  62.8 3.6 %shard_map.43 = f32[8,1,256]{2,1,0:T(1,128)S(1)} custom-call(bf16[272,768]{1,0:T(8,128)(2,1)S(1)} %copy-done, bf16[528,768]{1,0:T(8,128)(2,1)S(1)} %shard_map.39.refs_1_, bf16[272,768]{1,0:T(8,128)(2,1)S(1)} %shard_map.40.refs_2_, bf16[272,768]{1,0:T(8,128)(2,1)S(1)} %collective-permute-done.2.refs_3_, bf16[528,768]{1,0:T(8,128)(2,1)S(1)} %collective-permute-done.7.refs_4_, ...), custom_call_target="tpu_custom_call" | custom-call | flops 1283457024 | bytes 7864320 | tf_op jit(solution)/shard_map/pallas_call | solution.py:302
  66.4 11.1 %all_to_all.5.back_ref = f32[8,1,256]{2,1,0:T(1,128)S(1)} all-to-all(f32[8,1,256]{2,1,0:T(1,128)S(1)} %shard_map.43), channel_id=1, replica_groups=mesh['grp'=4,'mem'=8] {'mem'}, dimensions={0} | all-to-all | bytes 16384 | tf_op jit(solution)/shard_map/all_to_all | solution.py:510
  77.4 1.1 %shard_map.44 = f32[1,1024]{1,0:T(1,128)} custom-call(s32[1,1024]{1,0:T(1,128)S(1)} %copy-done.1, f32[8,1,256]{2,1,0:T(1,128)S(1)} %all_to_all.5.back_ref), custom_call_target="tpu_custom_call" | custom-call | tf_op jit(solution)/shard_map/pallas_call | solution.py:371
  (21 shorter events, 0.7 us)
Async XLA Ops:
  3.6 21.8 %collective-permute-start = (bf16[272,768]{1,0:T(8,128)(2,1)}, bf16[272,768]{1,0:T(8,128)(2,1)S(1)}, u32[]{:S(2)}, u32[]{:S(2)}) collective-permute-start(bf16[272,768]{1,0:T(8,128)(2,1)} %get-tuple-element.31), channel_id=1, source_target_pairs={{0,2},{1,3},{2,0},{3,1},{4,6},{5,7},{6,4},{7,5},{8,10},{9,11},{10,... | collective-permute-start | bytes 1253384 | tf_op jit(solution)/shard_map/ppermute | solution.py:396
  6.7 21.2 %collective-permute-start.1 = (bf16[272,768]{1,0:T(8,128)(2,1)}, bf16[272,768]{1,0:T(8,128)(2,1)S(1)}, u32[]{:S(2)}, u32[]{:S(2)}) collective-permute-start(bf16[272,768]{1,0:T(8,128)(2,1)} %get-tuple-element.32), channel_id=1, source_target_pairs={{0,4},{1,5},{2,6},{3,7},{4,0},{5,1},{6,2},{7,3},{8,12},{9,13},{10,... | collective-permute-start | bytes 1253384 | tf_op jit(solution)/shard_map/ppermute | solution.py:396
  13.5 14.5 %copy-start.2 = (bf16[272,768]{1,0:T(8,128)(2,1)S(1)}, bf16[272,768]{1,0:T(8,128)(2,1)}, u32[]{:S(2)}) copy-start(bf16[272,768]{1,0:T(8,128)(2,1)} %get-tuple-element.36) | copy-start | bytes 1253380
  13.5 14.4 %collective-permute-start.4 = (bf16[272,768]{1,0:T(8,128)(2,1)}, bf16[272,768]{1,0:T(8,128)(2,1)S(1)}, u32[]{:S(2)}, u32[]{:S(2)}) collective-permute-start(bf16[272,768]{1,0:T(8,128)(2,1)} %get-tuple-element.30.refs_0_), channel_id=1, source_target_pairs={{0,16},{1,17},{2,18},{3,19},{4,20},{5,21},{6,22},{7,23},{8,24},{9,... | collective-permute-start | bytes 1253384 | tf_op jit(solution)/shard_map/ppermute | solution.py:396
  15.0 12.9 %collective-permute-start.3 = (bf16[272,768]{1,0:T(8,128)(2,1)}, bf16[272,768]{1,0:T(8,128)(2,1)S(1)}, u32[]{:S(2)}, u32[]{:S(2)}) collective-permute-start(bf16[272,768]{1,0:T(8,128)(2,1)} %get-tuple-element.30.refs_0_), channel_id=1, source_target_pairs={{0,8},{1,9},{2,10},{3,11},{4,12},{5,13},{6,14},{7,15},{8,0},{9,1},... | collective-permute-start | bytes 1253384 | tf_op jit(solution)/shard_map/ppermute | solution.py:396
  15.0 12.9 %collective-permute-start.2 = (bf16[272,768]{1,0:T(8,128)(2,1)}, bf16[272,768]{1,0:T(8,128)(2,1)S(1)}, u32[]{:S(2)}, u32[]{:S(2)}) collective-permute-start(bf16[272,768]{1,0:T(8,128)(2,1)} %get-tuple-element.30.refs_0_), channel_id=1, source_target_pairs={{0,1},{1,0},{2,3},{3,2},{4,5},{5,4},{6,7},{7,6},{8,9},{9,8},{10,11... | collective-permute-start | bytes 1253384 | tf_op jit(solution)/shard_map/ppermute | solution.py:396
  28.0 22.6 %copy-start = (bf16[272,768]{1,0:T(8,128)(2,1)S(1)}, bf16[272,768]{1,0:T(8,128)(2,1)}, u32[]{:S(2)}) copy-start(bf16[272,768]{1,0:T(8,128)(2,1)} %get-tuple-element.30.refs_0_) | copy-start | bytes 1253380
  28.0 12.6 %collective-permute-start.5 = (bf16[272,768]{1,0:T(8,128)(2,1)S(1)}, bf16[272,768]{1,0:T(8,128)(2,1)S(1)}, u32[]{:S(2)}, u32[]{:S(2)}) collective-permute-start(bf16[272,768]{1,0:T(8,128)(2,1)S(1)} %copy-done.2), channel_id=1, source_target_pairs={{0,6},{1,7},{2,4},{3,5},{4,2},{5,3},{6,0},{7,1},{8,14},{9,15},{10,... | collective-permute-start | bytes 1253384 | tf_op jit(solution)/shard_map/ppermute | solution.py:396
  30.5 16.7 %collective-permute-start.7 = (bf16[528,768]{1,0:T(8,128)(2,1)S(1)}, bf16[528,768]{1,0:T(8,128)(2,1)S(1)}, u32[]{:S(2)}, u32[]{:S(2)}) collective-permute-start(bf16[528,768]{1,0:T(8,128)(2,1)S(1)} %shard_map.39.refs_1_), channel_id=1, source_target_pairs={{0,1},{1,0},{2,3},{3,2},{4,5},{5,4},{6,7},{7,6},{8,9},{9,8},{10,11... | collective-permute-start | bytes 2433032 | tf_op jit(solution)/shard_map/ppermute | solution.py:396
  32.1 16.4 %collective-permute-start.6 = (bf16[528,768]{1,0:T(8,128)(2,1)S(1)}, bf16[528,768]{1,0:T(8,128)(2,1)S(1)}, u32[]{:S(2)}, u32[]{:S(2)}) collective-permute-start(bf16[528,768]{1,0:T(8,128)(2,1)S(1)} %shard_map.39.refs_1_), channel_id=1, source_target_pairs={{0,16},{1,17},{2,18},{3,19},{4,20},{5,21},{6,22},{7,23},{8,24},{9,... | collective-permute-start | bytes 2433032 | tf_op jit(solution)/shard_map/ppermute | solution.py:396
  40.6 9.5 %collective-permute-start.9 = (bf16[528,768]{1,0:T(8,128)(2,1)S(1)}, bf16[528,768]{1,0:T(8,128)(2,1)S(1)}, u32[]{:S(2)}, u32[]{:S(2)}) collective-permute-start(bf16[528,768]{1,0:T(8,128)(2,1)S(1)} %shard_map.39.refs_1_), channel_id=1, source_target_pairs={{0,8},{1,9},{2,10},{3,11},{4,12},{5,13},{6,14},{7,15},{8,0},{9,1},... | collective-permute-start | bytes 2433032 | tf_op jit(solution)/shard_map/ppermute | solution.py:396
  48.5 6.2 %collective-permute-start.13 = (bf16[528,768]{1,0:T(8,128)(2,1)S(1)}, bf16[528,768]{1,0:T(8,128)(2,1)S(1)}, u32[]{:S(2)}, u32[]{:S(2)}) collective-permute-start(bf16[528,768]{1,0:T(8,128)(2,1)S(1)} %collective-permute-done.6.refs_8_.refs_9_.refs_10_), channel_id=1, source_target_pairs={{0,8},{1,9},{2,10},{3,11},{4,12},{5,13},{6,14},{7,15},{8,0},{9,1},... | collective-permute-start | bytes 2433032 | tf_op jit(solution)/shard_map/ppermute | solution.py:396
  48.5 6.2 %collective-permute-start.12 = (bf16[272,768]{1,0:T(8,128)(2,1)S(1)}, bf16[272,768]{1,0:T(8,128)(2,1)S(1)}, u32[]{:S(2)}, u32[]{:S(2)}) collective-permute-start(bf16[272,768]{1,0:T(8,128)(2,1)S(1)} %collective-permute-done.4.refs_7_.refs_8_.refs_9_), channel_id=1, source_target_pairs={{0,8},{1,9},{2,10},{3,11},{4,12},{5,13},{6,14},{7,15},{8,0},{9,1},... | collective-permute-start | bytes 1253384 | tf_op jit(solution)/shard_map/ppermute | solution.py:396
  49.0 5.7 %collective-permute-start.10 = (bf16[272,768]{1,0:T(8,128)(2,1)S(1)}, bf16[272,768]{1,0:T(8,128)(2,1)S(1)}, u32[]{:S(2)}, u32[]{:S(2)}) collective-permute-start(bf16[272,768]{1,0:T(8,128)(2,1)S(1)} %shard_map.40.refs_2_), channel_id=1, source_target_pairs={{0,8},{1,9},{2,10},{3,11},{4,12},{5,13},{6,14},{7,15},{8,0},{9,1},... | collective-permute-start | bytes 1253384 | tf_op jit(solution)/shard_map/ppermute | solution.py:396
  49.0 12.1 %collective-permute-start.11 = (bf16[272,768]{1,0:T(8,128)(2,1)S(1)}, bf16[272,768]{1,0:T(8,128)(2,1)S(1)}, u32[]{:S(2)}, u32[]{:S(2)}) collective-permute-start(bf16[272,768]{1,0:T(8,128)(2,1)S(1)} %shard_map.40.refs_2_), channel_id=1, source_target_pairs={{0,16},{1,17},{2,18},{3,19},{4,20},{5,21},{6,22},{7,23},{8,24},{9,... | collective-permute-start | bytes 1253384 | tf_op jit(solution)/shard_map/ppermute | solution.py:396
  50.1 11.8 %collective-permute-start.8 = (bf16[272,768]{1,0:T(8,128)(2,1)S(1)}, bf16[272,768]{1,0:T(8,128)(2,1)S(1)}, u32[]{:S(2)}, u32[]{:S(2)}) collective-permute-start(bf16[272,768]{1,0:T(8,128)(2,1)S(1)} %shard_map.40.refs_2_), channel_id=1, source_target_pairs={{0,1},{1,0},{2,3},{3,2},{4,5},{5,4},{6,7},{7,6},{8,9},{9,8},{10,11... | collective-permute-start | bytes 1253384 | tf_op jit(solution)/shard_map/ppermute | solution.py:396
  58.8 18.6 %copy-start.1 = (s32[1,1024]{1,0:T(1,128)S(1)}, s32[1,1024]{1,0:T(1,128)}, u32[]{:S(2)}) copy-start(s32[1,1024]{1,0:T(1,128)} %get-tuple-element.29.dest_ref) | copy-start | bytes 12292
  61.0 1.8 %collective-permute-start.14 = (bf16[272,768]{1,0:T(8,128)(2,1)S(1)}, bf16[272,768]{1,0:T(8,128)(2,1)S(1)}, u32[]{:S(2)}, u32[]{:S(2)}) collective-permute-start(bf16[272,768]{1,0:T(8,128)(2,1)S(1)} %collective-permute-done.11.refs_11_), channel_id=1, source_target_pairs={{0,8},{1,9},{2,10},{3,11},{4,12},{5,13},{6,14},{7,15},{8,0},{9,1},... | collective-permute-start | bytes 1253384 | tf_op jit(solution)/shard_map/ppermute | solution.py:396

commit v14 on v13

--- a/solution.py
+++ b/solution.py
@@ -11,7 +11,6 @@
 TILES = 4
 LABEL_ROWS = 16
 FAR = 1.0e9
-WANTED = 20_000_000_000
 PACK_VMEM = 60 * 1024 * 1024
 COMPARE_VMEM = 24 * 1024 * 1024
 NT = (((1,), (1,)), ((), ()))
@@ -157,7 +156,7 @@
     groups, halves, half, cap, blk = sizes
     array = dict(zip(names, refs))
     refs = refs[len(names) :]
-    block = {piece: (array[name], at * blk) for piece, (name, at) in spots.items()}
+    block = {piece: (array[name], row) for piece, (name, row, _, _) in spots.items()}
     prev = None
     if has_prev:
         prev, refs = refs[0], refs[1:]
@@ -171,9 +170,8 @@
     along = lax.axis_index("mem")
 
     def strip_of(piece):
-        ref, at = block[piece]
-        first = ref.shape[0] - LABEL_ROWS
-        return ref[first : first + LABEL_ROWS, at : at + blk]
+        name, _, first, left = spots[piece]
+        return array[name][first : first + LABEL_ROWS, left : left + blk]
 
     def keys_of(piece):
         strip = strip_of(piece).astype(jnp.float32)
@@ -278,12 +276,12 @@
     spots = {}
     arrays = {}
     for piece in sorted(used):
-        value, at = blocks[piece]
+        value, *where = blocks[piece]
         name = next((n for n, v in arrays.items() if v is value), None)
         if name is None:
             name = len(arrays)
             arrays[name] = value
-        spots[piece] = (name, at)
+        spots[piece] = (name, *where)
     names = list(arrays)
     width = arrays[0].shape[1]
     tile = groups * blk // TILES
@@ -318,7 +316,7 @@
     )(*operands)
 
 
-def join_kernel(*refs):
+def pair_kernel(*refs):
     out_ref, ins = refs[-1], refs[:-1]
     blk, width = ins[0].shape[0] - LABEL_ROWS, ins[0].shape[1]
     parts = []
@@ -329,17 +327,24 @@
     out_ref[len(ins) * blk :, :] = jnp.concatenate(parts, axis=1)
 
 
-def join(pieces, flops):
-    rows, width = pieces[0].shape
-    total = len(pieces) * (rows - LABEL_ROWS) + LABEL_ROWS
+def pile_kernel(*refs):
+    out_ref, ins = refs[-1], refs[:-1]
+    row, strip = 0, out_ref.shape[0] - LABEL_ROWS * len(ins)
+    for ref in ins:
+        rows = ref.shape[0] - LABEL_ROWS
+        out_ref[row : row + rows, :] = ref[0:rows, :]
+        out_ref[strip : strip + LABEL_ROWS, :] = ref[rows : rows + LABEL_ROWS, :]
+        row, strip = row + rows, strip + LABEL_ROWS
+
+
+def join(kernel, pieces, rows):
     vmem = pl.BlockSpec(memory_space=pltpu.VMEM)
     return pl.pallas_call(
-        join_kernel,
-        out_shape=jax.ShapeDtypeStruct((total, width), pieces[0].dtype),
+        kernel,
+        out_shape=jax.ShapeDtypeStruct((rows, pieces[0].shape[1]), pieces[0].dtype),
         in_specs=[vmem] * len(pieces),
         out_specs=vmem,
         compiler_params=pltpu.CompilerParams(vmem_limit_bytes=COMPARE_VMEM),
-        cost_estimate=pl.CostEstimate(flops=flops, bytes_accessed=0, transcendentals=0),
     )(*pieces)
 
 
@@ -422,47 +427,53 @@
         mine = swap(send, k, 0)
         if k < last:
             also = swap(sends[k + 1], k + 1, 0)
+            mine = join(pair_kernel, [mine, also], 2 * blk + LABEL_ROWS)
             if k == 1:
-                mine, also, *firsts = lax.optimization_barrier(
-                    (mine, also, *(held[d][0] for d in near))
-                )
+                mine, *firsts = lax.optimization_barrier((mine, *(held[d][0] for d in near)))
                 for d, value in zip(near, firsts):
                     held[d] = [value]
-            mine = join([mine, also], 0)
             after = mine
-        else:
-            mine = join([mine], WANTED)
         held[0].append(mine)
     spots = len(held[0])
     for spot in range(1, spots):
         for d in near:
             if d != side:
                 held[d].append(swap(held[0][spot], 0, d))
-    end, side_hop = held[0][-1], held[near[0]]
-    for spot in range(1, spots):
-        piece, end = lax.optimization_barrier((held[0][spot], end))
-        if spot == spots - 1:
-            piece, side_hop[spot - 1] = lax.optimization_barrier((piece, side_hop[spot - 1]))
-        held[side].append(swap(piece, 0, side))
-    for d in far:
-        held[d] = []
-        for spot in range(spots - 1):
-            piece, side_hop[spots - 2] = lax.optimization_barrier(
-                (held[d ^ side][spot], side_hop[spots - 2])
-            )
-            held[d].append(swap(piece, 0, side))
 
     index = {d: i for i, d in enumerate(offsets)}
     blocks = {}
 
-    def note():
-        for d in offsets:
-            for spot, value in enumerate(held[d]):
-                ks = [0] if spot == 0 else [k for k in (2 * spot - 1, 2 * spot) if k < groups]
-                for at, k in enumerate(ks):
-                    blocks[index[d], k] = (value, at)
-
-    note()
+    def ks_of(spot):
+        return [0] if spot == 0 else [k for k in (2 * spot - 1, 2 * spot) if k < groups]
+
+    def note(d, spot):
+        value = held[d][spot]
+        first = value.shape[0] - LABEL_ROWS
+        for at, k in enumerate(ks_of(spot)):
+            blocks[index[d], k] = (value, at * blk, first, at * blk)
+
+    for d in held:
+        for spot in range(len(held[d])):
+            note(d, spot)
+    pile = [(side, spot) for spot in range(1, spots)]
+    pile += [(d, spot) for d in far for spot in range(spots - 1)]
+    hops = [d for d in near if d != side and d not in [e ^ side for e in far]]
+    values = [held[d][spots - 2] for d in hops]
+    held[0][-1], *values = lax.optimization_barrier((held[0][-1], *values))
+    for d, value in zip(hops, values):
+        held[d][spots - 2] = value
+        note(d, spots - 2)
+    note(0, spots - 1)
+    parts = [held[d ^ side][spot] for d, spot in pile]
+    data = sum(part.shape[0] - LABEL_ROWS for part in parts)
+    moved = swap(join(pile_kernel, parts, data + LABEL_ROWS * len(parts)), 0, side)
+    row = 0
+    for n, (d, spot) in enumerate(pile):
+        for at, k in enumerate(ks_of(spot)):
+            blocks[index[d], k] = (moved, row + at * blk, data + LABEL_ROWS * n, at * blk)
+        row += parts[n].shape[0] - LABEL_ROWS
+    slow = {(index[d], k) for d, spot in pile for k in ks_of(spot)}
+
     starts = sorted({a for a, _ in pairs.values()})
     every = tuple(range(groups))
     early, middle, late = [], [], []
@@ -471,7 +482,6 @@
         pieces = [(b, k) for b in cols for k in every]
         soon = [(b, k) for b, k in pieces if k < last]
         if a == 0:
-            slow = {(index[d], k) for d in far for k in range(last)} | {(index[side], last)}
             ready = [piece for piece in pieces if piece in soon or piece[0] == 0]
             early.append((0, False, every, [piece for piece in ready if piece not in slow]))
             middle.append((0, False, every, [piece for piece in pieces if piece in slow]))
@@ -487,8 +497,8 @@
     prev = compare(blocks, middle, prev, (), 0, offsets, sizes)[0]
     for d in far:
         piece, prev = lax.optimization_barrier((held[d ^ side][-1], prev))
-        held[d].append(swap(piece, 0, side))
-    note()
+        held[d] = {spots - 1: swap(piece, 0, side)}
+        note(d, spots - 1)
     found = compare(blocks, late, prev, order, joined, offsets, sizes)
     if joined:
         back = found[0]

time: 78.8 us -> 77.2 us (0.980)
  waiting for transfers between devices: 30.1 us -> 27.6 us
  starting transfers between devices: 16.5 us -> 17.5 us
    ppermute x15 -> x12, waiting for transfers between devices: 30.1 us -> 27.6 us  [swap(): lax.ppermute(value, ('grp', 'mem'), [(i, i ^ mask) for i in range(devices)])]
    ppermute x15 -> x12, starting transfers between devices: 16.5 us -> 17.5 us  [swap(): lax.ppermute(value, ('grp', 'mem'), [(i, i ^ mask) for i in range(devices)])]
  transfers between devices with their start and end apart: 15 -> 12, of which waited for: 8 -> 8; matrix products, arithmetic and copies ran while one was open for 0% -> 0% of each run, Pallas kernels for 16% -> 16%
where the time goes in v14:
time: 77.2 us; the launch traced here: 77 us
  waiting for transfers between devices  27.6 us (36%)
  Pallas kernels  20.8 us (27%)
  starting transfers between devices  17.5 us (23%)
  blocking collectives  11 us (14%)
    ppermute x12, waiting for transfers between devices, swap(): lax.ppermute(value, ('grp', 'mem'), [(i, i ^ mask) for i in range(devices)])  27.6 us
    ppermute x12, starting transfers between devices, swap(): lax.ppermute(value, ('grp', 'mem'), [(i, i ^ mask) for i in range(devices)])  17.5 us
    pallas_call x3, Pallas kernels, compare(): pl.pallas_call(functools.partial(compare_kernel, sizes, jobs, names, spot...  11.8 us
    all_to_all x1, blocking collectives, on_device(): back = lax.all_to_all(back, 'mem', split_axis=0, concat_axis=0, tiled=True)  11 us
    pallas_call x2, Pallas kernels, pack(): pl.pallas_call(functools.partial(pack_kernel, sizes, ks, placed), out_sha...  7.74 us
  transfers between devices with their start and end apart: 12, of which 8 were waited for; matrix products, arithmetic and copies ran while one was open for 0% of the time, Pallas kernels for 16%

profile of v14, /device:TPU:0, one launch (start us, length us, event | category | flops | bytes accessed | tf_op | source)
XLA Modules:
  0.0 77.0 jit_solution(6783016055214875014)
XLA Ops:
  0.0 3.6 %shard_map.37 = (bf16[272,768]{1,0:T(8,128)(2,1)}, bf16[272,768]{1,0:T(8,128)(2,1)}) custom-call(bf16[1024,768]{1,0:T(8,128)(2,1)} %emb_hbm.3, s32[1,1024]{1,0:T(1,128)} %bitcast.4, s32[1,1024]{1,0:T(1,128)} %bitcast.6), custom_call_target="tpu_custom_call" | custom-call | flops 805306368 | bytes 3145728 | tf_op jit(solution)/shard_map/pallas_call | solution.py:135
  3.6 3.1 %collective-permute-start = (bf16[272,768]{1,0:T(8,128)(2,1)}, bf16[272,768]{1,0:T(8,128)(2,1)S(1)}, u32[]{:S(2)}, u32[]{:S(2)}) collective-permute-start(bf16[272,768]{1,0:T(8,128)(2,1)} %get-tuple-element.25), channel_id=1, source_target_pairs={{0,2},{1,3},{2,0},{3,1},{4,6},{5,7},{6,4},{7,5},{8,10},{9,11},{10,... | collective-permute-start | bytes 1253384 | tf_op jit(solution)/shard_map/ppermute | solution.py:401
  6.7 2.6 %collective-permute-start.1 = (bf16[272,768]{1,0:T(8,128)(2,1)}, bf16[272,768]{1,0:T(8,128)(2,1)S(1)}, u32[]{:S(2)}, u32[]{:S(2)}) collective-permute-start(bf16[272,768]{1,0:T(8,128)(2,1)} %get-tuple-element.26), channel_id=1, source_target_pairs={{0,4},{1,5},{2,6},{3,7},{4,0},{5,1},{6,2},{7,3},{8,12},{9,13},{10,... | collective-permute-start | bytes 1253384 | tf_op jit(solution)/shard_map/ppermute | solution.py:401
  9.3 4.2 %shard_map.38 = (bf16[272,768]{1,0:T(8,128)(2,1)}, bf16[272,768]{1,0:T(8,128)(2,1)}, s32[1,1024]{1,0:T(1,128)}) custom-call(bf16[1024,768]{1,0:T(8,128)(2,1)} %emb_hbm.3, s32[1,1024]{1,0:T(1,128)} %bitcast.5, s32[1,1024]{1,0:T(1,128)} %bitcast.7), custom_call_target="tpu_custom_call" | custom-call | flops 805306368 | bytes 3145728 | tf_op jit(solution)/shard_map/pallas_call | solution.py:135
  13.4 1.6 %collective-permute-start.2 = (bf16[272,768]{1,0:T(8,128)(2,1)}, bf16[272,768]{1,0:T(8,128)(2,1)S(1)}, u32[]{:S(2)}, u32[]{:S(2)}) collective-permute-start(bf16[272,768]{1,0:T(8,128)(2,1)} %get-tuple-element.24.refs_0_), channel_id=1, source_target_pairs={{0,1},{1,0},{2,3},{3,2},{4,5},{5,4},{6,7},{7,6},{8,9},{9,8},{10,11... | collective-permute-start | bytes 1253384 | tf_op jit(solution)/shard_map/ppermute | solution.py:401
  15.0 1.5 %collective-permute-start.4 = (bf16[272,768]{1,0:T(8,128)(2,1)}, bf16[272,768]{1,0:T(8,128)(2,1)S(1)}, u32[]{:S(2)}, u32[]{:S(2)}) collective-permute-start(bf16[272,768]{1,0:T(8,128)(2,1)} %get-tuple-element.24.refs_0_), channel_id=1, source_target_pairs={{0,16},{1,17},{2,18},{3,19},{4,20},{5,21},{6,22},{7,23},{8,24},{9,... | collective-permute-start | bytes 1253384 | tf_op jit(solution)/shard_map/ppermute | solution.py:401
  16.5 8.9 %collective-permute-done.refs_0_ = bf16[272,768]{1,0:T(8,128)(2,1)S(1)} collective-permute-done((bf16[272,768]{1,0:T(8,128)(2,1)}, bf16[272,768]{1,0:T(8,128)(2,1)S(1)}, u32[]{:S(2)}, u32[]{:S(2)}) %collective-permute-start) | collective-permute-done | bytes 417824 | tf_op jit(solution)/shard_map/ppermute | solution.py:401
  25.4 2.5 %collective-permute-done.1.refs_1_ = bf16[272,768]{1,0:T(8,128)(2,1)S(1)} collective-permute-done((bf16[272,768]{1,0:T(8,128)(2,1)}, bf16[272,768]{1,0:T(8,128)(2,1)S(1)}, u32[]{:S(2)}, u32[]{:S(2)}) %collective-permute-start.1) | collective-permute-done | bytes 417824 | tf_op jit(solution)/shard_map/ppermute | solution.py:401
  28.0 1.6 %collective-permute-start.6 = (bf16[528,768]{1,0:T(8,128)(2,1)S(1)}, bf16[528,768]{1,0:T(8,128)(2,1)S(1)}, u32[]{:S(2)}, u32[]{:S(2)}) collective-permute-start(bf16[528,768]{1,0:T(8,128)(2,1)S(1)} %shard_map.39.refs_0_.refs_1_), channel_id=1, source_target_pairs={{0,1},{1,0},{2,3},{3,2},{4,5},{5,4},{6,7},{7,6},{8,9},{9,8},{10,11... | collective-permute-start | bytes 2433032 | tf_op jit(solution)/shard_map/ppermute | solution.py:401
  29.6 1.5 %collective-permute-start.8 = (bf16[528,768]{1,0:T(8,128)(2,1)S(1)}, bf16[528,768]{1,0:T(8,128)(2,1)S(1)}, u32[]{:S(2)}, u32[]{:S(2)}) collective-permute-start(bf16[528,768]{1,0:T(8,128)(2,1)S(1)} %shard_map.39.refs_0_.refs_1_), channel_id=1, source_target_pairs={{0,16},{1,17},{2,18},{3,19},{4,20},{5,21},{6,22},{7,23},{8,24},{9,... | collective-permute-start | bytes 2433032 | tf_op jit(solution)/shard_map/ppermute | solution.py:401
  31.1 2.5 %collective-permute-start.5 = (bf16[272,768]{1,0:T(8,128)(2,1)}, bf16[272,768]{1,0:T(8,128)(2,1)S(1)}, u32[]{:S(2)}, u32[]{:S(2)}) collective-permute-start(bf16[272,768]{1,0:T(8,128)(2,1)} %get-tuple-element.29), channel_id=1, source_target_pairs={{0,6},{1,7},{2,4},{3,5},{4,2},{5,3},{6,0},{7,1},{8,14},{9,15},{10,... | collective-permute-start | bytes 1253384 | tf_op jit(solution)/shard_map/ppermute | solution.py:401
  33.5 8.6 %collective-permute-done.5.refs_1_.refs_2_ = bf16[272,768]{1,0:T(8,128)(2,1)S(1)} collective-permute-done((bf16[272,768]{1,0:T(8,128)(2,1)}, bf16[272,768]{1,0:T(8,128)(2,1)S(1)}, u32[]{:S(2)}, u32[]{:S(2)}) %collective-permute-start.5) | collective-permute-done | bytes 417824 | tf_op jit(solution)/shard_map/ppermute | solution.py:401
  42.1 4.9 %collective-permute-done.6.refs_4_ = bf16[528,768]{1,0:T(8,128)(2,1)S(1)} collective-permute-done((bf16[528,768]{1,0:T(8,128)(2,1)S(1)}, bf16[528,768]{1,0:T(8,128)(2,1)S(1)}, u32[]{:S(2)}, u32[]{:S(2)}) %collective-permute-start.6) | collective-permute-done | bytes 811040 | tf_op jit(solution)/shard_map/ppermute | solution.py:401
  47.0 0.2 collective-permute-done.8.refs_3_.refs_7_.refs_8_.refs_9_
  47.5 1.6 %collective-permute-start.10 = (bf16[272,768]{1,0:T(8,128)(2,1)S(1)}, bf16[272,768]{1,0:T(8,128)(2,1)S(1)}, u32[]{:S(2)}, u32[]{:S(2)}) collective-permute-start(bf16[272,768]{1,0:T(8,128)(2,1)S(1)} %collective-permute-done.5.refs_1_.refs_2_), channel_id=1, source_target_pairs={{0,16},{1,17},{2,18},{3,19},{4,20},{5,21},{6,22},{7,23},{8,24},{9,... | collective-permute-start | bytes 1253384 | tf_op jit(solution)/shard_map/ppermute | solution.py:401
  49.0 1.5 %collective-permute-start.7 = (bf16[272,768]{1,0:T(8,128)(2,1)S(1)}, bf16[272,768]{1,0:T(8,128)(2,1)S(1)}, u32[]{:S(2)}, u32[]{:S(2)}) collective-permute-start(bf16[272,768]{1,0:T(8,128)(2,1)S(1)} %collective-permute-done.5.refs_1_.refs_2_), channel_id=1, source_target_pairs={{0,1},{1,0},{2,3},{3,2},{4,5},{5,4},{6,7},{7,6},{8,9},{9,8},{10,11... | collective-permute-start | bytes 1253384 | tf_op jit(solution)/shard_map/ppermute | solution.py:401
  50.5 3.4 %shard_map.41.refs_9_ = f32[5,8,256]{2,1,0:T(8,128)S(1)} custom-call(bf16[272,768]{1,0:T(8,128)(2,1)S(1)} %copy-done, bf16[528,768]{1,0:T(8,128)(2,1)S(1)} %shard_map.39.refs_0_.refs_1_, bf16[272,768]{1,0:T(8,128)(2,1)S(1)} %collective-permute-done.5.refs_1_.refs_2_, bf16[272,768]{1,0:T(8,128)(2,1)S(1)} %collective-permute-done.2.refs_3_, ...), custom_call_target="tpu_custom_call" | custom-call | flops 692060160 | bytes 4325376 | tf_op jit(solution)/shard_map/pallas_call | solution.py:300
  54.0 4.7 %shard_map.42.refs_12_ = f32[5,8,256]{2,1,0:T(8,128)S(1)} custom-call(bf16[272,768]{1,0:T(8,128)(2,1)S(1)} %copy-done, bf16[528,768]{1,0:T(8,128)(2,1)S(1)} %shard_map.39.refs_0_.refs_1_, bf16[272,768]{1,0:T(8,128)(2,1)S(1)} %collective-permute-done.5.refs_1_.refs_2_, bf16[272,768]{1,0:T(8,128)(2,1)S(1)} %collective-permute-done.2.refs_3_, ...), custom_call_target="tpu_custom_call" | custom-call | flops 943718400 | bytes 6684672 | tf_op jit(solution)/shard_map/pallas_call | solution.py:300
  58.7 0.8 %collective-permute-done.10.refs_10_ = bf16[272,768]{1,0:T(8,128)(2,1)S(1)} collective-permute-done((bf16[272,768]{1,0:T(8,128)(2,1)S(1)}, bf16[272,768]{1,0:T(8,128)(2,1)S(1)}, u32[]{:S(2)}, u32[]{:S(2)}) %collective-permute-start.10) | collective-permute-done | bytes 417824 | tf_op jit(solution)/shard_map/ppermute | solution.py:401
  59.5 1.2 %collective-permute-done.7.refs_5_ = bf16[272,768]{1,0:T(8,128)(2,1)S(1)} collective-permute-done((bf16[272,768]{1,0:T(8,128)(2,1)S(1)}, bf16[272,768]{1,0:T(8,128)(2,1)S(1)}, u32[]{:S(2)}, u32[]{:S(2)}) %collective-permute-start.7) | collective-permute-done | bytes 417824 | tf_op jit(solution)/shard_map/ppermute | solution.py:401
  60.7 0.5 collective-permute-done.11.refs_11_
  61.3 3.6 %shard_map.43 = f32[8,1,256]{2,1,0:T(1,128)S(1)} custom-call(bf16[272,768]{1,0:T(8,128)(2,1)S(1)} %copy-done, bf16[528,768]{1,0:T(8,128)(2,1)S(1)} %shard_map.39.refs_0_.refs_1_, bf16[272,768]{1,0:T(8,128)(2,1)S(1)} %collective-permute-done.5.refs_1_.refs_2_, bf16[272,768]{1,0:T(8,128)(2,1)S(1)} %collective-permute-done.2.refs_3_, ...), custom_call_target="tpu_custom_call" | custom-call | flops 1283457024 | bytes 7864320 | tf_op jit(solution)/shard_map/pallas_call | solution.py:300
  64.9 11.0 %all_to_all.5.back_ref = f32[8,1,256]{2,1,0:T(1,128)S(1)} all-to-all(f32[8,1,256]{2,1,0:T(1,128)S(1)} %shard_map.43), channel_id=1, replica_groups=mesh['grp'=4,'mem'=8] {'mem'}, dimensions={0} | all-to-all | bytes 16384 | tf_op jit(solution)/shard_map/all_to_all | solution.py:520
  75.9 1.1 %shard_map.44 = f32[1,1024]{1,0:T(1,128)} custom-call(s32[1,1024]{1,0:T(1,128)S(1)} %copy-done.1, f32[8,1,256]{2,1,0:T(1,128)S(1)} %all_to_all.5.back_ref), custom_call_target="tpu_custom_call" | custom-call | tf_op jit(solution)/shard_map/pallas_call | solution.py:376
  (13 shorter events, 0.3 us)
Async XLA Ops:
  3.6 21.8 %collective-permute-start = (bf16[272,768]{1,0:T(8,128)(2,1)}, bf16[272,768]{1,0:T(8,128)(2,1)S(1)}, u32[]{:S(2)}, u32[]{:S(2)}) collective-permute-start(bf16[272,768]{1,0:T(8,128)(2,1)} %get-tuple-element.25), channel_id=1, source_target_pairs={{0,2},{1,3},{2,0},{3,1},{4,6},{5,7},{6,4},{7,5},{8,10},{9,11},{10,... | collective-permute-start | bytes 1253384 | tf_op jit(solution)/shard_map/ppermute | solution.py:401
  6.7 21.2 %collective-permute-start.1 = (bf16[272,768]{1,0:T(8,128)(2,1)}, bf16[272,768]{1,0:T(8,128)(2,1)S(1)}, u32[]{:S(2)}, u32[]{:S(2)}) collective-permute-start(bf16[272,768]{1,0:T(8,128)(2,1)} %get-tuple-element.26), channel_id=1, source_target_pairs={{0,4},{1,5},{2,6},{3,7},{4,0},{5,1},{6,2},{7,3},{8,12},{9,13},{10,... | collective-permute-start | bytes 1253384 | tf_op jit(solution)/shard_map/ppermute | solution.py:401
  13.4 14.5 %collective-permute-start.2 = (bf16[272,768]{1,0:T(8,128)(2,1)}, bf16[272,768]{1,0:T(8,128)(2,1)S(1)}, u32[]{:S(2)}, u32[]{:S(2)}) collective-permute-start(bf16[272,768]{1,0:T(8,128)(2,1)} %get-tuple-element.24.refs_0_), channel_id=1, source_target_pairs={{0,1},{1,0},{2,3},{3,2},{4,5},{5,4},{6,7},{7,6},{8,9},{9,8},{10,11... | collective-permute-start | bytes 1253384 | tf_op jit(solution)/shard_map/ppermute | solution.py:401
  15.0 12.9 %collective-permute-start.3 = (bf16[272,768]{1,0:T(8,128)(2,1)}, bf16[272,768]{1,0:T(8,128)(2,1)S(1)}, u32[]{:S(2)}, u32[]{:S(2)}) collective-permute-start(bf16[272,768]{1,0:T(8,128)(2,1)} %get-tuple-element.24.refs_0_), channel_id=1, source_target_pairs={{0,8},{1,9},{2,10},{3,11},{4,12},{5,13},{6,14},{7,15},{8,0},{9,1},... | collective-permute-start | bytes 1253384 | tf_op jit(solution)/shard_map/ppermute | solution.py:401
  15.0 12.9 %collective-permute-start.4 = (bf16[272,768]{1,0:T(8,128)(2,1)}, bf16[272,768]{1,0:T(8,128)(2,1)S(1)}, u32[]{:S(2)}, u32[]{:S(2)}) collective-permute-start(bf16[272,768]{1,0:T(8,128)(2,1)} %get-tuple-element.24.refs_0_), channel_id=1, source_target_pairs={{0,16},{1,17},{2,18},{3,19},{4,20},{5,21},{6,22},{7,23},{8,24},{9,... | collective-permute-start | bytes 1253384 | tf_op jit(solution)/shard_map/ppermute | solution.py:401
  28.0 19.0 %collective-permute-start.6 = (bf16[528,768]{1,0:T(8,128)(2,1)S(1)}, bf16[528,768]{1,0:T(8,128)(2,1)S(1)}, u32[]{:S(2)}, u32[]{:S(2)}) collective-permute-start(bf16[528,768]{1,0:T(8,128)(2,1)S(1)} %shard_map.39.refs_0_.refs_1_), channel_id=1, source_target_pairs={{0,1},{1,0},{2,3},{3,2},{4,5},{5,4},{6,7},{7,6},{8,9},{9,8},{10,11... | collective-permute-start | bytes 2433032 | tf_op jit(solution)/shard_map/ppermute | solution.py:401
  29.6 17.7 %collective-permute-start.8 = (bf16[528,768]{1,0:T(8,128)(2,1)S(1)}, bf16[528,768]{1,0:T(8,128)(2,1)S(1)}, u32[]{:S(2)}, u32[]{:S(2)}) collective-permute-start(bf16[528,768]{1,0:T(8,128)(2,1)S(1)} %shard_map.39.refs_0_.refs_1_), channel_id=1, source_target_pairs={{0,16},{1,17},{2,18},{3,19},{4,20},{5,21},{6,22},{7,23},{8,24},{9,... | collective-permute-start | bytes 2433032 | tf_op jit(solution)/shard_map/ppermute | solution.py:401
  31.1 19.5 %copy-start = (bf16[272,768]{1,0:T(8,128)(2,1)S(1)}, bf16[272,768]{1,0:T(8,128)(2,1)}, u32[]{:S(2)}) copy-start(bf16[272,768]{1,0:T(8,128)(2,1)} %get-tuple-element.24.refs_0_) | copy-start | bytes 1253380
  31.1 11.1 %collective-permute-start.5 = (bf16[272,768]{1,0:T(8,128)(2,1)}, bf16[272,768]{1,0:T(8,128)(2,1)S(1)}, u32[]{:S(2)}, u32[]{:S(2)}) collective-permute-start(bf16[272,768]{1,0:T(8,128)(2,1)} %get-tuple-element.29), channel_id=1, source_target_pairs={{0,6},{1,7},{2,4},{3,5},{4,2},{5,3},{6,0},{7,1},{8,14},{9,15},{10,... | collective-permute-start | bytes 1253384 | tf_op jit(solution)/shard_map/ppermute | solution.py:401
  47.4 6.6 %collective-permute-start.9 = (bf16[1600,768]{1,0:T(8,128)(2,1)S(1)}, bf16[1600,768]{1,0:T(8,128)(2,1)S(1)}, u32[]{:S(2)}, u32[]{:S(2)}) collective-permute-start(bf16[1600,768]{1,0:T(8,128)(2,1)S(1)} %shard_map.40), channel_id=1, source_target_pairs={{0,8},{1,9},{2,10},{3,11},{4,12},{5,13},{6,14},{7,15},{8,0},{9,1},... | collective-permute-start | bytes 7372808 | tf_op jit(solution)/shard_map/ppermute | solution.py:401
  47.5 12.1 %collective-permute-start.10 = (bf16[272,768]{1,0:T(8,128)(2,1)S(1)}, bf16[272,768]{1,0:T(8,128)(2,1)S(1)}, u32[]{:S(2)}, u32[]{:S(2)}) collective-permute-start(bf16[272,768]{1,0:T(8,128)(2,1)S(1)} %collective-permute-done.5.refs_1_.refs_2_), channel_id=1, source_target_pairs={{0,16},{1,17},{2,18},{3,19},{4,20},{5,21},{6,22},{7,23},{8,24},{9,... | collective-permute-start | bytes 1253384 | tf_op jit(solution)/shard_map/ppermute | solution.py:401
  49.0 11.7 %collective-permute-start.7 = (bf16[272,768]{1,0:T(8,128)(2,1)S(1)}, bf16[272,768]{1,0:T(8,128)(2,1)S(1)}, u32[]{:S(2)}, u32[]{:S(2)}) collective-permute-start(bf16[272,768]{1,0:T(8,128)(2,1)S(1)} %collective-permute-done.5.refs_1_.refs_2_), channel_id=1, source_target_pairs={{0,1},{1,0},{2,3},{3,2},{4,5},{5,4},{6,7},{7,6},{8,9},{9,8},{10,11... | collective-permute-start | bytes 1253384 | tf_op jit(solution)/shard_map/ppermute | solution.py:401
  58.7 17.2 %copy-start.1 = (s32[1,1024]{1,0:T(1,128)S(1)}, s32[1,1024]{1,0:T(1,128)}, u32[]{:S(2)}) copy-start(s32[1,1024]{1,0:T(1,128)} %get-tuple-element.23.dest_ref) | copy-start | bytes 12292
  59.5 1.8 %collective-permute-start.11 = (bf16[272,768]{1,0:T(8,128)(2,1)S(1)}, bf16[272,768]{1,0:T(8,128)(2,1)S(1)}, u32[]{:S(2)}, u32[]{:S(2)}) collective-permute-start(bf16[272,768]{1,0:T(8,128)(2,1)S(1)} %collective-permute-done.10.refs_10_), channel_id=1, source_target_pairs={{0,8},{1,9},{2,10},{3,11},{4,12},{5,13},{6,14},{7,15},{8,0},{9,1},... | collective-permute-start | bytes 1253384 | tf_op jit(solution)/shard_map/ppermute | solution.py:401

commit v15 on v14

--- a/solution.py
+++ b/solution.py
@@ -88,14 +88,6 @@
     here = lax.axis_index("mem") // side
     dest = jnp.where(dest >= 0, dest ^ (here * blk), -1)
 
-    units_of = []
-    for j in range(rows // step):
-        loads[2 + j].wait()
-        wide = emb_ref[j * step : (j + 1) * step, :].astype(jnp.float32)
-        total = jnp.sum(wide * wide, axis=1, keepdims=True)
-        units_of.append((wide * lax.rsqrt(total + 1e-06)).astype(jnp.bfloat16))
-    unit = jnp.concatenate(units_of, axis=0)
-
     field = lax.broadcasted_iota(jnp.int32, (LABEL_ROWS, rows), 0)
     labels = jnp.where(
         field == 0, safe_rank - which * half, jnp.where(field == 1, parity + 1, 0)
@@ -108,9 +100,12 @@
     leaving = []
     for n, k in enumerate(ks):
         pick = (slot + k * blk == dest).astype(jnp.float32).astype(jnp.bfloat16)
-        stage[n, 0:blk, :] = jnp.dot(pick, unit, preferred_element_type=jnp.float32).astype(
-            jnp.bfloat16
-        )
+        if n == 0:
+            for load in loads[2:]:
+                load.wait()
+        wide = jnp.dot(pick, emb_ref[...], preferred_element_type=jnp.float32)
+        total = jnp.sum(wide * wide, axis=1, keepdims=True)
+        stage[n, 0:blk, :] = (wide * lax.rsqrt(total + 1e-06)).astype(jnp.bfloat16)
         mine = lax.dot_general(labels, pick, NT, preferred_element_type=jnp.float32)
         high = unit_of + float(halves) * mine[1:2]
         strip = jnp.where(line == 0, mine[0:1], jnp.where(line == 1, high, 0.0))
@@ -152,7 +147,7 @@
     )(embeddings, cluster.reshape(1, rows), rank.reshape(1, rows))
 
 
-def compare_kernel(sizes, jobs, names, spots, starts, joined, has_prev, *refs):
+def compare_kernel(sizes, jobs, names, spots, starts, wholes, joined, has_prev, keep, reuse, *refs):
     groups, halves, half, cap, blk = sizes
     array = dict(zip(names, refs))
     refs = refs[len(names) :]
@@ -160,7 +155,13 @@
     prev = None
     if has_prev:
         prev, refs = refs[0], refs[1:]
-    outs, (key_col, turned, best) = refs[:-3], refs[-3:]
+    if reuse:
+        turned, *refs = refs
+        *outs, key_col, best = refs
+    elif keep:
+        *outs, turned, key_col, best = refs
+    else:
+        *outs, key_col, best, turned = refs
     rows = groups * blk
     per_tile = blk // TILES
     tile = rows // TILES
@@ -212,7 +213,8 @@
 
     def search(a, row, queries, mine, pieces, last, spot):
         width = mine.shape[1]
-        turned[spot, :, 0:width] = jnp.concatenate(queries, axis=0).T
+        if not reuse:
+            turned[spot, :, 0:width] = jnp.concatenate(queries, axis=0).T
         floor = floor_of(mine)
         acc = jnp.full((8, width), -1.0, jnp.float32)
         for at in range(0, len(pieces), groups):
@@ -258,7 +260,7 @@
                 turn = ((t - k) * per_tile) % tile
                 moved = pltpu.roll(found, turn, 1) if turn else found
                 total = jnp.where(lane == t, moved[t : t + 1], total)
-            if any(a == e and whole and k in ks for e, whole, ks, _ in jobs):
+            if (a, k) in wholes:
                 total = jnp.maximum(total, found[TILES : TILES + 1])
             at = (along // side) ^ k
             if joined:
@@ -267,7 +269,7 @@
                 outs[o][pl.ds(at, 1), 0, :] = total[:, :blk]
 
 
-def compare(blocks, jobs, prev, starts, joined, offsets, sizes):
+def compare(blocks, jobs, prev, starts, wholes, joined, offsets, sizes, keep=False, cache=None):
     groups, halves, half, cap, blk = sizes
     n_sets = len(offsets)
     used = {piece for *_, pieces in jobs for piece in pieces}
@@ -296,18 +298,36 @@
     else:
         out_shape = [jax.ShapeDtypeStruct((groups, 1, blk), jnp.float32)] * len(starts)
     operands = list(arrays.values()) + ([] if prev is None else [prev])
+    scratch = []
+    shape = (searches, width, tile)
+    if cache is not None:
+        operands.append(cache)
+    elif keep:
+        out_shape.append(jax.ShapeDtypeStruct(shape, jnp.bfloat16))
+    else:
+        scratch.append(pltpu.VMEM(shape, jnp.bfloat16))
     needed = {piece for *_, pieces in jobs for piece in pieces}
     return pl.pallas_call(
         functools.partial(
-            compare_kernel, sizes, jobs, names, spots, starts, joined, prev is not None
+            compare_kernel,
+            sizes,
+            jobs,
+            names,
+            spots,
+            starts,
+            wholes,
+            joined,
+            prev is not None,
+            keep,
+            cache is not None,
         ),
         out_shape=out_shape,
         in_specs=[vmem] * len(operands),
         out_specs=[vmem] * len(out_shape),
         scratch_shapes=[
             pltpu.VMEM((len(needed) * blk, 128), jnp.float32),
-            pltpu.VMEM((searches, width, tile), jnp.bfloat16),
             pltpu.VMEM((n_sets, 8, tile), jnp.float32),
+            *scratch,
         ],
         compiler_params=pltpu.CompilerParams(vmem_limit_bytes=COMPARE_VMEM),
         cost_estimate=pl.CostEstimate(
@@ -493,13 +513,22 @@
             late.append((index[a], True, (last,), soon))
     order = [index[a] for a in starts]
     joined = side if all(a < side for a in starts) else 0
-    prev = compare(blocks, early, None, (), 0, offsets, sizes)[0]
-    prev = compare(blocks, middle, prev, (), 0, offsets, sizes)[0]
-    for d in far:
-        piece, prev = lax.optimization_barrier((held[d ^ side][-1], prev))
-        held[d] = {spots - 1: swap(piece, 0, side)}
-        note(d, spots - 1)
-    found = compare(blocks, late, prev, order, joined, offsets, sizes)
+    prev = compare(blocks, early, None, (), (), 0, offsets, sizes)[0]
+    prev = compare(blocks, middle, prev, (), (), 0, offsets, sizes)[0]
+    wholes = [(a, k) for a, whole, ks, _ in late if whole for k in ks]
+    if far:
+        final = {(index[d], last) for d in far}
+        before = [(*job, [p for p in pieces if p not in final]) for *job, pieces in late]
+        late = [(*job, [p for p in pieces if p in final]) for *job, pieces in late]
+        late = [job for job in late if job[-1]]
+        for d in far:
+            piece, prev = lax.optimization_barrier((held[d ^ side][-1], prev))
+            held[d] = {spots - 1: swap(piece, 0, side)}
+            note(d, spots - 1)
+        prev, turned = compare(blocks, before, prev, (), (), 0, offsets, sizes, keep=True)
+        found = compare(blocks, late, prev, order, wholes, joined, offsets, sizes, cache=turned)
+    else:
+        found = compare(blocks, late, prev, order, wholes, joined, offsets, sizes)
     if joined:
         back = found[0]
     else:

time: 77.2 us -> 76 us (0.984)
  starting transfers between devices: 17.5 us -> 15.5 us
  waiting for transfers between devices: 27.6 us -> 29.3 us
  blocking collectives: 11 us -> 10 us
    ppermute x12, starting transfers between devices: 17.5 us -> 15.5 us  [swap(): lax.ppermute(value, ('grp', 'mem'), [(i, i ^ mask) for i in range(devices)])]
    ppermute x12, waiting for transfers between devices: 27.6 us -> 29.3 us  [swap(): lax.ppermute(value, ('grp', 'mem'), [(i, i ^ mask) for i in range(devices)])]
    all_to_all x1, blocking collectives: 11 us -> 10 us  [on_device(): back = lax.all_to_all(back, 'mem', split_axis=0, concat_axis=0, tiled=True)]
    pallas_call x3 -> x4, Pallas kernels: 11.8 us -> 11.9 us  [compare(): pl.pallas_call(functools.partial(compare_kernel, sizes, jobs, names, spot...]
  transfers between devices with their start and end apart: 12 -> 12, of which waited for: 8 -> 8; matrix products, arithmetic and copies ran while one was open for 0% -> 0% of each run, Pallas kernels for 16% -> 20%
where the time goes in v15:
time: 76 us; the launch traced here: 75.7 us
  waiting for transfers between devices  29.3 us (39%)
  Pallas kernels  20.8 us (27%)
  starting transfers between devices  15.5 us (20%)
  blocking collectives  10 us (13%)
    ppermute x12, waiting for transfers between devices, swap(): lax.ppermute(value, ('grp', 'mem'), [(i, i ^ mask) for i in range(devices)])  29.3 us
    ppermute x12, starting transfers between devices, swap(): lax.ppermute(value, ('grp', 'mem'), [(i, i ^ mask) for i in range(devices)])  15.5 us
    pallas_call x4, Pallas kernels, compare(): pl.pallas_call(functools.partial(compare_kernel, sizes, jobs, names, spot...  11.9 us
    all_to_all x1, blocking collectives, on_device(): back = lax.all_to_all(back, 'mem', split_axis=0, concat_axis=0, tiled=True)  10 us
    pallas_call x2, Pallas kernels, pack(): pl.pallas_call(functools.partial(pack_kernel, sizes, ks, placed), out_sha...  7.62 us
  transfers between devices with their start and end apart: 12, of which 8 were waited for; matrix products, arithmetic and copies ran while one was open for 0% of the time, Pallas kernels for 20%

profile of v15, /device:TPU:0, one launch (start us, length us, event | category | flops | bytes accessed | tf_op | source)
XLA Modules:
  0.0 75.7 jit_solution(2524440613755374695)
XLA Ops:
  0.0 3.5 %shard_map.37 = (bf16[272,768]{1,0:T(8,128)(2,1)}, bf16[272,768]{1,0:T(8,128)(2,1)}) custom-call(bf16[1024,768]{1,0:T(8,128)(2,1)} %emb_hbm.3, s32[1,1024]{1,0:T(1,128)} %bitcast.4, s32[1,1024]{1,0:T(1,128)} %bitcast.6), custom_call_target="tpu_custom_call" | custom-call | flops 805306368 | bytes 3145728 | tf_op jit(solution)/shard_map/pallas_call | solution.py:130
  3.5 3.1 %collective-permute-start = (bf16[272,768]{1,0:T(8,128)(2,1)}, bf16[272,768]{1,0:T(8,128)(2,1)S(1)}, u32[]{:S(2)}, u32[]{:S(2)}) collective-permute-start(bf16[272,768]{1,0:T(8,128)(2,1)} %get-tuple-element.27), channel_id=1, source_target_pairs={{0,2},{1,3},{2,0},{3,1},{4,6},{5,7},{6,4},{7,5},{8,10},{9,11},{10,... | collective-permute-start | bytes 1253384 | tf_op jit(solution)/shard_map/ppermute | solution.py:421
  6.6 2.6 %collective-permute-start.1 = (bf16[272,768]{1,0:T(8,128)(2,1)}, bf16[272,768]{1,0:T(8,128)(2,1)S(1)}, u32[]{:S(2)}, u32[]{:S(2)}) collective-permute-start(bf16[272,768]{1,0:T(8,128)(2,1)} %get-tuple-element.28), channel_id=1, source_target_pairs={{0,4},{1,5},{2,6},{3,7},{4,0},{5,1},{6,2},{7,3},{8,12},{9,13},{10,... | collective-permute-start | bytes 1253384 | tf_op jit(solution)/shard_map/ppermute | solution.py:421
  9.2 4.1 %shard_map.38 = (bf16[272,768]{1,0:T(8,128)(2,1)}, bf16[272,768]{1,0:T(8,128)(2,1)}, s32[1,1024]{1,0:T(1,128)}) custom-call(bf16[1024,768]{1,0:T(8,128)(2,1)} %emb_hbm.3, s32[1,1024]{1,0:T(1,128)} %bitcast.5, s32[1,1024]{1,0:T(1,128)} %bitcast.7), custom_call_target="tpu_custom_call" | custom-call | flops 805306368 | bytes 3145728 | tf_op jit(solution)/shard_map/pallas_call | solution.py:130
  13.3 1.6 %collective-permute-start.4 = (bf16[272,768]{1,0:T(8,128)(2,1)}, bf16[272,768]{1,0:T(8,128)(2,1)S(1)}, u32[]{:S(2)}, u32[]{:S(2)}) collective-permute-start(bf16[272,768]{1,0:T(8,128)(2,1)} %get-tuple-element.26.refs_0_), channel_id=1, source_target_pairs={{0,16},{1,17},{2,18},{3,19},{4,20},{5,21},{6,22},{7,23},{8,24},{9,... | collective-permute-start | bytes 1253384 | tf_op jit(solution)/shard_map/ppermute | solution.py:421
  14.9 1.5 %collective-permute-start.2 = (bf16[272,768]{1,0:T(8,128)(2,1)}, bf16[272,768]{1,0:T(8,128)(2,1)S(1)}, u32[]{:S(2)}, u32[]{:S(2)}) collective-permute-start(bf16[272,768]{1,0:T(8,128)(2,1)} %get-tuple-element.26.refs_0_), channel_id=1, source_target_pairs={{0,1},{1,0},{2,3},{3,2},{4,5},{5,4},{6,7},{7,6},{8,9},{9,8},{10,11... | collective-permute-start | bytes 1253384 | tf_op jit(solution)/shard_map/ppermute | solution.py:421
  16.4 8.9 %collective-permute-done.refs_0_ = bf16[272,768]{1,0:T(8,128)(2,1)S(1)} collective-permute-done((bf16[272,768]{1,0:T(8,128)(2,1)}, bf16[272,768]{1,0:T(8,128)(2,1)S(1)}, u32[]{:S(2)}, u32[]{:S(2)}) %collective-permute-start) | collective-permute-done | bytes 417824 | tf_op jit(solution)/shard_map/ppermute | solution.py:421
  25.3 2.5 %collective-permute-done.1.refs_1_ = bf16[272,768]{1,0:T(8,128)(2,1)S(1)} collective-permute-done((bf16[272,768]{1,0:T(8,128)(2,1)}, bf16[272,768]{1,0:T(8,128)(2,1)S(1)}, u32[]{:S(2)}, u32[]{:S(2)}) %collective-permute-start.1) | collective-permute-done | bytes 417824 | tf_op jit(solution)/shard_map/ppermute | solution.py:421
  27.9 1.6 %collective-permute-start.6 = (bf16[528,768]{1,0:T(8,128)(2,1)S(1)}, bf16[528,768]{1,0:T(8,128)(2,1)S(1)}, u32[]{:S(2)}, u32[]{:S(2)}) collective-permute-start(bf16[528,768]{1,0:T(8,128)(2,1)S(1)} %shard_map.39.refs_0_.refs_1_), channel_id=1, source_target_pairs={{0,1},{1,0},{2,3},{3,2},{4,5},{5,4},{6,7},{7,6},{8,9},{9,8},{10,11... | collective-permute-start | bytes 2433032 | tf_op jit(solution)/shard_map/ppermute | solution.py:421
  29.5 1.5 %collective-permute-start.9 = (bf16[528,768]{1,0:T(8,128)(2,1)S(1)}, bf16[528,768]{1,0:T(8,128)(2,1)S(1)}, u32[]{:S(2)}, u32[]{:S(2)}) collective-permute-start(bf16[528,768]{1,0:T(8,128)(2,1)S(1)} %shard_map.39.refs_0_.refs_1_), channel_id=1, source_target_pairs={{0,16},{1,17},{2,18},{3,19},{4,20},{5,21},{6,22},{7,23},{8,24},{9,... | collective-permute-start | bytes 2433032 | tf_op jit(solution)/shard_map/ppermute | solution.py:421
  31.0 2.5 %collective-permute-start.5 = (bf16[272,768]{1,0:T(8,128)(2,1)}, bf16[272,768]{1,0:T(8,128)(2,1)S(1)}, u32[]{:S(2)}, u32[]{:S(2)}) collective-permute-start(bf16[272,768]{1,0:T(8,128)(2,1)} %get-tuple-element.31), channel_id=1, source_target_pairs={{0,6},{1,7},{2,4},{3,5},{4,2},{5,3},{6,0},{7,1},{8,14},{9,15},{10,... | collective-permute-start | bytes 1253384 | tf_op jit(solution)/shard_map/ppermute | solution.py:421
  33.5 8.6 %collective-permute-done.5.refs_1_.refs_2_ = bf16[272,768]{1,0:T(8,128)(2,1)S(1)} collective-permute-done((bf16[272,768]{1,0:T(8,128)(2,1)}, bf16[272,768]{1,0:T(8,128)(2,1)S(1)}, u32[]{:S(2)}, u32[]{:S(2)}) %collective-permute-start.5) | collective-permute-done | bytes 417824 | tf_op jit(solution)/shard_map/ppermute | solution.py:421
  42.0 4.8 %collective-permute-done.6.refs_4_ = bf16[528,768]{1,0:T(8,128)(2,1)S(1)} collective-permute-done((bf16[528,768]{1,0:T(8,128)(2,1)S(1)}, bf16[528,768]{1,0:T(8,128)(2,1)S(1)}, u32[]{:S(2)}, u32[]{:S(2)}) %collective-permute-start.6) | collective-permute-done | bytes 811040 | tf_op jit(solution)/shard_map/ppermute | solution.py:421
  46.8 1.2 %collective-permute-done.9.refs_3_.refs_7_.refs_8_.refs_9_ = bf16[528,768]{1,0:T(8,128)(2,1)S(1)} collective-permute-done((bf16[528,768]{1,0:T(8,128)(2,1)S(1)}, bf16[528,768]{1,0:T(8,128)(2,1)S(1)}, u32[]{:S(2)}, u32[]{:S(2)}) %collective-permute-start.9) | collective-permute-done | bytes 811040 | tf_op jit(solution)/shard_map/ppermute | solution.py:421
  48.3 0.6 collective-permute-start.8
  48.9 0.5 collective-permute-start.7
  49.4 3.4 %shard_map.41.refs_9_ = f32[5,8,256]{2,1,0:T(8,128)S(1)} custom-call(bf16[272,768]{1,0:T(8,128)(2,1)S(1)} %copy-done, bf16[528,768]{1,0:T(8,128)(2,1)S(1)} %shard_map.39.refs_0_.refs_1_, bf16[272,768]{1,0:T(8,128)(2,1)S(1)} %collective-permute-done.5.refs_1_.refs_2_, bf16[272,768]{1,0:T(8,128)(2,1)S(1)} %collective-permute-done.2.refs_3_, ...), custom_call_target="tpu_custom_call" | custom-call | flops 692060160 | bytes 4325376 | tf_op jit(solution)/shard_map/pallas_call | solution.py:310
  53.0 4.5 %shard_map.42.refs_11_ = f32[5,8,256]{2,1,0:T(8,128)S(1)} custom-call(bf16[272,768]{1,0:T(8,128)(2,1)S(1)} %copy-done, bf16[528,768]{1,0:T(8,128)(2,1)S(1)} %shard_map.39.refs_0_.refs_1_, bf16[272,768]{1,0:T(8,128)(2,1)S(1)} %collective-permute-done.5.refs_1_.refs_2_, bf16[272,768]{1,0:T(8,128)(2,1)S(1)} %collective-permute-done.2.refs_3_, ...), custom_call_target="tpu_custom_call" | custom-call | flops 943718400 | bytes 6684672 | tf_op jit(solution)/shard_map/pallas_call | solution.py:310
  57.5 2.9 %collective-permute-done.8.refs_10_ = bf16[272,768]{1,0:T(8,128)(2,1)S(1)} collective-permute-done((bf16[272,768]{1,0:T(8,128)(2,1)S(1)}, bf16[272,768]{1,0:T(8,128)(2,1)S(1)}, u32[]{:S(2)}, u32[]{:S(2)}) %collective-permute-start.8) | collective-permute-done | bytes 417824 | tf_op jit(solution)/shard_map/ppermute | solution.py:421
  60.4 0.3 collective-permute-done.7.refs_5_
  60.6 3.0 %shard_map.43 = (f32[5,8,256]{2,1,0:T(8,128)S(1)}, bf16[9,768,256]{2,1,0:T(8,128)(2,1)S(1)}) custom-call(bf16[272,768]{1,0:T(8,128)(2,1)S(1)} %copy-done, bf16[528,768]{1,0:T(8,128)(2,1)S(1)} %shard_map.39.refs_0_.refs_1_, bf16[272,768]{1,0:T(8,128)(2,1)S(1)} %collective-permute-done.5.refs_1_.refs_2_, bf16[272,768]{1,0:T(8,128)(2,1)S(1)} %collective-permute-done.2.refs_3_, ...), custom_call_target="tpu_custom_call" | custom-call | flops 1157627904 | bytes 7471104 | tf_op jit(solution)/shard_map/pallas_call | solution.py:310
  63.7 0.9 %shard_map.44 = f32[8,1,256]{2,1,0:T(1,128)S(1)} custom-call(bf16[272,768]{1,0:T(8,128)(2,1)S(1)} %copy-done, bf16[528,768]{1,0:T(8,128)(2,1)S(1)} %shard_map.39.refs_0_.refs_1_, bf16[272,768]{1,0:T(8,128)(2,1)S(1)} %collective-permute-done.5.refs_1_.refs_2_, bf16[272,768]{1,0:T(8,128)(2,1)S(1)} %collective-permute-done.2.refs_3_, ...), custom_call_target="tpu_custom_call" | custom-call | flops 125829120 | bytes 3538944 | tf_op jit(solution)/shard_map/pallas_call | solution.py:310
  64.6 10.0 %all_to_all.5.back_ref = f32[8,1,256]{2,1,0:T(1,128)S(1)} all-to-all(f32[8,1,256]{2,1,0:T(1,128)S(1)} %shard_map.44), channel_id=1, replica_groups=mesh['grp'=4,'mem'=8] {'mem'}, dimensions={0} | all-to-all | bytes 16384 | tf_op jit(solution)/shard_map/all_to_all | solution.py:549
  74.6 1.1 %shard_map.45 = f32[1,1024]{1,0:T(1,128)} custom-call(s32[1,1024]{1,0:T(1,128)S(1)} %copy-done.1, f32[8,1,256]{2,1,0:T(1,128)S(1)} %all_to_all.5.back_ref), custom_call_target="tpu_custom_call" | custom-call | tf_op jit(solution)/shard_map/pallas_call | solution.py:396
  (14 shorter events, 0.4 us)
Async XLA Ops:
  3.5 21.8 %collective-permute-start = (bf16[272,768]{1,0:T(8,128)(2,1)}, bf16[272,768]{1,0:T(8,128)(2,1)S(1)}, u32[]{:S(2)}, u32[]{:S(2)}) collective-permute-start(bf16[272,768]{1,0:T(8,128)(2,1)} %get-tuple-element.27), channel_id=1, source_target_pairs={{0,2},{1,3},{2,0},{3,1},{4,6},{5,7},{6,4},{7,5},{8,10},{9,11},{10,... | collective-permute-start | bytes 1253384 | tf_op jit(solution)/shard_map/ppermute | solution.py:421
  6.6 21.2 %collective-permute-start.1 = (bf16[272,768]{1,0:T(8,128)(2,1)}, bf16[272,768]{1,0:T(8,128)(2,1)S(1)}, u32[]{:S(2)}, u32[]{:S(2)}) collective-permute-start(bf16[272,768]{1,0:T(8,128)(2,1)} %get-tuple-element.28), channel_id=1, source_target_pairs={{0,4},{1,5},{2,6},{3,7},{4,0},{5,1},{6,2},{7,3},{8,12},{9,13},{10,... | collective-permute-start | bytes 1253384 | tf_op jit(solution)/shard_map/ppermute | solution.py:421
  13.3 14.6 %collective-permute-start.4 = (bf16[272,768]{1,0:T(8,128)(2,1)}, bf16[272,768]{1,0:T(8,128)(2,1)S(1)}, u32[]{:S(2)}, u32[]{:S(2)}) collective-permute-start(bf16[272,768]{1,0:T(8,128)(2,1)} %get-tuple-element.26.refs_0_), channel_id=1, source_target_pairs={{0,16},{1,17},{2,18},{3,19},{4,20},{5,21},{6,22},{7,23},{8,24},{9,... | collective-permute-start | bytes 1253384 | tf_op jit(solution)/shard_map/ppermute | solution.py:421
  14.9 13.0 %collective-permute-start.3 = (bf16[272,768]{1,0:T(8,128)(2,1)}, bf16[272,768]{1,0:T(8,128)(2,1)S(1)}, u32[]{:S(2)}, u32[]{:S(2)}) collective-permute-start(bf16[272,768]{1,0:T(8,128)(2,1)} %get-tuple-element.26.refs_0_), channel_id=1, source_target_pairs={{0,8},{1,9},{2,10},{3,11},{4,12},{5,13},{6,14},{7,15},{8,0},{9,1},... | collective-permute-start | bytes 1253384 | tf_op jit(solution)/shard_map/ppermute | solution.py:421
  14.9 13.0 %collective-permute-start.2 = (bf16[272,768]{1,0:T(8,128)(2,1)}, bf16[272,768]{1,0:T(8,128)(2,1)S(1)}, u32[]{:S(2)}, u32[]{:S(2)}) collective-permute-start(bf16[272,768]{1,0:T(8,128)(2,1)} %get-tuple-element.26.refs_0_), channel_id=1, source_target_pairs={{0,1},{1,0},{2,3},{3,2},{4,5},{5,4},{6,7},{7,6},{8,9},{9,8},{10,11... | collective-permute-start | bytes 1253384 | tf_op jit(solution)/shard_map/ppermute | solution.py:421
  27.9 18.9 %collective-permute-start.6 = (bf16[528,768]{1,0:T(8,128)(2,1)S(1)}, bf16[528,768]{1,0:T(8,128)(2,1)S(1)}, u32[]{:S(2)}, u32[]{:S(2)}) collective-permute-start(bf16[528,768]{1,0:T(8,128)(2,1)S(1)} %shard_map.39.refs_0_.refs_1_), channel_id=1, source_target_pairs={{0,1},{1,0},{2,3},{3,2},{4,5},{5,4},{6,7},{7,6},{8,9},{9,8},{10,11... | collective-permute-start | bytes 2433032 | tf_op jit(solution)/shard_map/ppermute | solution.py:421
  29.5 18.6 %collective-permute-start.9 = (bf16[528,768]{1,0:T(8,128)(2,1)S(1)}, bf16[528,768]{1,0:T(8,128)(2,1)S(1)}, u32[]{:S(2)}, u32[]{:S(2)}) collective-permute-start(bf16[528,768]{1,0:T(8,128)(2,1)S(1)} %shard_map.39.refs_0_.refs_1_), channel_id=1, source_target_pairs={{0,16},{1,17},{2,18},{3,19},{4,20},{5,21},{6,22},{7,23},{8,24},{9,... | collective-permute-start | bytes 2433032 | tf_op jit(solution)/shard_map/ppermute | solution.py:421
  31.0 18.4 %copy-start = (bf16[272,768]{1,0:T(8,128)(2,1)S(1)}, bf16[272,768]{1,0:T(8,128)(2,1)}, u32[]{:S(2)}) copy-start(bf16[272,768]{1,0:T(8,128)(2,1)} %get-tuple-element.26.refs_0_) | copy-start | bytes 1253380
  31.0 11.0 %collective-permute-start.5 = (bf16[272,768]{1,0:T(8,128)(2,1)}, bf16[272,768]{1,0:T(8,128)(2,1)S(1)}, u32[]{:S(2)}, u32[]{:S(2)}) collective-permute-start(bf16[272,768]{1,0:T(8,128)(2,1)} %get-tuple-element.31), channel_id=1, source_target_pairs={{0,6},{1,7},{2,4},{3,5},{4,2},{5,3},{6,0},{7,1},{8,14},{9,15},{10,... | collective-permute-start | bytes 1253384 | tf_op jit(solution)/shard_map/ppermute | solution.py:421
  48.2 4.7 %collective-permute-start.10 = (bf16[1600,768]{1,0:T(8,128)(2,1)S(1)}, bf16[1600,768]{1,0:T(8,128)(2,1)S(1)}, u32[]{:S(2)}, u32[]{:S(2)}) collective-permute-start(bf16[1600,768]{1,0:T(8,128)(2,1)S(1)} %shard_map.40), channel_id=1, source_target_pairs={{0,8},{1,9},{2,10},{3,11},{4,12},{5,13},{6,14},{7,15},{8,0},{9,1},... | collective-permute-start | bytes 7372808 | tf_op jit(solution)/shard_map/ppermute | solution.py:421
  48.3 12.1 %collective-permute-start.8 = (bf16[272,768]{1,0:T(8,128)(2,1)S(1)}, bf16[272,768]{1,0:T(8,128)(2,1)S(1)}, u32[]{:S(2)}, u32[]{:S(2)}) collective-permute-start(bf16[272,768]{1,0:T(8,128)(2,1)S(1)} %collective-permute-done.5.refs_1_.refs_2_), channel_id=1, source_target_pairs={{0,16},{1,17},{2,18},{3,19},{4,20},{5,21},{6,22},{7,23},{8,24},{9,... | collective-permute-start | bytes 1253384 | tf_op jit(solution)/shard_map/ppermute | solution.py:421
  48.9 11.7 %collective-permute-start.7 = (bf16[272,768]{1,0:T(8,128)(2,1)S(1)}, bf16[272,768]{1,0:T(8,128)(2,1)S(1)}, u32[]{:S(2)}, u32[]{:S(2)}) collective-permute-start(bf16[272,768]{1,0:T(8,128)(2,1)S(1)} %collective-permute-done.5.refs_1_.refs_2_), channel_id=1, source_target_pairs={{0,1},{1,0},{2,3},{3,2},{4,5},{5,4},{6,7},{7,6},{8,9},{9,8},{10,11... | collective-permute-start | bytes 1253384 | tf_op jit(solution)/shard_map/ppermute | solution.py:421
  60.4 3.3 %collective-permute-start.11 = (bf16[272,768]{1,0:T(8,128)(2,1)S(1)}, bf16[272,768]{1,0:T(8,128)(2,1)S(1)}, u32[]{:S(2)}, u32[]{:S(2)}) collective-permute-start(bf16[272,768]{1,0:T(8,128)(2,1)S(1)} %collective-permute-done.8.refs_10_), channel_id=1, source_target_pairs={{0,8},{1,9},{2,10},{3,11},{4,12},{5,13},{6,14},{7,15},{8,0},{9,1},... | collective-permute-start | bytes 1253384 | tf_op jit(solution)/shard_map/ppermute | solution.py:421
  63.7 10.9 %copy-start.1 = (s32[1,1024]{1,0:T(1,128)S(1)}, s32[1,1024]{1,0:T(1,128)}, u32[]{:S(2)}) copy-start(s32[1,1024]{1,0:T(1,128)} %get-tuple-element.25.dest_ref) | copy-start | bytes 12292

commit v16 on v15

--- a/solution.py
+++ b/solution.py
@@ -11,6 +11,7 @@
 TILES = 4
 LABEL_ROWS = 16
 FAR = 1.0e9
+LONG = 20_000_000_000
 PACK_VMEM = 60 * 1024 * 1024
 COMPARE_VMEM = 24 * 1024 * 1024
 NT = (((1,), (1,)), ((), ()))
@@ -142,7 +143,7 @@
         ],
         compiler_params=pltpu.CompilerParams(vmem_limit_bytes=PACK_VMEM),
         cost_estimate=pl.CostEstimate(
-            flops=2 * len(ks) * blk * rows * width, bytes_accessed=4 * rows * width, transcendentals=0
+            flops=LONG if placed else 0, bytes_accessed=4 * rows * width, transcendentals=0
         ),
     )(embeddings, cluster.reshape(1, rows), rank.reshape(1, rows))
 
@@ -422,11 +423,11 @@
 
     offsets, pairs = cover(members)
     sends = [None] * groups
-    first = tuple(range(1, min(3, groups)))
+    first = (2,)
     for k, value in zip(first, pack(embeddings, cluster, rank, first, False, sizes)):
         sends[k] = value
-    rest = tuple(k for k in range(groups) if k not in first)
-    cluster, sends[1] = lax.optimization_barrier((cluster, sends[1]))
+    rest = (1, 0, *range(3, groups))
+    cluster, sends[2] = lax.optimization_barrier((cluster, sends[2]))
     *packed, dest = pack(embeddings, cluster, rank, rest, True, sizes)
     for k, value in zip(rest, packed):
         sends[k] = value

time: 76 us -> 79.8 us (1.050)
  waiting for transfers between devices: 29.3 us -> 32.2 us
  starting transfers between devices: 15.5 us -> 16.4 us
    ppermute x12, waiting for transfers between devices: 29.3 us -> 32.2 us  [swap(): lax.ppermute(value, ('grp', 'mem'), [(i, i ^ mask) for i in range(devices)])]
    ppermute x12, starting transfers between devices: 15.5 us -> 16.4 us  [swap(): lax.ppermute(value, ('grp', 'mem'), [(i, i ^ mask) for i in range(devices)])]
  transfers between devices with their start and end apart: 12 -> 12, of which waited for: 8 -> 7; matrix products, arithmetic and copies ran while one was open for 0% -> 0% of each run, Pallas kernels for 20% -> 20%
where the time goes in v16:
time: 79.8 us; the launch traced here: 79.6 us
  waiting for transfers between devices  32.2 us (40%)
  Pallas kernels  20.9 us (26%)
  starting transfers between devices  16.4 us (21%)
  blocking collectives  9.97 us (12%)
    ppermute x12, waiting for transfers between devices, swap(): lax.ppermute(value, ('grp', 'mem'), [(i, i ^ mask) for i in range(devices)])  32.2 us
    ppermute x12, starting transfers between devices, swap(): lax.ppermute(value, ('grp', 'mem'), [(i, i ^ mask) for i in range(devices)])  16.4 us
    pallas_call x4, Pallas kernels, compare(): pl.pallas_call(functools.partial(compare_kernel, sizes, jobs, names, spot...  11.9 us
    all_to_all x1, blocking collectives, on_device(): back = lax.all_to_all(back, 'mem', split_axis=0, concat_axis=0, tiled=True)  9.97 us
    pallas_call x2, Pallas kernels, pack(): pl.pallas_call(functools.partial(pack_kernel, sizes, ks, placed), out_sha...  7.68 us
  transfers between devices with their start and end apart: 12, of which 7 were waited for; matrix products, arithmetic and copies ran while one was open for 0% of the time, Pallas kernels for 20%

profile of v16, /device:TPU:0, one launch (start us, length us, event | category | flops | bytes accessed | tf_op | source)
XLA Modules:
  0.0 79.6 jit_solution(8962195220096570714)
XLA Ops:
  0.0 3.0 %shard_map.37 = bf16[272,768]{1,0:T(8,128)(2,1)} custom-call(bf16[1024,768]{1,0:T(8,128)(2,1)} %emb_hbm.3, s32[1,1024]{1,0:T(1,128)} %bitcast.4, s32[1,1024]{1,0:T(1,128)} %bitcast.6), custom_call_target="tpu_custom_call" | custom-call | bytes 3145728 | tf_op jit(solution)/shard_map/pallas_call | solution.py:131
  3.0 4.1 %collective-permute-start.1 = (bf16[272,768]{1,0:T(8,128)(2,1)}, bf16[272,768]{1,0:T(8,128)(2,1)S(1)}, u32[]{:S(2)}, u32[]{:S(2)}) collective-permute-start(bf16[272,768]{1,0:T(8,128)(2,1)} %shard_map.37), channel_id=1, source_target_pairs={{0,4},{1,5},{2,6},{3,7},{4,0},{5,1},{6,2},{7,3},{8,12},{9,13},{10,... | collective-permute-start | bytes 1253384 | tf_op jit(solution)/shard_map/ppermute | solution.py:422
  7.1 4.7 %shard_map.38 = (bf16[272,768]{1,0:T(8,128)(2,1)}, bf16[272,768]{1,0:T(8,128)(2,1)}, bf16[272,768]{1,0:T(8,128)(2,1)}, s32[1,1024]{1,0:T(1,128)}) custom-call(bf16[1024,768]{1,0:T(8,128)(2,1)} %emb_hbm.3, s32[1,1024]{1,0:T(1,128)} %bitcast.5, s32[1,1024]{1,0:T(1,128)} %bitcast.7), custom_call_target="tpu_custom_call" | custom-call | flops 20000000000 | bytes 3145728 | tf_op jit(solution)/shard_map/pallas_call | solution.py:131
  11.8 1.6 %collective-permute-start = (bf16[272,768]{1,0:T(8,128)(2,1)}, bf16[272,768]{1,0:T(8,128)(2,1)S(1)}, u32[]{:S(2)}, u32[]{:S(2)}) collective-permute-start(bf16[272,768]{1,0:T(8,128)(2,1)} %get-tuple-element.25), channel_id=1, source_target_pairs={{0,2},{1,3},{2,0},{3,1},{4,6},{5,7},{6,4},{7,5},{8,10},{9,11},{10,... | collective-permute-start | bytes 1253384 | tf_op jit(solution)/shard_map/ppermute | solution.py:422
  13.4 1.5 %collective-permute-start.4 = (bf16[272,768]{1,0:T(8,128)(2,1)}, bf16[272,768]{1,0:T(8,128)(2,1)S(1)}, u32[]{:S(2)}, u32[]{:S(2)}) collective-permute-start(bf16[272,768]{1,0:T(8,128)(2,1)} %get-tuple-element.24.refs_0_), channel_id=1, source_target_pairs={{0,16},{1,17},{2,18},{3,19},{4,20},{5,21},{6,22},{7,23},{8,24},{9,... | collective-permute-start | bytes 1253384 | tf_op jit(solution)/shard_map/ppermute | solution.py:422
  14.9 1.5 %collective-permute-start.2 = (bf16[272,768]{1,0:T(8,128)(2,1)}, bf16[272,768]{1,0:T(8,128)(2,1)S(1)}, u32[]{:S(2)}, u32[]{:S(2)}) collective-permute-start(bf16[272,768]{1,0:T(8,128)(2,1)} %get-tuple-element.24.refs_0_), channel_id=1, source_target_pairs={{0,1},{1,0},{2,3},{3,2},{4,5},{5,4},{6,7},{7,6},{8,9},{9,8},{10,11... | collective-permute-start | bytes 1253384 | tf_op jit(solution)/shard_map/ppermute | solution.py:422
  16.5 9.5 %collective-permute-done.1.refs_1_ = bf16[272,768]{1,0:T(8,128)(2,1)S(1)} collective-permute-done((bf16[272,768]{1,0:T(8,128)(2,1)}, bf16[272,768]{1,0:T(8,128)(2,1)S(1)}, u32[]{:S(2)}, u32[]{:S(2)}) %collective-permute-start.1) | collective-permute-done | bytes 417824 | tf_op jit(solution)/shard_map/ppermute | solution.py:422
  26.0 4.9 %collective-permute-done.refs_0_ = bf16[272,768]{1,0:T(8,128)(2,1)S(1)} collective-permute-done((bf16[272,768]{1,0:T(8,128)(2,1)}, bf16[272,768]{1,0:T(8,128)(2,1)S(1)}, u32[]{:S(2)}, u32[]{:S(2)}) %collective-permute-start) | collective-permute-done | bytes 417824 | tf_op jit(solution)/shard_map/ppermute | solution.py:422
  31.0 1.7 %collective-permute-start.6 = (bf16[528,768]{1,0:T(8,128)(2,1)S(1)}, bf16[528,768]{1,0:T(8,128)(2,1)S(1)}, u32[]{:S(2)}, u32[]{:S(2)}) collective-permute-start(bf16[528,768]{1,0:T(8,128)(2,1)S(1)} %shard_map.39.refs_0_.refs_1_), channel_id=1, source_target_pairs={{0,1},{1,0},{2,3},{3,2},{4,5},{5,4},{6,7},{7,6},{8,9},{9,8},{10,11... | collective-permute-start | bytes 2433032 | tf_op jit(solution)/shard_map/ppermute | solution.py:422
  32.7 1.5 %collective-permute-start.9 = (bf16[528,768]{1,0:T(8,128)(2,1)S(1)}, bf16[528,768]{1,0:T(8,128)(2,1)S(1)}, u32[]{:S(2)}, u32[]{:S(2)}) collective-permute-start(bf16[528,768]{1,0:T(8,128)(2,1)S(1)} %shard_map.39.refs_0_.refs_1_), channel_id=1, source_target_pairs={{0,16},{1,17},{2,18},{3,19},{4,20},{5,21},{6,22},{7,23},{8,24},{9,... | collective-permute-start | bytes 2433032 | tf_op jit(solution)/shard_map/ppermute | solution.py:422
  34.2 2.4 %collective-permute-start.5 = (bf16[272,768]{1,0:T(8,128)(2,1)}, bf16[272,768]{1,0:T(8,128)(2,1)S(1)}, u32[]{:S(2)}, u32[]{:S(2)}) collective-permute-start(bf16[272,768]{1,0:T(8,128)(2,1)} %get-tuple-element.29), channel_id=1, source_target_pairs={{0,6},{1,7},{2,4},{3,5},{4,2},{5,3},{6,0},{7,1},{8,14},{9,15},{10,... | collective-permute-start | bytes 1253384 | tf_op jit(solution)/shard_map/ppermute | solution.py:422
  36.5 9.4 %collective-permute-done.5.refs_1_.refs_2_ = bf16[272,768]{1,0:T(8,128)(2,1)S(1)} collective-permute-done((bf16[272,768]{1,0:T(8,128)(2,1)}, bf16[272,768]{1,0:T(8,128)(2,1)S(1)}, u32[]{:S(2)}, u32[]{:S(2)}) %collective-permute-start.5) | collective-permute-done | bytes 417824 | tf_op jit(solution)/shard_map/ppermute | solution.py:422
  45.9 3.8 %collective-permute-done.6.refs_4_ = bf16[528,768]{1,0:T(8,128)(2,1)S(1)} collective-permute-done((bf16[528,768]{1,0:T(8,128)(2,1)S(1)}, bf16[528,768]{1,0:T(8,128)(2,1)S(1)}, u32[]{:S(2)}, u32[]{:S(2)}) %collective-permute-start.6) | collective-permute-done | bytes 811040 | tf_op jit(solution)/shard_map/ppermute | solution.py:422
  49.7 1.3 %collective-permute-done.9.refs_3_.refs_7_.refs_8_.refs_9_ = bf16[528,768]{1,0:T(8,128)(2,1)S(1)} collective-permute-done((bf16[528,768]{1,0:T(8,128)(2,1)S(1)}, bf16[528,768]{1,0:T(8,128)(2,1)S(1)}, u32[]{:S(2)}, u32[]{:S(2)}) %collective-permute-start.9) | collective-permute-done | bytes 811040 | tf_op jit(solution)/shard_map/ppermute | solution.py:422
  51.3 1.5 %collective-permute-start.8 = (bf16[272,768]{1,0:T(8,128)(2,1)S(1)}, bf16[272,768]{1,0:T(8,128)(2,1)S(1)}, u32[]{:S(2)}, u32[]{:S(2)}) collective-permute-start(bf16[272,768]{1,0:T(8,128)(2,1)S(1)} %collective-permute-done.5.refs_1_.refs_2_), channel_id=1, source_target_pairs={{0,16},{1,17},{2,18},{3,19},{4,20},{5,21},{6,22},{7,23},{8,24},{9,... | collective-permute-start | bytes 1253384 | tf_op jit(solution)/shard_map/ppermute | solution.py:422
  52.8 0.5 collective-permute-start.7
  53.3 3.4 %shard_map.41.refs_9_ = f32[5,8,256]{2,1,0:T(8,128)S(1)} custom-call(bf16[272,768]{1,0:T(8,128)(2,1)S(1)} %copy-done, bf16[528,768]{1,0:T(8,128)(2,1)S(1)} %shard_map.39.refs_0_.refs_1_, bf16[272,768]{1,0:T(8,128)(2,1)S(1)} %collective-permute-done.5.refs_1_.refs_2_, bf16[272,768]{1,0:T(8,128)(2,1)S(1)} %collective-permute-done.2.refs_3_, ...), custom_call_target="tpu_custom_call" | custom-call | flops 692060160 | bytes 4325376 | tf_op jit(solution)/shard_map/pallas_call | solution.py:311
  56.8 4.5 %shard_map.42.refs_11_ = f32[5,8,256]{2,1,0:T(8,128)S(1)} custom-call(bf16[272,768]{1,0:T(8,128)(2,1)S(1)} %copy-done, bf16[528,768]{1,0:T(8,128)(2,1)S(1)} %shard_map.39.refs_0_.refs_1_, bf16[272,768]{1,0:T(8,128)(2,1)S(1)} %collective-permute-done.5.refs_1_.refs_2_, bf16[272,768]{1,0:T(8,128)(2,1)S(1)} %collective-permute-done.2.refs_3_, ...), custom_call_target="tpu_custom_call" | custom-call | flops 943718400 | bytes 6684672 | tf_op jit(solution)/shard_map/pallas_call | solution.py:311
  61.3 2.0 %collective-permute-done.8.refs_10_ = bf16[272,768]{1,0:T(8,128)(2,1)S(1)} collective-permute-done((bf16[272,768]{1,0:T(8,128)(2,1)S(1)}, bf16[272,768]{1,0:T(8,128)(2,1)S(1)}, u32[]{:S(2)}, u32[]{:S(2)}) %collective-permute-start.8) | collective-permute-done | bytes 417824 | tf_op jit(solution)/shard_map/ppermute | solution.py:422
  63.3 1.2 %collective-permute-done.7.refs_5_ = bf16[272,768]{1,0:T(8,128)(2,1)S(1)} collective-permute-done((bf16[272,768]{1,0:T(8,128)(2,1)S(1)}, bf16[272,768]{1,0:T(8,128)(2,1)S(1)}, u32[]{:S(2)}, u32[]{:S(2)}) %collective-permute-start.7) | collective-permute-done | bytes 417824 | tf_op jit(solution)/shard_map/ppermute | solution.py:422
  64.5 3.0 %shard_map.43 = (f32[5,8,256]{2,1,0:T(8,128)S(1)}, bf16[9,768,256]{2,1,0:T(8,128)(2,1)S(1)}) custom-call(bf16[272,768]{1,0:T(8,128)(2,1)S(1)} %copy-done, bf16[528,768]{1,0:T(8,128)(2,1)S(1)} %shard_map.39.refs_0_.refs_1_, bf16[272,768]{1,0:T(8,128)(2,1)S(1)} %collective-permute-done.5.refs_1_.refs_2_, bf16[272,768]{1,0:T(8,128)(2,1)S(1)} %collective-permute-done.2.refs_3_, ...), custom_call_target="tpu_custom_call" | custom-call | flops 1157627904 | bytes 7471104 | tf_op jit(solution)/shard_map/pallas_call | solution.py:311
  67.6 0.9 %shard_map.44 = f32[8,1,256]{2,1,0:T(1,128)S(1)} custom-call(bf16[272,768]{1,0:T(8,128)(2,1)S(1)} %copy-done, bf16[528,768]{1,0:T(8,128)(2,1)S(1)} %shard_map.39.refs_0_.refs_1_, bf16[272,768]{1,0:T(8,128)(2,1)S(1)} %collective-permute-done.5.refs_1_.refs_2_, bf16[272,768]{1,0:T(8,128)(2,1)S(1)} %collective-permute-done.2.refs_3_, ...), custom_call_target="tpu_custom_call" | custom-call | flops 125829120 | bytes 3538944 | tf_op jit(solution)/shard_map/pallas_call | solution.py:311
  68.5 10.0 %all_to_all.5.back_ref = f32[8,1,256]{2,1,0:T(1,128)S(1)} all-to-all(f32[8,1,256]{2,1,0:T(1,128)S(1)} %shard_map.44), channel_id=1, replica_groups=mesh['grp'=4,'mem'=8] {'mem'}, dimensions={0} | all-to-all | bytes 16384 | tf_op jit(solution)/shard_map/all_to_all | solution.py:550
  78.5 1.1 %shard_map.45 = f32[1,1024]{1,0:T(1,128)} custom-call(s32[1,1024]{1,0:T(1,128)S(1)} %copy-done.1, f32[8,1,256]{2,1,0:T(1,128)S(1)} %all_to_all.5.back_ref), custom_call_target="tpu_custom_call" | custom-call | tf_op jit(solution)/shard_map/pallas_call | solution.py:397
  (14 shorter events, 0.3 us)
Async XLA Ops:
  3.0 23.0 %collective-permute-start.1 = (bf16[272,768]{1,0:T(8,128)(2,1)}, bf16[272,768]{1,0:T(8,128)(2,1)S(1)}, u32[]{:S(2)}, u32[]{:S(2)}) collective-permute-start(bf16[272,768]{1,0:T(8,128)(2,1)} %shard_map.37), channel_id=1, source_target_pairs={{0,4},{1,5},{2,6},{3,7},{4,0},{5,1},{6,2},{7,3},{8,12},{9,13},{10,... | collective-permute-start | bytes 1253384 | tf_op jit(solution)/shard_map/ppermute | solution.py:422
  11.8 19.1 %collective-permute-start = (bf16[272,768]{1,0:T(8,128)(2,1)}, bf16[272,768]{1,0:T(8,128)(2,1)S(1)}, u32[]{:S(2)}, u32[]{:S(2)}) collective-permute-start(bf16[272,768]{1,0:T(8,128)(2,1)} %get-tuple-element.25), channel_id=1, source_target_pairs={{0,2},{1,3},{2,0},{3,1},{4,6},{5,7},{6,4},{7,5},{8,10},{9,11},{10,... | collective-permute-start | bytes 1253384 | tf_op jit(solution)/shard_map/ppermute | solution.py:422
  13.4 17.6 %collective-permute-start.4 = (bf16[272,768]{1,0:T(8,128)(2,1)}, bf16[272,768]{1,0:T(8,128)(2,1)S(1)}, u32[]{:S(2)}, u32[]{:S(2)}) collective-permute-start(bf16[272,768]{1,0:T(8,128)(2,1)} %get-tuple-element.24.refs_0_), channel_id=1, source_target_pairs={{0,16},{1,17},{2,18},{3,19},{4,20},{5,21},{6,22},{7,23},{8,24},{9,... | collective-permute-start | bytes 1253384 | tf_op jit(solution)/shard_map/ppermute | solution.py:422
  14.9 16.1 %collective-permute-start.3 = (bf16[272,768]{1,0:T(8,128)(2,1)}, bf16[272,768]{1,0:T(8,128)(2,1)S(1)}, u32[]{:S(2)}, u32[]{:S(2)}) collective-permute-start(bf16[272,768]{1,0:T(8,128)(2,1)} %get-tuple-element.24.refs_0_), channel_id=1, source_target_pairs={{0,8},{1,9},{2,10},{3,11},{4,12},{5,13},{6,14},{7,15},{8,0},{9,1},... | collective-permute-start | bytes 1253384 | tf_op jit(solution)/shard_map/ppermute | solution.py:422
  14.9 16.1 %collective-permute-start.2 = (bf16[272,768]{1,0:T(8,128)(2,1)}, bf16[272,768]{1,0:T(8,128)(2,1)S(1)}, u32[]{:S(2)}, u32[]{:S(2)}) collective-permute-start(bf16[272,768]{1,0:T(8,128)(2,1)} %get-tuple-element.24.refs_0_), channel_id=1, source_target_pairs={{0,1},{1,0},{2,3},{3,2},{4,5},{5,4},{6,7},{7,6},{8,9},{9,8},{10,11... | collective-permute-start | bytes 1253384 | tf_op jit(solution)/shard_map/ppermute | solution.py:422
  31.0 18.7 %collective-permute-start.6 = (bf16[528,768]{1,0:T(8,128)(2,1)S(1)}, bf16[528,768]{1,0:T(8,128)(2,1)S(1)}, u32[]{:S(2)}, u32[]{:S(2)}) collective-permute-start(bf16[528,768]{1,0:T(8,128)(2,1)S(1)} %shard_map.39.refs_0_.refs_1_), channel_id=1, source_target_pairs={{0,1},{1,0},{2,3},{3,2},{4,5},{5,4},{6,7},{7,6},{8,9},{9,8},{10,11... | collective-permute-start | bytes 2433032 | tf_op jit(solution)/shard_map/ppermute | solution.py:422
  32.7 18.3 %collective-permute-start.9 = (bf16[528,768]{1,0:T(8,128)(2,1)S(1)}, bf16[528,768]{1,0:T(8,128)(2,1)S(1)}, u32[]{:S(2)}, u32[]{:S(2)}) collective-permute-start(bf16[528,768]{1,0:T(8,128)(2,1)S(1)} %shard_map.39.refs_0_.refs_1_), channel_id=1, source_target_pairs={{0,16},{1,17},{2,18},{3,19},{4,20},{5,21},{6,22},{7,23},{8,24},{9,... | collective-permute-start | bytes 2433032 | tf_op jit(solution)/shard_map/ppermute | solution.py:422
  34.2 19.2 %copy-start = (bf16[272,768]{1,0:T(8,128)(2,1)S(1)}, bf16[272,768]{1,0:T(8,128)(2,1)}, u32[]{:S(2)}) copy-start(bf16[272,768]{1,0:T(8,128)(2,1)} %get-tuple-element.24.refs_0_) | copy-start | bytes 1253380
  34.2 11.7 %collective-permute-start.5 = (bf16[272,768]{1,0:T(8,128)(2,1)}, bf16[272,768]{1,0:T(8,128)(2,1)S(1)}, u32[]{:S(2)}, u32[]{:S(2)}) collective-permute-start(bf16[272,768]{1,0:T(8,128)(2,1)} %get-tuple-element.29), channel_id=1, source_target_pairs={{0,6},{1,7},{2,4},{3,5},{4,2},{5,3},{6,0},{7,1},{8,14},{9,15},{10,... | collective-permute-start | bytes 1253384 | tf_op jit(solution)/shard_map/ppermute | solution.py:422
  51.2 5.6 %collective-permute-start.10 = (bf16[1600,768]{1,0:T(8,128)(2,1)S(1)}, bf16[1600,768]{1,0:T(8,128)(2,1)S(1)}, u32[]{:S(2)}, u32[]{:S(2)}) collective-permute-start(bf16[1600,768]{1,0:T(8,128)(2,1)S(1)} %shard_map.40), channel_id=1, source_target_pairs={{0,8},{1,9},{2,10},{3,11},{4,12},{5,13},{6,14},{7,15},{8,0},{9,1},... | collective-permute-start | bytes 7372808 | tf_op jit(solution)/shard_map/ppermute | solution.py:422
  51.3 12.1 %collective-permute-start.8 = (bf16[272,768]{1,0:T(8,128)(2,1)S(1)}, bf16[272,768]{1,0:T(8,128)(2,1)S(1)}, u32[]{:S(2)}, u32[]{:S(2)}) collective-permute-start(bf16[272,768]{1,0:T(8,128)(2,1)S(1)} %collective-permute-done.5.refs_1_.refs_2_), channel_id=1, source_target_pairs={{0,16},{1,17},{2,18},{3,19},{4,20},{5,21},{6,22},{7,23},{8,24},{9,... | collective-permute-start | bytes 1253384 | tf_op jit(solution)/shard_map/ppermute | solution.py:422
  52.8 11.7 %collective-permute-start.7 = (bf16[272,768]{1,0:T(8,128)(2,1)S(1)}, bf16[272,768]{1,0:T(8,128)(2,1)S(1)}, u32[]{:S(2)}, u32[]{:S(2)}) collective-permute-start(bf16[272,768]{1,0:T(8,128)(2,1)S(1)} %collective-permute-done.5.refs_1_.refs_2_), channel_id=1, source_target_pairs={{0,1},{1,0},{2,3},{3,2},{4,5},{5,4},{6,7},{7,6},{8,9},{9,8},{10,11... | collective-permute-start | bytes 1253384 | tf_op jit(solution)/shard_map/ppermute | solution.py:422
  63.3 4.2 %collective-permute-start.11 = (bf16[272,768]{1,0:T(8,128)(2,1)S(1)}, bf16[272,768]{1,0:T(8,128)(2,1)S(1)}, u32[]{:S(2)}, u32[]{:S(2)}) collective-permute-start(bf16[272,768]{1,0:T(8,128)(2,1)S(1)} %collective-permute-done.8.refs_10_), channel_id=1, source_target_pairs={{0,8},{1,9},{2,10},{3,11},{4,12},{5,13},{6,14},{7,15},{8,0},{9,1},... | collective-permute-start | bytes 1253384 | tf_op jit(solution)/shard_map/ppermute | solution.py:422
  67.6 10.9 %copy-start.1 = (s32[1,1024]{1,0:T(1,128)S(1)}, s32[1,1024]{1,0:T(1,128)}, u32[]{:S(2)}) copy-start(s32[1,1024]{1,0:T(1,128)} %get-tuple-element.23.dest_ref) | copy-start | bytes 12292

commit v17 on v15

--- a/solution.py
+++ b/solution.py
@@ -484,15 +484,23 @@
         held[d][spots - 2] = value
         note(d, spots - 2)
     note(0, spots - 1)
-    parts = [held[d ^ side][spot] for d, spot in pile]
-    data = sum(part.shape[0] - LABEL_ROWS for part in parts)
-    moved = swap(join(pile_kernel, parts, data + LABEL_ROWS * len(parts)), 0, side)
-    row = 0
-    for n, (d, spot) in enumerate(pile):
-        for at, k in enumerate(ks_of(spot)):
-            blocks[index[d], k] = (moved, row + at * blk, data + LABEL_ROWS * n, at * blk)
-        row += parts[n].shape[0] - LABEL_ROWS
-    slow = {(index[d], k) for d, spot in pile for k in ks_of(spot)}
+    ahead = [(d, spot) for d, spot in pile if spot < (spots - 1 if d == side else 1)]
+    behind = [item for item in pile if item not in ahead] + [(d, spots - 1) for d in far]
+
+    def cross(some, after):
+        parts = [held[d ^ side][spot] for d, spot in some]
+        parts[0], *after = lax.optimization_barrier((parts[0], *after))
+        data = sum(part.shape[0] - LABEL_ROWS for part in parts)
+        moved = swap(join(pile_kernel, parts, data + LABEL_ROWS * len(parts)), 0, side)
+        row = 0
+        for n, (d, spot) in enumerate(some):
+            for at, k in enumerate(ks_of(spot)):
+                blocks[index[d], k] = (moved, row + at * blk, data + LABEL_ROWS * n, at * blk)
+            row += parts[n].shape[0] - LABEL_ROWS
+        return after
+
+    cross(ahead, [])
+    final = {(index[d], k) for d, spot in behind for k in ks_of(spot)}
 
     starts = sorted({a for a, _ in pairs.values()})
     every = tuple(range(groups))
@@ -501,34 +509,29 @@
         cols = [index[b] for _, (e, b) in sorted(pairs.items()) if e == a]
         pieces = [(b, k) for b in cols for k in every]
         soon = [(b, k) for b, k in pieces if k < last]
+        soon = [piece for piece in soon if piece not in final]
         if a == 0:
-            ready = [piece for piece in pieces if piece in soon or piece[0] == 0]
-            early.append((0, False, every, [piece for piece in ready if piece not in slow]))
-            middle.append((0, False, every, [piece for piece in pieces if piece in slow]))
-            done = early[-1][-1] + middle[-1][-1]
-            late.append((0, False, every, [piece for piece in pieces if piece not in done]))
+            done = [p for p in pieces if p in soon or p[0] == 0]
+            early.append((0, False, every, done))
+            late.append((0, False, every, [p for p in pieces if p not in done]))
         else:
             middle.append((index[a], False, every[:-1], soon))
-            late.append((index[a], False, every, [piece for piece in pieces if piece not in soon]))
+            late.append((index[a], False, every, [p for p in pieces if p not in soon]))
             late.append((index[a], True, (last,), soon))
     order = [index[a] for a in starts]
     joined = side if all(a < side for a in starts) else 0
     prev = compare(blocks, early, None, (), (), 0, offsets, sizes)[0]
     prev = compare(blocks, middle, prev, (), (), 0, offsets, sizes)[0]
     wholes = [(a, k) for a, whole, ks, _ in late if whole for k in ks]
-    if far:
-        final = {(index[d], last) for d in far}
-        before = [(*job, [p for p in pieces if p not in final]) for *job, pieces in late]
-        late = [(*job, [p for p in pieces if p in final]) for *job, pieces in late]
-        late = [job for job in late if job[-1]]
-        for d in far:
-            piece, prev = lax.optimization_barrier((held[d ^ side][-1], prev))
-            held[d] = {spots - 1: swap(piece, 0, side)}
-            note(d, spots - 1)
-        prev, turned = compare(blocks, before, prev, (), (), 0, offsets, sizes, keep=True)
-        found = compare(blocks, late, prev, order, wholes, joined, offsets, sizes, cache=turned)
-    else:
-        found = compare(blocks, late, prev, order, wholes, joined, offsets, sizes)
+    before = [(*job, [p for p in pieces if p not in final]) for *job, pieces in late]
+    late = [(*job, [p for p in pieces if p in final]) for *job, pieces in late]
+    late = [job for job in late if job[-1]]
+    hops = [d for d in near if d != side]
+    prev, *values = cross(behind, [prev, *(held[d][-1] for d in hops)])
+    for d, value in zip(hops, values):
+        blocks[index[d], last] = (value, *blocks[index[d], last][1:])
+    prev, turned = compare(blocks, before, prev, (), (), 0, offsets, sizes, keep=True)
+    found = compare(blocks, late, prev, order, wholes, joined, offsets, sizes, cache=turned)
     if joined:
         back = found[0]
     else:

time: 76 us -> 78 us (1.026)
  blocking collectives: 10 us -> 11.6 us
  waiting for transfers between devices: 29.3 us -> 30.1 us
    all_to_all x1, blocking collectives: 10 us -> 11.6 us  [on_device(): back = lax.all_to_all(back, 'mem', split_axis=0, concat_axis=0, tiled=True)]
    ppermute x12, waiting for transfers between devices: 29.3 us -> 30.1 us  [swap(): lax.ppermute(value, ('grp', 'mem'), [(i, i ^ mask) for i in range(devices)])]
  transfers between devices with their start and end apart: 12 -> 12, of which waited for: 8 -> 7; matrix products, arithmetic and copies ran while one was open for 0% -> 0% of each run, Pallas kernels for 20% -> 17%
where the time goes in v17:
time: 78 us; the launch traced here: 77.7 us
  waiting for transfers between devices  30.1 us (39%)
  Pallas kernels  20.4 us (26%)
  starting transfers between devices  15.5 us (20%)
  blocking collectives  11.6 us (15%)
    ppermute x12, waiting for transfers between devices, swap(): lax.ppermute(value, ('grp', 'mem'), [(i, i ^ mask) for i in range(devices)])  30.1 us
    ppermute x12, starting transfers between devices, swap(): lax.ppermute(value, ('grp', 'mem'), [(i, i ^ mask) for i in range(devices)])  15.5 us
    all_to_all x1, blocking collectives, on_device(): back = lax.all_to_all(back, 'mem', split_axis=0, concat_axis=0, tiled=True)  11.6 us
    pallas_call x4, Pallas kernels, compare(): pl.pallas_call(functools.partial(compare_kernel, sizes, jobs, names, spot...  11.4 us
    pallas_call x2, Pallas kernels, pack(): pl.pallas_call(functools.partial(pack_kernel, sizes, ks, placed), out_sha...  7.61 us
  transfers between devices with their start and end apart: 12, of which 7 were waited for; matrix products, arithmetic and copies ran while one was open for 0% of the time, Pallas kernels for 17%

profile of v17, /device:TPU:0, one launch (start us, length us, event | category | flops | bytes accessed | tf_op | source)
XLA Modules:
  0.0 77.7 jit_solution(5794774727092439532)
XLA Ops:
  0.0 3.5 %shard_map.37 = (bf16[272,768]{1,0:T(8,128)(2,1)}, bf16[272,768]{1,0:T(8,128)(2,1)}) custom-call(bf16[1024,768]{1,0:T(8,128)(2,1)} %emb_hbm.3, s32[1,1024]{1,0:T(1,128)} %bitcast.4, s32[1,1024]{1,0:T(1,128)} %bitcast.6), custom_call_target="tpu_custom_call" | custom-call | flops 805306368 | bytes 3145728 | tf_op jit(solution)/shard_map/pallas_call | solution.py:130
  3.5 3.1 %collective-permute-start = (bf16[272,768]{1,0:T(8,128)(2,1)}, bf16[272,768]{1,0:T(8,128)(2,1)S(1)}, u32[]{:S(2)}, u32[]{:S(2)}) collective-permute-start(bf16[272,768]{1,0:T(8,128)(2,1)} %get-tuple-element.29), channel_id=1, source_target_pairs={{0,2},{1,3},{2,0},{3,1},{4,6},{5,7},{6,4},{7,5},{8,10},{9,11},{10,... | collective-permute-start | bytes 1253384 | tf_op jit(solution)/shard_map/ppermute | solution.py:421
  6.6 2.6 %collective-permute-start.1 = (bf16[272,768]{1,0:T(8,128)(2,1)}, bf16[272,768]{1,0:T(8,128)(2,1)S(1)}, u32[]{:S(2)}, u32[]{:S(2)}) collective-permute-start(bf16[272,768]{1,0:T(8,128)(2,1)} %get-tuple-element.30), channel_id=1, source_target_pairs={{0,4},{1,5},{2,6},{3,7},{4,0},{5,1},{6,2},{7,3},{8,12},{9,13},{10,... | collective-permute-start | bytes 1253384 | tf_op jit(solution)/shard_map/ppermute | solution.py:421
  9.2 4.1 %shard_map.38 = (bf16[272,768]{1,0:T(8,128)(2,1)}, bf16[272,768]{1,0:T(8,128)(2,1)}, s32[1,1024]{1,0:T(1,128)}) custom-call(bf16[1024,768]{1,0:T(8,128)(2,1)} %emb_hbm.3, s32[1,1024]{1,0:T(1,128)} %bitcast.5, s32[1,1024]{1,0:T(1,128)} %bitcast.7), custom_call_target="tpu_custom_call" | custom-call | flops 805306368 | bytes 3145728 | tf_op jit(solution)/shard_map/pallas_call | solution.py:130
  13.3 1.6 %collective-permute-start.4 = (bf16[272,768]{1,0:T(8,128)(2,1)}, bf16[272,768]{1,0:T(8,128)(2,1)S(1)}, u32[]{:S(2)}, u32[]{:S(2)}) collective-permute-start(bf16[272,768]{1,0:T(8,128)(2,1)} %get-tuple-element.28.refs_0_), channel_id=1, source_target_pairs={{0,16},{1,17},{2,18},{3,19},{4,20},{5,21},{6,22},{7,23},{8,24},{9,... | collective-permute-start | bytes 1253384 | tf_op jit(solution)/shard_map/ppermute | solution.py:421
  14.9 1.5 %collective-permute-start.2 = (bf16[272,768]{1,0:T(8,128)(2,1)}, bf16[272,768]{1,0:T(8,128)(2,1)S(1)}, u32[]{:S(2)}, u32[]{:S(2)}) collective-permute-start(bf16[272,768]{1,0:T(8,128)(2,1)} %get-tuple-element.28.refs_0_), channel_id=1, source_target_pairs={{0,1},{1,0},{2,3},{3,2},{4,5},{5,4},{6,7},{7,6},{8,9},{9,8},{10,11... | collective-permute-start | bytes 1253384 | tf_op jit(solution)/shard_map/ppermute | solution.py:421
  16.4 8.9 %collective-permute-done.refs_0_ = bf16[272,768]{1,0:T(8,128)(2,1)S(1)} collective-permute-done((bf16[272,768]{1,0:T(8,128)(2,1)}, bf16[272,768]{1,0:T(8,128)(2,1)S(1)}, u32[]{:S(2)}, u32[]{:S(2)}) %collective-permute-start) | collective-permute-done | bytes 417824 | tf_op jit(solution)/shard_map/ppermute | solution.py:421
  25.3 2.5 %collective-permute-done.1.refs_1_ = bf16[272,768]{1,0:T(8,128)(2,1)S(1)} collective-permute-done((bf16[272,768]{1,0:T(8,128)(2,1)}, bf16[272,768]{1,0:T(8,128)(2,1)S(1)}, u32[]{:S(2)}, u32[]{:S(2)}) %collective-permute-start.1) | collective-permute-done | bytes 417824 | tf_op jit(solution)/shard_map/ppermute | solution.py:421
  28.1 1.6 %collective-permute-start.6 = (bf16[528,768]{1,0:T(8,128)(2,1)S(1)}, bf16[528,768]{1,0:T(8,128)(2,1)S(1)}, u32[]{:S(2)}, u32[]{:S(2)}) collective-permute-start(bf16[528,768]{1,0:T(8,128)(2,1)S(1)} %shard_map.39.refs_0_.refs_1_), channel_id=1, source_target_pairs={{0,1},{1,0},{2,3},{3,2},{4,5},{5,4},{6,7},{7,6},{8,9},{9,8},{10,11... | collective-permute-start | bytes 2433032 | tf_op jit(solution)/shard_map/ppermute | solution.py:421
  29.7 1.5 %collective-permute-start.8 = (bf16[528,768]{1,0:T(8,128)(2,1)S(1)}, bf16[528,768]{1,0:T(8,128)(2,1)S(1)}, u32[]{:S(2)}, u32[]{:S(2)}) collective-permute-start(bf16[528,768]{1,0:T(8,128)(2,1)S(1)} %shard_map.39.refs_0_.refs_1_), channel_id=1, source_target_pairs={{0,16},{1,17},{2,18},{3,19},{4,20},{5,21},{6,22},{7,23},{8,24},{9,... | collective-permute-start | bytes 2433032 | tf_op jit(solution)/shard_map/ppermute | solution.py:421
  31.2 2.5 %collective-permute-start.5 = (bf16[272,768]{1,0:T(8,128)(2,1)S(1)}, bf16[272,768]{1,0:T(8,128)(2,1)S(1)}, u32[]{:S(2)}, u32[]{:S(2)}) collective-permute-start(bf16[272,768]{1,0:T(8,128)(2,1)S(1)} %copy-done.2), channel_id=1, source_target_pairs={{0,6},{1,7},{2,4},{3,5},{4,2},{5,3},{6,0},{7,1},{8,14},{9,15},{10,... | collective-permute-start | bytes 1253384 | tf_op jit(solution)/shard_map/ppermute | solution.py:421
  33.6 10.9 %collective-permute-done.5.refs_2_.refs_0_ = bf16[272,768]{1,0:T(8,128)(2,1)S(1)} collective-permute-done((bf16[272,768]{1,0:T(8,128)(2,1)S(1)}, bf16[272,768]{1,0:T(8,128)(2,1)S(1)}, u32[]{:S(2)}, u32[]{:S(2)}) %collective-permute-start.5) | collective-permute-done | bytes 417824 | tf_op jit(solution)/shard_map/ppermute | solution.py:421
  44.5 0.5 collective-permute-start.10
  45.0 0.5 collective-permute-start.9
  45.5 3.5 %collective-permute-done.6.refs_4_.refs_1_ = bf16[528,768]{1,0:T(8,128)(2,1)S(1)} collective-permute-done((bf16[528,768]{1,0:T(8,128)(2,1)S(1)}, bf16[528,768]{1,0:T(8,128)(2,1)S(1)}, u32[]{:S(2)}, u32[]{:S(2)}) %collective-permute-start.6) | collective-permute-done | bytes 811040 | tf_op jit(solution)/shard_map/ppermute | solution.py:421
  49.0 1.6 %collective-permute-done.8.refs_8_.refs_5_.refs_1_.refs_9_ = bf16[528,768]{1,0:T(8,128)(2,1)S(1)} collective-permute-done((bf16[528,768]{1,0:T(8,128)(2,1)S(1)}, bf16[528,768]{1,0:T(8,128)(2,1)S(1)}, u32[]{:S(2)}, u32[]{:S(2)}) %collective-permute-start.8) | collective-permute-done | bytes 811040 | tf_op jit(solution)/shard_map/ppermute | solution.py:421
  50.6 4.3 %shard_map.41.refs_6_ = f32[5,8,256]{2,1,0:T(8,128)S(1)} custom-call(bf16[272,768]{1,0:T(8,128)(2,1)S(1)} %copy-done, bf16[528,768]{1,0:T(8,128)(2,1)S(1)} %shard_map.39.refs_0_.refs_1_, bf16[272,768]{1,0:T(8,128)(2,1)S(1)} %collective-permute-done.5.refs_2_.refs_0_, bf16[272,768]{1,0:T(8,128)(2,1)S(1)} %collective-permute-done.2.refs_3_.refs_0_, ...), custom_call_target="tpu_custom_call" | custom-call | flops 880803840 | bytes 5505024 | tf_op jit(solution)/shard_map/pallas_call | solution.py:310
  54.8 2.3 %shard_map.42.refs_11_ = f32[5,8,256]{2,1,0:T(8,128)S(1)} custom-call(bf16[272,768]{1,0:T(8,128)(2,1)S(1)} %collective-permute-done.2.refs_3_.refs_0_, bf16[528,768]{1,0:T(8,128)(2,1)S(1)} %collective-permute-done.6.refs_4_.refs_1_, bf16[272,768]{1,0:T(8,128)(2,1)S(1)} %collective-permute-done.3.refs_5_.refs_2_.refs_6_, ...), custom_call_target="tpu_custom_call" | custom-call | flops 440401920 | bytes 3932160 | tf_op jit(solution)/shard_map/pallas_call | solution.py:310
  57.2 1.6 %collective-permute-done.10.refs_2_.refs_10_ = bf16[272,768]{1,0:T(8,128)(2,1)S(1)} collective-permute-done((bf16[272,768]{1,0:T(8,128)(2,1)S(1)}, bf16[272,768]{1,0:T(8,128)(2,1)S(1)}, u32[]{:S(2)}, u32[]{:S(2)}) %collective-permute-start.10) | collective-permute-done | bytes 417824 | tf_op jit(solution)/shard_map/ppermute | solution.py:421
  58.9 2.3 %shard_map.44 = (f32[5,8,256]{2,1,0:T(8,128)S(1)}, bf16[9,768,256]{2,1,0:T(8,128)(2,1)S(1)}) custom-call(bf16[272,768]{1,0:T(8,128)(2,1)S(1)} %copy-done, bf16[528,768]{1,0:T(8,128)(2,1)S(1)} %shard_map.39.refs_0_.refs_1_, bf16[272,768]{1,0:T(8,128)(2,1)S(1)} %collective-permute-done.5.refs_2_.refs_0_, ...), custom_call_target="tpu_custom_call" | custom-call | flops 893386752 | bytes 6291456 | tf_op jit(solution)/shard_map/pallas_call | solution.py:310
  61.3 1.2 %collective-permute-done.11.refs_6_ = bf16[1072,768]{1,0:T(8,128)(2,1)S(1)} collective-permute-done((bf16[1072,768]{1,0:T(8,128)(2,1)S(1)}, bf16[1072,768]{1,0:T(8,128)(2,1)S(1)}, u32[]{:S(2)}, u32[]{:S(2)}) %collective-permute-start.11) | collective-permute-done | bytes 1646624 | tf_op jit(solution)/shard_map/ppermute | solution.py:421
  62.5 2.5 %shard_map.45 = f32[8,1,256]{2,1,0:T(1,128)S(1)} custom-call(bf16[272,768]{1,0:T(8,128)(2,1)S(1)} %copy-done, bf16[528,768]{1,0:T(8,128)(2,1)S(1)} %shard_map.39.refs_0_.refs_1_, bf16[272,768]{1,0:T(8,128)(2,1)S(1)} %collective-permute-done.5.refs_2_.refs_0_, bf16[272,768]{1,0:T(8,128)(2,1)S(1)} %collective-permute-done.2.refs_3_.refs_0_, ...), custom_call_target="tpu_custom_call" | custom-call | flops 503316480 | bytes 4718592 | tf_op jit(solution)/shard_map/pallas_call | solution.py:310
  65.0 11.6 %all_to_all.5.back_ref = f32[8,1,256]{2,1,0:T(1,128)S(1)} all-to-all(f32[8,1,256]{2,1,0:T(1,128)S(1)} %shard_map.45), channel_id=1, replica_groups=mesh['grp'=4,'mem'=8] {'mem'}, dimensions={0} | all-to-all | bytes 16384 | tf_op jit(solution)/shard_map/all_to_all | solution.py:552
  76.6 1.1 %shard_map.46 = f32[1,1024]{1,0:T(1,128)} custom-call(s32[1,1024]{1,0:T(1,128)S(1)} %copy-done.1, f32[8,1,256]{2,1,0:T(1,128)S(1)} %all_to_all.5.back_ref), custom_call_target="tpu_custom_call" | custom-call | tf_op jit(solution)/shard_map/pallas_call | solution.py:396
  (17 shorter events, 0.4 us)
Async XLA Ops:
  3.5 21.8 %collective-permute-start = (bf16[272,768]{1,0:T(8,128)(2,1)}, bf16[272,768]{1,0:T(8,128)(2,1)S(1)}, u32[]{:S(2)}, u32[]{:S(2)}) collective-permute-start(bf16[272,768]{1,0:T(8,128)(2,1)} %get-tuple-element.29), channel_id=1, source_target_pairs={{0,2},{1,3},{2,0},{3,1},{4,6},{5,7},{6,4},{7,5},{8,10},{9,11},{10,... | collective-permute-start | bytes 1253384 | tf_op jit(solution)/shard_map/ppermute | solution.py:421
  6.6 21.2 %collective-permute-start.1 = (bf16[272,768]{1,0:T(8,128)(2,1)}, bf16[272,768]{1,0:T(8,128)(2,1)S(1)}, u32[]{:S(2)}, u32[]{:S(2)}) collective-permute-start(bf16[272,768]{1,0:T(8,128)(2,1)} %get-tuple-element.30), channel_id=1, source_target_pairs={{0,4},{1,5},{2,6},{3,7},{4,0},{5,1},{6,2},{7,3},{8,12},{9,13},{10,... | collective-permute-start | bytes 1253384 | tf_op jit(solution)/shard_map/ppermute | solution.py:421
  13.3 17.8 %copy-start.2 = (bf16[272,768]{1,0:T(8,128)(2,1)S(1)}, bf16[272,768]{1,0:T(8,128)(2,1)}, u32[]{:S(2)}) copy-start(bf16[272,768]{1,0:T(8,128)(2,1)} %get-tuple-element.33) | copy-start | bytes 1253380
  13.3 37.3 %copy-start = (bf16[272,768]{1,0:T(8,128)(2,1)S(1)}, bf16[272,768]{1,0:T(8,128)(2,1)}, u32[]{:S(2)}) copy-start(bf16[272,768]{1,0:T(8,128)(2,1)} %get-tuple-element.28.refs_0_) | copy-start | bytes 1253380
  13.3 14.5 %collective-permute-start.4 = (bf16[272,768]{1,0:T(8,128)(2,1)}, bf16[272,768]{1,0:T(8,128)(2,1)S(1)}, u32[]{:S(2)}, u32[]{:S(2)}) collective-permute-start(bf16[272,768]{1,0:T(8,128)(2,1)} %get-tuple-element.28.refs_0_), channel_id=1, source_target_pairs={{0,16},{1,17},{2,18},{3,19},{4,20},{5,21},{6,22},{7,23},{8,24},{9,... | collective-permute-start | bytes 1253384 | tf_op jit(solution)/shard_map/ppermute | solution.py:421
  14.9 13.0 %collective-permute-start.3 = (bf16[272,768]{1,0:T(8,128)(2,1)}, bf16[272,768]{1,0:T(8,128)(2,1)S(1)}, u32[]{:S(2)}, u32[]{:S(2)}) collective-permute-start(bf16[272,768]{1,0:T(8,128)(2,1)} %get-tuple-element.28.refs_0_), channel_id=1, source_target_pairs={{0,8},{1,9},{2,10},{3,11},{4,12},{5,13},{6,14},{7,15},{8,0},{9,1},... | collective-permute-start | bytes 1253384 | tf_op jit(solution)/shard_map/ppermute | solution.py:421
  14.9 13.0 %collective-permute-start.2 = (bf16[272,768]{1,0:T(8,128)(2,1)}, bf16[272,768]{1,0:T(8,128)(2,1)S(1)}, u32[]{:S(2)}, u32[]{:S(2)}) collective-permute-start(bf16[272,768]{1,0:T(8,128)(2,1)} %get-tuple-element.28.refs_0_), channel_id=1, source_target_pairs={{0,1},{1,0},{2,3},{3,2},{4,5},{5,4},{6,7},{7,6},{8,9},{9,8},{10,11... | collective-permute-start | bytes 1253384 | tf_op jit(solution)/shard_map/ppermute | solution.py:421
  28.0 22.6 %collective-permute-start.7 = (bf16[800,768]{1,0:T(8,128)(2,1)S(1)}, bf16[800,768]{1,0:T(8,128)(2,1)S(1)}, u32[]{:S(2)}, u32[]{:S(2)}) collective-permute-start(bf16[800,768]{1,0:T(8,128)(2,1)S(1)} %shard_map.40), channel_id=1, source_target_pairs={{0,8},{1,9},{2,10},{3,11},{4,12},{5,13},{6,14},{7,15},{8,0},{9,1},... | collective-permute-start | bytes 3686408 | tf_op jit(solution)/shard_map/ppermute | solution.py:421
  28.1 20.9 %collective-permute-start.6 = (bf16[528,768]{1,0:T(8,128)(2,1)S(1)}, bf16[528,768]{1,0:T(8,128)(2,1)S(1)}, u32[]{:S(2)}, u32[]{:S(2)}) collective-permute-start(bf16[528,768]{1,0:T(8,128)(2,1)S(1)} %shard_map.39.refs_0_.refs_1_), channel_id=1, source_target_pairs={{0,1},{1,0},{2,3},{3,2},{4,5},{5,4},{6,7},{7,6},{8,9},{9,8},{10,11... | collective-permute-start | bytes 2433032 | tf_op jit(solution)/shard_map/ppermute | solution.py:421
  29.7 20.9 %collective-permute-start.8 = (bf16[528,768]{1,0:T(8,128)(2,1)S(1)}, bf16[528,768]{1,0:T(8,128)(2,1)S(1)}, u32[]{:S(2)}, u32[]{:S(2)}) collective-permute-start(bf16[528,768]{1,0:T(8,128)(2,1)S(1)} %shard_map.39.refs_0_.refs_1_), channel_id=1, source_target_pairs={{0,16},{1,17},{2,18},{3,19},{4,20},{5,21},{6,22},{7,23},{8,24},{9,... | collective-permute-start | bytes 2433032 | tf_op jit(solution)/shard_map/ppermute | solution.py:421
  31.2 13.3 %collective-permute-start.5 = (bf16[272,768]{1,0:T(8,128)(2,1)S(1)}, bf16[272,768]{1,0:T(8,128)(2,1)S(1)}, u32[]{:S(2)}, u32[]{:S(2)}) collective-permute-start(bf16[272,768]{1,0:T(8,128)(2,1)S(1)} %copy-done.2), channel_id=1, source_target_pairs={{0,6},{1,7},{2,4},{3,5},{4,2},{5,3},{6,0},{7,1},{8,14},{9,15},{10,... | collective-permute-start | bytes 1253384 | tf_op jit(solution)/shard_map/ppermute | solution.py:421
  44.5 14.3 %collective-permute-start.10 = (bf16[272,768]{1,0:T(8,128)(2,1)S(1)}, bf16[272,768]{1,0:T(8,128)(2,1)S(1)}, u32[]{:S(2)}, u32[]{:S(2)}) collective-permute-start(bf16[272,768]{1,0:T(8,128)(2,1)S(1)} %collective-permute-done.5.refs_2_.refs_0_), channel_id=1, source_target_pairs={{0,16},{1,17},{2,18},{3,19},{4,20},{5,21},{6,22},{7,23},{8,24},{9,... | collective-permute-start | bytes 1253384 | tf_op jit(solution)/shard_map/ppermute | solution.py:421
  45.0 13.7 %collective-permute-start.9 = (bf16[272,768]{1,0:T(8,128)(2,1)S(1)}, bf16[272,768]{1,0:T(8,128)(2,1)S(1)}, u32[]{:S(2)}, u32[]{:S(2)}) collective-permute-start(bf16[272,768]{1,0:T(8,128)(2,1)S(1)} %collective-permute-done.5.refs_2_.refs_0_), channel_id=1, source_target_pairs={{0,1},{1,0},{2,3},{3,2},{4,5},{5,4},{6,7},{7,6},{8,9},{9,8},{10,11... | collective-permute-start | bytes 1253384 | tf_op jit(solution)/shard_map/ppermute | solution.py:421
  58.9 3.6 %collective-permute-start.11 = (bf16[1072,768]{1,0:T(8,128)(2,1)S(1)}, bf16[1072,768]{1,0:T(8,128)(2,1)S(1)}, u32[]{:S(2)}, u32[]{:S(2)}) collective-permute-start(bf16[1072,768]{1,0:T(8,128)(2,1)S(1)} %shard_map.43), channel_id=1, source_target_pairs={{0,8},{1,9},{2,10},{3,11},{4,12},{5,13},{6,14},{7,15},{8,0},{9,1},... | collective-permute-start | bytes 4939784 | tf_op jit(solution)/shard_map/ppermute | solution.py:421
  62.4 14.2 %copy-start.1 = (s32[1,1024]{1,0:T(1,128)S(1)}, s32[1,1024]{1,0:T(1,128)}, u32[]{:S(2)}) copy-start(s32[1,1024]{1,0:T(1,128)} %get-tuple-element.27.dest_ref) | copy-start | bytes 12292
